TPU v7x, 32 devices: a whole 2x2x4 slice. The times are simulated.
32 devices in a mesh: section: 4 (over y, core), expert: 8 (over z, x).
Axes of the slice: x: 2, y: 2, z: 4, core: 2. Of those that a mesh axis runs over, the one named last changes fastest.
Arguments:
- act_in: bfloat16 [4, 1024, 2048], P('section', 'expert'), may hold values from -6 to 6
- saved_in: bfloat16 [4, 1024, 2048], P('section', 'expert'), may hold values from -6 to 6
- grad_in: bfloat16 [4, 1024, 2048], P('section', 'expert'), may hold values from -6 to 6
- norm_gain: float32 [4, 2048], P('section'), may hold values from 0.1 to 1.9
- w_gate: bfloat16 [4, 2048, 1536], P('section', None, 'expert'), may hold values from -0.125 to 0.125
- w_up: bfloat16 [4, 2048, 1536], P('section', None, 'expert'), may hold values from -0.125 to 0.125
- w_down: bfloat16 [4, 1536, 2048], P('section', 'expert'), may hold values from -0.21875 to 0.21875
- routes_fwd: int32 [4, 1024, 1], P('section', 'expert'), may hold values from 0 to 1; in each aligned block of 128 rows (0 to 127, 128 to 255, ..., all dimensions but the last counted through in order) at most 66 rows name the same one
- gates_fwd: float32 [4, 1024, 1], P('section', 'expert'), may hold values from 0.1 to 1
- routes_bwd: int32 [4, 1024, 1], P('section', 'expert'), may hold values from 0 to 1; in each aligned block of 128 rows (0 to 127, 128 to 255, ..., all dimensions but the last counted through in order) at most 66 rows name the same one
- gates_bwd: float32 [4, 1024, 1], P('section', 'expert'), may hold values from 0.1 to 1
Outputs:
- act_out: bfloat16 [4, 1024, 2048], P('section', 'expert')
- grad_out: bfloat16 [4, 1024, 2048], P('section', 'expert')
Inputs may be any that keep to these rules, and one draw needn't show every extreme that they name: `routes_fwd`: the 1 expert of a token differ; within the 128 tokens of one device no expert is named by more than 66 routes, and in some such blocks one expert is named by exactly 66. `routes_bwd`: as for routes_fwd.
All inputs are finite; a program needn't handle non-finite values.
Results may differ from a plain program's by a relative error of at most 0.005.
Values may be sent and summed in bfloat16 or wider, within the bound.
No kernel may reach another device: no remote copies, remote signals or barrier semaphores. Data moves between devices by JAX's collectives and lax.ppermute only.
A program may use at most 64 MiB of HBM per device.

v0:
```python
import jax
import jax.numpy as jnp
from jax import lax
from jax.sharding import PartitionSpec as P

SPLIT = 4


norm_eps = 1e-06


def passed_along(value, axis, steps):
    count = lax.axis_size(axis)
    pairs = [(source, (source + steps) % count) for source in range(count)]
    return lax.ppermute(value, axis, pairs)


def silu_parts(values):
    sigma = jax.nn.sigmoid(values)
    return (values * sigma, sigma * (1.0 + values * (1.0 - sigma)))


def normalize(block_rows, gain_row):
    values = block_rows.astype(jnp.float32)
    inv_scale = lax.rsqrt(jnp.mean(values * values, axis=-1, keepdims=True) + norm_eps)
    return (values * inv_scale * gain_row, inv_scale)


def slot_chooser(routes, experts, capacity):
    tok_count, top_count = routes.shape
    flat_routes = routes.reshape(tok_count * top_count)
    onehot = (flat_routes[:, None] == jnp.arange(experts, dtype=jnp.int32)[None, :]).astype(
        jnp.int32
    )
    before = jnp.cumsum(onehot, axis=0) - onehot
    slot_index = jnp.sum(before * onehot, axis=1)
    target = flat_routes * capacity + slot_index
    picks = (jnp.arange(experts * capacity, dtype=jnp.int32)[:, None] == target[None, :]).astype(
        jnp.int32
    )
    chooser = jnp.sum(picks.reshape(experts * capacity, tok_count, top_count), axis=2).astype(
        jnp.bfloat16
    )
    return (chooser, target)


def fan_out(packed, experts, capacity):
    row_width = packed.shape[1]
    spread = jnp.broadcast_to(
        packed.reshape(experts, 1, capacity, row_width), (experts, SPLIT, capacity, row_width)
    )
    return spread.reshape(experts * SPLIT, capacity, row_width)


def combine(returned, target, gate_rows, experts):
    row_groups, capacity, row_width = returned.shape
    summed = jnp.sum(
        returned.reshape(experts, SPLIT, capacity, row_width).astype(jnp.float32), axis=1
    )
    picked = jnp.take(summed.reshape(experts * capacity, row_width), target, axis=0)
    tok_count, top_count = gate_rows.shape
    return jnp.sum(picked.reshape(tok_count, top_count, row_width) * gate_rows[:, :, None], axis=1)


def forward_rows(slot_rows, gate_w, up_w, down_w):
    row_groups, row_count, row_width = slot_rows.shape
    flat_rows = slot_rows.reshape(row_groups * row_count, row_width)
    gate_pre = jnp.dot(flat_rows, gate_w, preferred_element_type=jnp.float32)
    up_pre = jnp.dot(flat_rows, up_w, preferred_element_type=jnp.float32)
    activation, _ = silu_parts(gate_pre)
    hidden = (activation * up_pre).astype(jnp.bfloat16)
    partial_value = jnp.dot(hidden, down_w, preferred_element_type=jnp.float32).astype(jnp.bfloat16)
    return partial_value.reshape(row_groups, row_count, row_width)


def backward_rows(slot_rows, grad_rows, gate_w, up_w, down_w):
    row_groups, row_count, row_width = slot_rows.shape
    flat_rows = slot_rows.reshape(row_groups * row_count, row_width)
    flat_grads = grad_rows.reshape(row_groups * row_count, row_width)
    contract = (((1,), (1,)), ((), ()))
    gate_pre = jnp.dot(flat_rows, gate_w, preferred_element_type=jnp.float32)
    up_pre = jnp.dot(flat_rows, up_w, preferred_element_type=jnp.float32)
    activation, derivative = silu_parts(gate_pre)
    d_hidden = lax.dot_general(flat_grads, down_w, contract, preferred_element_type=jnp.float32)
    d_gate = (d_hidden * up_pre * derivative).astype(jnp.bfloat16)
    d_up = (d_hidden * activation).astype(jnp.bfloat16)
    partial_value = lax.dot_general(d_gate, gate_w, contract, preferred_element_type=jnp.float32)
    partial_value = partial_value + lax.dot_general(
        d_up, up_w, contract, preferred_element_type=jnp.float32
    )
    return partial_value.astype(jnp.bfloat16).reshape(row_groups, row_count, row_width)


def per_device(
    act_in,
    saved_in,
    grad_in,
    norm_gain,
    w_gate,
    w_up,
    w_down,
    routes_fwd,
    gates_fwd,
    routes_bwd,
    gates_bwd,
):
    groups = lax.axis_size("expert")
    experts = groups // SPLIT
    tok_count = act_in.shape[1]
    top_count = routes_fwd.shape[2]
    capacity = min(tok_count, tok_count * top_count // experts + 2)
    gain_row = norm_gain[0]
    gate_w = w_gate[0]
    up_w = w_up[0]
    down_w = w_down[0]
    incoming = passed_along(act_in, "section", 1)[0]
    upstream = passed_along(grad_in, "section", -1)[0]
    n_fwd = normalize(incoming, gain_row)[0].astype(jnp.bfloat16)
    values_b, inv_scale = normalize(saved_in[0], gain_row)
    n_bwd = values_b.astype(jnp.bfloat16)
    chooser_f, target_f = slot_chooser(routes_fwd[0], experts, capacity)
    chooser_b, target_b = slot_chooser(routes_bwd[0], experts, capacity)
    packed_f = jnp.dot(chooser_f, n_fwd, preferred_element_type=jnp.float32).astype(jnp.bfloat16)
    packed_bg = jnp.dot(
        chooser_b, jnp.concatenate([n_bwd, upstream], axis=1), preferred_element_type=jnp.float32
    ).astype(jnp.bfloat16)
    width = n_fwd.shape[1]
    send_f = fan_out(packed_f, experts, capacity)
    send_b = fan_out(packed_bg[:, :width], experts, capacity)
    send_g = fan_out(packed_bg[:, width:], experts, capacity)
    back_f = lax.all_to_all(
        forward_rows(
            lax.all_to_all(send_f, "expert", split_axis=0, concat_axis=0, tiled=True),
            gate_w,
            up_w,
            down_w,
        ),
        "expert",
        split_axis=0,
        concat_axis=0,
        tiled=True,
    )
    back_b = lax.all_to_all(
        backward_rows(
            lax.all_to_all(send_b, "expert", split_axis=0, concat_axis=0, tiled=True),
            lax.all_to_all(send_g, "expert", split_axis=0, concat_axis=0, tiled=True),
            gate_w,
            up_w,
            down_w,
        ),
        "expert",
        split_axis=0,
        concat_axis=0,
        tiled=True,
    )
    mixed = combine(back_f, target_f, gates_fwd[0], experts)
    act_out = (incoming.astype(jnp.float32) + mixed).astype(jnp.bfloat16)
    d_norm = combine(back_b, target_b, gates_bwd[0], experts)
    scaled = d_norm * gain_row
    base = saved_in[0].astype(jnp.float32)
    d_input = inv_scale * (
        scaled - base * inv_scale * inv_scale * jnp.mean(scaled * base, axis=-1, keepdims=True)
    )
    grad_out = (upstream.astype(jnp.float32) + d_input).astype(jnp.bfloat16)
    return (act_out[None], grad_out[None])


def solution(mesh):
    in_specs = (
        P("section", "expert", None),
        P("section", "expert", None),
        P("section", "expert", None),
        P("section", None),
        P("section", None, "expert"),
        P("section", None, "expert"),
        P("section", "expert", None),
        P("section", "expert", None),
        P("section", "expert", None),
        P("section", "expert", None),
        P("section", "expert", None),
    )
    out_specs = (P("section", "expert", None), P("section", "expert", None))
    return jax.shard_map(
        per_device, mesh=mesh, in_specs=in_specs, out_specs=out_specs, check_vma=False
    )
```

profile of v0, /device:TPU:0, one launch (start us, length us, event | category | flops | bytes accessed | tf_op | source)
XLA Modules:
  0.0 322.4 jit_solution(13072038882653396403)
XLA Ops:
  0.6 2.5 collective-permute-start.1
  8.0 2.1 collective-permute-done.1
  13.3 5.8 %all-to-all-start.3 = ((bf16[8,66,2048]{2,1,0:T(8,128)(2,1)}), bf16[8,66,2048]{2,1,0:T(8,128)(2,1)S(1)}, u32[]{:S(2)}, u32[]{:S(2)}) async-start(bf16[8,66,2048]{2,1,0:T(8,128)(2,1)} %bitcast.70), calls=%async_computation.3 | async-start | bytes 4718592 | tf_op jit(solution)/shard_map/all_to_all | solution.py:145
  19.1 2.0 broadcast_in_dim.23
  21.1 52.8 %all-to-all-done.3 = bf16[8,66,2048]{2,1,0:T(8,128)(2,1)S(1)} async-done(((bf16[8,66,2048]{2,1,0:T(8,128)(2,1)}), bf16[8,66,2048]{2,1,0:T(8,128)(2,1)S(1)}, u32[]{:S(2)}, u32[]{:S(2)}) %all-to-all-start.3) | async-done | bytes 2162720 | tf_op jit(solution)/shard_map/all_to_all | solution.py:145
  73.9 2.8 broadcast_in_dim.24
  76.7 4.5 %all-to-all-start.2 = ((bf16[8,66,2048]{2,1,0:T(8,128)(2,1)}), bf16[8,66,2048]{2,1,0:T(8,128)(2,1)}, u32[]{:S(2)}, u32[]{:S(2)}) async-start(bf16[8,66,2048]{2,1,0:T(8,128)(2,1)} %bitcast.68), calls=%async_computation.2 | async-start | bytes 4718592 | tf_op jit(solution)/shard_map/all_to_all | solution.py:146
  81.7 8.4 %collective-permute-done = bf16[1,128,2048]{2,1,0:T(8,128)(2,1)} collective-permute-done((bf16[1,128,2048]{2,1,0:T(8,128)(2,1)}, bf16[1,128,2048]{2,1,0:T(8,128)(2,1)}, u32[]{:S(2)}, u32[]{:S(2)}) %collective-permute-start) | collective-permute-done | bytes 524320 | tf_op jit(solution)/shard_map/ppermute | solution.py:15
  91.4 2.3 convolution_convert_fusion.2
  93.7 2.0 broadcast_in_dim.18
  95.7 39.5 %all-to-all-done.2 = bf16[8,66,2048]{2,1,0:T(8,128)(2,1)} async-done(((bf16[8,66,2048]{2,1,0:T(8,128)(2,1)}), bf16[8,66,2048]{2,1,0:T(8,128)(2,1)}, u32[]{:S(2)}, u32[]{:S(2)}) %all-to-all-start.2) | async-done | bytes 2162720 | tf_op jit(solution)/shard_map/all_to_all | solution.py:146
  135.2 2.8 broadcast_in_dim.19
  138.0 4.4 %all-to-all-start = ((bf16[8,66,2048]{2,1,0:T(8,128)(2,1)}), bf16[8,66,2048]{2,1,0:T(8,128)(2,1)}, u32[]{:S(2)}, u32[]{:S(2)}) async-start(bf16[8,66,2048]{2,1,0:T(8,128)(2,1)} %bitcast.69), calls=%async_computation | async-start | bytes 4718592 | tf_op jit(solution)/shard_map/all_to_all | solution.py:133
  144.0 3.1 reshape.195
  147.1 2.3 fusion.34
  149.5 1.8 fusion.25
  151.3 5.4 %fusion.6 = f32[528,2048]{1,0:T(8,128)} fusion(f32[528,192]{0,1:T(8,128)} %fusion.25, bf16[528,2048]{1,0:T(8,128)(2,1)S(1)} %copy-done.1, bf16[1,2048,192]{1,2,0:T(8,128)(2,1)S(1)} %copy-done, bf16[1,2048,192]{1,2,0:T(8,128)(2,1)} %param.17, f32[528,192]{0,1:T(8,128)S(1)} %fusion.34), kind=kOutput, calls=%fused_computation.21 | convolution fusion | flops 831485952 | bytes 8871936 | tf_op jit(solution)/shard_map/dot_general | solution.py:87
  156.7 3.2 add_convert_fusion
  159.9 1.8 reshape.198
  161.7 34.1 %all-to-all-done = bf16[8,66,2048]{2,1,0:T(8,128)(2,1)} async-done(((bf16[8,66,2048]{2,1,0:T(8,128)(2,1)}), bf16[8,66,2048]{2,1,0:T(8,128)(2,1)}, u32[]{:S(2)}, u32[]{:S(2)}) %all-to-all-start) | async-done | bytes 2162720 | tf_op jit(solution)/shard_map/all_to_all | solution.py:133
  195.7 3.6 %all-to-all-start.4 = ((bf16[8,66,2048]{2,1,0:T(8,128)(2,1)}), bf16[8,66,2048]{2,1,0:T(8,128)(2,1)S(1)}, u32[]{:S(2)}, u32[]{:S(2)}) async-start(bf16[8,66,2048]{2,1,0:T(8,128)(2,1)} %reshape.198), calls=%async_computation.4 | async-start | bytes 4718592 | tf_op jit(solution)/shard_map/all_to_all | solution.py:143
  199.4 2.9 reshape.191
  202.3 3.6 %fusion.36 = f32[528,192]{0,1:T(8,128)} fusion(bf16[528,2048]{1,0:T(8,128)(2,1)} %reshape.191, bf16[1,2048,192]{1,2,0:T(8,128)(2,1)} %param.17), kind=kOutput, calls=%fused_computation.51 | convolution fusion | flops 415236096 | bytes 3354624 | tf_op jit(solution)/shard_map/dot_general | solution.py:68
  205.9 5.4 %convolution_convert_fusion.1 = bf16[528,2048]{1,0:T(8,128)(2,1)} fusion(bf16[528,2048]{1,0:T(8,128)(2,1)} %reshape.191, bf16[1,192,2048]{2,1,0:T(8,128)(2,1)} %param.19, bf16[1,2048,192]{1,2,0:T(8,128)(2,1)S(1)} %copy-done, f32[528,192]{0,1:T(8,128)} %fusion.36), kind=kOutput, calls=%fused_computation.6 | convolution fusion | flops 832161792 | bytes 6303744 | tf_op jit(solution)/shard_map/dot_general | solution.py:72
  211.3 3.0 reshape.192
  214.2 39.2 %all-to-all-done.4 = bf16[8,66,2048]{2,1,0:T(8,128)(2,1)S(1)} async-done(((bf16[8,66,2048]{2,1,0:T(8,128)(2,1)}), bf16[8,66,2048]{2,1,0:T(8,128)(2,1)S(1)}, u32[]{:S(2)}, u32[]{:S(2)}) %all-to-all-start.4) | async-done | bytes 2162720 | tf_op jit(solution)/shard_map/all_to_all | solution.py:143
  253.4 4.6 %all-to-all-start.1 = ((bf16[8,66,2048]{2,1,0:T(8,128)(2,1)}), bf16[8,66,2048]{2,1,0:T(8,128)(2,1)}, u32[]{:S(2)}, u32[]{:S(2)}) async-start(bf16[8,66,2048]{2,1,0:T(8,128)(2,1)} %reshape.192), calls=%async_computation.1 | async-start | bytes 4718592 | tf_op jit(solution)/shard_map/all_to_all | solution.py:131
  262.3 48.9 %all-to-all-done.1 = bf16[8,66,2048]{2,1,0:T(8,128)(2,1)} async-done(((bf16[8,66,2048]{2,1,0:T(8,128)(2,1)}), bf16[8,66,2048]{2,1,0:T(8,128)(2,1)}, u32[]{:S(2)}, u32[]{:S(2)}) %all-to-all-start.1) | async-done | bytes 2162720 | tf_op jit(solution)/shard_map/all_to_all | solution.py:131
  311.3 3.2 convert_reduce_fusion.1
  315.9 1.9 gather_fusion
  317.8 2.5 fusion.16
  320.3 2.1 fusion.20
  (51 shorter events, 17.1 us)
Async XLA Ops:
  0.6 150.6 %copy-start = (bf16[1,2048,192]{1,2,0:T(8,128)(2,1)S(1)}, bf16[1,2048,192]{1,2,0:T(8,128)(2,1)}, u32[]{:S(2)}) copy-start(bf16[1,2048,192]{1,2,0:T(8,128)(2,1)} %param.18) | copy-start | bytes 2359300
  0.6 9.5 %collective-permute-start.1 = (bf16[1,128,2048]{2,1,0:T(8,128)(2,1)}, bf16[1,128,2048]{2,1,0:T(8,128)(2,1)S(1)}, u32[]{:S(2)}, u32[]{:S(2)}) collective-permute-start(bf16[1,128,2048]{2,1,0:T(8,128)(2,1)} %param.15), channel_id=1, source_target_pairs={{0,24},{8,0},{16,8},{24,16},{1,25},{9,1},{17,9},{25,17},{2,26},{10... | collective-permute-start | bytes 1572872 | tf_op jit(solution)/shard_map/ppermute | solution.py:15
  10.1 1.3 copy-start.5
  13.3 60.6 %all-to-all-start.3 = ((bf16[8,66,2048]{2,1,0:T(8,128)(2,1)}), bf16[8,66,2048]{2,1,0:T(8,128)(2,1)S(1)}, u32[]{:S(2)}, u32[]{:S(2)}) async-start(bf16[8,66,2048]{2,1,0:T(8,128)(2,1)} %bitcast.70), calls=%async_computation.3 | async-start | bytes 4718592 | tf_op jit(solution)/shard_map/all_to_all | solution.py:145
  76.7 4.6 %copy-start.7 = (s32[1,128,1]{1,2,0:T(1,128)S(1)}, s32[1,128,1]{1,2,0:T(1,128)}, u32[]{:S(2)}) copy-start(s32[1,128,1]{1,2,0:T(1,128)} %param.20) | copy-start | bytes 1540
  76.7 14.7 %copy-start.6 = (f32[1,2048]{1,0:T(1,128)S(1)}, f32[1,2048]{1,0:T(1,128)}, u32[]{:S(2)}) copy-start(f32[1,2048]{1,0:T(1,128)} %param.16) | copy-start | bytes 24580
  76.7 58.5 %all-to-all-start.2 = ((bf16[8,66,2048]{2,1,0:T(8,128)(2,1)}), bf16[8,66,2048]{2,1,0:T(8,128)(2,1)}, u32[]{:S(2)}, u32[]{:S(2)}) async-start(bf16[8,66,2048]{2,1,0:T(8,128)(2,1)} %bitcast.68), calls=%async_computation.2 | async-start | bytes 4718592 | tf_op jit(solution)/shard_map/all_to_all | solution.py:146
  81.2 9.0 %collective-permute-start = (bf16[1,128,2048]{2,1,0:T(8,128)(2,1)}, bf16[1,128,2048]{2,1,0:T(8,128)(2,1)}, u32[]{:S(2)}, u32[]{:S(2)}) collective-permute-start(bf16[1,128,2048]{2,1,0:T(8,128)(2,1)} %param.13), channel_id=1, source_target_pairs={{0,8},{8,16},{16,24},{24,0},{1,9},{9,17},{17,25},{25,1},{2,10},{10... | collective-permute-start | bytes 1572872 | tf_op jit(solution)/shard_map/ppermute | solution.py:15
  138.0 57.8 %all-to-all-start = ((bf16[8,66,2048]{2,1,0:T(8,128)(2,1)}), bf16[8,66,2048]{2,1,0:T(8,128)(2,1)}, u32[]{:S(2)}, u32[]{:S(2)}) async-start(bf16[8,66,2048]{2,1,0:T(8,128)(2,1)} %bitcast.69), calls=%async_computation | async-start | bytes 4718592 | tf_op jit(solution)/shard_map/all_to_all | solution.py:133
  144.0 3.1 copy-start.1
  147.1 2.3 copy-start.4
  147.1 2.3 copy-start.10
  195.7 57.7 %all-to-all-start.4 = ((bf16[8,66,2048]{2,1,0:T(8,128)(2,1)}), bf16[8,66,2048]{2,1,0:T(8,128)(2,1)S(1)}, u32[]{:S(2)}, u32[]{:S(2)}) async-start(bf16[8,66,2048]{2,1,0:T(8,128)(2,1)} %reshape.198), calls=%async_computation.4 | async-start | bytes 4718592 | tf_op jit(solution)/shard_map/all_to_all | solution.py:143
  253.4 57.9 %all-to-all-start.1 = ((bf16[8,66,2048]{2,1,0:T(8,128)(2,1)}), bf16[8,66,2048]{2,1,0:T(8,128)(2,1)}, u32[]{:S(2)}, u32[]{:S(2)}) async-start(bf16[8,66,2048]{2,1,0:T(8,128)(2,1)} %reshape.192), calls=%async_computation.1 | async-start | bytes 4718592 | tf_op jit(solution)/shard_map/all_to_all | solution.py:131
  260.9 1.0 copy-start.2
  260.9 1.0 copy-start.8
  317.8 2.5 copy-start.3
  317.8 2.5 copy-start.9
where the time goes:
time: 324 us; the launch traced here: 322 us
  waiting for transfers between devices  225 us (69%)
  local copies, waits for them, and re-layouts  30.5 us (9%)
  starting transfers between devices  25.4 us (8%)
  matrix products  24.4 us (8%)
  other arithmetic  16.2 us (5%)
    all_to_all x1, waiting for transfers between devices, per_device(): lax.all_to_all(send_b, 'expert', split_axis=0, concat_axis=0, tiled=True)  52.8 us
    all_to_all x1, waiting for transfers between devices, per_device(): lax.all_to_all(forward_rows(lax.all_to_all(send_f, 'expert', split_axis=0...  48.9 us
    all_to_all x1, waiting for transfers between devices, per_device(): lax.all_to_all(send_g, 'expert', split_axis=0, concat_axis=0, tiled=True)  39.5 us
    all_to_all x1, waiting for transfers between devices, per_device(): lax.all_to_all(backward_rows(lax.all_to_all(send_b, 'expert', split_axis=...  39.2 us
    all_to_all x1, waiting for transfers between devices, per_device(): lax.all_to_all(send_f, 'expert', split_axis=0, concat_axis=0, tiled=True)  34.1 us
    broadcast_in_dim x6, local copies, waits for them, and re-layouts, fan_out(): jnp.broadcast_to(packed.reshape(experts, 1, capacity, row_width), (expert...  11.4 us
    ppermute x2, waiting for transfers between devices, passed_along(): return lax.ppermute(value, axis, pairs)  10.6 us
  transfers between devices with their start and end apart: 7, of which 7 were waited for; matrix products, arithmetic and copies ran while one was open for 16% of the time, Pallas kernels for 0%

commit v1 on v0

v1 whole, which is shorter than its diff:
```python
import jax
import jax.numpy as jnp
from jax import lax
from jax.sharding import PartitionSpec as P

SPLIT = 4
EPS = 1e-06


def shifted(value, axis, steps):
    count = lax.axis_size(axis)
    return lax.ppermute(value, axis, [(i, (i + steps) % count) for i in range(count)])


def swapped(value, axis, bit):
    count = lax.axis_size(axis)
    return lax.ppermute(value, axis, [(i, i ^ bit) for i in range(count)])


def silu_parts(values):
    sigma = jax.nn.sigmoid(values)
    return (values * sigma, sigma * (1.0 + values * (1.0 - sigma)))


def normalize(block_rows, gain_row):
    values = block_rows.astype(jnp.float32)
    inv_scale = lax.rsqrt(jnp.mean(values * values, axis=-1, keepdims=True) + EPS)
    return (values * inv_scale * gain_row, inv_scale)


def slot_targets(routes, own, experts, rows):
    flat = routes.reshape(-1)
    onehot = (flat[:, None] == jnp.arange(experts, dtype=jnp.int32)[None, :]).astype(jnp.int32)
    before = jnp.cumsum(onehot, axis=0) - onehot
    slot = jnp.sum(before * onehot, axis=1)
    return (lax.rem(flat - own + experts, experts) * rows + slot).reshape(routes.shape)


def chooser_of(target, total):
    picks = jnp.arange(total, dtype=jnp.int32)[:, None, None] == target[None]
    return jnp.sum(picks.astype(jnp.float32), axis=2).astype(jnp.bfloat16)


def pack(chooser, values, experts):
    packed = jnp.dot(chooser, values, preferred_element_type=jnp.float32).astype(jnp.bfloat16)
    return packed.reshape(experts, -1, values.shape[1])


def fetch_rows(blocks):
    mine = [blocks[0]]
    theirs = [swapped(blocks[0], "expert", 2)]
    for j in range(1, blocks.shape[0]):
        got = shifted(blocks[j], "expert", SPLIT * j)
        mine.append(got)
        theirs.append(swapped(got, "expert", 2))
    return jnp.concatenate(mine + theirs, axis=0)


def return_rows(partial, experts):
    half = partial.shape[0] // 2
    rows = half // experts
    own = partial[:half]
    away = partial[half:].astype(jnp.bfloat16)
    home = []
    for j in range(experts):
        cut = slice(j * rows, (j + 1) * rows)
        total = (own[cut] + swapped(away[cut], "expert", 2).astype(jnp.float32)).astype(jnp.bfloat16)
        home.append(total if j == 0 else shifted(total, "expert", -SPLIT * j))
    return jnp.concatenate(home, axis=0)


def weighted_sum(target, gates, rows):
    place = jnp.arange(rows.shape[0], dtype=jnp.int32)[None, None, :] == target[:, :, None]
    width = rows.shape[1]
    picked = jnp.dot(
        place.astype(jnp.bfloat16).reshape(-1, rows.shape[0]), rows, preferred_element_type=jnp.float32
    )
    return jnp.sum(picked.reshape(target.shape + (width,)) * gates[:, :, None], axis=1)


CONTRACT = (((1,), (1,)), ((), ()))


def forward_rows(rows, shares):
    out = None
    for gate_up, down in shares:
        units = down.shape[0]
        both = jnp.dot(rows, gate_up, preferred_element_type=jnp.float32)
        hidden = (silu_parts(both[:, :units])[0] * both[:, units:]).astype(jnp.bfloat16)
        part = jnp.dot(hidden, down, preferred_element_type=jnp.float32)
        out = part if out is None else out + part
    return out


def backward_rows(rows, grads, shares):
    out = None
    for gate_up, down in shares:
        units = down.shape[0]
        both = jnp.dot(rows, gate_up, preferred_element_type=jnp.float32)
        activation, derivative = silu_parts(both[:, :units])
        d_hidden = lax.dot_general(grads, down, CONTRACT, preferred_element_type=jnp.float32)
        d_gate = (d_hidden * both[:, units:] * derivative).astype(jnp.bfloat16)
        d_up = (d_hidden * activation).astype(jnp.bfloat16)
        d_both = jnp.concatenate([d_gate, d_up], axis=1)
        part = lax.dot_general(d_both, gate_up, CONTRACT, preferred_element_type=jnp.float32)
        out = part if out is None else out + part
    return out


def per_device(act_in, saved_in, grad_in, norm_gain, w_gate, w_up, w_down, routes_fwd, gates_fwd, routes_bwd, gates_bwd):
    experts = lax.axis_size("expert") // SPLIT
    own = lax.axis_index("expert") // SPLIT
    tok_count, top_count = routes_fwd.shape[1:]
    capacity = min(tok_count, tok_count * top_count // experts + 2)
    rows = -(-capacity // 8) * 8
    gain_row = norm_gain[0]

    incoming = shifted(act_in[0], "section", 1)
    upstream = shifted(grad_in[0], "section", -1)
    gate_up = jnp.concatenate([w_gate[0], w_up[0]], axis=1)
    down = w_down[0]
    other_gate_up = swapped(gate_up, "expert", 1)
    other_down = swapped(down, "expert", 1)
    shares = ((gate_up, down), (other_gate_up, other_down))

    target_b = slot_targets(routes_bwd[0], own, experts, rows)
    chooser_b = chooser_of(target_b, experts * rows)
    base = saved_in[0].astype(jnp.float32)
    values_b, inv_scale = normalize(saved_in[0], gain_row)
    rows_b = fetch_rows(pack(chooser_b, values_b.astype(jnp.bfloat16), experts))
    rows_g = fetch_rows(pack(chooser_b, upstream, experts))
    target_f = slot_targets(routes_fwd[0], own, experts, rows)
    chooser_f = chooser_of(target_f, experts * rows)
    n_fwd = normalize(incoming, gain_row)[0].astype(jnp.bfloat16)
    rows_f = fetch_rows(pack(chooser_f, n_fwd, experts))

    back_b = return_rows(backward_rows(rows_b, rows_g, shares), experts)
    back_f = return_rows(forward_rows(rows_f, shares), experts)

    d_norm = weighted_sum(target_b, gates_bwd[0], back_b)
    scaled = d_norm * gain_row
    d_input = inv_scale * (
        scaled - base * inv_scale * inv_scale * jnp.mean(scaled * base, axis=-1, keepdims=True)
    )
    grad_out = (upstream.astype(jnp.float32) + d_input).astype(jnp.bfloat16)
    mixed = weighted_sum(target_f, gates_fwd[0], back_f)
    act_out = (incoming.astype(jnp.float32) + mixed).astype(jnp.bfloat16)
    return (act_out[None], grad_out[None])


def solution(mesh):
    tokens = P("section", "expert", None)
    in_specs = (
        tokens,
        tokens,
        tokens,
        P("section", None),
        P("section", None, "expert"),
        P("section", None, "expert"),
        tokens,
        tokens,
        tokens,
        tokens,
        tokens,
    )
    return jax.shard_map(
        per_device, mesh=mesh, in_specs=in_specs, out_specs=(tokens, tokens), check_vma=False
    )
```

time: 324 us -> 131 us (0.40)
  waiting for transfers between devices: 225 us -> 85 us
  local copies, waits for them, and re-layouts: 30.5 us -> 0.26 us
  other arithmetic: 16.2 us -> 7.06 us
  matrix products: 24.4 us -> 16.1 us
  starting transfers between devices: 25.4 us -> 21.3 us
    all_to_all x5 -> x0, waiting for transfers between devices: 214 us -> none  [the longest x1 52.8 us: per_device(): lax.all_to_all(send_b, 'expert', split_axis=0, concat_axis=0, tiled=True)]
    ppermute x2 -> x19, waiting for transfers between devices: 10.6 us -> 85 us  [the longest x7 44.6 us: shifted(): lax.ppermute(value, axis, [(i, (i + steps) % count) for i in range(count)])]
    all_to_all x5 -> x0, starting transfers between devices: 22.9 us -> none  [the longest x1 5.81 us: per_device(): lax.all_to_all(send_b, 'expert', split_axis=0, concat_axis=0, tiled=True)]
    ppermute x2 -> x19, starting transfers between devices: 2.52 us -> 21.3 us  [the longest x12 11.9 us: swapped(): return lax.ppermute(value, axis, [(i, i ^ bit) for i in range(count)])]
    reshape x7 -> x0, local copies, waits for them, and re-layouts: 15.2 us -> none  [the longest x1 3.14 us: backward_rows(): flat_grads = grad_rows.reshape(row_groups * row_count, row_width)]
    broadcast_in_dim x6 -> x0, local copies, waits for them, and re-layouts: 11.4 us -> none  [fan_out(): jnp.broadcast_to(packed.reshape(experts, 1, capacity, row_width), (expert...]
    dot_general x8 -> x15, matrix products: 24.4 us -> 16.1 us  [the longest x2 4.23 us: backward_rows(): both = jnp.dot(rows, gate_up, preferred_element_type=jnp.float32)]
    reduce_sum x7 -> x4, other arithmetic: 8.51 us -> 2.42 us  [the longest x2 1.42 us: normalize(): jnp.mean(values * values, axis=-1, keepdims=True) + EPS]
  transfers between devices with their start and end apart: 7 -> 19, of which waited for: 7 -> 12; matrix products, arithmetic and copies ran while one was open for 16% -> 11% of each run, Pallas kernels for 0% -> 0%
where the time goes in v1:
time: 131 us
  waiting for transfers between devices  85 us (65%)
  starting transfers between devices  21.3 us (16%)
  matrix products  16.1 us (12%)
  other arithmetic  7.06 us (5%)
    ppermute x7, waiting for transfers between devices, shifted(): lax.ppermute(value, axis, [(i, (i + steps) % count) for i in range(count)])  44.6 us
    ppermute x12, waiting for transfers between devices, swapped(): return lax.ppermute(value, axis, [(i, i ^ bit) for i in range(count)])  40.4 us
    ppermute x12, starting transfers between devices, swapped(): return lax.ppermute(value, axis, [(i, i ^ bit) for i in range(count)])  11.9 us
    ppermute x7, starting transfers between devices, shifted(): lax.ppermute(value, axis, [(i, (i + steps) % count) for i in range(count)])  9.38 us
    dot_general x2, matrix products, backward_rows(): both = jnp.dot(rows, gate_up, preferred_element_type=jnp.float32)  4.23 us
    dot_general x2, matrix products, backward_rows(): lax.dot_general(d_both, gate_up, CONTRACT, preferred_element_type=jnp.flo...  3.08 us
    dot_general x2, matrix products, forward_rows(): both = jnp.dot(rows, gate_up, preferred_element_type=jnp.float32)  3 us
  transfers between devices with their start and end apart: 19, of which 12 were waited for; matrix products, arithmetic and copies ran while one was open for 11% of the time, Pallas kernels for 0%

profile of v1, /device:TPU:0, one launch (start us, length us, event | category | flops | bytes accessed | tf_op | source)
XLA Modules:
  0.0 130.7 jit_solution(15887341821097620801)
XLA Ops:
  0.7 0.9 fusion.63
  2.5 1.2 fusion.7
  4.5 1.4 %convolution_convert_fusion = bf16[144,2048]{1,0:T(8,128)(2,1)S(1)} fusion(bf16[1,128,2048]{2,1,0:T(8,128)(2,1)} %param.12, f32[2048]{0:T(1024)} %bitcast.78, f32[128]{0:T(128)S(1)} %add_rsqrt_fusion, s32[128]{0:T(128)S(1)} %fusion.81), kind=kOutput, calls=%fused_computation.6 | convolution fusion | flops 76896256 | bytes 1123328 | tf_op jit(solution)/shard_map/dot_general | solution.py:45
  5.9 4.1 %collective-permute-start.13 = (bf16[72,2048]{1,0:T(8,128)(2,1)S(1)}, bf16[72,2048]{1,0:T(8,128)(2,1)}, u32[]{:S(2)}, u32[]{:S(2)}) collective-permute-start(bf16[72,2048]{1,0:T(8,128)(2,1)S(1)} %get-tuple-element.15), channel_id=1, source_target_pairs={{0,4},{1,5},{2,6},{3,7},{4,0},{5,1},{6,2},{7,3},{8,12},{9,13},{10,... | collective-permute-start | bytes 884744 | tf_op jit(solution)/shard_map/ppermute | solution.py:12
  10.0 1.6 %collective-permute-start.14 = (bf16[72,2048]{1,0:T(8,128)(2,1)S(1)}, bf16[72,2048]{1,0:T(8,128)(2,1)}, u32[]{:S(2)}, u32[]{:S(2)}) collective-permute-start(bf16[72,2048]{1,0:T(8,128)(2,1)S(1)} %get-tuple-element.14), channel_id=1, source_target_pairs={{0,2},{1,3},{2,0},{3,1},{4,6},{5,7},{6,4},{7,5},{8,10},{9,11},{10,... | collective-permute-start | bytes 884744 | tf_op jit(solution)/shard_map/ppermute | solution.py:17
  12.0 1.2 pad_maximum_fusion
  13.3 1.5 %collective-permute-start.4 = (bf16[2048,384]{0,1:T(8,128)(2,1)}, bf16[2048,384]{0,1:T(8,128)(2,1)}, u32[]{:S(2)}, u32[]{:S(2)}) collective-permute-start(bf16[2048,384]{0,1:T(8,128)(2,1)} %pad_maximum_fusion), channel_id=1, source_target_pairs={{0,1},{1,0},{2,3},{3,2},{4,5},{5,4},{6,7},{7,6},{8,9},{9,8},{10,11... | collective-permute-start | bytes 4718600 | tf_op jit(solution)/shard_map/ppermute | solution.py:17
  15.2 8.4 %collective-permute-done.13 = bf16[72,2048]{1,0:T(8,128)(2,1)} collective-permute-done((bf16[72,2048]{1,0:T(8,128)(2,1)S(1)}, bf16[72,2048]{1,0:T(8,128)(2,1)}, u32[]{:S(2)}, u32[]{:S(2)}) %collective-permute-start.13) | collective-permute-done | bytes 294944 | tf_op jit(solution)/shard_map/ppermute | solution.py:12
  24.1 2.0 %collective-permute-done = bf16[128,2048]{1,0:T(8,128)(2,1)S(1)} collective-permute-done((bf16[128,2048]{1,0:T(8,128)(2,1)}, bf16[128,2048]{1,0:T(8,128)(2,1)S(1)}, u32[]{:S(2)}, u32[]{:S(2)}) %collective-permute-start) | collective-permute-done | bytes 524320 | tf_op jit(solution)/shard_map/ppermute | solution.py:12
  26.8 1.5 %collective-permute-start.1 = (bf16[72,2048]{1,0:T(8,128)(2,1)S(1)}, bf16[72,2048]{1,0:T(8,128)(2,1)S(1)}, u32[]{:S(2)}, u32[]{:S(2)}) collective-permute-start(bf16[72,2048]{1,0:T(8,128)(2,1)S(1)} %get-tuple-element.19), channel_id=1, source_target_pairs={{0,4},{1,5},{2,6},{3,7},{4,0},{5,1},{6,2},{7,3},{8,12},{9,13},{10,... | collective-permute-start | bytes 884744 | tf_op jit(solution)/shard_map/ppermute | solution.py:12
  28.7 1.5 %collective-permute-start.10 = (bf16[72,2048]{1,0:T(8,128)(2,1)S(1)}, bf16[72,2048]{1,0:T(8,128)(2,1)S(1)}, u32[]{:S(2)}, u32[]{:S(2)}) collective-permute-start(bf16[72,2048]{1,0:T(8,128)(2,1)S(1)} %get-tuple-element.17), channel_id=1, source_target_pairs={{0,4},{1,5},{2,6},{3,7},{4,0},{5,1},{6,2},{7,3},{8,12},{9,13},{10,... | collective-permute-start | bytes 884744 | tf_op jit(solution)/shard_map/ppermute | solution.py:12
  30.7 19.7 %collective-permute-done.1 = bf16[72,2048]{1,0:T(8,128)(2,1)S(1)} collective-permute-done((bf16[72,2048]{1,0:T(8,128)(2,1)S(1)}, bf16[72,2048]{1,0:T(8,128)(2,1)S(1)}, u32[]{:S(2)}, u32[]{:S(2)}) %collective-permute-start.1) | collective-permute-done | bytes 294944 | tf_op jit(solution)/shard_map/ppermute | solution.py:12
  50.5 2.1 %collective-permute-start.11 = (bf16[72,2048]{1,0:T(8,128)(2,1)S(1)}, bf16[72,2048]{1,0:T(8,128)(2,1)S(1)}, u32[]{:S(2)}, u32[]{:S(2)}) collective-permute-start(bf16[72,2048]{1,0:T(8,128)(2,1)S(1)} %get-tuple-element.16), channel_id=1, source_target_pairs={{0,2},{1,3},{2,0},{3,1},{4,6},{5,7},{6,4},{7,5},{8,10},{9,11},{10,... | collective-permute-start | bytes 884744 | tf_op jit(solution)/shard_map/ppermute | solution.py:17
  52.6 1.9 %collective-permute-done.10 = bf16[72,2048]{1,0:T(8,128)(2,1)S(1)} collective-permute-done((bf16[72,2048]{1,0:T(8,128)(2,1)S(1)}, bf16[72,2048]{1,0:T(8,128)(2,1)S(1)}, u32[]{:S(2)}, u32[]{:S(2)}) %collective-permute-start.10) | collective-permute-done | bytes 294944 | tf_op jit(solution)/shard_map/ppermute | solution.py:12
  54.4 1.8 %fusion.52 = f32[288,384]{1,0:T(8,128)S(1)} fusion(bf16[72,2048]{1,0:T(8,128)(2,1)S(1)} %collective-permute-done.15, bf16[72,2048]{1,0:T(8,128)(2,1)} %collective-permute-done.14, bf16[72,2048]{1,0:T(8,128)(2,1)} %collective-permute-done.13, bf16[72,2048]{1,0:T(8,128)(2,1)S(1)} %get-tuple-element.14, bf16[2048,192]{0,1:T(8,128)(2,1)S(1)} %bitcast.70, ...), kind=kOutput, calls=%fused_computation.77 | convolution fusion | flops 460849152 | bytes 3194880 | tf_op jit(solution)/shard_map/dot_general | solution.py:99
  56.3 1.6 %collective-permute-start.5 = (bf16[192,2048]{1,0:T(8,128)(2,1)S(1)}, bf16[192,2048]{1,0:T(8,128)(2,1)S(1)}, u32[]{:S(2)}, u32[]{:S(2)}) collective-permute-start(bf16[192,2048]{1,0:T(8,128)(2,1)S(1)} %bitcast.77), channel_id=1, source_target_pairs={{0,1},{1,0},{2,3},{3,2},{4,5},{5,4},{6,7},{7,6},{8,9},{9,8},{10,11... | collective-permute-start | bytes 2359304 | tf_op jit(solution)/shard_map/ppermute | solution.py:17
  57.9 2.9 %collective-permute-done.3 = bf16[72,2048]{1,0:T(8,128)(2,1)S(1)} collective-permute-done((bf16[72,2048]{1,0:T(8,128)(2,1)S(1)}, bf16[72,2048]{1,0:T(8,128)(2,1)S(1)}, u32[]{:S(2)}, u32[]{:S(2)}) %collective-permute-start.3) | collective-permute-done | bytes 294944 | tf_op jit(solution)/shard_map/ppermute | solution.py:17
  61.5 5.5 %collective-permute-done.11 = bf16[72,2048]{1,0:T(8,128)(2,1)S(1)} collective-permute-done((bf16[72,2048]{1,0:T(8,128)(2,1)S(1)}, bf16[72,2048]{1,0:T(8,128)(2,1)S(1)}, u32[]{:S(2)}, u32[]{:S(2)}) %collective-permute-start.11) | collective-permute-done | bytes 294944 | tf_op jit(solution)/shard_map/ppermute | solution.py:17
  67.1 6.0 %collective-permute-done.12 = bf16[72,2048]{1,0:T(8,128)(2,1)S(1)} collective-permute-done((bf16[72,2048]{1,0:T(8,128)(2,1)S(1)}, bf16[72,2048]{1,0:T(8,128)(2,1)S(1)}, u32[]{:S(2)}, u32[]{:S(2)}) %collective-permute-start.12) | collective-permute-done | bytes 294944 | tf_op jit(solution)/shard_map/ppermute | solution.py:17
  74.9 2.4 %fusion.51 = f32[288,384]{1,0:T(8,128)S(1)} fusion(bf16[2048,384]{0,1:T(8,128)(2,1)} %collective-permute-done.4, bf16[72,2048]{1,0:T(8,128)(2,1)S(1)} %collective-permute-done.15, bf16[72,2048]{1,0:T(8,128)(2,1)} %collective-permute-done.14, bf16[72,2048]{1,0:T(8,128)(2,1)} %collective-permute-done.13, bf16[72,2048]{1,0:T(8,128)(2,1)S(1)} %get-tuple-element.14), kind=kOutput, calls=%fused_computation.76 | convolution fusion | flops 457703424 | bytes 3194880 | tf_op jit(solution)/shard_map/dot_general | solution.py:99
  77.9 2.3 %fusion.103 = (bf16[288,2048]{1,0:T(8,128)(2,1)S(1)}, f32[288,2048]{1,0:T(8,128)S(1)}) fusion(f32[288,2048]{1,0:T(8,128)S(1)} %fusion.44, bf16[2048,384]{0,1:T(8,128)(2,1)} %collective-permute-done.4, bf16[288,192]{1,0:T(8,128)(2,1)S(1)} %get-tuple-element.11, bf16[288,192]{1,0:T(8,128)(2,1)S(1)} %get-tuple-element.10), kind=kOutput, calls=%fused_computation.147 | convolution fusion | flops 454606848 | bytes 7692288 | tf_op jit(solution)/shard_map/dot_general | solution.py:105
  80.3 2.0 %collective-permute-start.17 = (bf16[72,2048]{1,0:T(8,128)(2,1)S(1)}, bf16[72,2048]{1,0:T(8,128)(2,1)S(1)}, u32[]{:S(2)}, u32[]{:S(2)}) collective-permute-start(bf16[72,2048]{1,0:T(8,128)(2,1)S(1)} %get-tuple-element.7), channel_id=1, source_target_pairs={{0,2},{1,3},{2,0},{3,1},{4,6},{5,7},{6,4},{7,5},{8,10},{9,11},{10,... | collective-permute-start | bytes 884744 | tf_op jit(solution)/shard_map/ppermute | solution.py:17
  82.3 2.2 %fusion.53 = f32[288,384]{1,0:T(8,128)S(1)} fusion(bf16[2048,384]{0,1:T(8,128)(2,1)} %collective-permute-done.4, bf16[72,2048]{1,0:T(8,128)(2,1)S(1)} %collective-permute-done.3, bf16[72,2048]{1,0:T(8,128)(2,1)S(1)} %collective-permute-done.2, bf16[72,2048]{1,0:T(8,128)(2,1)S(1)} %collective-permute-done.1, bf16[72,2048]{1,0:T(8,128)(2,1)S(1)} %get-tuple-element.18), kind=kOutput, calls=%fused_computation.78 | convolution fusion | flops 457703424 | bytes 3194880 | tf_op jit(solution)/shard_map/dot_general | solution.py:88
  85.2 1.9 %collective-permute-start.7 = (bf16[72,2048]{1,0:T(8,128)(2,1)S(1)}, bf16[72,2048]{1,0:T(8,128)(2,1)S(1)}, u32[]{:S(2)}, u32[]{:S(2)}) collective-permute-start(bf16[72,2048]{1,0:T(8,128)(2,1)S(1)} %get-tuple-element.9), channel_id=1, source_target_pairs={{0,2},{1,3},{2,0},{3,1},{4,6},{5,7},{6,4},{7,5},{8,10},{9,11},{10,... | collective-permute-start | bytes 884744 | tf_op jit(solution)/shard_map/ppermute | solution.py:17
  87.2 3.0 %collective-permute-done.16 = bf16[72,2048]{1,0:T(8,128)(2,1)S(1)} collective-permute-done((bf16[72,2048]{1,0:T(8,128)(2,1)S(1)}, bf16[72,2048]{1,0:T(8,128)(2,1)S(1)}, u32[]{:S(2)}, u32[]{:S(2)}) %collective-permute-start.16) | collective-permute-done | bytes 294944 | tf_op jit(solution)/shard_map/ppermute | solution.py:17
  90.1 6.3 %collective-permute-done.17 = bf16[72,2048]{1,0:T(8,128)(2,1)S(1)} collective-permute-done((bf16[72,2048]{1,0:T(8,128)(2,1)S(1)}, bf16[72,2048]{1,0:T(8,128)(2,1)S(1)}, u32[]{:S(2)}, u32[]{:S(2)}) %collective-permute-start.17) | collective-permute-done | bytes 294944 | tf_op jit(solution)/shard_map/ppermute | solution.py:17
  96.6 1.0 collective-permute-start.18
  97.6 11.5 %collective-permute-done.6 = bf16[72,2048]{1,0:T(8,128)(2,1)S(1)} collective-permute-done((bf16[72,2048]{1,0:T(8,128)(2,1)S(1)}, bf16[72,2048]{1,0:T(8,128)(2,1)S(1)}, u32[]{:S(2)}, u32[]{:S(2)}) %collective-permute-start.6) | collective-permute-done | bytes 294944 | tf_op jit(solution)/shard_map/ppermute | solution.py:17
  109.1 5.2 %collective-permute-done.7 = bf16[72,2048]{1,0:T(8,128)(2,1)S(1)} collective-permute-done((bf16[72,2048]{1,0:T(8,128)(2,1)S(1)}, bf16[72,2048]{1,0:T(8,128)(2,1)S(1)}, u32[]{:S(2)}, u32[]{:S(2)}) %collective-permute-start.7) | collective-permute-done | bytes 294944 | tf_op jit(solution)/shard_map/ppermute | solution.py:17
  115.7 1.2 fusion.33
  116.9 12.7 %collective-permute-done.8 = bf16[72,2048]{1,0:T(8,128)(2,1)S(1)} collective-permute-done((bf16[72,2048]{1,0:T(8,128)(2,1)S(1)}, bf16[72,2048]{1,0:T(8,128)(2,1)S(1)}, u32[]{:S(2)}, u32[]{:S(2)}) %collective-permute-start.8) | collective-permute-done | bytes 294944 | tf_op jit(solution)/shard_map/ppermute | solution.py:12
  129.5 1.1 fusion.3
  (63 shorter events, 10.1 us)
Async XLA Ops:
  0.6 11.4 %copy-start.2 = (bf16[1,2048,192]{1,2,0:T(8,128)(2,1)S(1)}, bf16[1,2048,192]{1,2,0:T(8,128)(2,1)}, u32[]{:S(2)}) copy-start(bf16[1,2048,192]{1,2,0:T(8,128)(2,1)} %param.15) | copy-start | bytes 2359300
  0.6 11.4 %copy-start.1 = (bf16[1,2048,192]{1,2,0:T(8,128)(2,1)S(1)}, bf16[1,2048,192]{1,2,0:T(8,128)(2,1)}, u32[]{:S(2)}) copy-start(bf16[1,2048,192]{1,2,0:T(8,128)(2,1)} %param.16) | copy-start | bytes 2359300
  5.9 17.6 %collective-permute-start.13 = (bf16[72,2048]{1,0:T(8,128)(2,1)S(1)}, bf16[72,2048]{1,0:T(8,128)(2,1)}, u32[]{:S(2)}, u32[]{:S(2)}) collective-permute-start(bf16[72,2048]{1,0:T(8,128)(2,1)S(1)} %get-tuple-element.15), channel_id=1, source_target_pairs={{0,4},{1,5},{2,6},{3,7},{4,0},{5,1},{6,2},{7,3},{8,12},{9,13},{10,... | collective-permute-start | bytes 884744 | tf_op jit(solution)/shard_map/ppermute | solution.py:12
  10.0 20.2 %collective-permute-start.14 = (bf16[72,2048]{1,0:T(8,128)(2,1)S(1)}, bf16[72,2048]{1,0:T(8,128)(2,1)}, u32[]{:S(2)}, u32[]{:S(2)}) collective-permute-start(bf16[72,2048]{1,0:T(8,128)(2,1)S(1)} %get-tuple-element.14), channel_id=1, source_target_pairs={{0,2},{1,3},{2,0},{3,1},{4,6},{5,7},{6,4},{7,5},{8,10},{9,11},{10,... | collective-permute-start | bytes 884744 | tf_op jit(solution)/shard_map/ppermute | solution.py:17
  11.6 16.7 %collective-permute-start.9 = (bf16[128,2048]{1,0:T(8,128)(2,1)}, bf16[128,2048]{1,0:T(8,128)(2,1)S(1)}, u32[]{:S(2)}, u32[]{:S(2)}) collective-permute-start(bf16[128,2048]{1,0:T(8,128)(2,1)} %bitcast.10), channel_id=1, source_target_pairs={{0,24},{8,0},{16,8},{24,16},{1,25},{9,1},{17,9},{25,17},{2,26},{10... | collective-permute-start | bytes 1572872 | tf_op jit(solution)/shard_map/ppermute | solution.py:12
  12.0 2.7 %copy-start.6 = (s32[1,128,1]{1,2,0:T(1,128)S(1)}, s32[1,128,1]{1,2,0:T(1,128)}, u32[]{:S(2)}) copy-start(s32[1,128,1]{1,2,0:T(1,128)} %param.18) | copy-start | bytes 1540
  12.0 14.3 %copy-start.4 = (f32[1,2048]{1,0:T(1,128)S(1)}, f32[1,2048]{1,0:T(1,128)}, u32[]{:S(2)}) copy-start(f32[1,2048]{1,0:T(1,128)} %param.14) | copy-start | bytes 24580
  13.3 61.7 %collective-permute-start.4 = (bf16[2048,384]{0,1:T(8,128)(2,1)}, bf16[2048,384]{0,1:T(8,128)(2,1)}, u32[]{:S(2)}, u32[]{:S(2)}) collective-permute-start(bf16[2048,384]{0,1:T(8,128)(2,1)} %pad_maximum_fusion), channel_id=1, source_target_pairs={{0,1},{1,0},{2,3},{3,2},{4,5},{5,4},{6,7},{7,6},{8,9},{9,8},{10,11... | collective-permute-start | bytes 4718600 | tf_op jit(solution)/shard_map/ppermute | solution.py:17
  14.8 11.4 %collective-permute-start = (bf16[128,2048]{1,0:T(8,128)(2,1)}, bf16[128,2048]{1,0:T(8,128)(2,1)S(1)}, u32[]{:S(2)}, u32[]{:S(2)}) collective-permute-start(bf16[128,2048]{1,0:T(8,128)(2,1)} %bitcast), channel_id=1, source_target_pairs={{0,8},{8,16},{16,24},{24,0},{1,9},{9,17},{17,25},{25,1},{2,10},{10... | collective-permute-start | bytes 1572872 | tf_op jit(solution)/shard_map/ppermute | solution.py:12
  23.6 26.9 %collective-permute-start.15 = (bf16[72,2048]{1,0:T(8,128)(2,1)}, bf16[72,2048]{1,0:T(8,128)(2,1)S(1)}, u32[]{:S(2)}, u32[]{:S(2)}) collective-permute-start(bf16[72,2048]{1,0:T(8,128)(2,1)} %collective-permute-done.13), channel_id=1, source_target_pairs={{0,2},{1,3},{2,0},{3,1},{4,6},{5,7},{6,4},{7,5},{8,10},{9,11},{10,... | collective-permute-start | bytes 884744 | tf_op jit(solution)/shard_map/ppermute | solution.py:17
  26.7 3.5 %copy-start.5 = (s32[1,128,1]{1,2,0:T(1,128)S(1)}, s32[1,128,1]{1,2,0:T(1,128)}, u32[]{:S(2)}) copy-start(s32[1,128,1]{1,2,0:T(1,128)} %param.20) | copy-start | bytes 1540
  26.8 23.6 %collective-permute-start.1 = (bf16[72,2048]{1,0:T(8,128)(2,1)S(1)}, bf16[72,2048]{1,0:T(8,128)(2,1)S(1)}, u32[]{:S(2)}, u32[]{:S(2)}) collective-permute-start(bf16[72,2048]{1,0:T(8,128)(2,1)S(1)} %get-tuple-element.19), channel_id=1, source_target_pairs={{0,4},{1,5},{2,6},{3,7},{4,0},{5,1},{6,2},{7,3},{8,12},{9,13},{10,... | collective-permute-start | bytes 884744 | tf_op jit(solution)/shard_map/ppermute | solution.py:12
  28.7 25.7 %collective-permute-start.10 = (bf16[72,2048]{1,0:T(8,128)(2,1)S(1)}, bf16[72,2048]{1,0:T(8,128)(2,1)S(1)}, u32[]{:S(2)}, u32[]{:S(2)}) collective-permute-start(bf16[72,2048]{1,0:T(8,128)(2,1)S(1)} %get-tuple-element.17), channel_id=1, source_target_pairs={{0,4},{1,5},{2,6},{3,7},{4,0},{5,1},{6,2},{7,3},{8,12},{9,13},{10,... | collective-permute-start | bytes 884744 | tf_op jit(solution)/shard_map/ppermute | solution.py:12
  30.2 26.0 %collective-permute-start.2 = (bf16[72,2048]{1,0:T(8,128)(2,1)S(1)}, bf16[72,2048]{1,0:T(8,128)(2,1)S(1)}, u32[]{:S(2)}, u32[]{:S(2)}) collective-permute-start(bf16[72,2048]{1,0:T(8,128)(2,1)S(1)} %get-tuple-element.18), channel_id=1, source_target_pairs={{0,2},{1,3},{2,0},{3,1},{4,6},{5,7},{6,4},{7,5},{8,10},{9,11},{10,... | collective-permute-start | bytes 884744 | tf_op jit(solution)/shard_map/ppermute | solution.py:17
  50.4 10.3 %collective-permute-start.3 = (bf16[72,2048]{1,0:T(8,128)(2,1)S(1)}, bf16[72,2048]{1,0:T(8,128)(2,1)S(1)}, u32[]{:S(2)}, u32[]{:S(2)}) collective-permute-start(bf16[72,2048]{1,0:T(8,128)(2,1)S(1)} %collective-permute-done.1), channel_id=1, source_target_pairs={{0,2},{1,3},{2,0},{3,1},{4,6},{5,7},{6,4},{7,5},{8,10},{9,11},{10,... | collective-permute-start | bytes 884744 | tf_op jit(solution)/shard_map/ppermute | solution.py:17
  50.5 5.8 %copy-start.3 = (bf16[1,192,2048]{2,1,0:T(8,128)(2,1)S(1)}, bf16[1,192,2048]{2,1,0:T(8,128)(2,1)}, u32[]{:S(2)}) copy-start(bf16[1,192,2048]{2,1,0:T(8,128)(2,1)} %param.17) | copy-start | bytes 2359300
  50.5 16.6 %collective-permute-start.11 = (bf16[72,2048]{1,0:T(8,128)(2,1)S(1)}, bf16[72,2048]{1,0:T(8,128)(2,1)S(1)}, u32[]{:S(2)}, u32[]{:S(2)}) collective-permute-start(bf16[72,2048]{1,0:T(8,128)(2,1)S(1)} %get-tuple-element.16), channel_id=1, source_target_pairs={{0,2},{1,3},{2,0},{3,1},{4,6},{5,7},{6,4},{7,5},{8,10},{9,11},{10,... | collective-permute-start | bytes 884744 | tf_op jit(solution)/shard_map/ppermute | solution.py:17
  54.4 18.7 %collective-permute-start.12 = (bf16[72,2048]{1,0:T(8,128)(2,1)S(1)}, bf16[72,2048]{1,0:T(8,128)(2,1)S(1)}, u32[]{:S(2)}, u32[]{:S(2)}) collective-permute-start(bf16[72,2048]{1,0:T(8,128)(2,1)S(1)} %collective-permute-done.10), channel_id=1, source_target_pairs={{0,2},{1,3},{2,0},{3,1},{4,6},{5,7},{6,4},{7,5},{8,10},{9,11},{10,... | collective-permute-start | bytes 884744 | tf_op jit(solution)/shard_map/ppermute | solution.py:17
  56.3 21.1 %collective-permute-start.5 = (bf16[192,2048]{1,0:T(8,128)(2,1)S(1)}, bf16[192,2048]{1,0:T(8,128)(2,1)S(1)}, u32[]{:S(2)}, u32[]{:S(2)}) collective-permute-start(bf16[192,2048]{1,0:T(8,128)(2,1)S(1)} %bitcast.77), channel_id=1, source_target_pairs={{0,1},{1,0},{2,3},{3,2},{4,5},{5,4},{6,7},{7,6},{8,9},{9,8},{10,11... | collective-permute-start | bytes 2359304 | tf_op jit(solution)/shard_map/ppermute | solution.py:17
  80.2 10.0 %collective-permute-start.16 = (bf16[72,2048]{1,0:T(8,128)(2,1)S(1)}, bf16[72,2048]{1,0:T(8,128)(2,1)S(1)}, u32[]{:S(2)}, u32[]{:S(2)}) collective-permute-start(bf16[72,2048]{1,0:T(8,128)(2,1)S(1)} %get-tuple-element.6), channel_id=1, source_target_pairs={{0,2},{1,3},{2,0},{3,1},{4,6},{5,7},{6,4},{7,5},{8,10},{9,11},{10,... | collective-permute-start | bytes 884744 | tf_op jit(solution)/shard_map/ppermute | solution.py:17
  80.3 16.2 %collective-permute-start.17 = (bf16[72,2048]{1,0:T(8,128)(2,1)S(1)}, bf16[72,2048]{1,0:T(8,128)(2,1)S(1)}, u32[]{:S(2)}, u32[]{:S(2)}) collective-permute-start(bf16[72,2048]{1,0:T(8,128)(2,1)S(1)} %get-tuple-element.7), channel_id=1, source_target_pairs={{0,2},{1,3},{2,0},{3,1},{4,6},{5,7},{6,4},{7,5},{8,10},{9,11},{10,... | collective-permute-start | bytes 884744 | tf_op jit(solution)/shard_map/ppermute | solution.py:17
  85.1 24.0 %collective-permute-start.6 = (bf16[72,2048]{1,0:T(8,128)(2,1)S(1)}, bf16[72,2048]{1,0:T(8,128)(2,1)S(1)}, u32[]{:S(2)}, u32[]{:S(2)}) collective-permute-start(bf16[72,2048]{1,0:T(8,128)(2,1)S(1)} %get-tuple-element.8), channel_id=1, source_target_pairs={{0,2},{1,3},{2,0},{3,1},{4,6},{5,7},{6,4},{7,5},{8,10},{9,11},{10,... | collective-permute-start | bytes 884744 | tf_op jit(solution)/shard_map/ppermute | solution.py:17
  85.2 29.0 %collective-permute-start.7 = (bf16[72,2048]{1,0:T(8,128)(2,1)S(1)}, bf16[72,2048]{1,0:T(8,128)(2,1)S(1)}, u32[]{:S(2)}, u32[]{:S(2)}) collective-permute-start(bf16[72,2048]{1,0:T(8,128)(2,1)S(1)} %get-tuple-element.9), channel_id=1, source_target_pairs={{0,2},{1,3},{2,0},{3,1},{4,6},{5,7},{6,4},{7,5},{8,10},{9,11},{10,... | collective-permute-start | bytes 884744 | tf_op jit(solution)/shard_map/ppermute | solution.py:17
  96.6 18.6 %copy-start = (bf16[1,128,2048]{2,1,0:T(8,128)(2,1)S(1)}, bf16[1,128,2048]{2,1,0:T(8,128)(2,1)}, u32[]{:S(2)}) copy-start(bf16[1,128,2048]{2,1,0:T(8,128)(2,1)} %param.12) | copy-start | bytes 1572868
  96.6 18.6 %copy-start.7 = (f32[1,128,1]{1,2,0:T(1,128)S(1)}, f32[1,128,1]{1,2,0:T(1,128)}, u32[]{:S(2)}) copy-start(f32[1,128,1]{1,2,0:T(1,128)} %param.21) | copy-start | bytes 1540
  96.6 18.6 %collective-permute-start.18 = (bf16[72,2048]{1,0:T(8,128)(2,1)S(1)}, bf16[72,2048]{1,0:T(8,128)(2,1)S(1)}, u32[]{:S(2)}, u32[]{:S(2)}) collective-permute-start(bf16[72,2048]{1,0:T(8,128)(2,1)S(1)} %get-tuple-element.3), channel_id=1, source_target_pairs={{0,4},{1,5},{2,6},{3,7},{4,0},{5,1},{6,2},{7,3},{8,12},{9,13},{10,... | collective-permute-start | bytes 884744 | tf_op jit(solution)/shard_map/ppermute | solution.py:12
  114.4 15.1 %collective-permute-start.8 = (bf16[72,2048]{1,0:T(8,128)(2,1)S(1)}, bf16[72,2048]{1,0:T(8,128)(2,1)S(1)}, u32[]{:S(2)}, u32[]{:S(2)}) collective-permute-start(bf16[72,2048]{1,0:T(8,128)(2,1)S(1)} %get-tuple-element.5), channel_id=1, source_target_pairs={{0,4},{1,5},{2,6},{3,7},{4,0},{5,1},{6,2},{7,3},{8,12},{9,13},{10,... | collective-permute-start | bytes 884744 | tf_op jit(solution)/shard_map/ppermute | solution.py:12
  115.7 13.9 %copy-start.8 = (f32[1,128,1]{1,2,0:T(1,128)S(1)}, f32[1,128,1]{1,2,0:T(1,128)}, u32[]{:S(2)}) copy-start(f32[1,128,1]{1,2,0:T(1,128)} %param.19) | copy-start | bytes 1540

commit v2 on v1

v2 whole, which is shorter than its diff:
```python
import functools

import jax
import jax.numpy as jnp
from jax import lax
from jax.experimental import pallas as pl
from jax.experimental.pallas import tpu as pltpu
from jax.sharding import PartitionSpec as P

SPLIT = 4
EPS = 1e-06
CONTRACT = (((1,), (1,)), ((), ()))
OVER_ROWS = (((0,), (0,)), ((), ()))
F32 = jnp.float32
BF16 = jnp.bfloat16


def shifted(value, axis, steps):
    count = lax.axis_size(axis)
    return lax.ppermute(value, axis, [(i, (i + steps) % count) for i in range(count)])


def swapped(value, axis, bit):
    count = lax.axis_size(axis)
    return lax.ppermute(value, axis, [(i, i ^ bit) for i in range(count)])


def local_call(body, out_shape, scratch=(), vmem_mib=16, **names):
    return pl.pallas_call(
        body,
        out_shape=out_shape,
        scratch_shapes=scratch,
        compiler_params=pltpu.CompilerParams(vmem_limit_bytes=vmem_mib << 20),
        cost_estimate=pl.CostEstimate(flops=1000, bytes_accessed=1000, transcendentals=0),
        **names,
    )


def silu_parts(values):
    sigma = jax.nn.sigmoid(values)
    return (values * sigma, sigma * (1.0 + values * (1.0 - sigma)))


def inverse_rms(values):
    return lax.rsqrt(jnp.mean(values * values, axis=-1, keepdims=True) + EPS)


def slots_of(routes, own, experts):
    count = routes.shape[1]
    height = -(-experts // 8) * 8
    ids = lax.broadcasted_iota(jnp.int32, (height, count), 0)
    onehot = (ids == routes).astype(F32)
    earlier = (
        lax.broadcasted_iota(jnp.int32, (count, count), 0) < lax.broadcasted_iota(jnp.int32, (count, count), 1)
    ).astype(F32)
    before = jnp.dot(onehot.astype(BF16), earlier.astype(BF16), preferred_element_type=F32)
    slot = jnp.sum(before * onehot, axis=0, keepdims=True).astype(jnp.int32)
    block = routes - own
    return (jnp.where(block < 0, block + experts, block), slot)


def chooser_of(block, slot, j, rows):
    place = lax.broadcasted_iota(jnp.int32, (rows, block.shape[1]), 0)
    return jnp.where((place == slot) & (block == j), 1.0, 0.0).astype(BF16)


def pack_body(experts, own_ref, routes_ref, *refs):
    if len(refs) == experts + 2:
        gain_ref, x_ref, *outs = refs
        values = x_ref[...].astype(F32)
        values = (values * inverse_rms(values) * gain_ref[...]).astype(BF16)
    else:
        x_ref, *outs = refs
        values = x_ref[...]
    block, slot = slots_of(routes_ref[...], own_ref[0], experts)
    for j, out in enumerate(outs):
        chooser = chooser_of(block, slot, j, out.shape[0])
        out[...] = jnp.dot(chooser, values, preferred_element_type=F32).astype(BF16)


def gather_blocks(refs, wide_ref):
    rows = refs[0].shape[0]
    pitch = wide_ref.shape[0] // len(refs)
    for i, ref in enumerate(refs):
        wide_ref[pl.ds(i * pitch, rows), :] = ref[...]
    return pitch


def spread_out(total, refs, pitch):
    for i, ref in enumerate(refs):
        ref[...] = total[i * pitch:i * pitch + ref.shape[0]].astype(ref.dtype)


def forward_body(count, *refs):
    row_refs, refs = refs[:count], refs[count:]
    shares, refs = (refs[0:2], refs[2:4]), refs[4:]
    outs, wide_ref = refs[:-1], refs[-1]
    pitch = gather_blocks(row_refs, wide_ref)
    rows = wide_ref[...]
    total = None
    for gate_up, down in shares:
        units = down.shape[0]
        both = jnp.dot(rows, gate_up[...], preferred_element_type=F32)
        hidden = (silu_parts(both[:, :units])[0] * both[:, units:]).astype(BF16)
        part = jnp.dot(hidden, down[...], preferred_element_type=F32)
        total = part if total is None else total + part
    spread_out(total, outs, pitch)


def backward_body(count, *refs):
    row_refs, grad_refs, refs = refs[:count], refs[count:2 * count], refs[2 * count:]
    shares, refs = (refs[0:2], refs[2:4]), refs[4:]
    outs, wide_ref, grad_wide_ref = refs[:-2], refs[-2], refs[-1]
    pitch = gather_blocks(row_refs, wide_ref)
    gather_blocks(grad_refs, grad_wide_ref)
    rows = wide_ref[...]
    grads = grad_wide_ref[...]
    total = None
    for gate_up, down in shares:
        units = down.shape[0]
        both = jnp.dot(rows, gate_up[...], preferred_element_type=F32)
        activation, derivative = silu_parts(both[:, :units])
        d_hidden = lax.dot_general(grads, down[...], CONTRACT, preferred_element_type=F32)
        d_gate = (d_hidden * both[:, units:] * derivative).astype(BF16)
        d_up = (d_hidden * activation).astype(BF16)
        d_both = jnp.concatenate([d_gate, d_up], axis=1)
        part = lax.dot_general(d_both, gate_up[...], CONTRACT, preferred_element_type=F32)
        total = part if total is None else total + part
    spread_out(total, outs, pitch)


def routed_sum(experts, own_ref, routes_ref, gates_ref, home_refs):
    block, slot = slots_of(routes_ref[...], own_ref[0], experts)
    first, second, *crossed = home_refs
    own_rows = (first[...] + second[...].astype(F32)).astype(BF16)
    total = None
    for j in range(experts):
        rows = own_rows if j == 0 else crossed[j - 1][...]
        chooser = chooser_of(block, slot, j, rows.shape[0])
        part = lax.dot_general(chooser, rows, OVER_ROWS, preferred_element_type=F32)
        total = part if total is None else total + part
    count = block.shape[1]
    diagonal = lax.broadcasted_iota(jnp.int32, (count, count), 0) == lax.broadcasted_iota(
        jnp.int32, (count, count), 1
    )
    gates = jnp.sum(jnp.where(diagonal, gates_ref[...], 0.0), axis=1, keepdims=True)
    return total * gates


def forward_home_body(experts, own_ref, routes_ref, gates_ref, x_ref, *refs):
    mixed = routed_sum(experts, own_ref, routes_ref, gates_ref, refs[:-1])
    refs[-1][...] = (x_ref[...].astype(F32) + mixed).astype(BF16)


def backward_home_body(experts, own_ref, routes_ref, gates_ref, gain_ref, saved_ref, up_ref, *refs):
    d_norm = routed_sum(experts, own_ref, routes_ref, gates_ref, refs[:-1])
    base = saved_ref[...].astype(F32)
    inv_scale = inverse_rms(base)
    scaled = d_norm * gain_ref[...]
    d_input = inv_scale * (
        scaled - base * inv_scale * inv_scale * jnp.mean(scaled * base, axis=-1, keepdims=True)
    )
    refs[-1][...] = (up_ref[...].astype(F32) + d_input).astype(BF16)


def fetch_rows(blocks):
    got = [blocks[0]] + [shifted(blocks[j], "expert", SPLIT * j) for j in range(1, len(blocks))]
    return got + [swapped(block, "expert", 2) for block in got]


def return_rows(partial):
    experts = len(partial) // 2
    mine, theirs = partial[:experts], partial[experts:]
    home = []
    for j in range(1, experts):
        total = (mine[j] + swapped(theirs[j], "expert", 2).astype(F32)).astype(BF16)
        home.append(shifted(total, "expert", -SPLIT * j))
    return [mine[0], swapped(theirs[0], "expert", 2)] + home


def per_device(act_in, saved_in, grad_in, norm_gain, w_gate, w_up, w_down, routes_fwd, gates_fwd, routes_bwd, gates_bwd):
    experts = lax.axis_size("expert") // SPLIT
    own = (lax.axis_index("expert") // SPLIT).astype(jnp.int32).reshape(1)
    tok_count, top_count = routes_fwd.shape[1:]
    assert top_count == 1
    width = act_in.shape[2]
    rows = -(-min(tok_count, tok_count // experts + 2) // 8) * 8
    pitch = -(-rows // 16) * 16
    scalar = pl.BlockSpec(memory_space=pltpu.SMEM)
    whole = pl.BlockSpec(memory_space=pltpu.VMEM)

    packed = [jax.ShapeDtypeStruct((rows, width), BF16)] * experts
    partial = [jax.ShapeDtypeStruct((rows, width), F32)] * experts + packed
    tokens = jax.ShapeDtypeStruct((tok_count, width), BF16)
    wide = pltpu.VMEM((2 * experts * pitch, width), BF16)

    incoming = shifted(act_in[0], "section", 1)
    upstream = shifted(grad_in[0], "section", -1)
    gate_up = jnp.concatenate([w_gate[0], w_up[0]], axis=1)
    down = w_down[0]
    shares = (gate_up, down, swapped(gate_up, "expert", 1), swapped(down, "expert", 1))
    r_fwd = routes_fwd.reshape(1, tok_count)
    r_bwd = routes_bwd.reshape(1, tok_count)
    g_fwd = gates_fwd.reshape(1, tok_count)
    g_bwd = gates_bwd.reshape(1, tok_count)

    def pack(name, routes, *args):
        return local_call(
            functools.partial(pack_body, experts),
            packed,
            in_specs=[scalar] + [whole] * (len(args) + 1),
            out_specs=[whole] * experts,
            name=name,
        )(own, routes, *args)

    rows_b = fetch_rows(pack("pack_saved", r_bwd, norm_gain, saved_in[0]))
    rows_g = fetch_rows(pack("pack_grad", r_bwd, upstream))
    rows_f = fetch_rows(pack("pack_act", r_fwd, norm_gain, incoming))

    count = 2 * experts
    back_b = return_rows(
        local_call(
            functools.partial(backward_body, count), partial, scratch=[wide, wide], vmem_mib=40, name="experts_bwd"
        )(*rows_b, *rows_g, *shares)
    )
    back_f = return_rows(
        local_call(
            functools.partial(forward_body, count), partial, scratch=[wide], vmem_mib=32, name="experts_fwd"
        )(*rows_f, *shares)
    )

    grad_out = local_call(
        functools.partial(backward_home_body, experts),
        tokens,
        in_specs=[scalar] + [whole] * (6 + experts),
        out_specs=whole,
        name="home_bwd",
    )(own, r_bwd, g_bwd, norm_gain, saved_in[0], upstream, *back_b)
    act_out = local_call(
        functools.partial(forward_home_body, experts),
        tokens,
        in_specs=[scalar] + [whole] * (4 + experts),
        out_specs=whole,
        name="home_fwd",
    )(own, r_fwd, g_fwd, incoming, *back_f)
    return (act_out[None], grad_out[None])


def solution(mesh):
    tokens = P("section", "expert", None)
    in_specs = (
        tokens,
        tokens,
        tokens,
        P("section", None),
        P("section", None, "expert"),
        P("section", None, "expert"),
        tokens,
        tokens,
        tokens,
        tokens,
        tokens,
    )
    return jax.shard_map(
        per_device, mesh=mesh, in_specs=in_specs, out_specs=(tokens, tokens), check_vma=False
    )
```

time: 131 us -> 130 us (level)
  matrix products: 16.1 us -> 0 us
  Pallas kernels: 0 us -> 14.9 us
  other arithmetic: 7.06 us -> 1.98 us
  local copies, waits for them, and re-layouts: 0.26 us -> 3.97 us
  starting transfers between devices: 21.3 us -> 24.7 us
  waiting for transfers between devices: 85 us -> 83.2 us
    dot_general x15 -> x0, matrix products: 16.1 us -> none  [the longest x2 4.23 us: backward_rows(): both = jnp.dot(rows, gate_up, preferred_element_type=jnp.float32)]
    ppermute x7, waiting for transfers between devices: 44.6 us -> 29.1 us  [shifted(): lax.ppermute(value, axis, [(i, (i + steps) % count) for i in range(count)])]
    pallas_call x0 -> x7, Pallas kernels: none -> 14.9 us  [the longest x1 3.72 us: per_device(): local_call(functools.partial(backward_body, count), partial, scratch=[wid...]
    ppermute x12, waiting for transfers between devices: 40.4 us -> 54.1 us  [swapped(): return lax.ppermute(value, axis, [(i, i ^ bit) for i in range(count)])]
    unnamed x18 -> x20, local copies, waits for them, and re-layouts: 0.05 us -> 3.97 us
    ppermute x12, starting transfers between devices: 11.9 us -> 14.4 us  [swapped(): return lax.ppermute(value, axis, [(i, i ^ bit) for i in range(count)])]
    reduce_sum x4 -> x0, other arithmetic: 2.42 us -> none  [the longest x2 1.42 us: normalize(): jnp.mean(values * values, axis=-1, keepdims=True) + EPS]
  transfers between devices with their start and end apart: 19 -> 19, of which waited for: 12 -> 13; matrix products, arithmetic and copies ran while one was open for 11% -> 0% of each run, Pallas kernels for 0% -> 10%
where the time goes in v2:
time: 130 us
  waiting for transfers between devices  83.2 us (64%)
  starting transfers between devices  24.7 us (19%)
  Pallas kernels  14.9 us (11%)
  local copies, waits for them, and re-layouts  3.97 us (3%)
  other arithmetic  1.98 us (2%)
    ppermute x12, waiting for transfers between devices, swapped(): return lax.ppermute(value, axis, [(i, i ^ bit) for i in range(count)])  54.1 us
    ppermute x7, waiting for transfers between devices, shifted(): lax.ppermute(value, axis, [(i, (i + steps) % count) for i in range(count)])  29.1 us
    ppermute x12, starting transfers between devices, swapped(): return lax.ppermute(value, axis, [(i, i ^ bit) for i in range(count)])  14.4 us
    ppermute x7, starting transfers between devices, shifted(): lax.ppermute(value, axis, [(i, (i + steps) % count) for i in range(count)])  10.3 us
    unnamed x20, local copies, waits for them, and re-layouts  3.97 us
    pallas_call x1, Pallas kernels, per_device(): local_call(functools.partial(backward_body, count), partial, scratch=[wid...  3.72 us
    pallas_call x3, Pallas kernels, pack(): local_call(functools.partial(pack_body, experts), packed, in_specs=[scala...  3.57 us
    pallas_call x1, Pallas kernels, per_device(): local_call(functools.partial(backward_home_body, experts), tokens, in_spe...  2.81 us
  transfers between devices with their start and end apart: 19, of which 13 were waited for; matrix products, arithmetic and copies ran while one was open for 0% of the time, Pallas kernels for 10%

profile of v2, /device:TPU:0, one launch (start us, length us, event | category | flops | bytes accessed | tf_op | source)
XLA Modules:
  0.0 129.6 jit_solution(6750962085802752401)
XLA Ops:
  0.6 1.5 %copy.13 = bf16[1,2048,192]{2,1,0:T(8,128)(2,1)S(1)} copy(bf16[1,2048,192]{1,2,0:T(8,128)(2,1)} %param.15) | data formatting | bytes 1572864 | tf_op args[4]
  2.2 1.3 %copy.14 = bf16[1,2048,192]{2,1,0:T(8,128)(2,1)} copy(bf16[1,2048,192]{1,2,0:T(8,128)(2,1)S(1)} %copy-done.8) | data formatting | bytes 1572864 | tf_op args[5]
  3.5 1.9 %pad_maximum_fusion.refs_4_.refs_8_ = bf16[2048,384]{1,0:T(8,128)(2,1)S(1)} fusion(bf16[2048,192]{1,0:T(8,128)(2,1)} %bitcast.26, bf16[2048,192]{1,0:T(8,128)(2,1)S(1)} %bitcast.25), kind=kLoop, calls=%fused_computation | loop fusion | flops 3145728 | bytes 3145728 | tf_op jit(solution)/shard_map/concatenate | solution.py:199
  5.4 3.0 %collective-permute-start.4 = (bf16[2048,384]{1,0:T(8,128)(2,1)S(1)}, bf16[2048,384]{1,0:T(8,128)(2,1)S(1)}, u32[]{:S(2)}, u32[]{:S(2)}) collective-permute-start(bf16[2048,384]{1,0:T(8,128)(2,1)S(1)} %pad_maximum_fusion.refs_4_.refs_8_), channel_id=1, source_target_pairs={{0,1},{1,0},{2,3},{3,2},{4,5},{5,4},{6,7},{7,6},{8,9},{9,8},{10,11... | collective-permute-start | bytes 4718600 | tf_op jit(solution)/shard_map/ppermute | solution.py:25
  9.1 1.1 copy-done.1
  10.7 2.7 %collective-permute-start.10 = (bf16[72,2048]{1,0:T(8,128)(2,1)S(1)}, bf16[72,2048]{1,0:T(8,128)(2,1)S(1)}, u32[]{:S(2)}, u32[]{:S(2)}) collective-permute-start(bf16[72,2048]{1,0:T(8,128)(2,1)S(1)} %get-tuple-element.23), channel_id=1, source_target_pairs={{0,4},{1,5},{2,6},{3,7},{4,0},{5,1},{6,2},{7,3},{8,12},{9,13},{10,... | collective-permute-start | bytes 884744 | tf_op jit(solution)/shard_map/ppermute | solution.py:20
  13.9 14.0 %collective-permute-done.10.refs_1_ = bf16[72,2048]{1,0:T(8,128)(2,1)S(1)} collective-permute-done((bf16[72,2048]{1,0:T(8,128)(2,1)S(1)}, bf16[72,2048]{1,0:T(8,128)(2,1)S(1)}, u32[]{:S(2)}, u32[]{:S(2)}) %collective-permute-start.10) | collective-permute-done | bytes 294944 | tf_op jit(solution)/shard_map/ppermute | solution.py:20
  28.5 1.4 %collective-permute-start.12 = (bf16[72,2048]{1,0:T(8,128)(2,1)S(1)}, bf16[72,2048]{1,0:T(8,128)(2,1)S(1)}, u32[]{:S(2)}, u32[]{:S(2)}) collective-permute-start(bf16[72,2048]{1,0:T(8,128)(2,1)S(1)} %collective-permute-done.10.refs_1_), channel_id=1, source_target_pairs={{0,2},{1,3},{2,0},{3,1},{4,6},{5,7},{6,4},{7,5},{8,10},{9,11},{10,... | collective-permute-start | bytes 884744 | tf_op jit(solution)/shard_map/ppermute | solution.py:25
  29.9 1.5 %pack_grad.1 = (bf16[72,2048]{1,0:T(8,128)(2,1)S(1)}, bf16[72,2048]{1,0:T(8,128)(2,1)S(1)}) custom-call(s32[1]{0:T(128)} %bitcast.own_ref, s32[1,128]{1,0:T(1,128)S(1)} %bitcast.19, bf16[128,2048]{1,0:T(8,128)(2,1)} %collective-permute-done.9.refs_0_.up_ref), custom_call_target="tpu_custom_call" | custom-call | flops 1000 | bytes 1000 | tf_op jit(solution)/shard_map/pack_grad/pallas_call | solution.py:208
  31.4 2.1 %collective-permute-start.13 = (bf16[72,2048]{1,0:T(8,128)(2,1)S(1)}, bf16[72,2048]{1,0:T(8,128)(2,1)S(1)}, u32[]{:S(2)}, u32[]{:S(2)}) collective-permute-start(bf16[72,2048]{1,0:T(8,128)(2,1)S(1)} %get-tuple-element.25), channel_id=1, source_target_pairs={{0,4},{1,5},{2,6},{3,7},{4,0},{5,1},{6,2},{7,3},{8,12},{9,13},{10,... | collective-permute-start | bytes 884744 | tf_op jit(solution)/shard_map/ppermute | solution.py:20
  33.5 1.6 %pack_act.1 = (bf16[72,2048]{1,0:T(8,128)(2,1)S(1)}, bf16[72,2048]{1,0:T(8,128)(2,1)S(1)}) custom-call(s32[1]{0:T(128)} %bitcast.own_ref, s32[1,128]{1,0:T(1,128)S(1)} %bitcast.21, f32[1,2048]{1,0:T(1,128)S(1)} %copy-done.3, bf16[128,2048]{1,0:T(8,128)(2,1)} %collective-permute-done.refs_1_.x_ref), custom_call_target="tpu_custom_call" | custom-call | flops 1000 | bytes 1000 | tf_op jit(solution)/shard_map/pack_act/pallas_call | solution.py:208
  35.1 8.9 %collective-permute-done.11.refs_2_ = bf16[72,2048]{1,0:T(8,128)(2,1)S(1)} collective-permute-done((bf16[72,2048]{1,0:T(8,128)(2,1)S(1)}, bf16[72,2048]{1,0:T(8,128)(2,1)S(1)}, u32[]{:S(2)}, u32[]{:S(2)}) %collective-permute-start.11) | collective-permute-done | bytes 294944 | tf_op jit(solution)/shard_map/ppermute | solution.py:25
  44.0 1.6 %collective-permute-start.1 = (bf16[72,2048]{1,0:T(8,128)(2,1)S(1)}, bf16[72,2048]{1,0:T(8,128)(2,1)S(1)}, u32[]{:S(2)}, u32[]{:S(2)}) collective-permute-start(bf16[72,2048]{1,0:T(8,128)(2,1)S(1)} %get-tuple-element.17), channel_id=1, source_target_pairs={{0,4},{1,5},{2,6},{3,7},{4,0},{5,1},{6,2},{7,3},{8,12},{9,13},{10,... | collective-permute-start | bytes 884744 | tf_op jit(solution)/shard_map/ppermute | solution.py:20
  45.6 4.0 %collective-permute-done.12.refs_3_ = bf16[72,2048]{1,0:T(8,128)(2,1)S(1)} collective-permute-done((bf16[72,2048]{1,0:T(8,128)(2,1)S(1)}, bf16[72,2048]{1,0:T(8,128)(2,1)S(1)}, u32[]{:S(2)}, u32[]{:S(2)}) %collective-permute-start.12) | collective-permute-done | bytes 294944 | tf_op jit(solution)/shard_map/ppermute | solution.py:25
  49.6 2.8 %collective-permute-start.15 = (bf16[72,2048]{1,0:T(8,128)(2,1)S(1)}, bf16[72,2048]{1,0:T(8,128)(2,1)S(1)}, u32[]{:S(2)}, u32[]{:S(2)}) collective-permute-start(bf16[72,2048]{1,0:T(8,128)(2,1)S(1)} %collective-permute-done.13.refs_5_), channel_id=1, source_target_pairs={{0,2},{1,3},{2,0},{3,1},{4,6},{5,7},{6,4},{7,5},{8,10},{9,11},{10,... | collective-permute-start | bytes 884744 | tf_op jit(solution)/shard_map/ppermute | solution.py:25
  52.4 7.2 %collective-permute-done.5.refs_7_.refs_11_ = bf16[192,2048]{1,0:T(8,128)(2,1)S(1)} collective-permute-done((bf16[192,2048]{1,0:T(8,128)(2,1)}, bf16[192,2048]{1,0:T(8,128)(2,1)S(1)}, u32[]{:S(2)}, u32[]{:S(2)}) %collective-permute-start.5) | collective-permute-done | bytes 786464 | tf_op jit(solution)/shard_map/ppermute | solution.py:25
  59.6 1.8 %collective-permute-start.2 = (bf16[72,2048]{1,0:T(8,128)(2,1)S(1)}, bf16[72,2048]{1,0:T(8,128)(2,1)S(1)}, u32[]{:S(2)}, u32[]{:S(2)}) collective-permute-start(bf16[72,2048]{1,0:T(8,128)(2,1)S(1)} %get-tuple-element.16.refs_0_), channel_id=1, source_target_pairs={{0,2},{1,3},{2,0},{3,1},{4,6},{5,7},{6,4},{7,5},{8,10},{9,11},{10,... | collective-permute-start | bytes 884744 | tf_op jit(solution)/shard_map/ppermute | solution.py:25
  61.4 2.6 %collective-permute-done.1.refs_1_ = bf16[72,2048]{1,0:T(8,128)(2,1)S(1)} collective-permute-done((bf16[72,2048]{1,0:T(8,128)(2,1)S(1)}, bf16[72,2048]{1,0:T(8,128)(2,1)S(1)}, u32[]{:S(2)}, u32[]{:S(2)}) %collective-permute-start.1) | collective-permute-done | bytes 294944 | tf_op jit(solution)/shard_map/ppermute | solution.py:20
  64.0 1.7 %collective-permute-done.14.refs_6_ = bf16[72,2048]{1,0:T(8,128)(2,1)S(1)} collective-permute-done((bf16[72,2048]{1,0:T(8,128)(2,1)S(1)}, bf16[72,2048]{1,0:T(8,128)(2,1)S(1)}, u32[]{:S(2)}, u32[]{:S(2)}) %collective-permute-start.14) | collective-permute-done | bytes 294944 | tf_op jit(solution)/shard_map/ppermute | solution.py:25
  65.8 6.3 %collective-permute-done.15.refs_7_ = bf16[72,2048]{1,0:T(8,128)(2,1)S(1)} collective-permute-done((bf16[72,2048]{1,0:T(8,128)(2,1)S(1)}, bf16[72,2048]{1,0:T(8,128)(2,1)S(1)}, u32[]{:S(2)}, u32[]{:S(2)}) %collective-permute-start.15) | collective-permute-done | bytes 294944 | tf_op jit(solution)/shard_map/ppermute | solution.py:25
  72.1 3.7 %experts_bwd.1 = (f32[72,2048]{1,0:T(8,128)S(1)}, f32[72,2048]{1,0:T(8,128)S(1)}, bf16[72,2048]{1,0:T(8,128)(2,1)S(1)}, bf16[72,2048]{1,0:T(8,128)(2,1)S(1)}) custom-call(bf16[72,2048]{1,0:T(8,128)(2,1)S(1)} %get-tuple-element.22.refs_0_, bf16[72,2048]{1,0:T(8,128)(2,1)S(1)} %collective-permute-done.10.refs_1_, ...), custom_call_target="tpu_custom_call" | custom-call | flops 1000 | bytes 1000 | tf_op jit(solution)/shard_map/experts_bwd/pallas_call | solution.py:222
  75.9 2.0 %collective-permute-start.16 = (bf16[72,2048]{1,0:T(8,128)(2,1)S(1)}, bf16[72,2048]{1,0:T(8,128)(2,1)S(1)}, u32[]{:S(2)}, u32[]{:S(2)}) collective-permute-start(bf16[72,2048]{1,0:T(8,128)(2,1)S(1)} %get-tuple-element.27), channel_id=1, source_target_pairs={{0,2},{1,3},{2,0},{3,1},{4,6},{5,7},{6,4},{7,5},{8,10},{9,11},{10,... | collective-permute-start | bytes 884744 | tf_op jit(solution)/shard_map/ppermute | solution.py:25
  78.4 6.3 %collective-permute-done.3.refs_3_ = bf16[72,2048]{1,0:T(8,128)(2,1)S(1)} collective-permute-done((bf16[72,2048]{1,0:T(8,128)(2,1)S(1)}, bf16[72,2048]{1,0:T(8,128)(2,1)S(1)}, u32[]{:S(2)}, u32[]{:S(2)}) %collective-permute-start.3) | collective-permute-done | bytes 294944 | tf_op jit(solution)/shard_map/ppermute | solution.py:25
  84.7 2.3 %experts_fwd.1 = (f32[72,2048]{1,0:T(8,128)S(1)}, f32[72,2048]{1,0:T(8,128)S(1)}, bf16[72,2048]{1,0:T(8,128)(2,1)S(1)}, bf16[72,2048]{1,0:T(8,128)(2,1)S(1)}) custom-call(bf16[72,2048]{1,0:T(8,128)(2,1)S(1)} %get-tuple-element.16.refs_0_, bf16[72,2048]{1,0:T(8,128)(2,1)S(1)} %collective-permute-done.1.refs_1_, ...), custom_call_target="tpu_custom_call" | custom-call | flops 1000 | bytes 1000 | tf_op jit(solution)/shard_map/experts_fwd/pallas_call | solution.py:227
  87.2 2.0 %collective-permute-start.6 = (bf16[72,2048]{1,0:T(8,128)(2,1)S(1)}, bf16[72,2048]{1,0:T(8,128)(2,1)S(1)}, u32[]{:S(2)}, u32[]{:S(2)}) collective-permute-start(bf16[72,2048]{1,0:T(8,128)(2,1)S(1)} %get-tuple-element.19), channel_id=1, source_target_pairs={{0,2},{1,3},{2,0},{3,1},{4,6},{5,7},{6,4},{7,5},{8,10},{9,11},{10,... | collective-permute-start | bytes 884744 | tf_op jit(solution)/shard_map/ppermute | solution.py:25
  89.2 1.9 %collective-permute-done.17 = bf16[72,2048]{1,0:T(8,128)(2,1)S(1)} collective-permute-done((bf16[72,2048]{1,0:T(8,128)(2,1)S(1)}, bf16[72,2048]{1,0:T(8,128)(2,1)S(1)}, u32[]{:S(2)}, u32[]{:S(2)}) %collective-permute-start.17) | collective-permute-done | bytes 294944 | tf_op jit(solution)/shard_map/ppermute | solution.py:25
  91.1 1.7 %collective-permute-start.18 = (bf16[72,2048]{1,0:T(8,128)(2,1)S(1)}, bf16[72,2048]{1,0:T(8,128)(2,1)S(1)}, u32[]{:S(2)}, u32[]{:S(2)}) collective-permute-start(bf16[72,2048]{1,0:T(8,128)(2,1)S(1)} %add_convert_fusion), channel_id=1, source_target_pairs={{0,4},{1,5},{2,6},{3,7},{4,0},{5,1},{6,2},{7,3},{8,12},{9,13},{10,... | collective-permute-start | bytes 884744 | tf_op jit(solution)/shard_map/ppermute | solution.py:20
  92.8 17.2 %collective-permute-done.7 = bf16[72,2048]{1,0:T(8,128)(2,1)S(1)} collective-permute-done((bf16[72,2048]{1,0:T(8,128)(2,1)S(1)}, bf16[72,2048]{1,0:T(8,128)(2,1)S(1)}, u32[]{:S(2)}, u32[]{:S(2)}) %collective-permute-start.7) | collective-permute-done | bytes 294944 | tf_op jit(solution)/shard_map/ppermute | solution.py:25
  110.1 1.7 %collective-permute-start.8 = (bf16[72,2048]{1,0:T(8,128)(2,1)S(1)}, bf16[72,2048]{1,0:T(8,128)(2,1)S(1)}, u32[]{:S(2)}, u32[]{:S(2)}) collective-permute-start(bf16[72,2048]{1,0:T(8,128)(2,1)S(1)} %add_convert_fusion.1), channel_id=1, source_target_pairs={{0,4},{1,5},{2,6},{3,7},{4,0},{5,1},{6,2},{7,3},{8,12},{9,13},{10,... | collective-permute-start | bytes 884744 | tf_op jit(solution)/shard_map/ppermute | solution.py:20
  111.8 2.8 %home_bwd.1 = bf16[128,2048]{1,0:T(8,128)(2,1)} custom-call(s32[1]{0:T(128)} %bitcast.own_ref, s32[1,128]{1,0:T(1,128)S(1)} %bitcast.20, f32[1,128]{1,0:T(1,128)S(1)} %bitcast.24, f32[1,2048]{1,0:T(1,128)S(1)} %copy-done.3, bf16[128,2048]{1,0:T(8,128)(2,1)S(1)} %bitcast.17, bf16[128,2048]{1,0:T(8,128)(2,1)} %collective-permute-done.9.refs_0_.up_ref, ...), custom_call_target="tpu_custom_call" | custom-call | flops 1000 | bytes 1000 | tf_op jit(solution)/shard_map/home_bwd/pallas_call | solution.py:232
  114.6 12.5 %collective-permute-done.8.refs_2_ = bf16[72,2048]{1,0:T(8,128)(2,1)S(1)} collective-permute-done((bf16[72,2048]{1,0:T(8,128)(2,1)S(1)}, bf16[72,2048]{1,0:T(8,128)(2,1)S(1)}, u32[]{:S(2)}, u32[]{:S(2)}) %collective-permute-start.8) | collective-permute-done | bytes 294944 | tf_op jit(solution)/shard_map/ppermute | solution.py:20
  127.1 2.4 %home_fwd.1 = bf16[128,2048]{1,0:T(8,128)(2,1)} custom-call(s32[1]{0:T(128)} %bitcast.own_ref, s32[1,128]{1,0:T(1,128)S(1)} %bitcast.22, f32[1,128]{1,0:T(1,128)S(1)} %bitcast.23, bf16[128,2048]{1,0:T(8,128)(2,1)} %collective-permute-done.refs_1_.x_ref, f32[72,2048]{1,0:T(8,128)S(1)} %get-tuple-element.18.refs_0_, ...), custom_call_target="tpu_custom_call" | custom-call | flops 1000 | bytes 1000 | tf_op jit(solution)/shard_map/home_fwd/pallas_call | solution.py:239
  (36 shorter events, 3.3 us)
Async XLA Ops:
  0.6 1.5 %copy-start.8 = (bf16[1,2048,192]{1,2,0:T(8,128)(2,1)S(1)}, bf16[1,2048,192]{1,2,0:T(8,128)(2,1)}, u32[]{:S(2)}) copy-start(bf16[1,2048,192]{1,2,0:T(8,128)(2,1)} %param.16) | copy-start | bytes 2359300
  3.5 5.6 %copy-start.3 = (f32[1,2048]{1,0:T(1,128)S(1)}, f32[1,2048]{1,0:T(1,128)}, u32[]{:S(2)}) copy-start(f32[1,2048]{1,0:T(1,128)} %gain_ref.1) | copy-start | bytes 24580
  3.5 5.6 %copy-start.4 = (s32[1,128,1]{1,2,0:T(1,128)S(1)}, s32[1,128,1]{1,2,0:T(1,128)}, u32[]{:S(2)}) copy-start(s32[1,128,1]{1,2,0:T(1,128)} %param.20) | copy-start | bytes 1540
  3.5 30.0 %copy-start.5 = (s32[1,128,1]{1,2,0:T(1,128)S(1)}, s32[1,128,1]{1,2,0:T(1,128)}, u32[]{:S(2)}) copy-start(s32[1,128,1]{1,2,0:T(1,128)} %param.18) | copy-start | bytes 1540
  5.4 66.7 %collective-permute-start.4 = (bf16[2048,384]{1,0:T(8,128)(2,1)S(1)}, bf16[2048,384]{1,0:T(8,128)(2,1)S(1)}, u32[]{:S(2)}, u32[]{:S(2)}) collective-permute-start(bf16[2048,384]{1,0:T(8,128)(2,1)S(1)} %pad_maximum_fusion.refs_4_.refs_8_), channel_id=1, source_target_pairs={{0,1},{1,0},{2,3},{3,2},{4,5},{5,4},{6,7},{7,6},{8,9},{9,8},{10,11... | collective-permute-start | bytes 4718600 | tf_op jit(solution)/shard_map/ppermute | solution.py:25
  8.4 20.2 %collective-permute-start.9 = (bf16[128,2048]{1,0:T(8,128)(2,1)}, bf16[128,2048]{1,0:T(8,128)(2,1)}, u32[]{:S(2)}, u32[]{:S(2)}) collective-permute-start(bf16[128,2048]{1,0:T(8,128)(2,1)} %bitcast.11), channel_id=1, source_target_pairs={{0,24},{8,0},{16,8},{24,16},{1,25},{9,1},{17,9},{25,17},{2,26},{10... | collective-permute-start | bytes 1572872 | tf_op jit(solution)/shard_map/ppermute | solution.py:20
  9.0 22.3 %collective-permute-start = (bf16[128,2048]{1,0:T(8,128)(2,1)}, bf16[128,2048]{1,0:T(8,128)(2,1)}, u32[]{:S(2)}, u32[]{:S(2)}) collective-permute-start(bf16[128,2048]{1,0:T(8,128)(2,1)} %bitcast.3), channel_id=1, source_target_pairs={{0,8},{8,16},{16,24},{24,0},{1,9},{9,17},{17,25},{25,1},{2,10},{10... | collective-permute-start | bytes 1572872 | tf_op jit(solution)/shard_map/ppermute | solution.py:20
  9.1 63.0 %copy-start = (bf16[1,192,2048]{2,1,0:T(8,128)(2,1)S(1)}, bf16[1,192,2048]{2,1,0:T(8,128)(2,1)}, u32[]{:S(2)}) copy-start(bf16[1,192,2048]{2,1,0:T(8,128)(2,1)} %param.17) | copy-start | bytes 2359300
  9.1 1.1 copy-start.1
  10.7 17.1 %collective-permute-start.10 = (bf16[72,2048]{1,0:T(8,128)(2,1)S(1)}, bf16[72,2048]{1,0:T(8,128)(2,1)S(1)}, u32[]{:S(2)}, u32[]{:S(2)}) collective-permute-start(bf16[72,2048]{1,0:T(8,128)(2,1)S(1)} %get-tuple-element.23), channel_id=1, source_target_pairs={{0,4},{1,5},{2,6},{3,7},{4,0},{5,1},{6,2},{7,3},{8,12},{9,13},{10,... | collective-permute-start | bytes 884744 | tf_op jit(solution)/shard_map/ppermute | solution.py:20
  13.4 46.3 %collective-permute-start.5 = (bf16[192,2048]{1,0:T(8,128)(2,1)}, bf16[192,2048]{1,0:T(8,128)(2,1)S(1)}, u32[]{:S(2)}, u32[]{:S(2)}) collective-permute-start(bf16[192,2048]{1,0:T(8,128)(2,1)} %bitcast.13), channel_id=1, source_target_pairs={{0,1},{1,0},{2,3},{3,2},{4,5},{5,4},{6,7},{7,6},{8,9},{9,8},{10,11... | collective-permute-start | bytes 2359304 | tf_op jit(solution)/shard_map/ppermute | solution.py:25
  27.9 16.2 %collective-permute-start.11 = (bf16[72,2048]{1,0:T(8,128)(2,1)S(1)}, bf16[72,2048]{1,0:T(8,128)(2,1)S(1)}, u32[]{:S(2)}, u32[]{:S(2)}) collective-permute-start(bf16[72,2048]{1,0:T(8,128)(2,1)S(1)} %get-tuple-element.22.refs_0_), channel_id=1, source_target_pairs={{0,2},{1,3},{2,0},{3,1},{4,6},{5,7},{6,4},{7,5},{8,10},{9,11},{10,... | collective-permute-start | bytes 884744 | tf_op jit(solution)/shard_map/ppermute | solution.py:25
  28.5 21.1 %collective-permute-start.12 = (bf16[72,2048]{1,0:T(8,128)(2,1)S(1)}, bf16[72,2048]{1,0:T(8,128)(2,1)S(1)}, u32[]{:S(2)}, u32[]{:S(2)}) collective-permute-start(bf16[72,2048]{1,0:T(8,128)(2,1)S(1)} %collective-permute-done.10.refs_1_), channel_id=1, source_target_pairs={{0,2},{1,3},{2,0},{3,1},{4,6},{5,7},{6,4},{7,5},{8,10},{9,11},{10,... | collective-permute-start | bytes 884744 | tf_op jit(solution)/shard_map/ppermute | solution.py:25
  31.4 18.2 %collective-permute-start.13 = (bf16[72,2048]{1,0:T(8,128)(2,1)S(1)}, bf16[72,2048]{1,0:T(8,128)(2,1)S(1)}, u32[]{:S(2)}, u32[]{:S(2)}) collective-permute-start(bf16[72,2048]{1,0:T(8,128)(2,1)S(1)} %get-tuple-element.25), channel_id=1, source_target_pairs={{0,4},{1,5},{2,6},{3,7},{4,0},{5,1},{6,2},{7,3},{8,12},{9,13},{10,... | collective-permute-start | bytes 884744 | tf_op jit(solution)/shard_map/ppermute | solution.py:20
  44.0 20.0 %collective-permute-start.1 = (bf16[72,2048]{1,0:T(8,128)(2,1)S(1)}, bf16[72,2048]{1,0:T(8,128)(2,1)S(1)}, u32[]{:S(2)}, u32[]{:S(2)}) collective-permute-start(bf16[72,2048]{1,0:T(8,128)(2,1)S(1)} %get-tuple-element.17), channel_id=1, source_target_pairs={{0,4},{1,5},{2,6},{3,7},{4,0},{5,1},{6,2},{7,3},{8,12},{9,13},{10,... | collective-permute-start | bytes 884744 | tf_op jit(solution)/shard_map/ppermute | solution.py:20
  49.6 16.2 %collective-permute-start.14 = (bf16[72,2048]{1,0:T(8,128)(2,1)S(1)}, bf16[72,2048]{1,0:T(8,128)(2,1)S(1)}, u32[]{:S(2)}, u32[]{:S(2)}) collective-permute-start(bf16[72,2048]{1,0:T(8,128)(2,1)S(1)} %get-tuple-element.24.refs_4_), channel_id=1, source_target_pairs={{0,2},{1,3},{2,0},{3,1},{4,6},{5,7},{6,4},{7,5},{8,10},{9,11},{10,... | collective-permute-start | bytes 884744 | tf_op jit(solution)/shard_map/ppermute | solution.py:25
  49.6 22.5 %collective-permute-start.15 = (bf16[72,2048]{1,0:T(8,128)(2,1)S(1)}, bf16[72,2048]{1,0:T(8,128)(2,1)S(1)}, u32[]{:S(2)}, u32[]{:S(2)}) collective-permute-start(bf16[72,2048]{1,0:T(8,128)(2,1)S(1)} %collective-permute-done.13.refs_5_), channel_id=1, source_target_pairs={{0,2},{1,3},{2,0},{3,1},{4,6},{5,7},{6,4},{7,5},{8,10},{9,11},{10,... | collective-permute-start | bytes 884744 | tf_op jit(solution)/shard_map/ppermute | solution.py:25
  59.6 18.8 %collective-permute-start.2 = (bf16[72,2048]{1,0:T(8,128)(2,1)S(1)}, bf16[72,2048]{1,0:T(8,128)(2,1)S(1)}, u32[]{:S(2)}, u32[]{:S(2)}) collective-permute-start(bf16[72,2048]{1,0:T(8,128)(2,1)S(1)} %get-tuple-element.16.refs_0_), channel_id=1, source_target_pairs={{0,2},{1,3},{2,0},{3,1},{4,6},{5,7},{6,4},{7,5},{8,10},{9,11},{10,... | collective-permute-start | bytes 884744 | tf_op jit(solution)/shard_map/ppermute | solution.py:25
  64.0 20.7 %collective-permute-start.3 = (bf16[72,2048]{1,0:T(8,128)(2,1)S(1)}, bf16[72,2048]{1,0:T(8,128)(2,1)S(1)}, u32[]{:S(2)}, u32[]{:S(2)}) collective-permute-start(bf16[72,2048]{1,0:T(8,128)(2,1)S(1)} %collective-permute-done.1.refs_1_), channel_id=1, source_target_pairs={{0,2},{1,3},{2,0},{3,1},{4,6},{5,7},{6,4},{7,5},{8,10},{9,11},{10,... | collective-permute-start | bytes 884744 | tf_op jit(solution)/shard_map/ppermute | solution.py:25
  75.8 15.2 %collective-permute-start.17 = (bf16[72,2048]{1,0:T(8,128)(2,1)S(1)}, bf16[72,2048]{1,0:T(8,128)(2,1)S(1)}, u32[]{:S(2)}, u32[]{:S(2)}) collective-permute-start(bf16[72,2048]{1,0:T(8,128)(2,1)S(1)} %get-tuple-element.29), channel_id=1, source_target_pairs={{0,2},{1,3},{2,0},{3,1},{4,6},{5,7},{6,4},{7,5},{8,10},{9,11},{10,... | collective-permute-start | bytes 884744 | tf_op jit(solution)/shard_map/ppermute | solution.py:25
  75.9 35.8 %collective-permute-start.16 = (bf16[72,2048]{1,0:T(8,128)(2,1)S(1)}, bf16[72,2048]{1,0:T(8,128)(2,1)S(1)}, u32[]{:S(2)}, u32[]{:S(2)}) collective-permute-start(bf16[72,2048]{1,0:T(8,128)(2,1)S(1)} %get-tuple-element.27), channel_id=1, source_target_pairs={{0,2},{1,3},{2,0},{3,1},{4,6},{5,7},{6,4},{7,5},{8,10},{9,11},{10,... | collective-permute-start | bytes 884744 | tf_op jit(solution)/shard_map/ppermute | solution.py:25
  87.1 24.8 %copy-start.2 = (bf16[1,128,2048]{2,1,0:T(8,128)(2,1)S(1)}, bf16[1,128,2048]{2,1,0:T(8,128)(2,1)}, u32[]{:S(2)}) copy-start(bf16[1,128,2048]{2,1,0:T(8,128)(2,1)} %param.12) | copy-start | bytes 1572868
  87.1 24.8 %copy-start.7 = (f32[1,128,1]{1,2,0:T(1,128)S(1)}, f32[1,128,1]{1,2,0:T(1,128)}, u32[]{:S(2)}) copy-start(f32[1,128,1]{1,2,0:T(1,128)} %param.21) | copy-start | bytes 1540
  87.1 22.9 %collective-permute-start.7 = (bf16[72,2048]{1,0:T(8,128)(2,1)S(1)}, bf16[72,2048]{1,0:T(8,128)(2,1)S(1)}, u32[]{:S(2)}, u32[]{:S(2)}) collective-permute-start(bf16[72,2048]{1,0:T(8,128)(2,1)S(1)} %get-tuple-element.21), channel_id=1, source_target_pairs={{0,2},{1,3},{2,0},{3,1},{4,6},{5,7},{6,4},{7,5},{8,10},{9,11},{10,... | collective-permute-start | bytes 884744 | tf_op jit(solution)/shard_map/ppermute | solution.py:25
  87.2 27.5 %collective-permute-start.6 = (bf16[72,2048]{1,0:T(8,128)(2,1)S(1)}, bf16[72,2048]{1,0:T(8,128)(2,1)S(1)}, u32[]{:S(2)}, u32[]{:S(2)}) collective-permute-start(bf16[72,2048]{1,0:T(8,128)(2,1)S(1)} %get-tuple-element.19), channel_id=1, source_target_pairs={{0,2},{1,3},{2,0},{3,1},{4,6},{5,7},{6,4},{7,5},{8,10},{9,11},{10,... | collective-permute-start | bytes 884744 | tf_op jit(solution)/shard_map/ppermute | solution.py:25
  91.1 20.7 %collective-permute-start.18 = (bf16[72,2048]{1,0:T(8,128)(2,1)S(1)}, bf16[72,2048]{1,0:T(8,128)(2,1)S(1)}, u32[]{:S(2)}, u32[]{:S(2)}) collective-permute-start(bf16[72,2048]{1,0:T(8,128)(2,1)S(1)} %add_convert_fusion), channel_id=1, source_target_pairs={{0,4},{1,5},{2,6},{3,7},{4,0},{5,1},{6,2},{7,3},{8,12},{9,13},{10,... | collective-permute-start | bytes 884744 | tf_op jit(solution)/shard_map/ppermute | solution.py:20
  110.1 17.1 %copy-start.6 = (f32[1,128,1]{1,2,0:T(1,128)S(1)}, f32[1,128,1]{1,2,0:T(1,128)}, u32[]{:S(2)}) copy-start(f32[1,128,1]{1,2,0:T(1,128)} %param.19) | copy-start | bytes 1540
  110.1 17.1 %collective-permute-start.8 = (bf16[72,2048]{1,0:T(8,128)(2,1)S(1)}, bf16[72,2048]{1,0:T(8,128)(2,1)S(1)}, u32[]{:S(2)}, u32[]{:S(2)}) collective-permute-start(bf16[72,2048]{1,0:T(8,128)(2,1)S(1)} %add_convert_fusion.1), channel_id=1, source_target_pairs={{0,4},{1,5},{2,6},{3,7},{4,0},{5,1},{6,2},{7,3},{8,12},{9,13},{10,... | collective-permute-start | bytes 884744 | tf_op jit(solution)/shard_map/ppermute | solution.py:20

commit v3 on v2

--- a/solution.py
+++ b/solution.py
@@ -64,6 +64,18 @@
     return jnp.where((place == slot) & (block == j), 1.0, 0.0).astype(BF16)
 
 
+def join_body(*refs):
+    *parts, out, sems = refs
+    units = parts[0].shape[0]
+    copies = [
+        pltpu.make_async_copy(part, out.at[pl.ds(i * units, units), :], sems.at[i]) for i, part in enumerate(parts)
+    ]
+    for copy in copies:
+        copy.start()
+    for copy in copies:
+        copy.wait()
+
+
 def pack_body(experts, own_ref, routes_ref, *refs):
     if len(refs) == experts + 2:
         gain_ref, x_ref, *outs = refs
@@ -91,40 +103,47 @@
         ref[...] = total[i * pitch:i * pitch + ref.shape[0]].astype(ref.dtype)
 
 
+def thirds(share):
+    units = share.shape[0] // 3
+    return [share[pl.ds(i * units, units), :] for i in range(3)]
+
+
 def forward_body(count, *refs):
     row_refs, refs = refs[:count], refs[count:]
-    shares, refs = (refs[0:2], refs[2:4]), refs[4:]
+    shares, refs = refs[:2], refs[2:]
     outs, wide_ref = refs[:-1], refs[-1]
     pitch = gather_blocks(row_refs, wide_ref)
     rows = wide_ref[...]
     total = None
-    for gate_up, down in shares:
-        units = down.shape[0]
-        both = jnp.dot(rows, gate_up[...], preferred_element_type=F32)
-        hidden = (silu_parts(both[:, :units])[0] * both[:, units:]).astype(BF16)
-        part = jnp.dot(hidden, down[...], preferred_element_type=F32)
+    for share in shares:
+        gate, up, down = thirds(share)
+        gate_pre = lax.dot_general(rows, gate, CONTRACT, preferred_element_type=F32)
+        up_pre = lax.dot_general(rows, up, CONTRACT, preferred_element_type=F32)
+        hidden = (silu_parts(gate_pre)[0] * up_pre).astype(BF16)
+        part = jnp.dot(hidden, down, preferred_element_type=F32)
         total = part if total is None else total + part
     spread_out(total, outs, pitch)
 
 
 def backward_body(count, *refs):
     row_refs, grad_refs, refs = refs[:count], refs[count:2 * count], refs[2 * count:]
-    shares, refs = (refs[0:2], refs[2:4]), refs[4:]
+    shares, refs = refs[:2], refs[2:]
     outs, wide_ref, grad_wide_ref = refs[:-2], refs[-2], refs[-1]
     pitch = gather_blocks(row_refs, wide_ref)
     gather_blocks(grad_refs, grad_wide_ref)
     rows = wide_ref[...]
     grads = grad_wide_ref[...]
     total = None
-    for gate_up, down in shares:
-        units = down.shape[0]
-        both = jnp.dot(rows, gate_up[...], preferred_element_type=F32)
-        activation, derivative = silu_parts(both[:, :units])
-        d_hidden = lax.dot_general(grads, down[...], CONTRACT, preferred_element_type=F32)
-        d_gate = (d_hidden * both[:, units:] * derivative).astype(BF16)
+    for share in shares:
+        gate, up, down = thirds(share)
+        gate_pre = lax.dot_general(rows, gate, CONTRACT, preferred_element_type=F32)
+        up_pre = lax.dot_general(rows, up, CONTRACT, preferred_element_type=F32)
+        activation, derivative = silu_parts(gate_pre)
+        d_hidden = lax.dot_general(grads, down, CONTRACT, preferred_element_type=F32)
+        d_gate = (d_hidden * up_pre * derivative).astype(BF16)
         d_up = (d_hidden * activation).astype(BF16)
-        d_both = jnp.concatenate([d_gate, d_up], axis=1)
-        part = lax.dot_general(d_both, gate_up[...], CONTRACT, preferred_element_type=F32)
+        part = jnp.dot(d_gate, gate, preferred_element_type=F32)
+        part = part + jnp.dot(d_up, up, preferred_element_type=F32)
         total = part if total is None else total + part
     spread_out(total, outs, pitch)
 
@@ -163,19 +182,25 @@
     refs[-1][...] = (up_ref[...].astype(F32) + d_input).astype(BF16)
 
 
-def fetch_rows(blocks):
-    got = [blocks[0]] + [shifted(blocks[j], "expert", SPLIT * j) for j in range(1, len(blocks))]
-    return got + [swapped(block, "expert", 2) for block in got]
-
-
-def return_rows(partial):
+def after(value, *others):
+    return lax.optimization_barrier((value, *others))[0]
+
+
+def crossed(blocks):
+    return [blocks[0]] + [shifted(blocks[j], "expert", SPLIT * j) for j in range(1, len(blocks))]
+
+
+def partners(blocks, *others):
+    return [swapped(after(block, *others) if others else block, "expert", 2) for block in blocks]
+
+
+def crossing_home(partial):
     experts = len(partial) // 2
     mine, theirs = partial[:experts], partial[experts:]
-    home = []
-    for j in range(1, experts):
-        total = (mine[j] + swapped(theirs[j], "expert", 2).astype(F32)).astype(BF16)
-        home.append(shifted(total, "expert", -SPLIT * j))
-    return [mine[0], swapped(theirs[0], "expert", 2)] + home
+    totals = [
+        (mine[j] + swapped(theirs[j], "expert", 2).astype(F32)).astype(BF16) for j in range(1, experts)
+    ]
+    return totals, [shifted(totals[j - 1], "expert", -SPLIT * j) for j in range(1, experts)]
 
 
 def per_device(act_in, saved_in, grad_in, norm_gain, w_gate, w_up, w_down, routes_fwd, gates_fwd, routes_bwd, gates_bwd):
@@ -196,9 +221,6 @@
 
     incoming = shifted(act_in[0], "section", 1)
     upstream = shifted(grad_in[0], "section", -1)
-    gate_up = jnp.concatenate([w_gate[0], w_up[0]], axis=1)
-    down = w_down[0]
-    shares = (gate_up, down, swapped(gate_up, "expert", 1), swapped(down, "expert", 1))
     r_fwd = routes_fwd.reshape(1, tok_count)
     r_bwd = routes_bwd.reshape(1, tok_count)
     g_fwd = gates_fwd.reshape(1, tok_count)
@@ -213,21 +235,40 @@
             name=name,
         )(own, routes, *args)
 
-    rows_b = fetch_rows(pack("pack_saved", r_bwd, norm_gain, saved_in[0]))
-    rows_g = fetch_rows(pack("pack_grad", r_bwd, upstream))
-    rows_f = fetch_rows(pack("pack_act", r_fwd, norm_gain, incoming))
+    own_share = local_call(
+        join_body,
+        jax.ShapeDtypeStruct((3 * w_down.shape[1], width), BF16),
+        in_specs=[pl.BlockSpec(memory_space=pl.ANY)] * 3,
+        out_specs=pl.BlockSpec(memory_space=pl.ANY),
+        scratch=[pltpu.SemaphoreType.DMA((3,))],
+        name="join_weights",
+    )(w_gate[0].T, w_up[0].T, w_down[0])
+    shares = (own_share, swapped(own_share, "expert", 1))
+
+    packed_b = pack("pack_saved", r_bwd, norm_gain, saved_in[0])
+    rows_b = crossed(packed_b)
+    swap_b = partners(rows_b[:1])
+    packed_g = pack("pack_grad", r_bwd, after(upstream, packed_b[0]))
+    rows_g = crossed(packed_g)
+    packed_f = pack("pack_act", r_fwd, norm_gain, after(incoming, packed_g[0], rows_b[-1]))
+    rows_f = crossed(packed_f)
+    swap_g = partners(rows_g[:1], rows_b[-1])
+    swap_f = partners(rows_f[:1], rows_g[-1])
+    rows_b = rows_b + swap_b + partners(rows_b[1:], swap_b[0])
+    rows_g = rows_g + swap_g + partners(rows_g[1:], swap_g[0])
+    rows_f = rows_f + swap_f + partners(rows_f[1:], swap_f[0], rows_b[-1])
 
     count = 2 * experts
-    back_b = return_rows(
-        local_call(
-            functools.partial(backward_body, count), partial, scratch=[wide, wide], vmem_mib=40, name="experts_bwd"
-        )(*rows_b, *rows_g, *shares)
-    )
-    back_f = return_rows(
-        local_call(
-            functools.partial(forward_body, count), partial, scratch=[wide], vmem_mib=32, name="experts_fwd"
-        )(*rows_f, *shares)
-    )
+    partial_b = local_call(
+        functools.partial(backward_body, count), partial, scratch=[wide, wide], vmem_mib=40, name="experts_bwd"
+    )(*rows_b, *rows_g, *shares)
+    partial_f = local_call(
+        functools.partial(forward_body, count), partial, scratch=[wide], vmem_mib=32, name="experts_fwd"
+    )(after(rows_f[0], partial_b[0]), *rows_f[1:], *shares)
+    totals_b, home_b = crossing_home(partial_b)
+    totals_f, home_f = crossing_home(partial_f)
+    back_b = [partial_b[0]] + partners(partial_b[experts:experts + 1], *totals_f) + home_b
+    back_f = [partial_f[0]] + partners(partial_f[experts:experts + 1], *totals_f) + home_f
 
     grad_out = local_call(
         functools.partial(backward_home_body, experts),

time: 130 us -> 113 us (0.87)
  waiting for transfers between devices: 83.2 us -> 63.6 us
  starting transfers between devices: 24.7 us -> 29.1 us
  other arithmetic: 1.98 us -> 0.11 us
    ppermute x7, waiting for transfers between devices: 29.1 us -> 18.8 us  [shifted(): lax.ppermute(value, axis, [(i, (i + steps) % count) for i in range(count)])]
    ppermute x12 -> x11, waiting for transfers between devices: 54.1 us -> 44.7 us  [swapped(): return lax.ppermute(value, axis, [(i, i ^ bit) for i in range(count)])]
    ppermute x7, starting transfers between devices: 10.3 us -> 19.2 us  [shifted(): lax.ppermute(value, axis, [(i, (i + steps) % count) for i in range(count)])]
    ppermute x12 -> x11, starting transfers between devices: 14.4 us -> 9.91 us  [swapped(): return lax.ppermute(value, axis, [(i, i ^ bit) for i in range(count)])]
    pallas_call x1, Pallas kernels: 3.72 us -> 7.33 us  [per_device(): local_call(functools.partial(backward_body, count), partial, scratch=[wid...]
    pallas_call x3, Pallas kernels: 3.57 us -> 1.5 us  [pack(): local_call(functools.partial(pack_body, experts), packed, in_specs=[scala...]
    concatenate x1 -> x0, other arithmetic: 1.87 us -> none  [per_device(): gate_up = jnp.concatenate([w_gate[0], w_up[0]], axis=1)]
    pallas_call x1, Pallas kernels: 2.33 us -> 3.95 us  [per_device(): local_call(functools.partial(forward_body, count), partial, scratch=[wide...]
  transfers between devices with their start and end apart: 19 -> 18, of which waited for: 13 -> 13; matrix products, arithmetic and copies ran while one was open for 0% -> 0% of each run, Pallas kernels for 10% -> 13%
where the time goes in v3:
time: 113 us
  waiting for transfers between devices  63.6 us (56%)
  starting transfers between devices  29.1 us (26%)
  Pallas kernels  16.2 us (14%)
  local copies, waits for them, and re-layouts  3.42 us (3%)
    ppermute x11, waiting for transfers between devices, swapped(): return lax.ppermute(value, axis, [(i, i ^ bit) for i in range(count)])  44.7 us
    ppermute x7, starting transfers between devices, shifted(): lax.ppermute(value, axis, [(i, (i + steps) % count) for i in range(count)])  19.2 us
    ppermute x7, waiting for transfers between devices, shifted(): lax.ppermute(value, axis, [(i, (i + steps) % count) for i in range(count)])  18.8 us
    ppermute x11, starting transfers between devices, swapped(): return lax.ppermute(value, axis, [(i, i ^ bit) for i in range(count)])  9.91 us
    pallas_call x1, Pallas kernels, per_device(): local_call(functools.partial(backward_body, count), partial, scratch=[wid...  7.33 us
    pallas_call x1, Pallas kernels, per_device(): local_call(functools.partial(forward_body, count), partial, scratch=[wide...  3.95 us
    unnamed x18, local copies, waits for them, and re-layouts  3.42 us
  transfers between devices with their start and end apart: 18, of which 13 were waited for; matrix products, arithmetic and copies ran while one was open for 0% of the time, Pallas kernels for 13%

profile of v3, /device:TPU:0, one launch (start us, length us, event | category | flops | bytes accessed | tf_op | source)
XLA Modules:
  0.0 113.1 jit_solution(16715115200980206606)
XLA Ops:
  0.6 1.1 copy-done.1
  1.8 1.1 copy-done.2
  2.9 1.1 copy-done.3
  4.2 3.0 %collective-permute-start.8 = (bf16[576,2048]{1,0:T(8,128)(2,1)S(1)}, bf16[576,2048]{1,0:T(8,128)(2,1)}, u32[]{:S(2)}, u32[]{:S(2)}) collective-permute-start(bf16[576,2048]{1,0:T(8,128)(2,1)S(1)} %join_weights.1.refs_8_.refs_4_), channel_id=1, source_target_pairs={{0,1},{1,0},{2,3},{3,2},{4,5},{5,4},{6,7},{7,6},{8,9},{9,8},{10,11... | collective-permute-start | bytes 7077896 | tf_op jit(solution)/shard_map/ppermute | solution.py:25
  7.3 0.7 collective-permute-start.1
  8.5 2.6 %collective-permute-start.2 = (bf16[72,2048]{1,0:T(8,128)(2,1)S(1)}, bf16[72,2048]{1,0:T(8,128)(2,1)S(1)}, u32[]{:S(2)}, u32[]{:S(2)}) collective-permute-start(bf16[72,2048]{1,0:T(8,128)(2,1)S(1)} %get-tuple-element.29), channel_id=1, source_target_pairs={{0,4},{1,5},{2,6},{3,7},{4,0},{5,1},{6,2},{7,3},{8,12},{9,13},{10,... | collective-permute-start | bytes 884744 | tf_op jit(solution)/shard_map/ppermute | solution.py:20
  11.1 1.6 %collective-permute-start.3 = (bf16[72,2048]{1,0:T(8,128)(2,1)S(1)}, bf16[72,2048]{1,0:T(8,128)(2,1)S(1)}, u32[]{:S(2)}, u32[]{:S(2)}) collective-permute-start(bf16[72,2048]{1,0:T(8,128)(2,1)S(1)} %get-tuple-element.26.refs_0_), channel_id=1, source_target_pairs={{0,2},{1,3},{2,0},{3,1},{4,6},{5,7},{6,4},{7,5},{8,10},{9,11},{10,... | collective-permute-start | bytes 884744 | tf_op jit(solution)/shard_map/ppermute | solution.py:25
  12.7 4.3 %collective-permute-done.1.refs_0_.up_ref = bf16[128,2048]{1,0:T(8,128)(2,1)S(1)} collective-permute-done((bf16[128,2048]{1,0:T(8,128)(2,1)}, bf16[128,2048]{1,0:T(8,128)(2,1)S(1)}, u32[]{:S(2)}, u32[]{:S(2)}) %collective-permute-start.1) | collective-permute-done | bytes 524320 | tf_op jit(solution)/shard_map/ppermute | solution.py:20
  17.5 4.9 %collective-permute-start.5 = (bf16[72,2048]{1,0:T(8,128)(2,1)S(1)}, bf16[72,2048]{1,0:T(8,128)(2,1)S(1)}, u32[]{:S(2)}, u32[]{:S(2)}) collective-permute-start(bf16[72,2048]{1,0:T(8,128)(2,1)S(1)} %get-tuple-element.33), channel_id=1, source_target_pairs={{0,4},{1,5},{2,6},{3,7},{4,0},{5,1},{6,2},{7,3},{8,12},{9,13},{10,... | collective-permute-start | bytes 884744 | tf_op jit(solution)/shard_map/ppermute | solution.py:20
  22.4 2.3 %collective-permute-done.2.refs_1_ = bf16[72,2048]{1,0:T(8,128)(2,1)S(1)} collective-permute-done((bf16[72,2048]{1,0:T(8,128)(2,1)S(1)}, bf16[72,2048]{1,0:T(8,128)(2,1)S(1)}, u32[]{:S(2)}, u32[]{:S(2)}) %collective-permute-start.2) | collective-permute-done | bytes 294944 | tf_op jit(solution)/shard_map/ppermute | solution.py:20
  24.7 0.6 collective-permute-start.6
  25.3 2.0 %collective-permute-done.3.refs_2_ = bf16[72,2048]{1,0:T(8,128)(2,1)S(1)} collective-permute-done((bf16[72,2048]{1,0:T(8,128)(2,1)S(1)}, bf16[72,2048]{1,0:T(8,128)(2,1)S(1)}, u32[]{:S(2)}, u32[]{:S(2)}) %collective-permute-start.3) | collective-permute-done | bytes 294944 | tf_op jit(solution)/shard_map/ppermute | solution.py:25
  27.9 2.0 %collective-permute-start.9 = (bf16[72,2048]{1,0:T(8,128)(2,1)S(1)}, bf16[72,2048]{1,0:T(8,128)(2,1)S(1)}, u32[]{:S(2)}, u32[]{:S(2)}) collective-permute-start(bf16[72,2048]{1,0:T(8,128)(2,1)S(1)} %get-tuple-element.38), channel_id=1, source_target_pairs={{0,4},{1,5},{2,6},{3,7},{4,0},{5,1},{6,2},{7,3},{8,12},{9,13},{10,... | collective-permute-start | bytes 884744 | tf_op jit(solution)/shard_map/ppermute | solution.py:20
  29.9 7.5 %collective-permute-done.5.refs_5_ = bf16[72,2048]{1,0:T(8,128)(2,1)S(1)} collective-permute-done((bf16[72,2048]{1,0:T(8,128)(2,1)S(1)}, bf16[72,2048]{1,0:T(8,128)(2,1)S(1)}, u32[]{:S(2)}, u32[]{:S(2)}) %collective-permute-start.5) | collective-permute-done | bytes 294944 | tf_op jit(solution)/shard_map/ppermute | solution.py:20
  37.9 8.3 %collective-permute-done.6.refs_6_ = bf16[72,2048]{1,0:T(8,128)(2,1)S(1)} collective-permute-done((bf16[72,2048]{1,0:T(8,128)(2,1)S(1)}, bf16[72,2048]{1,0:T(8,128)(2,1)S(1)}, u32[]{:S(2)}, u32[]{:S(2)}) %collective-permute-start.6) | collective-permute-done | bytes 294944 | tf_op jit(solution)/shard_map/ppermute | solution.py:25
  46.2 6.3 %collective-permute-done.4.refs_3_ = bf16[72,2048]{1,0:T(8,128)(2,1)S(1)} collective-permute-done((bf16[72,2048]{1,0:T(8,128)(2,1)S(1)}, bf16[72,2048]{1,0:T(8,128)(2,1)S(1)}, u32[]{:S(2)}, u32[]{:S(2)}) %collective-permute-start.4) | collective-permute-done | bytes 294944 | tf_op jit(solution)/shard_map/ppermute | solution.py:25
  52.5 6.3 %collective-permute-done.10.refs_2_ = bf16[72,2048]{1,0:T(8,128)(2,1)S(1)} collective-permute-done((bf16[72,2048]{1,0:T(8,128)(2,1)S(1)}, bf16[72,2048]{1,0:T(8,128)(2,1)S(1)}, u32[]{:S(2)}, u32[]{:S(2)}) %collective-permute-start.10) | collective-permute-done | bytes 294944 | tf_op jit(solution)/shard_map/ppermute | solution.py:25
  58.8 6.3 %collective-permute-done.7.refs_7_ = bf16[72,2048]{1,0:T(8,128)(2,1)S(1)} collective-permute-done((bf16[72,2048]{1,0:T(8,128)(2,1)S(1)}, bf16[72,2048]{1,0:T(8,128)(2,1)S(1)}, u32[]{:S(2)}, u32[]{:S(2)}) %collective-permute-start.7) | collective-permute-done | bytes 294944 | tf_op jit(solution)/shard_map/ppermute | solution.py:25
  65.2 7.3 %experts_bwd.1 = (f32[72,2048]{1,0:T(8,128)S(1)}, f32[72,2048]{1,0:T(8,128)S(1)}, bf16[72,2048]{1,0:T(8,128)(2,1)S(1)}, bf16[72,2048]{1,0:T(8,128)(2,1)S(1)}) custom-call(bf16[72,2048]{1,0:T(8,128)(2,1)S(1)} %get-tuple-element.26.refs_0_, bf16[72,2048]{1,0:T(8,128)(2,1)S(1)} %collective-permute-done.2.refs_1_, ...), custom_call_target="tpu_custom_call" | custom-call | flops 1000 | bytes 1000 | tf_op jit(solution)/shard_map/experts_bwd/pallas_call | solution.py:262
  72.6 3.9 %experts_fwd.1 = (f32[72,2048]{1,0:T(8,128)S(1)}, f32[72,2048]{1,0:T(8,128)S(1)}, bf16[72,2048]{1,0:T(8,128)(2,1)S(1)}, bf16[72,2048]{1,0:T(8,128)(2,1)S(1)}) custom-call(bf16[72,2048]{1,0:T(8,128)(2,1)S(1)} %get-tuple-element.39.refs_0_, bf16[72,2048]{1,0:T(8,128)(2,1)S(1)} %collective-permute-done.9.refs_1_, ...), custom_call_target="tpu_custom_call" | custom-call | flops 1000 | bytes 1000 | tf_op jit(solution)/shard_map/experts_fwd/pallas_call | solution.py:265
  76.6 2.1 %collective-permute-start.12 = (bf16[72,2048]{1,0:T(8,128)(2,1)S(1)}, bf16[72,2048]{1,0:T(8,128)(2,1)S(1)}, u32[]{:S(2)}, u32[]{:S(2)}) collective-permute-start(bf16[72,2048]{1,0:T(8,128)(2,1)S(1)} %get-tuple-element.44), channel_id=1, source_target_pairs={{0,2},{1,3},{2,0},{3,1},{4,6},{5,7},{6,4},{7,5},{8,10},{9,11},{10,... | collective-permute-start | bytes 884744 | tf_op jit(solution)/shard_map/ppermute | solution.py:25
  78.6 2.4 %collective-permute-done.16 = bf16[72,2048]{1,0:T(8,128)(2,1)S(1)} collective-permute-done((bf16[72,2048]{1,0:T(8,128)(2,1)S(1)}, bf16[72,2048]{1,0:T(8,128)(2,1)S(1)}, u32[]{:S(2)}, u32[]{:S(2)}) %collective-permute-start.16) | collective-permute-done | bytes 294944 | tf_op jit(solution)/shard_map/ppermute | solution.py:25
  81.1 6.2 %collective-permute-start.17 = (bf16[72,2048]{1,0:T(8,128)(2,1)S(1)}, bf16[72,2048]{1,0:T(8,128)(2,1)S(1)}, u32[]{:S(2)}, u32[]{:S(2)}) collective-permute-start(bf16[72,2048]{1,0:T(8,128)(2,1)S(1)} %add_convert_fusion), channel_id=1, source_target_pairs={{0,4},{1,5},{2,6},{3,7},{4,0},{5,1},{6,2},{7,3},{8,12},{9,13},{10,... | collective-permute-start | bytes 884744 | tf_op jit(solution)/shard_map/ppermute | solution.py:20
  87.3 1.9 %collective-permute-done.12 = bf16[72,2048]{1,0:T(8,128)(2,1)S(1)} collective-permute-done((bf16[72,2048]{1,0:T(8,128)(2,1)S(1)}, bf16[72,2048]{1,0:T(8,128)(2,1)S(1)}, u32[]{:S(2)}, u32[]{:S(2)}) %collective-permute-start.12) | collective-permute-done | bytes 294944 | tf_op jit(solution)/shard_map/ppermute | solution.py:25
  89.2 0.8 collective-permute-start.15
  90.1 1.3 %collective-permute-start.13 = (bf16[72,2048]{1,0:T(8,128)(2,1)S(1)}, bf16[72,2048]{1,0:T(8,128)(2,1)S(1)}, u32[]{:S(2)}, u32[]{:S(2)}) collective-permute-start(bf16[72,2048]{1,0:T(8,128)(2,1)S(1)} %get-tuple-element.45), channel_id=1, source_target_pairs={{0,2},{1,3},{2,0},{3,1},{4,6},{5,7},{6,4},{7,5},{8,10},{9,11},{10,... | collective-permute-start | bytes 884744 | tf_op jit(solution)/shard_map/ppermute | solution.py:25
  91.3 2.7 %collective-permute-start.14 = (bf16[72,2048]{1,0:T(8,128)(2,1)S(1)}, bf16[72,2048]{1,0:T(8,128)(2,1)S(1)}, u32[]{:S(2)}, u32[]{:S(2)}) collective-permute-start(bf16[72,2048]{1,0:T(8,128)(2,1)S(1)} %add_convert_fusion.1), channel_id=1, source_target_pairs={{0,4},{1,5},{2,6},{3,7},{4,0},{5,1},{6,2},{7,3},{8,12},{9,13},{10,... | collective-permute-start | bytes 884744 | tf_op jit(solution)/shard_map/ppermute | solution.py:20
  94.1 4.7 %collective-permute-done.17.refs_2_ = bf16[72,2048]{1,0:T(8,128)(2,1)S(1)} collective-permute-done((bf16[72,2048]{1,0:T(8,128)(2,1)S(1)}, bf16[72,2048]{1,0:T(8,128)(2,1)S(1)}, u32[]{:S(2)}, u32[]{:S(2)}) %collective-permute-start.17) | collective-permute-done | bytes 294944 | tf_op jit(solution)/shard_map/ppermute | solution.py:20
  98.7 8.6 %collective-permute-done.15.refs_1_ = bf16[72,2048]{1,0:T(8,128)(2,1)S(1)} collective-permute-done((bf16[72,2048]{1,0:T(8,128)(2,1)S(1)}, bf16[72,2048]{1,0:T(8,128)(2,1)S(1)}, u32[]{:S(2)}, u32[]{:S(2)}) %collective-permute-start.15) | collective-permute-done | bytes 294944 | tf_op jit(solution)/shard_map/ppermute | solution.py:25
  107.3 1.8 %home_bwd.1 = bf16[128,2048]{1,0:T(8,128)(2,1)} custom-call(s32[1]{0:T(128)} %bitcast.own_ref, s32[1,128]{1,0:T(1,128)S(1)} %bitcast.24, f32[1,128]{1,0:T(1,128)S(1)} %bitcast.28, f32[1,2048]{1,0:T(1,128)S(1)} %copy-done.4, bf16[128,2048]{1,0:T(8,128)(2,1)S(1)} %bitcast.18, bf16[128,2048]{1,0:T(8,128)(2,1)S(1)} %collective-permute-done.1.refs_0_.up_ref, ...), custom_call_target="tpu_custom_call" | custom-call | flops 1000 | bytes 1000 | tf_op jit(solution)/shard_map/home_bwd/pallas_call | solution.py:273
  109.1 2.6 %collective-permute-done.13.refs_1_ = bf16[72,2048]{1,0:T(8,128)(2,1)S(1)} collective-permute-done((bf16[72,2048]{1,0:T(8,128)(2,1)S(1)}, bf16[72,2048]{1,0:T(8,128)(2,1)S(1)}, u32[]{:S(2)}, u32[]{:S(2)}) %collective-permute-start.13) | collective-permute-done | bytes 294944 | tf_op jit(solution)/shard_map/ppermute | solution.py:25
  111.7 1.4 %home_fwd.1 = bf16[128,2048]{1,0:T(8,128)(2,1)} custom-call(s32[1]{0:T(128)} %bitcast.own_ref, s32[1,128]{1,0:T(1,128)S(1)} %bitcast.26, f32[1,128]{1,0:T(1,128)S(1)} %bitcast.27, bf16[128,2048]{1,0:T(8,128)(2,1)S(1)} %collective-permute-done.refs_1_.x_ref, f32[72,2048]{1,0:T(8,128)S(1)} %get-tuple-element.41.refs_0_, ...), custom_call_target="tpu_custom_call" | custom-call | flops 1000 | bytes 1000 | tf_op jit(solution)/shard_map/home_fwd/pallas_call | solution.py:280
  (32 shorter events, 2.4 us)
Async XLA Ops:
  0.6 1.1 %copy-start.1 = (bf16[1,2048,192]{1,2,0:T(8,128)(2,1)S(1)}, bf16[1,2048,192]{1,2,0:T(8,128)(2,1)}, u32[]{:S(2)}) copy-start(bf16[1,2048,192]{1,2,0:T(8,128)(2,1)} %param.15) | copy-start | bytes 2359300
  1.8 1.1 %copy-start.2 = (bf16[1,2048,192]{1,2,0:T(8,128)(2,1)S(1)}, bf16[1,2048,192]{1,2,0:T(8,128)(2,1)}, u32[]{:S(2)}) copy-start(bf16[1,2048,192]{1,2,0:T(8,128)(2,1)} %param.16) | copy-start | bytes 2359300
  2.9 1.1 %copy-start.3 = (bf16[1,192,2048]{2,1,0:T(8,128)(2,1)S(1)}, bf16[1,192,2048]{2,1,0:T(8,128)(2,1)}, u32[]{:S(2)}) copy-start(bf16[1,192,2048]{2,1,0:T(8,128)(2,1)} %param.17) | copy-start | bytes 2359300
  4.0 3.9 %copy-start = (bf16[1,128,2048]{2,1,0:T(8,128)(2,1)S(1)}, bf16[1,128,2048]{2,1,0:T(8,128)(2,1)}, u32[]{:S(2)}) copy-start(bf16[1,128,2048]{2,1,0:T(8,128)(2,1)} %param.12) | copy-start | bytes 1572868
  4.0 3.9 %copy-start.4 = (f32[1,2048]{1,0:T(1,128)S(1)}, f32[1,2048]{1,0:T(1,128)}, u32[]{:S(2)}) copy-start(f32[1,2048]{1,0:T(1,128)} %gain_ref.1) | copy-start | bytes 24580
  4.0 3.9 %copy-start.5 = (s32[1,128,1]{1,2,0:T(1,128)S(1)}, s32[1,128,1]{1,2,0:T(1,128)}, u32[]{:S(2)}) copy-start(s32[1,128,1]{1,2,0:T(1,128)} %param.20) | copy-start | bytes 1540
  4.0 23.3 %copy-start.6 = (s32[1,128,1]{1,2,0:T(1,128)S(1)}, s32[1,128,1]{1,2,0:T(1,128)}, u32[]{:S(2)}) copy-start(s32[1,128,1]{1,2,0:T(1,128)} %param.18) | copy-start | bytes 1540
  4.2 60.9 %collective-permute-start.8 = (bf16[576,2048]{1,0:T(8,128)(2,1)S(1)}, bf16[576,2048]{1,0:T(8,128)(2,1)}, u32[]{:S(2)}, u32[]{:S(2)}) collective-permute-start(bf16[576,2048]{1,0:T(8,128)(2,1)S(1)} %join_weights.1.refs_8_.refs_4_), channel_id=1, source_target_pairs={{0,1},{1,0},{2,3},{3,2},{4,5},{5,4},{6,7},{7,6},{8,9},{9,8},{10,11... | collective-permute-start | bytes 7077896 | tf_op jit(solution)/shard_map/ppermute | solution.py:25
  7.3 9.8 %collective-permute-start.1 = (bf16[128,2048]{1,0:T(8,128)(2,1)}, bf16[128,2048]{1,0:T(8,128)(2,1)S(1)}, u32[]{:S(2)}, u32[]{:S(2)}) collective-permute-start(bf16[128,2048]{1,0:T(8,128)(2,1)} %bitcast.5), channel_id=1, source_target_pairs={{0,24},{8,0},{16,8},{24,16},{1,25},{9,1},{17,9},{25,17},{2,26},{10... | collective-permute-start | bytes 1572872 | tf_op jit(solution)/shard_map/ppermute | solution.py:20
  8.5 16.3 %collective-permute-start.2 = (bf16[72,2048]{1,0:T(8,128)(2,1)S(1)}, bf16[72,2048]{1,0:T(8,128)(2,1)S(1)}, u32[]{:S(2)}, u32[]{:S(2)}) collective-permute-start(bf16[72,2048]{1,0:T(8,128)(2,1)S(1)} %get-tuple-element.29), channel_id=1, source_target_pairs={{0,4},{1,5},{2,6},{3,7},{4,0},{5,1},{6,2},{7,3},{8,12},{9,13},{10,... | collective-permute-start | bytes 884744 | tf_op jit(solution)/shard_map/ppermute | solution.py:20
  11.1 16.2 %collective-permute-start = (bf16[128,2048]{1,0:T(8,128)(2,1)}, bf16[128,2048]{1,0:T(8,128)(2,1)S(1)}, u32[]{:S(2)}, u32[]{:S(2)}) collective-permute-start(bf16[128,2048]{1,0:T(8,128)(2,1)} %bitcast.31), channel_id=1, source_target_pairs={{0,8},{8,16},{16,24},{24,0},{1,9},{9,17},{17,25},{25,1},{2,10},{10... | collective-permute-start | bytes 1572872 | tf_op jit(solution)/shard_map/ppermute | solution.py:20
  11.1 16.2 %collective-permute-start.3 = (bf16[72,2048]{1,0:T(8,128)(2,1)S(1)}, bf16[72,2048]{1,0:T(8,128)(2,1)S(1)}, u32[]{:S(2)}, u32[]{:S(2)}) collective-permute-start(bf16[72,2048]{1,0:T(8,128)(2,1)S(1)} %get-tuple-element.26.refs_0_), channel_id=1, source_target_pairs={{0,2},{1,3},{2,0},{3,1},{4,6},{5,7},{6,4},{7,5},{8,10},{9,11},{10,... | collective-permute-start | bytes 884744 | tf_op jit(solution)/shard_map/ppermute | solution.py:25
  17.5 19.9 %collective-permute-start.5 = (bf16[72,2048]{1,0:T(8,128)(2,1)S(1)}, bf16[72,2048]{1,0:T(8,128)(2,1)S(1)}, u32[]{:S(2)}, u32[]{:S(2)}) collective-permute-start(bf16[72,2048]{1,0:T(8,128)(2,1)S(1)} %get-tuple-element.33), channel_id=1, source_target_pairs={{0,4},{1,5},{2,6},{3,7},{4,0},{5,1},{6,2},{7,3},{8,12},{9,13},{10,... | collective-permute-start | bytes 884744 | tf_op jit(solution)/shard_map/ppermute | solution.py:20
  24.7 21.5 %collective-permute-start.6 = (bf16[72,2048]{1,0:T(8,128)(2,1)S(1)}, bf16[72,2048]{1,0:T(8,128)(2,1)S(1)}, u32[]{:S(2)}, u32[]{:S(2)}) collective-permute-start(bf16[72,2048]{1,0:T(8,128)(2,1)S(1)} %get-tuple-element.34.refs_4_), channel_id=1, source_target_pairs={{0,2},{1,3},{2,0},{3,1},{4,6},{5,7},{6,4},{7,5},{8,10},{9,11},{10,... | collective-permute-start | bytes 884744 | tf_op jit(solution)/shard_map/ppermute | solution.py:25
  27.3 25.2 %collective-permute-start.4 = (bf16[72,2048]{1,0:T(8,128)(2,1)S(1)}, bf16[72,2048]{1,0:T(8,128)(2,1)S(1)}, u32[]{:S(2)}, u32[]{:S(2)}) collective-permute-start(bf16[72,2048]{1,0:T(8,128)(2,1)S(1)} %collective-permute-done.2.refs_1_), channel_id=1, source_target_pairs={{0,2},{1,3},{2,0},{3,1},{4,6},{5,7},{6,4},{7,5},{8,10},{9,11},{10,... | collective-permute-start | bytes 884744 | tf_op jit(solution)/shard_map/ppermute | solution.py:25
  27.9 24.7 %collective-permute-start.9 = (bf16[72,2048]{1,0:T(8,128)(2,1)S(1)}, bf16[72,2048]{1,0:T(8,128)(2,1)S(1)}, u32[]{:S(2)}, u32[]{:S(2)}) collective-permute-start(bf16[72,2048]{1,0:T(8,128)(2,1)S(1)} %get-tuple-element.38), channel_id=1, source_target_pairs={{0,4},{1,5},{2,6},{3,7},{4,0},{5,1},{6,2},{7,3},{8,12},{9,13},{10,... | collective-permute-start | bytes 884744 | tf_op jit(solution)/shard_map/ppermute | solution.py:20
  37.4 21.4 %collective-permute-start.10 = (bf16[72,2048]{1,0:T(8,128)(2,1)S(1)}, bf16[72,2048]{1,0:T(8,128)(2,1)S(1)}, u32[]{:S(2)}, u32[]{:S(2)}) collective-permute-start(bf16[72,2048]{1,0:T(8,128)(2,1)S(1)} %get-tuple-element.39.refs_0_), channel_id=1, source_target_pairs={{0,2},{1,3},{2,0},{3,1},{4,6},{5,7},{6,4},{7,5},{8,10},{9,11},{10,... | collective-permute-start | bytes 884744 | tf_op jit(solution)/shard_map/ppermute | solution.py:25
  46.2 19.0 %collective-permute-start.7 = (bf16[72,2048]{1,0:T(8,128)(2,1)S(1)}, bf16[72,2048]{1,0:T(8,128)(2,1)S(1)}, u32[]{:S(2)}, u32[]{:S(2)}) collective-permute-start(bf16[72,2048]{1,0:T(8,128)(2,1)S(1)} %collective-permute-done.5.refs_5_), channel_id=1, source_target_pairs={{0,2},{1,3},{2,0},{3,1},{4,6},{5,7},{6,4},{7,5},{8,10},{9,11},{10,... | collective-permute-start | bytes 884744 | tf_op jit(solution)/shard_map/ppermute | solution.py:25
  58.8 13.7 %collective-permute-start.11 = (bf16[72,2048]{1,0:T(8,128)(2,1)S(1)}, bf16[72,2048]{1,0:T(8,128)(2,1)S(1)}, u32[]{:S(2)}, u32[]{:S(2)}) collective-permute-start(bf16[72,2048]{1,0:T(8,128)(2,1)S(1)} %collective-permute-done.9.refs_1_), channel_id=1, source_target_pairs={{0,2},{1,3},{2,0},{3,1},{4,6},{5,7},{6,4},{7,5},{8,10},{9,11},{10,... | collective-permute-start | bytes 884744 | tf_op jit(solution)/shard_map/ppermute | solution.py:25
  72.5 8.5 %collective-permute-start.16 = (bf16[72,2048]{1,0:T(8,128)(2,1)S(1)}, bf16[72,2048]{1,0:T(8,128)(2,1)S(1)}, u32[]{:S(2)}, u32[]{:S(2)}) collective-permute-start(bf16[72,2048]{1,0:T(8,128)(2,1)S(1)} %get-tuple-element.49), channel_id=1, source_target_pairs={{0,2},{1,3},{2,0},{3,1},{4,6},{5,7},{6,4},{7,5},{8,10},{9,11},{10,... | collective-permute-start | bytes 884744 | tf_op jit(solution)/shard_map/ppermute | solution.py:25
  76.5 30.8 %copy-start.8 = (f32[1,128,1]{1,2,0:T(1,128)S(1)}, f32[1,128,1]{1,2,0:T(1,128)}, u32[]{:S(2)}) copy-start(f32[1,128,1]{1,2,0:T(1,128)} %param.21) | copy-start | bytes 1540
  76.6 12.6 %collective-permute-start.12 = (bf16[72,2048]{1,0:T(8,128)(2,1)S(1)}, bf16[72,2048]{1,0:T(8,128)(2,1)S(1)}, u32[]{:S(2)}, u32[]{:S(2)}) collective-permute-start(bf16[72,2048]{1,0:T(8,128)(2,1)S(1)} %get-tuple-element.44), channel_id=1, source_target_pairs={{0,2},{1,3},{2,0},{3,1},{4,6},{5,7},{6,4},{7,5},{8,10},{9,11},{10,... | collective-permute-start | bytes 884744 | tf_op jit(solution)/shard_map/ppermute | solution.py:25
  81.0 30.7 %copy-start.7 = (f32[1,128,1]{1,2,0:T(1,128)S(1)}, f32[1,128,1]{1,2,0:T(1,128)}, u32[]{:S(2)}) copy-start(f32[1,128,1]{1,2,0:T(1,128)} %param.19) | copy-start | bytes 1540
  81.1 17.6 %collective-permute-start.17 = (bf16[72,2048]{1,0:T(8,128)(2,1)S(1)}, bf16[72,2048]{1,0:T(8,128)(2,1)S(1)}, u32[]{:S(2)}, u32[]{:S(2)}) collective-permute-start(bf16[72,2048]{1,0:T(8,128)(2,1)S(1)} %add_convert_fusion), channel_id=1, source_target_pairs={{0,4},{1,5},{2,6},{3,7},{4,0},{5,1},{6,2},{7,3},{8,12},{9,13},{10,... | collective-permute-start | bytes 884744 | tf_op jit(solution)/shard_map/ppermute | solution.py:20
  89.2 18.1 %collective-permute-start.15 = (bf16[72,2048]{1,0:T(8,128)(2,1)S(1)}, bf16[72,2048]{1,0:T(8,128)(2,1)S(1)}, u32[]{:S(2)}, u32[]{:S(2)}) collective-permute-start(bf16[72,2048]{1,0:T(8,128)(2,1)S(1)} %get-tuple-element.47), channel_id=1, source_target_pairs={{0,2},{1,3},{2,0},{3,1},{4,6},{5,7},{6,4},{7,5},{8,10},{9,11},{10,... | collective-permute-start | bytes 884744 | tf_op jit(solution)/shard_map/ppermute | solution.py:25
  90.1 21.7 %collective-permute-start.13 = (bf16[72,2048]{1,0:T(8,128)(2,1)S(1)}, bf16[72,2048]{1,0:T(8,128)(2,1)S(1)}, u32[]{:S(2)}, u32[]{:S(2)}) collective-permute-start(bf16[72,2048]{1,0:T(8,128)(2,1)S(1)} %get-tuple-element.45), channel_id=1, source_target_pairs={{0,2},{1,3},{2,0},{3,1},{4,6},{5,7},{6,4},{7,5},{8,10},{9,11},{10,... | collective-permute-start | bytes 884744 | tf_op jit(solution)/shard_map/ppermute | solution.py:25
  91.3 20.4 %collective-permute-start.14 = (bf16[72,2048]{1,0:T(8,128)(2,1)S(1)}, bf16[72,2048]{1,0:T(8,128)(2,1)S(1)}, u32[]{:S(2)}, u32[]{:S(2)}) collective-permute-start(bf16[72,2048]{1,0:T(8,128)(2,1)S(1)} %add_convert_fusion.1), channel_id=1, source_target_pairs={{0,4},{1,5},{2,6},{3,7},{4,0},{5,1},{6,2},{7,3},{8,12},{9,13},{10,... | collective-permute-start | bytes 884744 | tf_op jit(solution)/shard_map/ppermute | solution.py:20

commit v4 on v3

v4 whole, which is shorter than its diff:
```python
import functools
import math

import jax
import jax.numpy as jnp
from jax import lax
from jax.experimental import pallas as pl
from jax.experimental.pallas import tpu as pltpu
from jax.sharding import PartitionSpec as P

SPLIT = 4
EPS = 1e-06
CONTRACT = (((1,), (1,)), ((), ()))
OVER_ROWS = (((0,), (0,)), ((), ()))
F32 = jnp.float32
BF16 = jnp.bfloat16


def shifted(value, axis, steps):
    count = lax.axis_size(axis)
    return lax.ppermute(value, axis, [(i, (i + steps) % count) for i in range(count)])


def swapped(value, axis, bit):
    count = lax.axis_size(axis)
    return lax.ppermute(value, axis, [(i, i ^ bit) for i in range(count)])


def after(value, *others):
    return lax.optimization_barrier((value, *others))[0] if others else value


def local_call(body, out_shape, scratch=(), vmem_mib=16, **names):
    return pl.pallas_call(
        body,
        out_shape=out_shape,
        scratch_shapes=scratch,
        compiler_params=pltpu.CompilerParams(vmem_limit_bytes=vmem_mib << 20),
        cost_estimate=pl.CostEstimate(flops=1000, bytes_accessed=1000, transcendentals=0),
        **names,
    )


def silu_parts(values):
    sigma = jax.nn.sigmoid(values)
    return (values * sigma, sigma * (1.0 + values * (1.0 - sigma)))


def inverse_rms(values):
    return lax.rsqrt(jnp.mean(values * values, axis=-1, keepdims=True) + EPS)


def slots_of(routes, own, experts):
    count = routes.shape[1]
    height = -(-experts // 8) * 8
    ids = lax.broadcasted_iota(jnp.int32, (height, count), 0)
    onehot = (ids == routes).astype(F32)
    earlier = (
        lax.broadcasted_iota(jnp.int32, (count, count), 0) < lax.broadcasted_iota(jnp.int32, (count, count), 1)
    ).astype(F32)
    before = jnp.dot(onehot.astype(BF16), earlier.astype(BF16), preferred_element_type=F32)
    slot = jnp.sum(before * onehot, axis=0, keepdims=True).astype(jnp.int32)
    block = routes - own
    return (jnp.where(block < 0, block + experts, block), slot)


def chooser_of(block, slot, j, piece, rows, height):
    place = lax.broadcasted_iota(jnp.int32, (height, block.shape[1]), 0)
    return jnp.where((place == slot + piece * rows) & (block == j), 1.0, 0.0).astype(BF16)


def pack(values, own_ref, routes_ref, outs):
    experts = len(outs)
    height, cols = outs[0].shape
    pieces = values.shape[1] // cols
    rows = height // pieces
    block, slot = slots_of(routes_ref[...], own_ref[0], experts)
    for j, out in enumerate(outs):
        total = None
        for p in range(pieces):
            chooser = chooser_of(block, slot, j, p, rows, height)
            part = jnp.dot(chooser, values[:, p * cols:(p + 1) * cols], preferred_element_type=F32)
            total = part if total is None else total + part
        out[...] = total.astype(BF16)


def normed(x_ref, gain_ref):
    values = x_ref[...].astype(F32)
    return (values * inverse_rms(values) * gain_ref[...]).astype(BF16)


def pack_grad_body(own_ref, routes_ref, x_ref, *outs):
    pack(x_ref[...], own_ref, routes_ref, outs)


def pack_act_body(own_ref, routes_ref, gain_ref, x_ref, *outs):
    pack(normed(x_ref, gain_ref), own_ref, routes_ref, outs)


def first_body(own_ref, routes_ref, gain_ref, x_ref, *refs):
    parts, joined, outs, sems = refs[:3], refs[3], refs[4:-1], refs[-1]
    units = parts[0].shape[0]
    copies = [
        pltpu.make_async_copy(part, joined.at[pl.ds(i * units, units), :], sems.at[i]) for i, part in enumerate(parts)
    ]
    for copy in copies:
        copy.start()
    pack(normed(x_ref, gain_ref), own_ref, routes_ref, outs)
    for copy in copies:
        copy.wait()


def unpack(refs, wide_ref, rows):
    pitch = wide_ref.shape[0] // len(refs)
    pieces = refs[0].shape[0] // rows
    for i, ref in enumerate(refs):
        value = ref[...].astype(F32)
        whole = jnp.concatenate([value[p * rows:(p + 1) * rows] for p in range(pieces)], axis=1)
        wide_ref[pl.ds(i * pitch, rows), :] = whole.astype(BF16)
    return wide_ref[...]


def spread_out(total, refs, pitch, rows):
    for i, ref in enumerate(refs):
        cols = ref.shape[1]
        whole = total[i * pitch:i * pitch + rows]
        pieces = [whole[:, p * cols:(p + 1) * cols] for p in range(ref.shape[0] // rows)]
        ref[...] = jnp.concatenate(pieces, axis=0).astype(ref.dtype)


def third(shares, i):
    units = shares[0].shape[0] // 3
    return jnp.concatenate([share[pl.ds(i * units, units), :] for share in shares], axis=0)


def forward_body(count, rows, *refs):
    row_refs, shares, outs, wide_ref = refs[:count], refs[count:count + 2], refs[count + 2:-1], refs[-1]
    x = unpack(row_refs, wide_ref, rows)
    gate_pre = lax.dot_general(x, third(shares, 0), CONTRACT, preferred_element_type=F32)
    up_pre = lax.dot_general(x, third(shares, 1), CONTRACT, preferred_element_type=F32)
    hidden = (silu_parts(gate_pre)[0] * up_pre).astype(BF16)
    total = jnp.dot(hidden, third(shares, 2), preferred_element_type=F32)
    spread_out(total, outs, x.shape[0] // count, rows)


def backward_body(count, rows, *refs):
    row_refs, grad_refs, shares = refs[:count], refs[count:2 * count], refs[2 * count:2 * count + 2]
    outs, wide_ref, grad_wide_ref = refs[2 * count + 2:-2], refs[-2], refs[-1]
    x = unpack(row_refs, wide_ref, rows)
    gate, up = third(shares, 0), third(shares, 1)
    gate_pre = lax.dot_general(x, gate, CONTRACT, preferred_element_type=F32)
    up_pre = lax.dot_general(x, up, CONTRACT, preferred_element_type=F32)
    activation, derivative = silu_parts(gate_pre)
    grads = unpack(grad_refs, grad_wide_ref, rows)
    d_hidden = lax.dot_general(grads, third(shares, 2), CONTRACT, preferred_element_type=F32)
    d_gate = (d_hidden * up_pre * derivative).astype(BF16)
    d_up = (d_hidden * activation).astype(BF16)
    total = jnp.dot(d_gate, gate, preferred_element_type=F32) + jnp.dot(d_up, up, preferred_element_type=F32)
    spread_out(total, outs, x.shape[0] // count, rows)


def routed_sum(experts, rows, own_ref, routes_ref, gates_ref, home_refs):
    block, slot = slots_of(routes_ref[...], own_ref[0], experts)
    mine, theirs, *crossed_refs = home_refs
    blocks = [(mine[...] + theirs[...].astype(F32)).astype(BF16)] + [ref[...] for ref in crossed_refs]
    height = blocks[0].shape[0]
    columns = []
    for p in range(height // rows):
        total = None
        for j in range(experts):
            chooser = chooser_of(block, slot, j, p, rows, height)
            part = lax.dot_general(chooser, blocks[j], OVER_ROWS, preferred_element_type=F32)
            total = part if total is None else total + part
        columns.append(total)
    count = block.shape[1]
    diagonal = lax.broadcasted_iota(jnp.int32, (count, count), 0) == lax.broadcasted_iota(
        jnp.int32, (count, count), 1
    )
    gates = jnp.sum(jnp.where(diagonal, gates_ref[...], 0.0), axis=1, keepdims=True)
    return jnp.concatenate(columns, axis=1) * gates


def forward_home_body(experts, rows, own_ref, routes_ref, gates_ref, x_ref, *refs):
    mixed = routed_sum(experts, rows, own_ref, routes_ref, gates_ref, refs[:-1])
    refs[-1][...] = (x_ref[...].astype(F32) + mixed).astype(BF16)


def backward_home_body(experts, rows, own_ref, routes_ref, gates_ref, gain_ref, saved_ref, up_ref, *refs):
    d_norm = routed_sum(experts, rows, own_ref, routes_ref, gates_ref, refs[:-1])
    base = saved_ref[...].astype(F32)
    inv_scale = inverse_rms(base)
    scaled = d_norm * gain_ref[...]
    d_input = inv_scale * (
        scaled - base * inv_scale * inv_scale * jnp.mean(scaled * base, axis=-1, keepdims=True)
    )
    refs[-1][...] = (up_ref[...].astype(F32) + d_input).astype(BF16)


def crossed(blocks):
    return [blocks[0]] + [shifted(blocks[j], "expert", SPLIT * j) for j in range(1, len(blocks))]


def partners(blocks, *others):
    return [swapped(after(block, *others), "expert", 2) for block in blocks]


def crossing_home(partial):
    experts = len(partial) // 2
    mine, theirs = partial[:experts], partial[experts:]
    totals = [
        (mine[j] + swapped(theirs[j], "expert", 2).astype(F32)).astype(BF16) for j in range(1, experts)
    ]
    return totals, [shifted(totals[j - 1], "expert", -SPLIT * j) for j in range(1, experts)]


def per_device(act_in, saved_in, grad_in, norm_gain, w_gate, w_up, w_down, routes_fwd, gates_fwd, routes_bwd, gates_bwd):
    experts = lax.axis_size("expert") // SPLIT
    own = (lax.axis_index("expert") // SPLIT).astype(jnp.int32).reshape(1)
    tok_count, top_count = routes_fwd.shape[1:]
    assert top_count == 1
    width = act_in.shape[2]
    rows = min(tok_count, tok_count // experts + 2)
    pieces = 8 // math.gcd(rows, 8)
    pitch = -(-rows // 16) * 16
    scalar = pl.BlockSpec(memory_space=pltpu.SMEM)
    whole = pl.BlockSpec(memory_space=pltpu.VMEM)

    shape = (pieces * rows, width // pieces)
    packed = [jax.ShapeDtypeStruct(shape, BF16)] * experts
    partial = [jax.ShapeDtypeStruct(shape, F32)] * experts + packed
    tokens = jax.ShapeDtypeStruct((tok_count, width), BF16)
    wide = pltpu.VMEM((2 * experts * pitch, width), BF16)

    incoming = shifted(act_in[0], "section", 1)
    upstream = shifted(grad_in[0], "section", -1)
    r_fwd = routes_fwd.reshape(1, tok_count)
    r_bwd = routes_bwd.reshape(1, tok_count)
    g_fwd = gates_fwd.reshape(1, tok_count)
    g_bwd = gates_bwd.reshape(1, tok_count)

    own_share, *packed_b = local_call(
        first_body,
        [jax.ShapeDtypeStruct((3 * w_down.shape[1], width), BF16)] + packed,
        in_specs=[scalar] + [whole] * 3 + [pl.BlockSpec(memory_space=pltpu.HBM)] * 3,
        out_specs=[pl.BlockSpec(memory_space=pl.ANY)] + [whole] * experts,
        scratch=[pltpu.SemaphoreType.DMA((3,))],
        name="join_weights_pack_saved",
    )(own, r_bwd, norm_gain, saved_in[0], w_gate[0].T, w_up[0].T, w_down[0])
    shares = (own_share, swapped(own_share, "expert", 1))

    rows_b = crossed(packed_b)
    swap_b = partners(rows_b[:1])
    packed_g = local_call(
        pack_grad_body,
        packed,
        in_specs=[scalar] + [whole] * 2,
        out_specs=[whole] * experts,
        name="pack_grad",
    )(own, r_bwd, after(upstream, packed_b[0]))
    rows_g = crossed(packed_g)
    packed_f = local_call(
        pack_act_body,
        packed,
        in_specs=[scalar] + [whole] * 3,
        out_specs=[whole] * experts,
        name="pack_act",
    )(own, r_fwd, norm_gain, after(incoming, packed_g[0], rows_b[-1]))
    rows_f = crossed(packed_f)
    swap_g = partners(rows_g[:1], rows_b[-1])
    swap_f = partners(rows_f[:1], rows_g[-1])
    rows_b = rows_b + swap_b + partners(rows_b[1:], swap_b[0])
    rows_g = rows_g + swap_g + partners(rows_g[1:], swap_g[0])
    rows_f = rows_f + swap_f + partners(rows_f[1:], swap_f[0], rows_b[-1])

    count = 2 * experts
    partial_b = local_call(
        functools.partial(backward_body, count, rows), partial, scratch=[wide, wide], vmem_mib=40, name="experts_bwd"
    )(*rows_b, *rows_g, *shares)
    partial_f = local_call(
        functools.partial(forward_body, count, rows), partial, scratch=[wide], vmem_mib=32, name="experts_fwd"
    )(after(rows_f[0], partial_b[0]), *rows_f[1:], *shares)
    totals_b, home_b = crossing_home(partial_b)
    totals_f, home_f = crossing_home(partial_f)
    back_b = [partial_b[0]] + partners(partial_b[experts:experts + 1], *totals_b) + home_b
    back_f = [partial_f[0]] + partners(partial_f[experts:experts + 1], *totals_f) + home_f

    grad_out = local_call(
        functools.partial(backward_home_body, experts, rows),
        tokens,
        in_specs=[scalar] + [whole] * (6 + experts),
        out_specs=whole,
        name="home_bwd",
    )(own, r_bwd, g_bwd, norm_gain, saved_in[0], upstream, *back_b)
    act_out = local_call(
        functools.partial(forward_home_body, experts, rows),
        tokens,
        in_specs=[scalar] + [whole] * (4 + experts),
        out_specs=whole,
        name="home_fwd",
    )(own, r_fwd, g_fwd, incoming, *back_f)
    return (act_out[None], grad_out[None])


def solution(mesh):
    tokens = P("section", "expert", None)
    in_specs = (
        tokens,
        tokens,
        tokens,
        P("section", None),
        P("section", None, "expert"),
        P("section", None, "expert"),
        tokens,
        tokens,
        tokens,
        tokens,
        tokens,
    )
    return jax.shard_map(
        per_device, mesh=mesh, in_specs=in_specs, out_specs=(tokens, tokens), check_vma=False
    )
```

time: 113 us -> 107 us (0.947)
  Pallas kernels: 16.2 us -> 12.6 us
  waiting for transfers between devices: 63.6 us -> 60.2 us
  local copies, waits for them, and re-layouts: 3.42 us -> 5.82 us
  starting transfers between devices: 29.1 us -> 27.1 us
    ppermute x7, starting transfers between devices: 19.2 us -> 12.6 us  [shifted(): lax.ppermute(value, axis, [(i, (i + steps) % count) for i in range(count)])]
    ppermute x11, starting transfers between devices: 9.91 us -> 14.5 us  [swapped(): return lax.ppermute(value, axis, [(i, i ^ bit) for i in range(count)])]
    pallas_call x8 -> x7, Pallas kernels: 16.2 us -> 12.6 us  [the longest x1 3.63 us: per_device(): local_call(functools.partial(backward_body, count, rows), partial, scratc...]
    ppermute x7, waiting for transfers between devices: 18.8 us -> 16.2 us  [shifted(): lax.ppermute(value, axis, [(i, (i + steps) % count) for i in range(count)])]
    unnamed x18 -> x28, local copies, waits for them, and re-layouts: 3.42 us -> 5.82 us
  transfers between devices with their start and end apart: 18 -> 18, of which waited for: 13 -> 12; matrix products, arithmetic and copies ran while one was open for 0% -> 0% of each run, Pallas kernels for 13% -> 9%
where the time goes in v4:
time: 107 us
  waiting for transfers between devices  60.2 us (56%)
  starting transfers between devices  27.1 us (25%)
  Pallas kernels  12.6 us (12%)
  local copies, waits for them, and re-layouts  5.82 us (5%)
    ppermute x11, waiting for transfers between devices, swapped(): return lax.ppermute(value, axis, [(i, i ^ bit) for i in range(count)])  44 us
    ppermute x7, waiting for transfers between devices, shifted(): lax.ppermute(value, axis, [(i, (i + steps) % count) for i in range(count)])  16.2 us
    ppermute x11, starting transfers between devices, swapped(): return lax.ppermute(value, axis, [(i, i ^ bit) for i in range(count)])  14.5 us
    ppermute x7, starting transfers between devices, shifted(): lax.ppermute(value, axis, [(i, (i + steps) % count) for i in range(count)])  12.6 us
    unnamed x28, local copies, waits for them, and re-layouts  5.82 us
    pallas_call x1, Pallas kernels, per_device(): local_call(functools.partial(backward_body, count, rows), partial, scratc...  3.63 us
    pallas_call x1, Pallas kernels, per_device(): local_call(functools.partial(forward_body, count, rows), partial, scratch...  2.25 us
  transfers between devices with their start and end apart: 18, of which 12 were waited for; matrix products, arithmetic and copies ran while one was open for 0% of the time, Pallas kernels for 9%

profile of v4, /device:TPU:0, one launch (start us, length us, event | category | flops | bytes accessed | tf_op | source)
XLA Modules:
  0.0 106.6 jit_solution(11373461773045006613)
XLA Ops:
  0.7 1.0 copy-done
  1.7 1.1 %copy-done.2 = bf16[1,2048,192]{1,2,0:T(8,128)(2,1)S(1)} copy-done((bf16[1,2048,192]{1,2,0:T(8,128)(2,1)S(1)}, bf16[1,2048,192]{1,2,0:T(8,128)(2,1)}, u32[]{:S(2)}) %copy-start.2) | copy-done | bytes 786456
  2.8 1.1 %copy-done.3 = bf16[1,2048,192]{1,2,0:T(8,128)(2,1)S(1)} copy-done((bf16[1,2048,192]{1,2,0:T(8,128)(2,1)S(1)}, bf16[1,2048,192]{1,2,0:T(8,128)(2,1)}, u32[]{:S(2)}) %copy-start.3) | copy-done | bytes 786456
  4.0 1.1 %copy-done.4 = bf16[1,192,2048]{2,1,0:T(8,128)(2,1)S(1)} copy-done((bf16[1,192,2048]{2,1,0:T(8,128)(2,1)S(1)}, bf16[1,192,2048]{2,1,0:T(8,128)(2,1)}, u32[]{:S(2)}) %copy-start.4) | copy-done | bytes 786456
  6.5 1.1 %join_weights_pack_saved.1 = (bf16[576,2048]{1,0:T(8,128)(2,1)S(1)}, bf16[264,512]{1,0:T(8,128)(2,1)S(1)}, bf16[264,512]{1,0:T(8,128)(2,1)S(1)}) custom-call(s32[1]{0:T(128)} %bitcast.own_ref, s32[1,128]{1,0:T(1,128)S(1)} %bitcast.22, f32[1,2048]{1,0:T(1,128)S(1)} %copy-done.5, bf16[128,2048]{1,0:T(8,128)(2,1)S(1)} %bitcast.17, ...), custom_call_target="tpu_custom_call" | custom-call | flops 1000 | bytes 1000 | tf_op jit(solution)/shard_map/join_weights_pack_saved/pallas_call | solution.py:241
  7.6 3.0 %collective-permute-start.8 = (bf16[576,2048]{1,0:T(8,128)(2,1)S(1)}, bf16[576,2048]{1,0:T(8,128)(2,1)S(1)}, u32[]{:S(2)}, u32[]{:S(2)}) collective-permute-start(bf16[576,2048]{1,0:T(8,128)(2,1)S(1)} %get-tuple-element.37.refs_8_.refs_4_), channel_id=1, source_target_pairs={{0,1},{1,0},{2,3},{3,2},{4,5},{5,4},{6,7},{7,6},{8,9},{9,8},{10,11... | collective-permute-start | bytes 7077896 | tf_op jit(solution)/shard_map/ppermute | solution.py:26
  11.3 2.6 %collective-permute-start.2 = (bf16[264,512]{1,0:T(8,128)(2,1)S(1)}, bf16[264,512]{1,0:T(8,128)(2,1)S(1)}, u32[]{:S(2)}, u32[]{:S(2)}) collective-permute-start(bf16[264,512]{1,0:T(8,128)(2,1)S(1)} %get-tuple-element.30), channel_id=1, source_target_pairs={{0,4},{1,5},{2,6},{3,7},{4,0},{5,1},{6,2},{7,3},{8,12},{9,13},{10,... | collective-permute-start | bytes 811016 | tf_op jit(solution)/shard_map/ppermute | solution.py:21
  13.9 1.6 %collective-permute-start.3 = (bf16[264,512]{1,0:T(8,128)(2,1)S(1)}, bf16[264,512]{1,0:T(8,128)(2,1)S(1)}, u32[]{:S(2)}, u32[]{:S(2)}) collective-permute-start(bf16[264,512]{1,0:T(8,128)(2,1)S(1)} %get-tuple-element.27.refs_0_), channel_id=1, source_target_pairs={{0,2},{1,3},{2,0},{3,1},{4,6},{5,7},{6,4},{7,5},{8,10},{9,11},{10,... | collective-permute-start | bytes 811016 | tf_op jit(solution)/shard_map/ppermute | solution.py:26
  15.4 7.8 %collective-permute-done.1.x_ref.up_ref = bf16[128,2048]{1,0:T(8,128)(2,1)S(1)} collective-permute-done((bf16[128,2048]{1,0:T(8,128)(2,1)S(1)}, bf16[128,2048]{1,0:T(8,128)(2,1)S(1)}, u32[]{:S(2)}, u32[]{:S(2)}) %collective-permute-start.1) | collective-permute-done | bytes 524320 | tf_op jit(solution)/shard_map/ppermute | solution.py:21
  24.1 2.7 %collective-permute-start.5 = (bf16[264,512]{1,0:T(8,128)(2,1)S(1)}, bf16[264,512]{1,0:T(8,128)(2,1)S(1)}, u32[]{:S(2)}, u32[]{:S(2)}) collective-permute-start(bf16[264,512]{1,0:T(8,128)(2,1)S(1)} %get-tuple-element.34), channel_id=1, source_target_pairs={{0,4},{1,5},{2,6},{3,7},{4,0},{5,1},{6,2},{7,3},{8,12},{9,13},{10,... | collective-permute-start | bytes 811016 | tf_op jit(solution)/shard_map/ppermute | solution.py:21
  27.4 1.0 collective-permute-start.6
  28.4 1.0 collective-permute-start.4
  29.4 0.9 pack_act.1
  30.3 2.1 %collective-permute-start.9 = (bf16[264,512]{1,0:T(8,128)(2,1)S(1)}, bf16[264,512]{1,0:T(8,128)(2,1)S(1)}, u32[]{:S(2)}, u32[]{:S(2)}) collective-permute-start(bf16[264,512]{1,0:T(8,128)(2,1)S(1)} %get-tuple-element.40), channel_id=1, source_target_pairs={{0,4},{1,5},{2,6},{3,7},{4,0},{5,1},{6,2},{7,3},{8,12},{9,13},{10,... | collective-permute-start | bytes 811016 | tf_op jit(solution)/shard_map/ppermute | solution.py:21
  32.4 7.7 %collective-permute-done.5.refs_5_ = bf16[264,512]{1,0:T(8,128)(2,1)S(1)} collective-permute-done((bf16[264,512]{1,0:T(8,128)(2,1)S(1)}, bf16[264,512]{1,0:T(8,128)(2,1)S(1)}, u32[]{:S(2)}, u32[]{:S(2)}) %collective-permute-start.5) | collective-permute-done | bytes 270368 | tf_op jit(solution)/shard_map/ppermute | solution.py:21
  41.0 6.2 %collective-permute-done.6.refs_6_ = bf16[264,512]{1,0:T(8,128)(2,1)S(1)} collective-permute-done((bf16[264,512]{1,0:T(8,128)(2,1)S(1)}, bf16[264,512]{1,0:T(8,128)(2,1)S(1)}, u32[]{:S(2)}, u32[]{:S(2)}) %collective-permute-start.6) | collective-permute-done | bytes 270368 | tf_op jit(solution)/shard_map/ppermute | solution.py:26
  47.2 5.8 %collective-permute-done.4.refs_3_ = bf16[264,512]{1,0:T(8,128)(2,1)S(1)} collective-permute-done((bf16[264,512]{1,0:T(8,128)(2,1)S(1)}, bf16[264,512]{1,0:T(8,128)(2,1)S(1)}, u32[]{:S(2)}, u32[]{:S(2)}) %collective-permute-start.4) | collective-permute-done | bytes 270368 | tf_op jit(solution)/shard_map/ppermute | solution.py:26
  53.0 5.8 %collective-permute-done.10.refs_2_ = bf16[264,512]{1,0:T(8,128)(2,1)S(1)} collective-permute-done((bf16[264,512]{1,0:T(8,128)(2,1)S(1)}, bf16[264,512]{1,0:T(8,128)(2,1)S(1)}, u32[]{:S(2)}, u32[]{:S(2)}) %collective-permute-start.10) | collective-permute-done | bytes 270368 | tf_op jit(solution)/shard_map/ppermute | solution.py:26
  59.1 5.4 %collective-permute-done.7.refs_7_ = bf16[264,512]{1,0:T(8,128)(2,1)S(1)} collective-permute-done((bf16[264,512]{1,0:T(8,128)(2,1)S(1)}, bf16[264,512]{1,0:T(8,128)(2,1)S(1)}, u32[]{:S(2)}, u32[]{:S(2)}) %collective-permute-start.7) | collective-permute-done | bytes 270368 | tf_op jit(solution)/shard_map/ppermute | solution.py:26
  64.5 3.6 %experts_bwd.1 = (f32[264,512]{1,0:T(8,128)S(1)}, f32[264,512]{1,0:T(8,128)S(1)}, bf16[264,512]{1,0:T(8,128)(2,1)S(1)}, bf16[264,512]{1,0:T(8,128)(2,1)S(1)}) custom-call(bf16[264,512]{1,0:T(8,128)(2,1)S(1)} %get-tuple-element.27.refs_0_, bf16[264,512]{1,0:T(8,128)(2,1)S(1)} %collective-permute-done.2.refs_1_, ...), custom_call_target="tpu_custom_call" | custom-call | flops 1000 | bytes 1000 | tf_op jit(solution)/shard_map/experts_bwd/pallas_call | solution.py:276
  68.7 1.1 %collective-permute-done.11.refs_3_ = bf16[264,512]{1,0:T(8,128)(2,1)S(1)} collective-permute-done((bf16[264,512]{1,0:T(8,128)(2,1)S(1)}, bf16[264,512]{1,0:T(8,128)(2,1)S(1)}, u32[]{:S(2)}, u32[]{:S(2)}) %collective-permute-start.11) | collective-permute-done | bytes 270368 | tf_op jit(solution)/shard_map/ppermute | solution.py:26
  69.7 2.3 %experts_fwd.1 = (f32[264,512]{1,0:T(8,128)S(1)}, f32[264,512]{1,0:T(8,128)S(1)}, bf16[264,512]{1,0:T(8,128)(2,1)S(1)}, bf16[264,512]{1,0:T(8,128)(2,1)S(1)}) custom-call(bf16[264,512]{1,0:T(8,128)(2,1)S(1)} %get-tuple-element.41.refs_0_, bf16[264,512]{1,0:T(8,128)(2,1)S(1)} %collective-permute-done.9.refs_1_, ...), custom_call_target="tpu_custom_call" | custom-call | flops 1000 | bytes 1000 | tf_op jit(solution)/shard_map/experts_fwd/pallas_call | solution.py:279
  72.0 1.1 collective-permute-start.12
  73.1 4.4 %collective-permute-done.15 = bf16[264,512]{1,0:T(8,128)(2,1)S(1)} collective-permute-done((bf16[264,512]{1,0:T(8,128)(2,1)S(1)}, bf16[264,512]{1,0:T(8,128)(2,1)S(1)}, u32[]{:S(2)}, u32[]{:S(2)}) %collective-permute-start.15) | collective-permute-done | bytes 270368 | tf_op jit(solution)/shard_map/ppermute | solution.py:26
  77.5 2.3 %collective-permute-start.17 = (bf16[264,512]{1,0:T(8,128)(2,1)S(1)}, bf16[264,512]{1,0:T(8,128)(2,1)S(1)}, u32[]{:S(2)}, u32[]{:S(2)}) collective-permute-start(bf16[264,512]{1,0:T(8,128)(2,1)S(1)} %add_convert_fusion), channel_id=1, source_target_pairs={{0,4},{1,5},{2,6},{3,7},{4,0},{5,1},{6,2},{7,3},{8,12},{9,13},{10,... | collective-permute-start | bytes 811016 | tf_op jit(solution)/shard_map/ppermute | solution.py:21
  79.8 5.1 %collective-permute-start.16 = (bf16[264,512]{1,0:T(8,128)(2,1)S(1)}, bf16[264,512]{1,0:T(8,128)(2,1)S(1)}, u32[]{:S(2)}, u32[]{:S(2)}) collective-permute-start(bf16[264,512]{1,0:T(8,128)(2,1)S(1)} %get-tuple-element.51), channel_id=1, source_target_pairs={{0,2},{1,3},{2,0},{3,1},{4,6},{5,7},{6,4},{7,5},{8,10},{9,11},{10,... | collective-permute-start | bytes 811016 | tf_op jit(solution)/shard_map/ppermute | solution.py:26
  84.9 3.4 %collective-permute-done.12 = bf16[264,512]{1,0:T(8,128)(2,1)S(1)} collective-permute-done((bf16[264,512]{1,0:T(8,128)(2,1)S(1)}, bf16[264,512]{1,0:T(8,128)(2,1)S(1)}, u32[]{:S(2)}, u32[]{:S(2)}) %collective-permute-start.12) | collective-permute-done | bytes 270368 | tf_op jit(solution)/shard_map/ppermute | solution.py:26
  88.5 2.3 %collective-permute-start.14 = (bf16[264,512]{1,0:T(8,128)(2,1)S(1)}, bf16[264,512]{1,0:T(8,128)(2,1)S(1)}, u32[]{:S(2)}, u32[]{:S(2)}) collective-permute-start(bf16[264,512]{1,0:T(8,128)(2,1)S(1)} %add_convert_fusion.1), channel_id=1, source_target_pairs={{0,4},{1,5},{2,6},{3,7},{4,0},{5,1},{6,2},{7,3},{8,12},{9,13},{10,... | collective-permute-start | bytes 811016 | tf_op jit(solution)/shard_map/ppermute | solution.py:21
  90.8 9.8 %collective-permute-done.16.refs_1_ = bf16[264,512]{1,0:T(8,128)(2,1)S(1)} collective-permute-done((bf16[264,512]{1,0:T(8,128)(2,1)S(1)}, bf16[264,512]{1,0:T(8,128)(2,1)S(1)}, u32[]{:S(2)}, u32[]{:S(2)}) %collective-permute-start.16) | collective-permute-done | bytes 270368 | tf_op jit(solution)/shard_map/ppermute | solution.py:26
  100.6 2.0 %home_bwd.1 = bf16[128,2048]{1,0:T(8,128)(2,1)} custom-call(s32[1]{0:T(128)} %bitcast.own_ref, s32[1,128]{1,0:T(1,128)S(1)} %bitcast.24, f32[1,128]{1,0:T(1,128)S(1)} %bitcast.28, f32[1,2048]{1,0:T(1,128)S(1)} %copy-done.6, bf16[128,2048]{1,0:T(8,128)(2,1)S(1)} %bitcast.18, bf16[128,2048]{1,0:T(8,128)(2,1)S(1)} %collective-permute-done.1.x_ref.up_ref, ...), custom_call_target="tpu_custom_call" | custom-call | flops 1000 | bytes 1000 | tf_op jit(solution)/shard_map/home_bwd/pallas_call | solution.py:287
  102.7 2.1 %collective-permute-done.13.refs_1_ = bf16[264,512]{1,0:T(8,128)(2,1)S(1)} collective-permute-done((bf16[264,512]{1,0:T(8,128)(2,1)S(1)}, bf16[264,512]{1,0:T(8,128)(2,1)S(1)}, u32[]{:S(2)}, u32[]{:S(2)}) %collective-permute-start.13) | collective-permute-done | bytes 270368 | tf_op jit(solution)/shard_map/ppermute | solution.py:26
  104.8 1.7 %home_fwd.1 = bf16[128,2048]{1,0:T(8,128)(2,1)} custom-call(s32[1]{0:T(128)} %bitcast.own_ref, s32[1,128]{1,0:T(1,128)S(1)} %bitcast.26, f32[1,128]{1,0:T(1,128)S(1)} %bitcast.27, bf16[128,2048]{1,0:T(8,128)(2,1)S(1)} %collective-permute-done.x_ref, f32[264,512]{1,0:T(8,128)S(1)} %get-tuple-element.43.refs_0_, ...), custom_call_target="tpu_custom_call" | custom-call | flops 1000 | bytes 1000 | tf_op jit(solution)/shard_map/home_fwd/pallas_call | solution.py:294
  (41 shorter events, 5.5 us)
Async XLA Ops:
  0.6 28.8 %copy-start.6 = (f32[1,2048]{1,0:T(1,128)S(1)}, f32[1,2048]{1,0:T(1,128)}, u32[]{:S(2)}) copy-start(f32[1,2048]{1,0:T(1,128)} %gain_ref.5) | copy-start | bytes 24580
  0.6 28.8 %copy-start.9 = (s32[1,128,1]{1,2,0:T(1,128)S(1)}, s32[1,128,1]{1,2,0:T(1,128)}, u32[]{:S(2)}) copy-start(s32[1,128,1]{1,2,0:T(1,128)} %param.18) | copy-start | bytes 1540
  0.7 1.0 copy-start
  1.7 1.1 %copy-start.2 = (bf16[1,2048,192]{1,2,0:T(8,128)(2,1)S(1)}, bf16[1,2048,192]{1,2,0:T(8,128)(2,1)}, u32[]{:S(2)}) copy-start(bf16[1,2048,192]{1,2,0:T(8,128)(2,1)} %param.15) | copy-start | bytes 2359300
  2.8 1.1 %copy-start.3 = (bf16[1,2048,192]{1,2,0:T(8,128)(2,1)S(1)}, bf16[1,2048,192]{1,2,0:T(8,128)(2,1)}, u32[]{:S(2)}) copy-start(bf16[1,2048,192]{1,2,0:T(8,128)(2,1)} %param.16) | copy-start | bytes 2359300
  4.0 1.1 %copy-start.4 = (bf16[1,192,2048]{2,1,0:T(8,128)(2,1)S(1)}, bf16[1,192,2048]{2,1,0:T(8,128)(2,1)}, u32[]{:S(2)}) copy-start(bf16[1,192,2048]{2,1,0:T(8,128)(2,1)} %param.17) | copy-start | bytes 2359300
  5.1 0.7 copy-start.5
  5.8 0.7 copy-start.7
  6.5 4.1 %copy-start.12 = (bf16[1,128,2048]{2,1,0:T(8,128)(2,1)S(1)}, bf16[1,128,2048]{2,1,0:T(8,128)(2,1)}, u32[]{:S(2)}) copy-start(bf16[1,128,2048]{2,1,0:T(8,128)(2,1)} %param.13) | copy-start | bytes 1572868
  6.5 4.8 %copy-start.13 = (bf16[1,128,2048]{2,1,0:T(8,128)(2,1)S(1)}, bf16[1,128,2048]{2,1,0:T(8,128)(2,1)}, u32[]{:S(2)}) copy-start(bf16[1,128,2048]{2,1,0:T(8,128)(2,1)} %param.11) | copy-start | bytes 1572868
  7.6 57.0 %collective-permute-start.8 = (bf16[576,2048]{1,0:T(8,128)(2,1)S(1)}, bf16[576,2048]{1,0:T(8,128)(2,1)S(1)}, u32[]{:S(2)}, u32[]{:S(2)}) collective-permute-start(bf16[576,2048]{1,0:T(8,128)(2,1)S(1)} %get-tuple-element.37.refs_8_.refs_4_), channel_id=1, source_target_pairs={{0,1},{1,0},{2,3},{3,2},{4,5},{5,4},{6,7},{7,6},{8,9},{9,8},{10,11... | collective-permute-start | bytes 7077896 | tf_op jit(solution)/shard_map/ppermute | solution.py:26
  10.6 12.7 %collective-permute-start.1 = (bf16[128,2048]{1,0:T(8,128)(2,1)S(1)}, bf16[128,2048]{1,0:T(8,128)(2,1)S(1)}, u32[]{:S(2)}, u32[]{:S(2)}) collective-permute-start(bf16[128,2048]{1,0:T(8,128)(2,1)S(1)} %bitcast.31), channel_id=1, source_target_pairs={{0,24},{8,0},{16,8},{24,16},{1,25},{9,1},{17,9},{25,17},{2,26},{10... | collective-permute-start | bytes 1572872 | tf_op jit(solution)/shard_map/ppermute | solution.py:21
  11.3 18.1 %collective-permute-start = (bf16[128,2048]{1,0:T(8,128)(2,1)S(1)}, bf16[128,2048]{1,0:T(8,128)(2,1)S(1)}, u32[]{:S(2)}, u32[]{:S(2)}) collective-permute-start(bf16[128,2048]{1,0:T(8,128)(2,1)S(1)} %bitcast.32), channel_id=1, source_target_pairs={{0,8},{8,16},{16,24},{24,0},{1,9},{9,17},{17,25},{25,1},{2,10},{10... | collective-permute-start | bytes 1572872 | tf_op jit(solution)/shard_map/ppermute | solution.py:21
  11.3 16.1 %collective-permute-start.2 = (bf16[264,512]{1,0:T(8,128)(2,1)S(1)}, bf16[264,512]{1,0:T(8,128)(2,1)S(1)}, u32[]{:S(2)}, u32[]{:S(2)}) collective-permute-start(bf16[264,512]{1,0:T(8,128)(2,1)S(1)} %get-tuple-element.30), channel_id=1, source_target_pairs={{0,4},{1,5},{2,6},{3,7},{4,0},{5,1},{6,2},{7,3},{8,12},{9,13},{10,... | collective-permute-start | bytes 811016 | tf_op jit(solution)/shard_map/ppermute | solution.py:21
  13.9 14.5 %collective-permute-start.3 = (bf16[264,512]{1,0:T(8,128)(2,1)S(1)}, bf16[264,512]{1,0:T(8,128)(2,1)S(1)}, u32[]{:S(2)}, u32[]{:S(2)}) collective-permute-start(bf16[264,512]{1,0:T(8,128)(2,1)S(1)} %get-tuple-element.27.refs_0_), channel_id=1, source_target_pairs={{0,2},{1,3},{2,0},{3,1},{4,6},{5,7},{6,4},{7,5},{8,10},{9,11},{10,... | collective-permute-start | bytes 811016 | tf_op jit(solution)/shard_map/ppermute | solution.py:26
  24.1 16.0 %collective-permute-start.5 = (bf16[264,512]{1,0:T(8,128)(2,1)S(1)}, bf16[264,512]{1,0:T(8,128)(2,1)S(1)}, u32[]{:S(2)}, u32[]{:S(2)}) collective-permute-start(bf16[264,512]{1,0:T(8,128)(2,1)S(1)} %get-tuple-element.34), channel_id=1, source_target_pairs={{0,4},{1,5},{2,6},{3,7},{4,0},{5,1},{6,2},{7,3},{8,12},{9,13},{10,... | collective-permute-start | bytes 811016 | tf_op jit(solution)/shard_map/ppermute | solution.py:21
  27.4 19.8 %collective-permute-start.6 = (bf16[264,512]{1,0:T(8,128)(2,1)S(1)}, bf16[264,512]{1,0:T(8,128)(2,1)S(1)}, u32[]{:S(2)}, u32[]{:S(2)}) collective-permute-start(bf16[264,512]{1,0:T(8,128)(2,1)S(1)} %get-tuple-element.35.refs_4_), channel_id=1, source_target_pairs={{0,2},{1,3},{2,0},{3,1},{4,6},{5,7},{6,4},{7,5},{8,10},{9,11},{10,... | collective-permute-start | bytes 811016 | tf_op jit(solution)/shard_map/ppermute | solution.py:26
  28.4 24.6 %collective-permute-start.4 = (bf16[264,512]{1,0:T(8,128)(2,1)S(1)}, bf16[264,512]{1,0:T(8,128)(2,1)S(1)}, u32[]{:S(2)}, u32[]{:S(2)}) collective-permute-start(bf16[264,512]{1,0:T(8,128)(2,1)S(1)} %collective-permute-done.2.refs_1_), channel_id=1, source_target_pairs={{0,2},{1,3},{2,0},{3,1},{4,6},{5,7},{6,4},{7,5},{8,10},{9,11},{10,... | collective-permute-start | bytes 811016 | tf_op jit(solution)/shard_map/ppermute | solution.py:26
  30.3 22.6 %collective-permute-start.9 = (bf16[264,512]{1,0:T(8,128)(2,1)S(1)}, bf16[264,512]{1,0:T(8,128)(2,1)S(1)}, u32[]{:S(2)}, u32[]{:S(2)}) collective-permute-start(bf16[264,512]{1,0:T(8,128)(2,1)S(1)} %get-tuple-element.40), channel_id=1, source_target_pairs={{0,4},{1,5},{2,6},{3,7},{4,0},{5,1},{6,2},{7,3},{8,12},{9,13},{10,... | collective-permute-start | bytes 811016 | tf_op jit(solution)/shard_map/ppermute | solution.py:21
  40.1 18.6 %collective-permute-start.10 = (bf16[264,512]{1,0:T(8,128)(2,1)S(1)}, bf16[264,512]{1,0:T(8,128)(2,1)S(1)}, u32[]{:S(2)}, u32[]{:S(2)}) collective-permute-start(bf16[264,512]{1,0:T(8,128)(2,1)S(1)} %get-tuple-element.41.refs_0_), channel_id=1, source_target_pairs={{0,2},{1,3},{2,0},{3,1},{4,6},{5,7},{6,4},{7,5},{8,10},{9,11},{10,... | collective-permute-start | bytes 811016 | tf_op jit(solution)/shard_map/ppermute | solution.py:26
  47.2 17.4 %collective-permute-start.7 = (bf16[264,512]{1,0:T(8,128)(2,1)S(1)}, bf16[264,512]{1,0:T(8,128)(2,1)S(1)}, u32[]{:S(2)}, u32[]{:S(2)}) collective-permute-start(bf16[264,512]{1,0:T(8,128)(2,1)S(1)} %collective-permute-done.5.refs_5_), channel_id=1, source_target_pairs={{0,2},{1,3},{2,0},{3,1},{4,6},{5,7},{6,4},{7,5},{8,10},{9,11},{10,... | collective-permute-start | bytes 811016 | tf_op jit(solution)/shard_map/ppermute | solution.py:26
  58.7 11.0 %collective-permute-start.11 = (bf16[264,512]{1,0:T(8,128)(2,1)S(1)}, bf16[264,512]{1,0:T(8,128)(2,1)S(1)}, u32[]{:S(2)}, u32[]{:S(2)}) collective-permute-start(bf16[264,512]{1,0:T(8,128)(2,1)S(1)} %collective-permute-done.9.refs_1_), channel_id=1, source_target_pairs={{0,2},{1,3},{2,0},{3,1},{4,6},{5,7},{6,4},{7,5},{8,10},{9,11},{10,... | collective-permute-start | bytes 811016 | tf_op jit(solution)/shard_map/ppermute | solution.py:26
  68.2 9.2 %collective-permute-start.15 = (bf16[264,512]{1,0:T(8,128)(2,1)S(1)}, bf16[264,512]{1,0:T(8,128)(2,1)S(1)}, u32[]{:S(2)}, u32[]{:S(2)}) collective-permute-start(bf16[264,512]{1,0:T(8,128)(2,1)S(1)} %get-tuple-element.50), channel_id=1, source_target_pairs={{0,2},{1,3},{2,0},{3,1},{4,6},{5,7},{6,4},{7,5},{8,10},{9,11},{10,... | collective-permute-start | bytes 811016 | tf_op jit(solution)/shard_map/ppermute | solution.py:26
  68.6 32.0 %copy-start.8 = (s32[1,128,1]{1,2,0:T(1,128)S(1)}, s32[1,128,1]{1,2,0:T(1,128)}, u32[]{:S(2)}) copy-start(s32[1,128,1]{1,2,0:T(1,128)} %param.20) | copy-start | bytes 1540
  68.6 32.0 %copy-start.11 = (f32[1,128,1]{1,2,0:T(1,128)S(1)}, f32[1,128,1]{1,2,0:T(1,128)}, u32[]{:S(2)}) copy-start(f32[1,128,1]{1,2,0:T(1,128)} %param.21) | copy-start | bytes 1540
  72.0 28.6 %copy-start.1 = (bf16[1,128,2048]{2,1,0:T(8,128)(2,1)S(1)}, bf16[1,128,2048]{2,1,0:T(8,128)(2,1)}, u32[]{:S(2)}) copy-start(bf16[1,128,2048]{2,1,0:T(8,128)(2,1)} %param.12) | copy-start | bytes 1572868
  72.0 16.3 %collective-permute-start.12 = (bf16[264,512]{1,0:T(8,128)(2,1)S(1)}, bf16[264,512]{1,0:T(8,128)(2,1)S(1)}, u32[]{:S(2)}, u32[]{:S(2)}) collective-permute-start(bf16[264,512]{1,0:T(8,128)(2,1)S(1)} %get-tuple-element.46), channel_id=1, source_target_pairs={{0,2},{1,3},{2,0},{3,1},{4,6},{5,7},{6,4},{7,5},{8,10},{9,11},{10,... | collective-permute-start | bytes 811016 | tf_op jit(solution)/shard_map/ppermute | solution.py:26
  77.4 27.4 %copy-start.10 = (f32[1,128,1]{1,2,0:T(1,128)S(1)}, f32[1,128,1]{1,2,0:T(1,128)}, u32[]{:S(2)}) copy-start(f32[1,128,1]{1,2,0:T(1,128)} %param.19) | copy-start | bytes 1540
  77.5 23.1 %collective-permute-start.17 = (bf16[264,512]{1,0:T(8,128)(2,1)S(1)}, bf16[264,512]{1,0:T(8,128)(2,1)S(1)}, u32[]{:S(2)}, u32[]{:S(2)}) collective-permute-start(bf16[264,512]{1,0:T(8,128)(2,1)S(1)} %add_convert_fusion), channel_id=1, source_target_pairs={{0,4},{1,5},{2,6},{3,7},{4,0},{5,1},{6,2},{7,3},{8,12},{9,13},{10,... | collective-permute-start | bytes 811016 | tf_op jit(solution)/shard_map/ppermute | solution.py:21
  79.8 20.8 %collective-permute-start.16 = (bf16[264,512]{1,0:T(8,128)(2,1)S(1)}, bf16[264,512]{1,0:T(8,128)(2,1)S(1)}, u32[]{:S(2)}, u32[]{:S(2)}) collective-permute-start(bf16[264,512]{1,0:T(8,128)(2,1)S(1)} %get-tuple-element.51), channel_id=1, source_target_pairs={{0,2},{1,3},{2,0},{3,1},{4,6},{5,7},{6,4},{7,5},{8,10},{9,11},{10,... | collective-permute-start | bytes 811016 | tf_op jit(solution)/shard_map/ppermute | solution.py:26
  88.4 16.4 %collective-permute-start.13 = (bf16[264,512]{1,0:T(8,128)(2,1)S(1)}, bf16[264,512]{1,0:T(8,128)(2,1)S(1)}, u32[]{:S(2)}, u32[]{:S(2)}) collective-permute-start(bf16[264,512]{1,0:T(8,128)(2,1)S(1)} %get-tuple-element.47), channel_id=1, source_target_pairs={{0,2},{1,3},{2,0},{3,1},{4,6},{5,7},{6,4},{7,5},{8,10},{9,11},{10,... | collective-permute-start | bytes 811016 | tf_op jit(solution)/shard_map/ppermute | solution.py:26
  88.5 16.3 %collective-permute-start.14 = (bf16[264,512]{1,0:T(8,128)(2,1)S(1)}, bf16[264,512]{1,0:T(8,128)(2,1)S(1)}, u32[]{:S(2)}, u32[]{:S(2)}) collective-permute-start(bf16[264,512]{1,0:T(8,128)(2,1)S(1)} %add_convert_fusion.1), channel_id=1, source_target_pairs={{0,4},{1,5},{2,6},{3,7},{4,0},{5,1},{6,2},{7,3},{8,12},{9,13},{10,... | collective-permute-start | bytes 811016 | tf_op jit(solution)/shard_map/ppermute | solution.py:21

commit v5 on v4

--- a/solution.py
+++ b/solution.py
@@ -244,6 +244,7 @@
         in_specs=[scalar] + [whole] * 3 + [pl.BlockSpec(memory_space=pltpu.HBM)] * 3,
         out_specs=[pl.BlockSpec(memory_space=pl.ANY)] + [whole] * experts,
         scratch=[pltpu.SemaphoreType.DMA((3,))],
+        vmem_mib=60,
         name="join_weights_pack_saved",
     )(own, r_bwd, norm_gain, saved_in[0], w_gate[0].T, w_up[0].T, w_down[0])
     shares = (own_share, swapped(own_share, "expert", 1))

time: 107 us -> 177 us (1.65)
  Pallas kernels: 12.6 us -> 86 us
  waiting for transfers between devices: 60.2 us -> 55.3 us
  starting transfers between devices: 27.1 us -> 31.9 us
  local copies, waits for them, and re-layouts: 5.82 us -> 2.65 us
    pallas_call x1, Pallas kernels: 1.1 us -> 74.5 us  [per_device(): local_call(first_body, [jax.ShapeDtypeStruct((3 * w_down.shape[1], width)...]
    ppermute x7, starting transfers between devices: 12.6 us -> 19.6 us  [shifted(): lax.ppermute(value, axis, [(i, (i + steps) % count) for i in range(count)])]
    ppermute x11, waiting for transfers between devices: 44 us -> 39.2 us  [swapped(): return lax.ppermute(value, axis, [(i, i ^ bit) for i in range(count)])]
    unnamed x28 -> x20, local copies, waits for them, and re-layouts: 5.82 us -> 2.65 us
    ppermute x11, starting transfers between devices: 14.5 us -> 12.3 us  [swapped(): return lax.ppermute(value, axis, [(i, i ^ bit) for i in range(count)])]
  transfers between devices with their start and end apart: 18 -> 18, of which waited for: 12 -> 11; matrix products, arithmetic and copies ran while one was open for 0% -> 0% of each run, Pallas kernels for 9% -> 5%
where the time goes in v5:
time: 177 us
  Pallas kernels  86 us (49%)
  waiting for transfers between devices  55.3 us (31%)
  starting transfers between devices  31.9 us (18%)
  local copies, waits for them, and re-layouts  2.65 us (1%)
    pallas_call x1, Pallas kernels, per_device(): local_call(first_body, [jax.ShapeDtypeStruct((3 * w_down.shape[1], width)...  74.5 us
    ppermute x11, waiting for transfers between devices, swapped(): return lax.ppermute(value, axis, [(i, i ^ bit) for i in range(count)])  39.2 us
    ppermute x7, starting transfers between devices, shifted(): lax.ppermute(value, axis, [(i, (i + steps) % count) for i in range(count)])  19.6 us
    ppermute x7, waiting for transfers between devices, shifted(): lax.ppermute(value, axis, [(i, (i + steps) % count) for i in range(count)])  16.1 us
    ppermute x11, starting transfers between devices, swapped(): return lax.ppermute(value, axis, [(i, i ^ bit) for i in range(count)])  12.3 us
    pallas_call x1, Pallas kernels, per_device(): local_call(functools.partial(backward_body, count, rows), partial, scratc...  3.63 us
  transfers between devices with their start and end apart: 18, of which 11 were waited for; matrix products, arithmetic and copies ran while one was open for 0% of the time, Pallas kernels for 5%

profile of v5, /device:TPU:0, one launch (start us, length us, event | category | flops | bytes accessed | tf_op | source)
XLA Modules:
  0.0 176.8 jit_solution(1267676937390906084)
XLA Ops:
  0.7 74.5 %join_weights_pack_saved.1 = (bf16[576,2048]{1,0:T(8,128)(2,1)}, bf16[264,512]{1,0:T(8,128)(2,1)}, bf16[264,512]{1,0:T(8,128)(2,1)}) custom-call(s32[1]{0:T(128)} %bitcast.own_ref, s32[1,128]{1,0:T(1,128)} %bitcast.19, f32[1,2048]{1,0:T(1,128)} %gain_ref.5, bf16[128,2048]{1,0:T(8,128)(2,1)} %bitcast.17, bf16[192,2048]{1,0:T(8,128)(2,1)} %bitcast.26, ...), custom_call_target="tpu_custom_call" | custom-call | flops 1000 | bytes 1000 | tf_op jit(solution)/shard_map/join_weights_pack_saved/pallas_call | solution.py:241
  75.3 3.0 %collective-permute-start.8 = (bf16[576,2048]{1,0:T(8,128)(2,1)}, bf16[576,2048]{1,0:T(8,128)(2,1)S(1)}, u32[]{:S(2)}, u32[]{:S(2)}) collective-permute-start(bf16[576,2048]{1,0:T(8,128)(2,1)} %get-tuple-element.37.refs_8_.refs_4_), channel_id=1, source_target_pairs={{0,1},{1,0},{2,3},{3,2},{4,5},{5,4},{6,7},{7,6},{8,9},{9,8},{10,11... | collective-permute-start | bytes 7077896 | tf_op jit(solution)/shard_map/ppermute | solution.py:26
  78.9 2.6 %collective-permute-start.2 = (bf16[264,512]{1,0:T(8,128)(2,1)}, bf16[264,512]{1,0:T(8,128)(2,1)S(1)}, u32[]{:S(2)}, u32[]{:S(2)}) collective-permute-start(bf16[264,512]{1,0:T(8,128)(2,1)} %get-tuple-element.30), channel_id=1, source_target_pairs={{0,4},{1,5},{2,6},{3,7},{4,0},{5,1},{6,2},{7,3},{8,12},{9,13},{10,... | collective-permute-start | bytes 811016 | tf_op jit(solution)/shard_map/ppermute | solution.py:21
  81.5 1.6 collective-permute-start.3
  83.1 7.8 %collective-permute-done.1.x_ref.up_ref = bf16[128,2048]{1,0:T(8,128)(2,1)S(1)} collective-permute-done((bf16[128,2048]{1,0:T(8,128)(2,1)S(1)}, bf16[128,2048]{1,0:T(8,128)(2,1)S(1)}, u32[]{:S(2)}, u32[]{:S(2)}) %collective-permute-start.1) | collective-permute-done | bytes 524320 | tf_op jit(solution)/shard_map/ppermute | solution.py:21
  90.9 0.9 pack_grad.1
  91.8 2.7 %collective-permute-start.5 = (bf16[264,512]{1,0:T(8,128)(2,1)S(1)}, bf16[264,512]{1,0:T(8,128)(2,1)S(1)}, u32[]{:S(2)}, u32[]{:S(2)}) collective-permute-start(bf16[264,512]{1,0:T(8,128)(2,1)S(1)} %get-tuple-element.34), channel_id=1, source_target_pairs={{0,4},{1,5},{2,6},{3,7},{4,0},{5,1},{6,2},{7,3},{8,12},{9,13},{10,... | collective-permute-start | bytes 811016 | tf_op jit(solution)/shard_map/ppermute | solution.py:21
  94.5 0.8 collective-permute-done.2.refs_1_
  95.3 0.8 collective-permute-start.6
  96.0 1.2 collective-permute-start.4
  97.3 0.9 pack_act.1
  98.2 2.1 %collective-permute-start.9 = (bf16[264,512]{1,0:T(8,128)(2,1)S(1)}, bf16[264,512]{1,0:T(8,128)(2,1)S(1)}, u32[]{:S(2)}, u32[]{:S(2)}) collective-permute-start(bf16[264,512]{1,0:T(8,128)(2,1)S(1)} %get-tuple-element.40), channel_id=1, source_target_pairs={{0,4},{1,5},{2,6},{3,7},{4,0},{5,1},{6,2},{7,3},{8,12},{9,13},{10,... | collective-permute-start | bytes 811016 | tf_op jit(solution)/shard_map/ppermute | solution.py:21
  100.3 7.5 %collective-permute-done.5.refs_5_ = bf16[264,512]{1,0:T(8,128)(2,1)S(1)} collective-permute-done((bf16[264,512]{1,0:T(8,128)(2,1)S(1)}, bf16[264,512]{1,0:T(8,128)(2,1)S(1)}, u32[]{:S(2)}, u32[]{:S(2)}) %collective-permute-start.5) | collective-permute-done | bytes 270368 | tf_op jit(solution)/shard_map/ppermute | solution.py:21
  107.8 0.8 collective-permute-start.10
  108.6 6.4 %collective-permute-done.6.refs_6_ = bf16[264,512]{1,0:T(8,128)(2,1)S(1)} collective-permute-done((bf16[264,512]{1,0:T(8,128)(2,1)S(1)}, bf16[264,512]{1,0:T(8,128)(2,1)S(1)}, u32[]{:S(2)}, u32[]{:S(2)}) %collective-permute-start.6) | collective-permute-done | bytes 270368 | tf_op jit(solution)/shard_map/ppermute | solution.py:26
  115.1 5.8 %collective-permute-done.4.refs_3_ = bf16[264,512]{1,0:T(8,128)(2,1)S(1)} collective-permute-done((bf16[264,512]{1,0:T(8,128)(2,1)S(1)}, bf16[264,512]{1,0:T(8,128)(2,1)S(1)}, u32[]{:S(2)}, u32[]{:S(2)}) %collective-permute-start.4) | collective-permute-done | bytes 270368 | tf_op jit(solution)/shard_map/ppermute | solution.py:26
  120.9 5.8 %collective-permute-done.10.refs_2_ = bf16[264,512]{1,0:T(8,128)(2,1)S(1)} collective-permute-done((bf16[264,512]{1,0:T(8,128)(2,1)S(1)}, bf16[264,512]{1,0:T(8,128)(2,1)S(1)}, u32[]{:S(2)}, u32[]{:S(2)}) %collective-permute-start.10) | collective-permute-done | bytes 270368 | tf_op jit(solution)/shard_map/ppermute | solution.py:26
  126.8 5.6 %collective-permute-done.7.refs_7_ = bf16[264,512]{1,0:T(8,128)(2,1)S(1)} collective-permute-done((bf16[264,512]{1,0:T(8,128)(2,1)S(1)}, bf16[264,512]{1,0:T(8,128)(2,1)S(1)}, u32[]{:S(2)}, u32[]{:S(2)}) %collective-permute-start.7) | collective-permute-done | bytes 270368 | tf_op jit(solution)/shard_map/ppermute | solution.py:26
  132.5 1.7 copy-done
  134.1 1.0 copy-done.2
  135.1 3.6 %experts_bwd.1 = (f32[264,512]{1,0:T(8,128)S(1)}, f32[264,512]{1,0:T(8,128)S(1)}, bf16[264,512]{1,0:T(8,128)(2,1)S(1)}, bf16[264,512]{1,0:T(8,128)(2,1)S(1)}) custom-call(bf16[264,512]{1,0:T(8,128)(2,1)S(1)} %copy-done.2, bf16[264,512]{1,0:T(8,128)(2,1)S(1)} %collective-permute-done.2.refs_1_, bf16[264,512]{1,0:T(8,128)(2,1)S(1)} %collective-permute-done.3.refs_2_, ...), custom_call_target="tpu_custom_call" | custom-call | flops 1000 | bytes 1000 | tf_op jit(solution)/shard_map/experts_bwd/pallas_call | solution.py:277
  138.9 2.3 %experts_fwd.1 = (f32[264,512]{1,0:T(8,128)S(1)}, f32[264,512]{1,0:T(8,128)S(1)}, bf16[264,512]{1,0:T(8,128)(2,1)S(1)}, bf16[264,512]{1,0:T(8,128)(2,1)S(1)}) custom-call(bf16[264,512]{1,0:T(8,128)(2,1)S(1)} %get-tuple-element.41.refs_0_, bf16[264,512]{1,0:T(8,128)(2,1)S(1)} %collective-permute-done.9.refs_1_, ...), custom_call_target="tpu_custom_call" | custom-call | flops 1000 | bytes 1000 | tf_op jit(solution)/shard_map/experts_fwd/pallas_call | solution.py:280
  141.2 1.9 %collective-permute-start.12 = (bf16[264,512]{1,0:T(8,128)(2,1)S(1)}, bf16[264,512]{1,0:T(8,128)(2,1)S(1)}, u32[]{:S(2)}, u32[]{:S(2)}) collective-permute-start(bf16[264,512]{1,0:T(8,128)(2,1)S(1)} %get-tuple-element.46), channel_id=1, source_target_pairs={{0,2},{1,3},{2,0},{3,1},{4,6},{5,7},{6,4},{7,5},{8,10},{9,11},{10,... | collective-permute-start | bytes 811016 | tf_op jit(solution)/shard_map/ppermute | solution.py:26
  143.1 4.9 %collective-permute-done.15 = bf16[264,512]{1,0:T(8,128)(2,1)S(1)} collective-permute-done((bf16[264,512]{1,0:T(8,128)(2,1)S(1)}, bf16[264,512]{1,0:T(8,128)(2,1)S(1)}, u32[]{:S(2)}, u32[]{:S(2)}) %collective-permute-start.15) | collective-permute-done | bytes 270368 | tf_op jit(solution)/shard_map/ppermute | solution.py:26
  148.1 5.6 %collective-permute-start.17 = (bf16[264,512]{1,0:T(8,128)(2,1)S(1)}, bf16[264,512]{1,0:T(8,128)(2,1)S(1)}, u32[]{:S(2)}, u32[]{:S(2)}) collective-permute-start(bf16[264,512]{1,0:T(8,128)(2,1)S(1)} %add_convert_fusion), channel_id=1, source_target_pairs={{0,4},{1,5},{2,6},{3,7},{4,0},{5,1},{6,2},{7,3},{8,12},{9,13},{10,... | collective-permute-start | bytes 811016 | tf_op jit(solution)/shard_map/ppermute | solution.py:21
  153.8 2.5 %collective-permute-start.16 = (bf16[264,512]{1,0:T(8,128)(2,1)S(1)}, bf16[264,512]{1,0:T(8,128)(2,1)S(1)}, u32[]{:S(2)}, u32[]{:S(2)}) collective-permute-start(bf16[264,512]{1,0:T(8,128)(2,1)S(1)} %get-tuple-element.51), channel_id=1, source_target_pairs={{0,2},{1,3},{2,0},{3,1},{4,6},{5,7},{6,4},{7,5},{8,10},{9,11},{10,... | collective-permute-start | bytes 811016 | tf_op jit(solution)/shard_map/ppermute | solution.py:26
  156.3 0.9 collective-permute-done.12
  157.4 6.0 %collective-permute-start.14 = (bf16[264,512]{1,0:T(8,128)(2,1)S(1)}, bf16[264,512]{1,0:T(8,128)(2,1)S(1)}, u32[]{:S(2)}, u32[]{:S(2)}) collective-permute-start(bf16[264,512]{1,0:T(8,128)(2,1)S(1)} %add_convert_fusion.1), channel_id=1, source_target_pairs={{0,4},{1,5},{2,6},{3,7},{4,0},{5,1},{6,2},{7,3},{8,12},{9,13},{10,... | collective-permute-start | bytes 811016 | tf_op jit(solution)/shard_map/ppermute | solution.py:21
  163.4 8.1 %collective-permute-done.16.refs_1_ = bf16[264,512]{1,0:T(8,128)(2,1)S(1)} collective-permute-done((bf16[264,512]{1,0:T(8,128)(2,1)S(1)}, bf16[264,512]{1,0:T(8,128)(2,1)S(1)}, u32[]{:S(2)}, u32[]{:S(2)}) %collective-permute-start.16) | collective-permute-done | bytes 270368 | tf_op jit(solution)/shard_map/ppermute | solution.py:26
  171.5 2.0 %home_bwd.1 = bf16[128,2048]{1,0:T(8,128)(2,1)} custom-call(s32[1]{0:T(128)} %bitcast.own_ref, s32[1,128]{1,0:T(1,128)S(1)} %bitcast.21, f32[1,128]{1,0:T(1,128)S(1)} %bitcast.25, f32[1,2048]{1,0:T(1,128)S(1)} %copy-done.3, bf16[128,2048]{1,0:T(8,128)(2,1)S(1)} %bitcast.18, bf16[128,2048]{1,0:T(8,128)(2,1)S(1)} %collective-permute-done.1.x_ref.up_ref, ...), custom_call_target="tpu_custom_call" | custom-call | flops 1000 | bytes 1000 | tf_op jit(solution)/shard_map/home_bwd/pallas_call | solution.py:288
  173.5 1.6 collective-permute-done.13.refs_1_
  175.1 1.7 home_fwd.1
  (33 shorter events, 1.4 us)
Async XLA Ops:
  0.6 90.3 %copy-start.4 = (s32[1,128,1]{1,2,0:T(1,128)S(1)}, s32[1,128,1]{1,2,0:T(1,128)}, u32[]{:S(2)}) copy-start(s32[1,128,1]{1,2,0:T(1,128)} %param.20) | copy-start | bytes 1540
  0.6 96.7 %copy-start.3 = (f32[1,2048]{1,0:T(1,128)S(1)}, f32[1,2048]{1,0:T(1,128)}, u32[]{:S(2)}) copy-start(f32[1,2048]{1,0:T(1,128)} %gain_ref.5) | copy-start | bytes 24580
  0.7 77.6 %copy-start.8 = (bf16[1,128,2048]{2,1,0:T(8,128)(2,1)S(1)}, bf16[1,128,2048]{2,1,0:T(8,128)(2,1)}, u32[]{:S(2)}) copy-start(bf16[1,128,2048]{2,1,0:T(8,128)(2,1)} %param.13) | copy-start | bytes 1572868
  0.7 78.3 %copy-start.9 = (bf16[1,128,2048]{2,1,0:T(8,128)(2,1)S(1)}, bf16[1,128,2048]{2,1,0:T(8,128)(2,1)}, u32[]{:S(2)}) copy-start(bf16[1,128,2048]{2,1,0:T(8,128)(2,1)} %param.11) | copy-start | bytes 1572868
  0.7 96.6 %copy-start.5 = (s32[1,128,1]{1,2,0:T(1,128)S(1)}, s32[1,128,1]{1,2,0:T(1,128)}, u32[]{:S(2)}) copy-start(s32[1,128,1]{1,2,0:T(1,128)} %param.18) | copy-start | bytes 1540
  75.3 57.2 %collective-permute-start.8 = (bf16[576,2048]{1,0:T(8,128)(2,1)}, bf16[576,2048]{1,0:T(8,128)(2,1)S(1)}, u32[]{:S(2)}, u32[]{:S(2)}) collective-permute-start(bf16[576,2048]{1,0:T(8,128)(2,1)} %get-tuple-element.37.refs_8_.refs_4_), channel_id=1, source_target_pairs={{0,1},{1,0},{2,3},{3,2},{4,5},{5,4},{6,7},{7,6},{8,9},{9,8},{10,11... | collective-permute-start | bytes 7077896 | tf_op jit(solution)/shard_map/ppermute | solution.py:26
  78.3 12.7 %collective-permute-start.1 = (bf16[128,2048]{1,0:T(8,128)(2,1)S(1)}, bf16[128,2048]{1,0:T(8,128)(2,1)S(1)}, u32[]{:S(2)}, u32[]{:S(2)}) collective-permute-start(bf16[128,2048]{1,0:T(8,128)(2,1)S(1)} %bitcast.31), channel_id=1, source_target_pairs={{0,24},{8,0},{16,8},{24,16},{1,25},{9,1},{17,9},{25,17},{2,26},{10... | collective-permute-start | bytes 1572872 | tf_op jit(solution)/shard_map/ppermute | solution.py:21
  78.9 18.4 %collective-permute-start = (bf16[128,2048]{1,0:T(8,128)(2,1)S(1)}, bf16[128,2048]{1,0:T(8,128)(2,1)S(1)}, u32[]{:S(2)}, u32[]{:S(2)}) collective-permute-start(bf16[128,2048]{1,0:T(8,128)(2,1)S(1)} %bitcast.32), channel_id=1, source_target_pairs={{0,8},{8,16},{16,24},{24,0},{1,9},{9,17},{17,25},{25,1},{2,10},{10... | collective-permute-start | bytes 1572872 | tf_op jit(solution)/shard_map/ppermute | solution.py:21
  78.9 16.3 %collective-permute-start.2 = (bf16[264,512]{1,0:T(8,128)(2,1)}, bf16[264,512]{1,0:T(8,128)(2,1)S(1)}, u32[]{:S(2)}, u32[]{:S(2)}) collective-permute-start(bf16[264,512]{1,0:T(8,128)(2,1)} %get-tuple-element.30), channel_id=1, source_target_pairs={{0,4},{1,5},{2,6},{3,7},{4,0},{5,1},{6,2},{7,3},{8,12},{9,13},{10,... | collective-permute-start | bytes 811016 | tf_op jit(solution)/shard_map/ppermute | solution.py:21
  81.5 14.5 %collective-permute-start.3 = (bf16[264,512]{1,0:T(8,128)(2,1)}, bf16[264,512]{1,0:T(8,128)(2,1)S(1)}, u32[]{:S(2)}, u32[]{:S(2)}) collective-permute-start(bf16[264,512]{1,0:T(8,128)(2,1)} %get-tuple-element.27.refs_0_), channel_id=1, source_target_pairs={{0,2},{1,3},{2,0},{3,1},{4,6},{5,7},{6,4},{7,5},{8,10},{9,11},{10,... | collective-permute-start | bytes 811016 | tf_op jit(solution)/shard_map/ppermute | solution.py:26
  91.8 16.0 %collective-permute-start.5 = (bf16[264,512]{1,0:T(8,128)(2,1)S(1)}, bf16[264,512]{1,0:T(8,128)(2,1)S(1)}, u32[]{:S(2)}, u32[]{:S(2)}) collective-permute-start(bf16[264,512]{1,0:T(8,128)(2,1)S(1)} %get-tuple-element.34), channel_id=1, source_target_pairs={{0,4},{1,5},{2,6},{3,7},{4,0},{5,1},{6,2},{7,3},{8,12},{9,13},{10,... | collective-permute-start | bytes 811016 | tf_op jit(solution)/shard_map/ppermute | solution.py:21
  95.3 19.8 %collective-permute-start.6 = (bf16[264,512]{1,0:T(8,128)(2,1)S(1)}, bf16[264,512]{1,0:T(8,128)(2,1)S(1)}, u32[]{:S(2)}, u32[]{:S(2)}) collective-permute-start(bf16[264,512]{1,0:T(8,128)(2,1)S(1)} %get-tuple-element.35.refs_4_), channel_id=1, source_target_pairs={{0,2},{1,3},{2,0},{3,1},{4,6},{5,7},{6,4},{7,5},{8,10},{9,11},{10,... | collective-permute-start | bytes 811016 | tf_op jit(solution)/shard_map/ppermute | solution.py:26
  96.0 24.8 %collective-permute-start.4 = (bf16[264,512]{1,0:T(8,128)(2,1)S(1)}, bf16[264,512]{1,0:T(8,128)(2,1)S(1)}, u32[]{:S(2)}, u32[]{:S(2)}) collective-permute-start(bf16[264,512]{1,0:T(8,128)(2,1)S(1)} %collective-permute-done.2.refs_1_), channel_id=1, source_target_pairs={{0,2},{1,3},{2,0},{3,1},{4,6},{5,7},{6,4},{7,5},{8,10},{9,11},{10,... | collective-permute-start | bytes 811016 | tf_op jit(solution)/shard_map/ppermute | solution.py:26
  98.2 22.6 %collective-permute-start.9 = (bf16[264,512]{1,0:T(8,128)(2,1)S(1)}, bf16[264,512]{1,0:T(8,128)(2,1)S(1)}, u32[]{:S(2)}, u32[]{:S(2)}) collective-permute-start(bf16[264,512]{1,0:T(8,128)(2,1)S(1)} %get-tuple-element.40), channel_id=1, source_target_pairs={{0,4},{1,5},{2,6},{3,7},{4,0},{5,1},{6,2},{7,3},{8,12},{9,13},{10,... | collective-permute-start | bytes 811016 | tf_op jit(solution)/shard_map/ppermute | solution.py:21
  107.8 18.8 %collective-permute-start.10 = (bf16[264,512]{1,0:T(8,128)(2,1)S(1)}, bf16[264,512]{1,0:T(8,128)(2,1)S(1)}, u32[]{:S(2)}, u32[]{:S(2)}) collective-permute-start(bf16[264,512]{1,0:T(8,128)(2,1)S(1)} %get-tuple-element.41.refs_0_), channel_id=1, source_target_pairs={{0,2},{1,3},{2,0},{3,1},{4,6},{5,7},{6,4},{7,5},{8,10},{9,11},{10,... | collective-permute-start | bytes 811016 | tf_op jit(solution)/shard_map/ppermute | solution.py:26
  115.1 17.4 %collective-permute-start.7 = (bf16[264,512]{1,0:T(8,128)(2,1)S(1)}, bf16[264,512]{1,0:T(8,128)(2,1)S(1)}, u32[]{:S(2)}, u32[]{:S(2)}) collective-permute-start(bf16[264,512]{1,0:T(8,128)(2,1)S(1)} %collective-permute-done.5.refs_5_), channel_id=1, source_target_pairs={{0,2},{1,3},{2,0},{3,1},{4,6},{5,7},{6,4},{7,5},{8,10},{9,11},{10,... | collective-permute-start | bytes 811016 | tf_op jit(solution)/shard_map/ppermute | solution.py:26
  126.7 12.3 %collective-permute-start.11 = (bf16[264,512]{1,0:T(8,128)(2,1)S(1)}, bf16[264,512]{1,0:T(8,128)(2,1)S(1)}, u32[]{:S(2)}, u32[]{:S(2)}) collective-permute-start(bf16[264,512]{1,0:T(8,128)(2,1)S(1)} %collective-permute-done.9.refs_1_), channel_id=1, source_target_pairs={{0,2},{1,3},{2,0},{3,1},{4,6},{5,7},{6,4},{7,5},{8,10},{9,11},{10,... | collective-permute-start | bytes 811016 | tf_op jit(solution)/shard_map/ppermute | solution.py:26
  132.5 1.7 copy-start
  134.1 1.0 copy-start.2
  138.7 9.3 %collective-permute-start.15 = (bf16[264,512]{1,0:T(8,128)(2,1)S(1)}, bf16[264,512]{1,0:T(8,128)(2,1)S(1)}, u32[]{:S(2)}, u32[]{:S(2)}) collective-permute-start(bf16[264,512]{1,0:T(8,128)(2,1)S(1)} %get-tuple-element.50), channel_id=1, source_target_pairs={{0,2},{1,3},{2,0},{3,1},{4,6},{5,7},{6,4},{7,5},{8,10},{9,11},{10,... | collective-permute-start | bytes 811016 | tf_op jit(solution)/shard_map/ppermute | solution.py:26
  138.9 32.5 %copy-start.7 = (f32[1,128,1]{1,2,0:T(1,128)S(1)}, f32[1,128,1]{1,2,0:T(1,128)}, u32[]{:S(2)}) copy-start(f32[1,128,1]{1,2,0:T(1,128)} %param.21) | copy-start | bytes 1540
  141.2 30.2 %copy-start.1 = (bf16[1,128,2048]{2,1,0:T(8,128)(2,1)S(1)}, bf16[1,128,2048]{2,1,0:T(8,128)(2,1)}, u32[]{:S(2)}) copy-start(bf16[1,128,2048]{2,1,0:T(8,128)(2,1)} %param.12) | copy-start | bytes 1572868
  141.2 16.0 %collective-permute-start.12 = (bf16[264,512]{1,0:T(8,128)(2,1)S(1)}, bf16[264,512]{1,0:T(8,128)(2,1)S(1)}, u32[]{:S(2)}, u32[]{:S(2)}) collective-permute-start(bf16[264,512]{1,0:T(8,128)(2,1)S(1)} %get-tuple-element.46), channel_id=1, source_target_pairs={{0,2},{1,3},{2,0},{3,1},{4,6},{5,7},{6,4},{7,5},{8,10},{9,11},{10,... | collective-permute-start | bytes 811016 | tf_op jit(solution)/shard_map/ppermute | solution.py:26
  148.0 27.1 %copy-start.6 = (f32[1,128,1]{1,2,0:T(1,128)S(1)}, f32[1,128,1]{1,2,0:T(1,128)}, u32[]{:S(2)}) copy-start(f32[1,128,1]{1,2,0:T(1,128)} %param.19) | copy-start | bytes 1540
  148.1 23.3 %collective-permute-start.17 = (bf16[264,512]{1,0:T(8,128)(2,1)S(1)}, bf16[264,512]{1,0:T(8,128)(2,1)S(1)}, u32[]{:S(2)}, u32[]{:S(2)}) collective-permute-start(bf16[264,512]{1,0:T(8,128)(2,1)S(1)} %add_convert_fusion), channel_id=1, source_target_pairs={{0,4},{1,5},{2,6},{3,7},{4,0},{5,1},{6,2},{7,3},{8,12},{9,13},{10,... | collective-permute-start | bytes 811016 | tf_op jit(solution)/shard_map/ppermute | solution.py:21
  153.8 17.7 %collective-permute-start.16 = (bf16[264,512]{1,0:T(8,128)(2,1)S(1)}, bf16[264,512]{1,0:T(8,128)(2,1)S(1)}, u32[]{:S(2)}, u32[]{:S(2)}) collective-permute-start(bf16[264,512]{1,0:T(8,128)(2,1)S(1)} %get-tuple-element.51), channel_id=1, source_target_pairs={{0,2},{1,3},{2,0},{3,1},{4,6},{5,7},{6,4},{7,5},{8,10},{9,11},{10,... | collective-permute-start | bytes 811016 | tf_op jit(solution)/shard_map/ppermute | solution.py:26
  157.3 17.8 %collective-permute-start.13 = (bf16[264,512]{1,0:T(8,128)(2,1)S(1)}, bf16[264,512]{1,0:T(8,128)(2,1)S(1)}, u32[]{:S(2)}, u32[]{:S(2)}) collective-permute-start(bf16[264,512]{1,0:T(8,128)(2,1)S(1)} %get-tuple-element.47), channel_id=1, source_target_pairs={{0,2},{1,3},{2,0},{3,1},{4,6},{5,7},{6,4},{7,5},{8,10},{9,11},{10,... | collective-permute-start | bytes 811016 | tf_op jit(solution)/shard_map/ppermute | solution.py:26
  157.4 17.7 %collective-permute-start.14 = (bf16[264,512]{1,0:T(8,128)(2,1)S(1)}, bf16[264,512]{1,0:T(8,128)(2,1)S(1)}, u32[]{:S(2)}, u32[]{:S(2)}) collective-permute-start(bf16[264,512]{1,0:T(8,128)(2,1)S(1)} %add_convert_fusion.1), channel_id=1, source_target_pairs={{0,4},{1,5},{2,6},{3,7},{4,0},{5,1},{6,2},{7,3},{8,12},{9,13},{10,... | collective-permute-start | bytes 811016 | tf_op jit(solution)/shard_map/ppermute | solution.py:21

commit v6 on v4

--- a/solution.py
+++ b/solution.py
@@ -24,6 +24,11 @@
 def swapped(value, axis, bit):
     count = lax.axis_size(axis)
     return lax.ppermute(value, axis, [(i, i ^ bit) for i in range(count)])
+
+
+def both_shares(share):
+    pairs = [[i, i + 1] for i in range(0, lax.axis_size("expert"), 2)]
+    return lax.all_gather(share, "expert", axis_index_groups=pairs, tiled=True)
 
 
 def after(value, *others):
@@ -97,19 +102,6 @@
     pack(normed(x_ref, gain_ref), own_ref, routes_ref, outs)
 
 
-def first_body(own_ref, routes_ref, gain_ref, x_ref, *refs):
-    parts, joined, outs, sems = refs[:3], refs[3], refs[4:-1], refs[-1]
-    units = parts[0].shape[0]
-    copies = [
-        pltpu.make_async_copy(part, joined.at[pl.ds(i * units, units), :], sems.at[i]) for i, part in enumerate(parts)
-    ]
-    for copy in copies:
-        copy.start()
-    pack(normed(x_ref, gain_ref), own_ref, routes_ref, outs)
-    for copy in copies:
-        copy.wait()
-
-
 def unpack(refs, wide_ref, rows):
     pitch = wide_ref.shape[0] // len(refs)
     pieces = refs[0].shape[0] // rows
@@ -128,31 +120,26 @@
         ref[...] = jnp.concatenate(pieces, axis=0).astype(ref.dtype)
 
 
-def third(shares, i):
-    units = shares[0].shape[0] // 3
-    return jnp.concatenate([share[pl.ds(i * units, units), :] for share in shares], axis=0)
-
-
 def forward_body(count, rows, *refs):
-    row_refs, shares, outs, wide_ref = refs[:count], refs[count:count + 2], refs[count + 2:-1], refs[-1]
+    row_refs, shares, outs, wide_ref = refs[:count], refs[count:count + 3], refs[count + 3:-1], refs[-1]
     x = unpack(row_refs, wide_ref, rows)
-    gate_pre = lax.dot_general(x, third(shares, 0), CONTRACT, preferred_element_type=F32)
-    up_pre = lax.dot_general(x, third(shares, 1), CONTRACT, preferred_element_type=F32)
+    gate_pre = lax.dot_general(x, shares[0][...], CONTRACT, preferred_element_type=F32)
+    up_pre = lax.dot_general(x, shares[1][...], CONTRACT, preferred_element_type=F32)
     hidden = (silu_parts(gate_pre)[0] * up_pre).astype(BF16)
-    total = jnp.dot(hidden, third(shares, 2), preferred_element_type=F32)
+    total = jnp.dot(hidden, shares[2][...], preferred_element_type=F32)
     spread_out(total, outs, x.shape[0] // count, rows)
 
 
 def backward_body(count, rows, *refs):
-    row_refs, grad_refs, shares = refs[:count], refs[count:2 * count], refs[2 * count:2 * count + 2]
-    outs, wide_ref, grad_wide_ref = refs[2 * count + 2:-2], refs[-2], refs[-1]
+    row_refs, grad_refs, shares = refs[:count], refs[count:2 * count], refs[2 * count:2 * count + 3]
+    outs, wide_ref, grad_wide_ref = refs[2 * count + 3:-2], refs[-2], refs[-1]
     x = unpack(row_refs, wide_ref, rows)
-    gate, up = third(shares, 0), third(shares, 1)
+    gate, up = shares[0][...], shares[1][...]
     gate_pre = lax.dot_general(x, gate, CONTRACT, preferred_element_type=F32)
     up_pre = lax.dot_general(x, up, CONTRACT, preferred_element_type=F32)
     activation, derivative = silu_parts(gate_pre)
     grads = unpack(grad_refs, grad_wide_ref, rows)
-    d_hidden = lax.dot_general(grads, third(shares, 2), CONTRACT, preferred_element_type=F32)
+    d_hidden = lax.dot_general(grads, shares[2][...], CONTRACT, preferred_element_type=F32)
     d_gate = (d_hidden * up_pre * derivative).astype(BF16)
     d_up = (d_hidden * activation).astype(BF16)
     total = jnp.dot(d_gate, gate, preferred_element_type=F32) + jnp.dot(d_up, up, preferred_element_type=F32)
@@ -238,15 +225,14 @@
     g_fwd = gates_fwd.reshape(1, tok_count)
     g_bwd = gates_bwd.reshape(1, tok_count)
 
-    own_share, *packed_b = local_call(
-        first_body,
-        [jax.ShapeDtypeStruct((3 * w_down.shape[1], width), BF16)] + packed,
-        in_specs=[scalar] + [whole] * 3 + [pl.BlockSpec(memory_space=pltpu.HBM)] * 3,
-        out_specs=[pl.BlockSpec(memory_space=pl.ANY)] + [whole] * experts,
-        scratch=[pltpu.SemaphoreType.DMA((3,))],
-        name="join_weights_pack_saved",
-    )(own, r_bwd, norm_gain, saved_in[0], w_gate[0].T, w_up[0].T, w_down[0])
-    shares = (own_share, swapped(own_share, "expert", 1))
+    packed_b = local_call(
+        pack_act_body,
+        packed,
+        in_specs=[scalar] + [whole] * 3,
+        out_specs=[whole] * experts,
+        name="pack_saved",
+    )(own, r_bwd, norm_gain, saved_in[0])
+    shares = [both_shares(share) for share in (w_gate[0].T, w_up[0].T, w_down[0])]
 
     rows_b = crossed(packed_b)
     swap_b = partners(rows_b[:1])
@@ -282,7 +268,7 @@
     totals_b, home_b = crossing_home(partial_b)
     totals_f, home_f = crossing_home(partial_f)
     back_b = [partial_b[0]] + partners(partial_b[experts:experts + 1], *totals_b) + home_b
-    back_f = [partial_f[0]] + partners(partial_f[experts:experts + 1], *totals_f) + home_f
+    back_f = [partial_f[0]] + partners(partial_f[experts:experts + 1], *totals_f, back_b[1]) + home_f
 
     grad_out = local_call(
         functools.partial(backward_home_body, experts, rows),

time: 107 us -> 157 us (1.47)
  waiting for transfers between devices: 60.2 us -> 96.5 us
  between operations: 0.77 us -> 13.9 us
  local copies, waits for them, and re-layouts: 5.82 us -> 11.9 us
  starting transfers between devices: 27.1 us -> 22.2 us
    all_gather x0 -> x3, waiting for transfers between devices: none -> 31.5 us  [both_shares(): return lax.all_gather(share, 'expert', axis_index_groups=pairs, tiled=True)]
    ppermute x11 -> x10, starting transfers between devices: 14.5 us -> 6.45 us  [swapped(): return lax.ppermute(value, axis, [(i, i ^ bit) for i in range(count)])]
    unnamed x28 -> x40, local copies, waits for them, and re-layouts: 5.82 us -> 11.9 us
    ppermute x7, waiting for transfers between devices: 16.2 us -> 21.8 us  [shifted(): lax.ppermute(value, axis, [(i, (i + steps) % count) for i in range(count)])]
    ppermute x7, starting transfers between devices: 12.6 us -> 15.6 us  [shifted(): lax.ppermute(value, axis, [(i, (i + steps) % count) for i in range(count)])]
    ppermute x11 -> x10, waiting for transfers between devices: 44 us -> 41.1 us  [swapped(): return lax.ppermute(value, axis, [(i, i ^ bit) for i in range(count)])]
    unnamed x0 -> x3, waiting for transfers between devices: none -> 2.05 us
  transfers between devices with their start and end apart: 18 -> 20, of which waited for: 12 -> 14; matrix products, arithmetic and copies ran while one was open for 0% -> 0% of each run, Pallas kernels for 9% -> 7%
where the time goes in v6:
time: 157 us
  waiting for transfers between devices  96.5 us (61%)
  starting transfers between devices  22.2 us (14%)
  between operations  13.9 us (9%)
  Pallas kernels  12.3 us (8%)
  local copies, waits for them, and re-layouts  11.9 us (8%)
    ppermute x10, waiting for transfers between devices, swapped(): return lax.ppermute(value, axis, [(i, i ^ bit) for i in range(count)])  41.1 us
    all_gather x3, waiting for transfers between devices, both_shares(): return lax.all_gather(share, 'expert', axis_index_groups=pairs, tiled=True)  31.5 us
    ppermute x7, waiting for transfers between devices, shifted(): lax.ppermute(value, axis, [(i, (i + steps) % count) for i in range(count)])  21.8 us
    ppermute x7, starting transfers between devices, shifted(): lax.ppermute(value, axis, [(i, (i + steps) % count) for i in range(count)])  15.6 us
    unnamed x40, local copies, waits for them, and re-layouts  11.9 us
    ppermute x10, starting transfers between devices, swapped(): return lax.ppermute(value, axis, [(i, i ^ bit) for i in range(count)])  6.45 us
    pallas_call x1, Pallas kernels, per_device(): local_call(functools.partial(backward_body, count, rows), partial, scratc...  3.64 us
  transfers between devices with their start and end apart: 20, of which 14 were waited for; matrix products, arithmetic and copies ran while one was open for 0% of the time, Pallas kernels for 7%

profile of v6, /device:TPU:0, one launch (start us, length us, event | category | flops | bytes accessed | tf_op | source)
XLA Modules:
  0.0 156.9 jit_solution(13639777075515731036)
XLA Ops:
  9.4 2.5 %collective-permute-start.1 = (bf16[128,2048]{1,0:T(8,128)(2,1)S(1)}, bf16[128,2048]{1,0:T(8,128)(2,1)S(1)}, u32[]{:S(2)}, u32[]{:S(2)}) collective-permute-start(bf16[128,2048]{1,0:T(8,128)(2,1)S(1)} %bitcast.32), channel_id=1, source_target_pairs={{0,24},{8,0},{16,8},{24,16},{1,25},{9,1},{17,9},{25,17},{2,26},{10... | collective-permute-start | bytes 1572872 | tf_op jit(solution)/shard_map/ppermute | solution.py:21
  12.8 2.7 %collective-permute-start.2 = (bf16[264,512]{1,0:T(8,128)(2,1)S(1)}, bf16[264,512]{1,0:T(8,128)(2,1)S(1)}, u32[]{:S(2)}, u32[]{:S(2)}) collective-permute-start(bf16[264,512]{1,0:T(8,128)(2,1)S(1)} %get-tuple-element.29), channel_id=1, source_target_pairs={{0,4},{1,5},{2,6},{3,7},{4,0},{5,1},{6,2},{7,3},{8,12},{9,13},{10,... | collective-permute-start | bytes 811016 | tf_op jit(solution)/shard_map/ppermute | solution.py:21
  15.5 1.6 %collective-permute-start.3 = (bf16[264,512]{1,0:T(8,128)(2,1)S(1)}, bf16[264,512]{1,0:T(8,128)(2,1)S(1)}, u32[]{:S(2)}, u32[]{:S(2)}) collective-permute-start(bf16[264,512]{1,0:T(8,128)(2,1)S(1)} %get-tuple-element.26.refs_0_), channel_id=1, source_target_pairs={{0,2},{1,3},{2,0},{3,1},{4,6},{5,7},{6,4},{7,5},{8,10},{9,11},{10,... | collective-permute-start | bytes 811016 | tf_op jit(solution)/shard_map/ppermute | solution.py:26
  17.1 3.3 %collective-permute-done.1.x_ref.up_ref = bf16[128,2048]{1,0:T(8,128)(2,1)S(1)} collective-permute-done((bf16[128,2048]{1,0:T(8,128)(2,1)S(1)}, bf16[128,2048]{1,0:T(8,128)(2,1)S(1)}, u32[]{:S(2)}, u32[]{:S(2)}) %collective-permute-start.1) | collective-permute-done | bytes 524320 | tf_op jit(solution)/shard_map/ppermute | solution.py:21
  21.2 4.9 %collective-permute-start.5 = (bf16[264,512]{1,0:T(8,128)(2,1)S(1)}, bf16[264,512]{1,0:T(8,128)(2,1)S(1)}, u32[]{:S(2)}, u32[]{:S(2)}) collective-permute-start(bf16[264,512]{1,0:T(8,128)(2,1)S(1)} %get-tuple-element.33), channel_id=1, source_target_pairs={{0,4},{1,5},{2,6},{3,7},{4,0},{5,1},{6,2},{7,3},{8,12},{9,13},{10,... | collective-permute-start | bytes 811016 | tf_op jit(solution)/shard_map/ppermute | solution.py:21
  26.1 1.5 collective-permute-done.2.refs_1_
  28.2 2.4 %collective-permute-done.3.refs_2_ = bf16[264,512]{1,0:T(8,128)(2,1)S(1)} collective-permute-done((bf16[264,512]{1,0:T(8,128)(2,1)S(1)}, bf16[264,512]{1,0:T(8,128)(2,1)S(1)}, u32[]{:S(2)}, u32[]{:S(2)}) %collective-permute-start.3) | collective-permute-done | bytes 270368 | tf_op jit(solution)/shard_map/ppermute | solution.py:26
  31.6 1.7 %collective-permute-start.8 = (bf16[264,512]{1,0:T(8,128)(2,1)S(1)}, bf16[264,512]{1,0:T(8,128)(2,1)S(1)}, u32[]{:S(2)}, u32[]{:S(2)}) collective-permute-start(bf16[264,512]{1,0:T(8,128)(2,1)S(1)} %get-tuple-element.38), channel_id=1, source_target_pairs={{0,4},{1,5},{2,6},{3,7},{4,0},{5,1},{6,2},{7,3},{8,12},{9,13},{10,... | collective-permute-start | bytes 811016 | tf_op jit(solution)/shard_map/ppermute | solution.py:21
  33.3 6.0 %collective-permute-done.5.refs_5_ = bf16[264,512]{1,0:T(8,128)(2,1)S(1)} collective-permute-done((bf16[264,512]{1,0:T(8,128)(2,1)S(1)}, bf16[264,512]{1,0:T(8,128)(2,1)S(1)}, u32[]{:S(2)}, u32[]{:S(2)}) %collective-permute-start.5) | collective-permute-done | bytes 270368 | tf_op jit(solution)/shard_map/ppermute | solution.py:21
  39.9 7.6 %collective-permute-done.6.refs_6_ = bf16[264,512]{1,0:T(8,128)(2,1)S(1)} collective-permute-done((bf16[264,512]{1,0:T(8,128)(2,1)S(1)}, bf16[264,512]{1,0:T(8,128)(2,1)S(1)}, u32[]{:S(2)}, u32[]{:S(2)}) %collective-permute-start.6) | collective-permute-done | bytes 270368 | tf_op jit(solution)/shard_map/ppermute | solution.py:26
  48.9 4.3 %collective-permute-done.4.refs_3_ = bf16[264,512]{1,0:T(8,128)(2,1)S(1)} collective-permute-done((bf16[264,512]{1,0:T(8,128)(2,1)S(1)}, bf16[264,512]{1,0:T(8,128)(2,1)S(1)}, u32[]{:S(2)}, u32[]{:S(2)}) %collective-permute-start.4) | collective-permute-done | bytes 270368 | tf_op jit(solution)/shard_map/ppermute | solution.py:26
  54.0 5.1 %collective-permute-done.9.refs_2_ = bf16[264,512]{1,0:T(8,128)(2,1)S(1)} collective-permute-done((bf16[264,512]{1,0:T(8,128)(2,1)S(1)}, bf16[264,512]{1,0:T(8,128)(2,1)S(1)}, u32[]{:S(2)}, u32[]{:S(2)}) %collective-permute-start.9) | collective-permute-done | bytes 270368 | tf_op jit(solution)/shard_map/ppermute | solution.py:26
  59.1 5.8 %collective-permute-done.7.refs_7_ = bf16[264,512]{1,0:T(8,128)(2,1)S(1)} collective-permute-done((bf16[264,512]{1,0:T(8,128)(2,1)S(1)}, bf16[264,512]{1,0:T(8,128)(2,1)S(1)}, u32[]{:S(2)}, u32[]{:S(2)}) %collective-permute-start.7) | collective-permute-done | bytes 270368 | tf_op jit(solution)/shard_map/ppermute | solution.py:26
  65.6 2.7 %all-gather.7.cloned.1.call-done.refs_9_.refs_5_ = bf16[384,2048]{1,0:T(8,128)(2,1)} async-done(((bf16[192,2048]{1,0:T(8,128)(2,1)}), bf16[384,2048]{1,0:T(8,128)(2,1)}) %all-gather.7.cloned.1.call-update) | async-done | bytes 1572880 | tf_op jit(solution)/shard_map/all_gather | solution.py:31
  68.3 28.8 %all-gather.9.cloned.1.call-done = bf16[1,384,2048]{2,1,0:T(8,128)(2,1)} async-done(((bf16[1,192,2048]{2,1,0:T(8,128)(2,1)}), bf16[1,384,2048]{2,1,0:T(8,128)(2,1)}) %all-gather.9.cloned.1.call-update) | async-done | bytes 1572880 | tf_op jit(solution)/shard_map/all_gather | solution.py:31
  97.1 1.4 copy-done
  98.5 1.4 copy-done.1
  99.9 1.4 copy-done.2
  101.3 1.0 copy-done.5
  105.1 1.0 copy-done.13
  106.1 3.6 %experts_bwd.1 = (f32[264,512]{1,0:T(8,128)S(1)}, f32[264,512]{1,0:T(8,128)S(1)}, bf16[264,512]{1,0:T(8,128)(2,1)S(1)}, bf16[264,512]{1,0:T(8,128)(2,1)S(1)}) custom-call(bf16[264,512]{1,0:T(8,128)(2,1)S(1)} %get-tuple-element.26.refs_0_, bf16[264,512]{1,0:T(8,128)(2,1)S(1)} %collective-permute-done.2.refs_1_, ...), custom_call_target="tpu_custom_call" | custom-call | flops 1000 | bytes 1000 | tf_op jit(solution)/shard_map/experts_bwd/pallas_call | solution.py:262
  109.7 1.6 collective-permute-start.12
  111.3 2.3 %experts_fwd.1 = (f32[264,512]{1,0:T(8,128)S(1)}, f32[264,512]{1,0:T(8,128)S(1)}, bf16[264,512]{1,0:T(8,128)(2,1)S(1)}, bf16[264,512]{1,0:T(8,128)(2,1)S(1)}) custom-call(bf16[264,512]{1,0:T(8,128)(2,1)S(1)} %get-tuple-element.39.refs_0_, bf16[264,512]{1,0:T(8,128)(2,1)S(1)} %collective-permute-done.8.refs_1_, ...), custom_call_target="tpu_custom_call" | custom-call | flops 1000 | bytes 1000 | tf_op jit(solution)/shard_map/experts_fwd/pallas_call | solution.py:265
  114.2 5.0 %collective-permute-done.12 = bf16[264,512]{1,0:T(8,128)(2,1)S(1)} collective-permute-done((bf16[264,512]{1,0:T(8,128)(2,1)S(1)}, bf16[264,512]{1,0:T(8,128)(2,1)S(1)}, u32[]{:S(2)}, u32[]{:S(2)}) %collective-permute-start.12) | collective-permute-done | bytes 270368 | tf_op jit(solution)/shard_map/ppermute | solution.py:26
  119.2 1.6 collective-permute-start.13
  120.8 2.4 %collective-permute-start.16 = (bf16[264,512]{1,0:T(8,128)(2,1)S(1)}, bf16[264,512]{1,0:T(8,128)(2,1)S(1)}, u32[]{:S(2)}, u32[]{:S(2)}) collective-permute-start(bf16[264,512]{1,0:T(8,128)(2,1)S(1)} %add_convert_fusion), channel_id=1, source_target_pairs={{0,4},{1,5},{2,6},{3,7},{4,0},{5,1},{6,2},{7,3},{8,12},{9,13},{10,... | collective-permute-start | bytes 811016 | tf_op jit(solution)/shard_map/ppermute | solution.py:21
  123.2 7.5 %collective-permute-done.11 = bf16[264,512]{1,0:T(8,128)(2,1)S(1)} collective-permute-done((bf16[264,512]{1,0:T(8,128)(2,1)S(1)}, bf16[264,512]{1,0:T(8,128)(2,1)S(1)}, u32[]{:S(2)}, u32[]{:S(2)}) %collective-permute-start.11) | collective-permute-done | bytes 270368 | tf_op jit(solution)/shard_map/ppermute | solution.py:26
  130.9 1.5 collective-permute-start.15
  132.3 3.4 %collective-permute-done.13.refs_1_ = bf16[264,512]{1,0:T(8,128)(2,1)S(1)} collective-permute-done((bf16[264,512]{1,0:T(8,128)(2,1)S(1)}, bf16[264,512]{1,0:T(8,128)(2,1)S(1)}, u32[]{:S(2)}, u32[]{:S(2)}) %collective-permute-start.13) | collective-permute-done | bytes 270368 | tf_op jit(solution)/shard_map/ppermute | solution.py:26
  135.7 2.0 %home_bwd.1 = bf16[128,2048]{1,0:T(8,128)(2,1)} custom-call(s32[1]{0:T(128)} %bitcast.own_ref, s32[1,128]{1,0:T(1,128)S(1)} %bitcast.23, f32[1,128]{1,0:T(1,128)S(1)} %bitcast.27, f32[1,2048]{1,0:T(1,128)S(1)} %copy-done.14, bf16[128,2048]{1,0:T(8,128)(2,1)S(1)} %bitcast.20, bf16[128,2048]{1,0:T(8,128)(2,1)S(1)} %collective-permute-done.1.x_ref.up_ref, ...), custom_call_target="tpu_custom_call" | custom-call | flops 1000 | bytes 1000 | tf_op jit(solution)/shard_map/home_bwd/pallas_call | solution.py:273
  137.7 10.9 %collective-permute-done.15.refs_2_ = bf16[264,512]{1,0:T(8,128)(2,1)S(1)} collective-permute-done((bf16[264,512]{1,0:T(8,128)(2,1)S(1)}, bf16[264,512]{1,0:T(8,128)(2,1)S(1)}, u32[]{:S(2)}, u32[]{:S(2)}) %collective-permute-start.15) | collective-permute-done | bytes 270368 | tf_op jit(solution)/shard_map/ppermute | solution.py:21
  148.7 1.7 %home_fwd.1 = bf16[128,2048]{1,0:T(8,128)(2,1)} custom-call(s32[1]{0:T(128)} %bitcast.own_ref, s32[1,128]{1,0:T(1,128)S(1)} %bitcast.25, f32[1,128]{1,0:T(1,128)S(1)} %bitcast.26, bf16[128,2048]{1,0:T(8,128)(2,1)S(1)} %collective-permute-done.x_ref, f32[264,512]{1,0:T(8,128)S(1)} %get-tuple-element.41.refs_0_, ...), custom_call_target="tpu_custom_call" | custom-call | flops 1000 | bytes 1000 | tf_op jit(solution)/shard_map/home_fwd/pallas_call | solution.py:280
  (60 shorter events, 12.6 us)
Async XLA Ops:
  7.2 2.3 %copy-start.19 = (bf16[1,128,2048]{2,1,0:T(8,128)(2,1)S(1)}, bf16[1,128,2048]{2,1,0:T(8,128)(2,1)}, u32[]{:S(2)}) copy-start(bf16[1,128,2048]{2,1,0:T(8,128)(2,1)} %param.13) | copy-start | bytes 1572868
  7.2 4.7 %copy-start.15 = (s32[1,128,1]{1,2,0:T(1,128)S(1)}, s32[1,128,1]{1,2,0:T(1,128)}, u32[]{:S(2)}) copy-start(s32[1,128,1]{1,2,0:T(1,128)} %param.20) | copy-start | bytes 1540
  7.2 4.7 %copy-start.3 = (bf16[1,128,2048]{2,1,0:T(8,128)(2,1)S(1)}, bf16[1,128,2048]{2,1,0:T(8,128)(2,1)}, u32[]{:S(2)}) copy-start(bf16[1,128,2048]{2,1,0:T(8,128)(2,1)} %param.12) | copy-start | bytes 1572868
  7.2 4.7 %copy-start.14 = (f32[1,2048]{1,0:T(1,128)S(1)}, f32[1,2048]{1,0:T(1,128)}, u32[]{:S(2)}) copy-start(f32[1,2048]{1,0:T(1,128)} %gain_ref.5) | copy-start | bytes 24580
  7.2 58.4 %all-gather.5.cloned.1.call-start = ((), (), s32[]{:S(2)}) async-start(), calls=%async_computation | async-start | bytes 2359296 | tf_op jit(solution)/shard_map/all_gather | solution.py:31
  7.3 23.4 %copy-start.16 = (s32[1,128,1]{1,2,0:T(1,128)S(1)}, s32[1,128,1]{1,2,0:T(1,128)}, u32[]{:S(2)}) copy-start(s32[1,128,1]{1,2,0:T(1,128)} %param.18) | copy-start | bytes 1540
  7.9 60.4 %all-gather.7.cloned.1.call-start = ((), (), s32[]{:S(2)}) async-start(), calls=%async_computation.1 | async-start | bytes 2359296 | tf_op jit(solution)/shard_map/all_gather | solution.py:31
  8.7 88.4 %all-gather.9.cloned.1.call-start = ((), (), s32[]{:S(2)}) async-start(), calls=%async_computation.2 | async-start | bytes 2359296 | tf_op jit(solution)/shard_map/all_gather | solution.py:31
  9.4 10.9 %collective-permute-start.1 = (bf16[128,2048]{1,0:T(8,128)(2,1)S(1)}, bf16[128,2048]{1,0:T(8,128)(2,1)S(1)}, u32[]{:S(2)}, u32[]{:S(2)}) collective-permute-start(bf16[128,2048]{1,0:T(8,128)(2,1)S(1)} %bitcast.32), channel_id=1, source_target_pairs={{0,24},{8,0},{16,8},{24,16},{1,25},{9,1},{17,9},{25,17},{2,26},{10... | collective-permute-start | bytes 1572872 | tf_op jit(solution)/shard_map/ppermute | solution.py:21
  12.8 14.8 %collective-permute-start.2 = (bf16[264,512]{1,0:T(8,128)(2,1)S(1)}, bf16[264,512]{1,0:T(8,128)(2,1)S(1)}, u32[]{:S(2)}, u32[]{:S(2)}) collective-permute-start(bf16[264,512]{1,0:T(8,128)(2,1)S(1)} %get-tuple-element.29), channel_id=1, source_target_pairs={{0,4},{1,5},{2,6},{3,7},{4,0},{5,1},{6,2},{7,3},{8,12},{9,13},{10,... | collective-permute-start | bytes 811016 | tf_op jit(solution)/shard_map/ppermute | solution.py:21
  15.5 15.2 %collective-permute-start = (bf16[128,2048]{1,0:T(8,128)(2,1)}, bf16[128,2048]{1,0:T(8,128)(2,1)S(1)}, u32[]{:S(2)}, u32[]{:S(2)}) collective-permute-start(bf16[128,2048]{1,0:T(8,128)(2,1)} %bitcast.33), channel_id=1, source_target_pairs={{0,8},{8,16},{16,24},{24,0},{1,9},{9,17},{17,25},{25,1},{2,10},{10... | collective-permute-start | bytes 1572872 | tf_op jit(solution)/shard_map/ppermute | solution.py:21
  15.5 15.1 %collective-permute-start.3 = (bf16[264,512]{1,0:T(8,128)(2,1)S(1)}, bf16[264,512]{1,0:T(8,128)(2,1)S(1)}, u32[]{:S(2)}, u32[]{:S(2)}) collective-permute-start(bf16[264,512]{1,0:T(8,128)(2,1)S(1)} %get-tuple-element.26.refs_0_), channel_id=1, source_target_pairs={{0,2},{1,3},{2,0},{3,1},{4,6},{5,7},{6,4},{7,5},{8,10},{9,11},{10,... | collective-permute-start | bytes 811016 | tf_op jit(solution)/shard_map/ppermute | solution.py:26
  21.2 32.8 %copy-start.4 = (bf16[264,512]{1,0:T(8,128)(2,1)}, bf16[264,512]{1,0:T(8,128)(2,1)S(1)}, u32[]{:S(2)}) copy-start(bf16[264,512]{1,0:T(8,128)(2,1)S(1)} %get-tuple-element.34.refs_4_) | copy-start | bytes 811012
  21.2 18.1 %collective-permute-start.5 = (bf16[264,512]{1,0:T(8,128)(2,1)S(1)}, bf16[264,512]{1,0:T(8,128)(2,1)S(1)}, u32[]{:S(2)}, u32[]{:S(2)}) collective-permute-start(bf16[264,512]{1,0:T(8,128)(2,1)S(1)} %get-tuple-element.33), channel_id=1, source_target_pairs={{0,4},{1,5},{2,6},{3,7},{4,0},{5,1},{6,2},{7,3},{8,12},{9,13},{10,... | collective-permute-start | bytes 811016 | tf_op jit(solution)/shard_map/ppermute | solution.py:21
  27.6 19.8 %collective-permute-start.6 = (bf16[264,512]{1,0:T(8,128)(2,1)S(1)}, bf16[264,512]{1,0:T(8,128)(2,1)S(1)}, u32[]{:S(2)}, u32[]{:S(2)}) collective-permute-start(bf16[264,512]{1,0:T(8,128)(2,1)S(1)} %get-tuple-element.34.refs_4_), channel_id=1, source_target_pairs={{0,2},{1,3},{2,0},{3,1},{4,6},{5,7},{6,4},{7,5},{8,10},{9,11},{10,... | collective-permute-start | bytes 811016 | tf_op jit(solution)/shard_map/ppermute | solution.py:26
  30.6 22.7 %collective-permute-start.4 = (bf16[264,512]{1,0:T(8,128)(2,1)S(1)}, bf16[264,512]{1,0:T(8,128)(2,1)S(1)}, u32[]{:S(2)}, u32[]{:S(2)}) collective-permute-start(bf16[264,512]{1,0:T(8,128)(2,1)S(1)} %collective-permute-done.2.refs_1_), channel_id=1, source_target_pairs={{0,2},{1,3},{2,0},{3,1},{4,6},{5,7},{6,4},{7,5},{8,10},{9,11},{10,... | collective-permute-start | bytes 811016 | tf_op jit(solution)/shard_map/ppermute | solution.py:26
  31.6 22.4 %collective-permute-start.8 = (bf16[264,512]{1,0:T(8,128)(2,1)S(1)}, bf16[264,512]{1,0:T(8,128)(2,1)S(1)}, u32[]{:S(2)}, u32[]{:S(2)}) collective-permute-start(bf16[264,512]{1,0:T(8,128)(2,1)S(1)} %get-tuple-element.38), channel_id=1, source_target_pairs={{0,4},{1,5},{2,6},{3,7},{4,0},{5,1},{6,2},{7,3},{8,12},{9,13},{10,... | collective-permute-start | bytes 811016 | tf_op jit(solution)/shard_map/ppermute | solution.py:21
  39.3 19.7 %collective-permute-start.9 = (bf16[264,512]{1,0:T(8,128)(2,1)S(1)}, bf16[264,512]{1,0:T(8,128)(2,1)S(1)}, u32[]{:S(2)}, u32[]{:S(2)}) collective-permute-start(bf16[264,512]{1,0:T(8,128)(2,1)S(1)} %get-tuple-element.39.refs_0_), channel_id=1, source_target_pairs={{0,2},{1,3},{2,0},{3,1},{4,6},{5,7},{6,4},{7,5},{8,10},{9,11},{10,... | collective-permute-start | bytes 811016 | tf_op jit(solution)/shard_map/ppermute | solution.py:26
  48.2 16.6 %collective-permute-start.7 = (bf16[264,512]{1,0:T(8,128)(2,1)S(1)}, bf16[264,512]{1,0:T(8,128)(2,1)S(1)}, u32[]{:S(2)}, u32[]{:S(2)}) collective-permute-start(bf16[264,512]{1,0:T(8,128)(2,1)S(1)} %collective-permute-done.5.refs_5_), channel_id=1, source_target_pairs={{0,2},{1,3},{2,0},{3,1},{4,6},{5,7},{6,4},{7,5},{8,10},{9,11},{10,... | collective-permute-start | bytes 811016 | tf_op jit(solution)/shard_map/ppermute | solution.py:26
  59.1 52.2 %collective-permute-start.10 = (bf16[264,512]{1,0:T(8,128)(2,1)S(1)}, bf16[264,512]{1,0:T(8,128)(2,1)S(1)}, u32[]{:S(2)}, u32[]{:S(2)}) collective-permute-start(bf16[264,512]{1,0:T(8,128)(2,1)S(1)} %collective-permute-done.8.refs_1_), channel_id=1, source_target_pairs={{0,2},{1,3},{2,0},{3,1},{4,6},{5,7},{6,4},{7,5},{8,10},{9,11},{10,... | collective-permute-start | bytes 811016 | tf_op jit(solution)/shard_map/ppermute | solution.py:26
  97.1 1.4 copy-start
  98.5 1.4 copy-start.1
  99.9 1.4 copy-start.2
  103.2 1.0 copy-start.9
  109.7 9.4 %collective-permute-start.12 = (bf16[264,512]{1,0:T(8,128)(2,1)S(1)}, bf16[264,512]{1,0:T(8,128)(2,1)S(1)}, u32[]{:S(2)}, u32[]{:S(2)}) collective-permute-start(bf16[264,512]{1,0:T(8,128)(2,1)S(1)} %get-tuple-element.47), channel_id=1, source_target_pairs={{0,2},{1,3},{2,0},{3,1},{4,6},{5,7},{6,4},{7,5},{8,10},{9,11},{10,... | collective-permute-start | bytes 811016 | tf_op jit(solution)/shard_map/ppermute | solution.py:26
  113.6 22.1 %copy-start.18 = (f32[1,128,1]{1,2,0:T(1,128)S(1)}, f32[1,128,1]{1,2,0:T(1,128)}, u32[]{:S(2)}) copy-start(f32[1,128,1]{1,2,0:T(1,128)} %param.21) | copy-start | bytes 1540
  113.6 17.2 %collective-permute-start.11 = (bf16[264,512]{1,0:T(8,128)(2,1)S(1)}, bf16[264,512]{1,0:T(8,128)(2,1)S(1)}, u32[]{:S(2)}, u32[]{:S(2)}) collective-permute-start(bf16[264,512]{1,0:T(8,128)(2,1)S(1)} %get-tuple-element.44), channel_id=1, source_target_pairs={{0,2},{1,3},{2,0},{3,1},{4,6},{5,7},{6,4},{7,5},{8,10},{9,11},{10,... | collective-permute-start | bytes 811016 | tf_op jit(solution)/shard_map/ppermute | solution.py:26
  119.2 16.4 %collective-permute-start.13 = (bf16[264,512]{1,0:T(8,128)(2,1)S(1)}, bf16[264,512]{1,0:T(8,128)(2,1)S(1)}, u32[]{:S(2)}, u32[]{:S(2)}) collective-permute-start(bf16[264,512]{1,0:T(8,128)(2,1)S(1)} %get-tuple-element.48), channel_id=1, source_target_pairs={{0,2},{1,3},{2,0},{3,1},{4,6},{5,7},{6,4},{7,5},{8,10},{9,11},{10,... | collective-permute-start | bytes 811016 | tf_op jit(solution)/shard_map/ppermute | solution.py:26
  120.8 14.9 %collective-permute-start.16 = (bf16[264,512]{1,0:T(8,128)(2,1)S(1)}, bf16[264,512]{1,0:T(8,128)(2,1)S(1)}, u32[]{:S(2)}, u32[]{:S(2)}) collective-permute-start(bf16[264,512]{1,0:T(8,128)(2,1)S(1)} %add_convert_fusion), channel_id=1, source_target_pairs={{0,4},{1,5},{2,6},{3,7},{4,0},{5,1},{6,2},{7,3},{8,12},{9,13},{10,... | collective-permute-start | bytes 811016 | tf_op jit(solution)/shard_map/ppermute | solution.py:21
  130.8 17.8 %copy-start.17 = (f32[1,128,1]{1,2,0:T(1,128)S(1)}, f32[1,128,1]{1,2,0:T(1,128)}, u32[]{:S(2)}) copy-start(f32[1,128,1]{1,2,0:T(1,128)} %param.19) | copy-start | bytes 1540
  130.9 17.8 %collective-permute-start.15 = (bf16[264,512]{1,0:T(8,128)(2,1)S(1)}, bf16[264,512]{1,0:T(8,128)(2,1)S(1)}, u32[]{:S(2)}, u32[]{:S(2)}) collective-permute-start(bf16[264,512]{1,0:T(8,128)(2,1)S(1)} %add_convert_fusion.1), channel_id=1, source_target_pairs={{0,4},{1,5},{2,6},{3,7},{4,0},{5,1},{6,2},{7,3},{8,12},{9,13},{10,... | collective-permute-start | bytes 811016 | tf_op jit(solution)/shard_map/ppermute | solution.py:21
  135.7 13.0 %collective-permute-start.14 = (bf16[264,512]{1,0:T(8,128)(2,1)S(1)}, bf16[264,512]{1,0:T(8,128)(2,1)S(1)}, u32[]{:S(2)}, u32[]{:S(2)}) collective-permute-start(bf16[264,512]{1,0:T(8,128)(2,1)S(1)} %get-tuple-element.49), channel_id=1, source_target_pairs={{0,2},{1,3},{2,0},{3,1},{4,6},{5,7},{6,4},{7,5},{8,10},{9,11},{10,... | collective-permute-start | bytes 811016 | tf_op jit(solution)/shard_map/ppermute | solution.py:26
  (8 other events, 6.7 us)
Sparse Core Ops, SparseCore 0:
  9.6 29.8 all-gather.4
  41.1 27.2 all-gather.6
  69.9 27.1 all-gather.8

commit v7 on v6

--- a/solution.py
+++ b/solution.py
@@ -120,26 +120,38 @@
         ref[...] = jnp.concatenate(pieces, axis=0).astype(ref.dtype)
 
 
+def whole_shares(refs):
+    side_ref, gate, other_gate, up, other_up, both_down = refs
+    units = gate.shape[0]
+    first = pl.multiple_of(side_ref[0] * units, units)
+    down = [both_down[pl.ds(first, units), :], both_down[pl.ds(units - first, units), :]]
+    return [
+        jnp.concatenate(parts, axis=0)
+        for parts in ((gate[...], other_gate[...]), (up[...], other_up[...]), down)
+    ]
+
+
 def forward_body(count, rows, *refs):
-    row_refs, shares, outs, wide_ref = refs[:count], refs[count:count + 3], refs[count + 3:-1], refs[-1]
+    row_refs, shares, outs, wide_ref = refs[:count], refs[count:count + 6], refs[count + 6:-1], refs[-1]
     x = unpack(row_refs, wide_ref, rows)
-    gate_pre = lax.dot_general(x, shares[0][...], CONTRACT, preferred_element_type=F32)
-    up_pre = lax.dot_general(x, shares[1][...], CONTRACT, preferred_element_type=F32)
+    gate, up, down = whole_shares(shares)
+    gate_pre = lax.dot_general(x, gate, CONTRACT, preferred_element_type=F32)
+    up_pre = lax.dot_general(x, up, CONTRACT, preferred_element_type=F32)
     hidden = (silu_parts(gate_pre)[0] * up_pre).astype(BF16)
-    total = jnp.dot(hidden, shares[2][...], preferred_element_type=F32)
+    total = jnp.dot(hidden, down, preferred_element_type=F32)
     spread_out(total, outs, x.shape[0] // count, rows)
 
 
 def backward_body(count, rows, *refs):
-    row_refs, grad_refs, shares = refs[:count], refs[count:2 * count], refs[2 * count:2 * count + 3]
-    outs, wide_ref, grad_wide_ref = refs[2 * count + 3:-2], refs[-2], refs[-1]
+    row_refs, grad_refs, shares = refs[:count], refs[count:2 * count], refs[2 * count:2 * count + 6]
+    outs, wide_ref, grad_wide_ref = refs[2 * count + 6:-2], refs[-2], refs[-1]
     x = unpack(row_refs, wide_ref, rows)
-    gate, up = shares[0][...], shares[1][...]
+    gate, up, down = whole_shares(shares)
     gate_pre = lax.dot_general(x, gate, CONTRACT, preferred_element_type=F32)
     up_pre = lax.dot_general(x, up, CONTRACT, preferred_element_type=F32)
     activation, derivative = silu_parts(gate_pre)
     grads = unpack(grad_refs, grad_wide_ref, rows)
-    d_hidden = lax.dot_general(grads, shares[2][...], CONTRACT, preferred_element_type=F32)
+    d_hidden = lax.dot_general(grads, down, CONTRACT, preferred_element_type=F32)
     d_gate = (d_hidden * up_pre * derivative).astype(BF16)
     d_up = (d_hidden * activation).astype(BF16)
     total = jnp.dot(d_gate, gate, preferred_element_type=F32) + jnp.dot(d_up, up, preferred_element_type=F32)
@@ -232,7 +244,9 @@
         out_specs=[whole] * experts,
         name="pack_saved",
     )(own, r_bwd, norm_gain, saved_in[0])
-    shares = [both_shares(share) for share in (w_gate[0].T, w_up[0].T, w_down[0])]
+    gate, up = w_gate[0].T, w_up[0].T
+    both_down = both_shares(w_down[0])
+    other_gate = swapped(gate, "expert", 1)
 
     rows_b = crossed(packed_b)
     swap_b = partners(rows_b[:1])
@@ -254,16 +268,20 @@
     rows_f = crossed(packed_f)
     swap_g = partners(rows_g[:1], rows_b[-1])
     swap_f = partners(rows_f[:1], rows_g[-1])
+    other_up = swapped(up, "expert", 1)
+    side = (lax.axis_index("expert") % 2).astype(jnp.int32).reshape(1)
+    shares = (side, gate, other_gate, up, other_up, both_down)
     rows_b = rows_b + swap_b + partners(rows_b[1:], swap_b[0])
     rows_g = rows_g + swap_g + partners(rows_g[1:], swap_g[0])
     rows_f = rows_f + swap_f + partners(rows_f[1:], swap_f[0], rows_b[-1])
 
     count = 2 * experts
+    weight_specs = [scalar] + [whole] * 5
     partial_b = local_call(
-        functools.partial(backward_body, count, rows), partial, scratch=[wide, wide], vmem_mib=40, name="experts_bwd"
+        functools.partial(backward_body, count, rows), partial, scratch=[wide, wide], vmem_mib=32, in_specs=[whole] * 2 * count + weight_specs, name="experts_bwd"
     )(*rows_b, *rows_g, *shares)
     partial_f = local_call(
-        functools.partial(forward_body, count, rows), partial, scratch=[wide], vmem_mib=32, name="experts_fwd"
+        functools.partial(forward_body, count, rows), partial, scratch=[wide], vmem_mib=24, in_specs=[whole] * count + weight_specs, name="experts_fwd"
     )(after(rows_f[0], partial_b[0]), *rows_f[1:], *shares)
     totals_b, home_b = crossing_home(partial_b)
     totals_f, home_f = crossing_home(partial_f)

time: 157 us -> 131 us (0.83)
  waiting for transfers between devices: 96.5 us -> 64.9 us
  Pallas kernels: 12.3 us -> 17.4 us
  starting transfers between devices: 22.2 us -> 17.3 us
  local copies, waits for them, and re-layouts: 11.9 us -> 16 us
    all_gather x3 -> x1, waiting for transfers between devices: 31.5 us -> 0.01 us  [both_shares(): return lax.all_gather(share, 'expert', axis_index_groups=pairs, tiled=True)]
    ppermute x7, starting transfers between devices: 15.6 us -> 6.4 us  [shifted(): lax.ppermute(value, axis, [(i, (i + steps) % count) for i in range(count)])]
    ppermute x10 -> x12, starting transfers between devices: 6.45 us -> 10.9 us  [swapped(): return lax.ppermute(value, axis, [(i, i ^ bit) for i in range(count)])]
    unnamed x40 -> x56, local copies, waits for them, and re-layouts: 11.9 us -> 16 us
    pallas_call x2, Pallas kernels: 1.82 us -> 3.58 us  [per_device(): local_call(pack_act_body, packed, in_specs=[scalar] + [whole] * 3, out_sp...]
    ppermute x10 -> x12, waiting for transfers between devices: 41.1 us -> 42.1 us  [swapped(): return lax.ppermute(value, axis, [(i, i ^ bit) for i in range(count)])]
  transfers between devices with their start and end apart: 20 -> 20, of which waited for: 14 -> 13; matrix products, arithmetic and copies ran while one was open for 0% -> 0% of each run, Pallas kernels for 7% -> 11%
where the time goes in v7:
time: 131 us; the launch traced here: 130 us
  waiting for transfers between devices  64.9 us (50%)
  Pallas kernels  17.4 us (13%)
  starting transfers between devices  17.3 us (13%)
  local copies, waits for them, and re-layouts  16 us (12%)
  between operations  14.2 us (11%)
    ppermute x12, waiting for transfers between devices, swapped(): return lax.ppermute(value, axis, [(i, i ^ bit) for i in range(count)])  42.1 us
    ppermute x7, waiting for transfers between devices, shifted(): lax.ppermute(value, axis, [(i, (i + steps) % count) for i in range(count)])  22.1 us
    unnamed x56, local copies, waits for them, and re-layouts  16 us
    ppermute x12, starting transfers between devices, swapped(): return lax.ppermute(value, axis, [(i, i ^ bit) for i in range(count)])  10.9 us
    ppermute x7, starting transfers between devices, shifted(): lax.ppermute(value, axis, [(i, (i + steps) % count) for i in range(count)])  6.4 us
    pallas_call x1, Pallas kernels, per_device(): local_call(functools.partial(backward_body, count, rows), partial, scratc...  4.67 us
    pallas_call x2, Pallas kernels, per_device(): local_call(pack_act_body, packed, in_specs=[scalar] + [whole] * 3, out_sp...  3.58 us
    pallas_call x1, Pallas kernels, per_device(): local_call(functools.partial(forward_body, count, rows), partial, scratch...  3.44 us
  transfers between devices with their start and end apart: 20, of which 13 were waited for; matrix products, arithmetic and copies ran while one was open for 0% of the time, Pallas kernels for 11%

profile of v7, /device:TPU:0, one launch (start us, length us, event | category | flops | bytes accessed | tf_op | source)
XLA Modules:
  0.0 130.0 jit_solution(17501877799883797942)
XLA Ops:
  7.9 2.5 %collective-permute-start.1 = (bf16[128,2048]{1,0:T(8,128)(2,1)}, bf16[128,2048]{1,0:T(8,128)(2,1)S(1)}, u32[]{:S(2)}, u32[]{:S(2)}) collective-permute-start(bf16[128,2048]{1,0:T(8,128)(2,1)} %bitcast.37), channel_id=1, source_target_pairs={{0,24},{8,0},{16,8},{24,16},{1,25},{9,1},{17,9},{25,17},{2,26},{10... | collective-permute-start | bytes 1572872 | tf_op jit(solution)/shard_map/ppermute | solution.py:21
  10.4 1.0 copy-done.3
  13.7 2.7 %collective-permute-start.2 = (bf16[264,512]{1,0:T(8,128)(2,1)S(1)}, bf16[264,512]{1,0:T(8,128)(2,1)S(1)}, u32[]{:S(2)}, u32[]{:S(2)}) collective-permute-start(bf16[264,512]{1,0:T(8,128)(2,1)S(1)} %get-tuple-element.29), channel_id=1, source_target_pairs={{0,4},{1,5},{2,6},{3,7},{4,0},{5,1},{6,2},{7,3},{8,12},{9,13},{10,... | collective-permute-start | bytes 811016 | tf_op jit(solution)/shard_map/ppermute | solution.py:21
  16.3 1.6 %collective-permute-start.3 = (bf16[264,512]{1,0:T(8,128)(2,1)S(1)}, bf16[264,512]{1,0:T(8,128)(2,1)S(1)}, u32[]{:S(2)}, u32[]{:S(2)}) collective-permute-start(bf16[264,512]{1,0:T(8,128)(2,1)S(1)} %get-tuple-element.26.refs_0_), channel_id=1, source_target_pairs={{0,2},{1,3},{2,0},{3,1},{4,6},{5,7},{6,4},{7,5},{8,10},{9,11},{10,... | collective-permute-start | bytes 811016 | tf_op jit(solution)/shard_map/ppermute | solution.py:26
  17.9 1.5 %collective-permute-start.8 = (bf16[192,2048]{1,0:T(8,128)(2,1)}, bf16[192,2048]{1,0:T(8,128)(2,1)S(1)}, u32[]{:S(2)}, u32[]{:S(2)}) collective-permute-start(bf16[192,2048]{1,0:T(8,128)(2,1)} %bitcast.20), channel_id=1, source_target_pairs={{0,1},{1,0},{2,3},{3,2},{4,5},{5,4},{6,7},{7,6},{8,9},{9,8},{10,11... | collective-permute-start | bytes 2359304 | tf_op jit(solution)/shard_map/ppermute | solution.py:26
  19.4 3.5 %collective-permute-done.1.x_ref.up_ref = bf16[128,2048]{1,0:T(8,128)(2,1)S(1)} collective-permute-done((bf16[128,2048]{1,0:T(8,128)(2,1)}, bf16[128,2048]{1,0:T(8,128)(2,1)S(1)}, u32[]{:S(2)}, u32[]{:S(2)}) %collective-permute-start.1) | collective-permute-done | bytes 524320 | tf_op jit(solution)/shard_map/ppermute | solution.py:21
  23.8 1.5 %collective-permute-start.9 = (bf16[192,2048]{1,0:T(8,128)(2,1)}, bf16[192,2048]{1,0:T(8,128)(2,1)S(1)}, u32[]{:S(2)}, u32[]{:S(2)}) collective-permute-start(bf16[192,2048]{1,0:T(8,128)(2,1)} %bitcast.23), channel_id=1, source_target_pairs={{0,1},{1,0},{2,3},{3,2},{4,5},{5,4},{6,7},{7,6},{8,9},{9,8},{10,11... | collective-permute-start | bytes 2359304 | tf_op jit(solution)/shard_map/ppermute | solution.py:26
  25.2 1.0 copy-done.6
  27.8 1.9 %collective-permute-done.2.refs_1_ = bf16[264,512]{1,0:T(8,128)(2,1)S(1)} collective-permute-done((bf16[264,512]{1,0:T(8,128)(2,1)S(1)}, bf16[264,512]{1,0:T(8,128)(2,1)S(1)}, u32[]{:S(2)}, u32[]{:S(2)}) %collective-permute-start.2) | collective-permute-done | bytes 270368 | tf_op jit(solution)/shard_map/ppermute | solution.py:21
  31.2 3.1 %collective-permute-start.6 = (bf16[264,512]{1,0:T(8,128)(2,1)S(1)}, bf16[264,512]{1,0:T(8,128)(2,1)S(1)}, u32[]{:S(2)}, u32[]{:S(2)}) collective-permute-start(bf16[264,512]{1,0:T(8,128)(2,1)S(1)} %get-tuple-element.34.refs_4_), channel_id=1, source_target_pairs={{0,2},{1,3},{2,0},{3,1},{4,6},{5,7},{6,4},{7,5},{8,10},{9,11},{10,... | collective-permute-start | bytes 811016 | tf_op jit(solution)/shard_map/ppermute | solution.py:26
  37.1 2.7 %pack_act.1 = (bf16[264,512]{1,0:T(8,128)(2,1)}, bf16[264,512]{1,0:T(8,128)(2,1)}) custom-call(s32[1]{0:T(128)} %bitcast.own_ref, s32[1,128]{1,0:T(1,128)S(1)} %bitcast.31, f32[1,2048]{1,0:T(1,128)S(1)} %copy-done.19, bf16[128,2048]{1,0:T(8,128)(2,1)} %collective-permute-done.x_ref), custom_call_target="tpu_custom_call" | custom-call | flops 1000 | bytes 1000 | tf_op jit(solution)/shard_map/pack_act/pallas_call | solution.py:261
  39.8 5.0 %collective-permute-done.5.refs_5_ = bf16[264,512]{1,0:T(8,128)(2,1)} collective-permute-done((bf16[264,512]{1,0:T(8,128)(2,1)S(1)}, bf16[264,512]{1,0:T(8,128)(2,1)}, u32[]{:S(2)}, u32[]{:S(2)}) %collective-permute-start.5) | collective-permute-done | bytes 270368 | tf_op jit(solution)/shard_map/ppermute | solution.py:21
  44.8 1.5 %collective-permute-done.6.refs_6_ = bf16[264,512]{1,0:T(8,128)(2,1)S(1)} collective-permute-done((bf16[264,512]{1,0:T(8,128)(2,1)S(1)}, bf16[264,512]{1,0:T(8,128)(2,1)S(1)}, u32[]{:S(2)}, u32[]{:S(2)}) %collective-permute-start.6) | collective-permute-done | bytes 270368 | tf_op jit(solution)/shard_map/ppermute | solution.py:26
  48.0 8.2 %collective-permute-done.4.refs_3_ = bf16[264,512]{1,0:T(8,128)(2,1)S(1)} collective-permute-done((bf16[264,512]{1,0:T(8,128)(2,1)S(1)}, bf16[264,512]{1,0:T(8,128)(2,1)S(1)}, u32[]{:S(2)}, u32[]{:S(2)}) %collective-permute-start.4) | collective-permute-done | bytes 270368 | tf_op jit(solution)/shard_map/ppermute | solution.py:26
  56.9 2.3 %collective-permute-done.10.refs_1_ = bf16[264,512]{1,0:T(8,128)(2,1)} collective-permute-done((bf16[264,512]{1,0:T(8,128)(2,1)}, bf16[264,512]{1,0:T(8,128)(2,1)}, u32[]{:S(2)}, u32[]{:S(2)}) %collective-permute-start.10) | collective-permute-done | bytes 270368 | tf_op jit(solution)/shard_map/ppermute | solution.py:21
  59.3 4.6 %collective-permute-done.11.refs_2_ = bf16[264,512]{1,0:T(8,128)(2,1)} collective-permute-done((bf16[264,512]{1,0:T(8,128)(2,1)}, bf16[264,512]{1,0:T(8,128)(2,1)}, u32[]{:S(2)}, u32[]{:S(2)}) %collective-permute-start.11) | collective-permute-done | bytes 270368 | tf_op jit(solution)/shard_map/ppermute | solution.py:26
  63.8 7.6 %collective-permute-done.9.refs_12_.refs_8_ = bf16[192,2048]{1,0:T(8,128)(2,1)S(1)} collective-permute-done((bf16[192,2048]{1,0:T(8,128)(2,1)}, bf16[192,2048]{1,0:T(8,128)(2,1)S(1)}, u32[]{:S(2)}, u32[]{:S(2)}) %collective-permute-start.9) | collective-permute-done | bytes 786464 | tf_op jit(solution)/shard_map/ppermute | solution.py:26
  71.5 1.4 %copy-done = bf16[1,384,2048]{2,1,0:T(8,128)(2,1)S(1)} copy-done((bf16[1,384,2048]{2,1,0:T(8,128)(2,1)S(1)}, bf16[1,384,2048]{2,1,0:T(8,128)(2,1)}, u32[]{:S(2)}) %copy-start) | copy-done | bytes 1572888
  72.9 1.0 copy-done.9
  73.9 1.0 copy-done.11
  74.8 1.0 copy-done.13
  75.8 1.0 copy-done.15
  77.7 4.7 %experts_bwd.1 = (f32[264,512]{1,0:T(8,128)S(1)}, f32[264,512]{1,0:T(8,128)S(1)}, bf16[264,512]{1,0:T(8,128)(2,1)S(1)}, bf16[264,512]{1,0:T(8,128)(2,1)S(1)}) custom-call(bf16[264,512]{1,0:T(8,128)(2,1)S(1)} %get-tuple-element.26.refs_0_, bf16[264,512]{1,0:T(8,128)(2,1)S(1)} %copy-done.9, bf16[264,512]{1,0:T(8,128)(2,1)S(1)} %copy-done.11, ...), custom_call_target="tpu_custom_call" | custom-call | flops 1000 | bytes 1000 | tf_op jit(solution)/shard_map/experts_bwd/pallas_call | solution.py:280
  82.9 3.4 %experts_fwd.1 = (f32[264,512]{1,0:T(8,128)S(1)}, f32[264,512]{1,0:T(8,128)S(1)}, bf16[264,512]{1,0:T(8,128)(2,1)S(1)}, bf16[264,512]{1,0:T(8,128)(2,1)S(1)}) custom-call(bf16[264,512]{1,0:T(8,128)(2,1)} %get-tuple-element.39.refs_0_, bf16[264,512]{1,0:T(8,128)(2,1)} %collective-permute-done.10.refs_1_, bf16[264,512]{1,0:T(8,128)(2,1)} %collective-permute-done.11.refs_2_, ...), custom_call_target="tpu_custom_call" | custom-call | flops 1000 | bytes 1000 | tf_op jit(solution)/shard_map/experts_fwd/pallas_call | solution.py:283
  86.4 1.6 %collective-permute-start.13 = (bf16[264,512]{1,0:T(8,128)(2,1)S(1)}, bf16[264,512]{1,0:T(8,128)(2,1)S(1)}, u32[]{:S(2)}, u32[]{:S(2)}) collective-permute-start(bf16[264,512]{1,0:T(8,128)(2,1)S(1)} %get-tuple-element.44), channel_id=1, source_target_pairs={{0,2},{1,3},{2,0},{3,1},{4,6},{5,7},{6,4},{7,5},{8,10},{9,11},{10,... | collective-permute-start | bytes 811016 | tf_op jit(solution)/shard_map/ppermute | solution.py:26
  88.0 3.8 %collective-permute-done.14 = bf16[264,512]{1,0:T(8,128)(2,1)S(1)} collective-permute-done((bf16[264,512]{1,0:T(8,128)(2,1)S(1)}, bf16[264,512]{1,0:T(8,128)(2,1)S(1)}, u32[]{:S(2)}, u32[]{:S(2)}) %collective-permute-start.14) | collective-permute-done | bytes 270368 | tf_op jit(solution)/shard_map/ppermute | solution.py:26
  92.4 11.0 %collective-permute-done.13 = bf16[264,512]{1,0:T(8,128)(2,1)S(1)} collective-permute-done((bf16[264,512]{1,0:T(8,128)(2,1)S(1)}, bf16[264,512]{1,0:T(8,128)(2,1)S(1)}, u32[]{:S(2)}, u32[]{:S(2)}) %collective-permute-start.13) | collective-permute-done | bytes 270368 | tf_op jit(solution)/shard_map/ppermute | solution.py:26
  103.6 4.1 %collective-permute-done.15.refs_1_ = bf16[264,512]{1,0:T(8,128)(2,1)S(1)} collective-permute-done((bf16[264,512]{1,0:T(8,128)(2,1)S(1)}, bf16[264,512]{1,0:T(8,128)(2,1)S(1)}, u32[]{:S(2)}, u32[]{:S(2)}) %collective-permute-start.15) | collective-permute-done | bytes 270368 | tf_op jit(solution)/shard_map/ppermute | solution.py:26
  107.8 2.0 %home_bwd.1 = bf16[128,2048]{1,0:T(8,128)(2,1)} custom-call(s32[1]{0:T(128)} %bitcast.own_ref, s32[1,128]{1,0:T(1,128)S(1)} %bitcast.30, f32[1,128]{1,0:T(1,128)S(1)} %bitcast.34, f32[1,2048]{1,0:T(1,128)S(1)} %copy-done.20, bf16[128,2048]{1,0:T(8,128)(2,1)S(1)} %bitcast.27, bf16[128,2048]{1,0:T(8,128)(2,1)S(1)} %copy-done.7, ...), custom_call_target="tpu_custom_call" | custom-call | flops 1000 | bytes 1000 | tf_op jit(solution)/shard_map/home_bwd/pallas_call | solution.py:291
  109.8 9.3 %collective-permute-done.17.refs_2_ = bf16[264,512]{1,0:T(8,128)(2,1)S(1)} collective-permute-done((bf16[264,512]{1,0:T(8,128)(2,1)S(1)}, bf16[264,512]{1,0:T(8,128)(2,1)S(1)}, u32[]{:S(2)}, u32[]{:S(2)}) %collective-permute-start.17) | collective-permute-done | bytes 270368 | tf_op jit(solution)/shard_map/ppermute | solution.py:21
  119.1 1.2 collective-permute-done.16.refs_1_
  120.4 2.8 %home_fwd.1 = bf16[128,2048]{1,0:T(8,128)(2,1)} custom-call(s32[1]{0:T(128)} %bitcast.own_ref, s32[1,128]{1,0:T(1,128)S(1)} %bitcast.32, f32[1,128]{1,0:T(1,128)S(1)} %bitcast.33, bf16[128,2048]{1,0:T(8,128)(2,1)} %collective-permute-done.x_ref, f32[264,512]{1,0:T(8,128)S(1)} %get-tuple-element.41.refs_0_, ...), custom_call_target="tpu_custom_call" | custom-call | flops 1000 | bytes 1000 | tf_op jit(solution)/shard_map/home_fwd/pallas_call | solution.py:298
  (74 shorter events, 14.3 us)
Async XLA Ops:
  7.2 64.3 %copy-start.1 = (bf16[1,2048,192]{1,2,0:T(8,128)(2,1)S(1)}, bf16[1,2048,192]{1,2,0:T(8,128)(2,1)}, u32[]{:S(2)}) copy-start(bf16[1,2048,192]{1,2,0:T(8,128)(2,1)} %param.15) | copy-start | bytes 2359300
  7.2 64.3 %copy-start.2 = (bf16[1,2048,192]{1,2,0:T(8,128)(2,1)S(1)}, bf16[1,2048,192]{1,2,0:T(8,128)(2,1)}, u32[]{:S(2)}) copy-start(bf16[1,2048,192]{1,2,0:T(8,128)(2,1)} %param.16) | copy-start | bytes 2359300
  7.2 64.3 %all-gather.3.cloned.1.call-start = ((), (), s32[]{:S(2)}) async-start(), calls=%async_computation | async-start | bytes 2359296 | tf_op jit(solution)/shard_map/all_gather | solution.py:31
  7.9 15.0 %collective-permute-start.1 = (bf16[128,2048]{1,0:T(8,128)(2,1)}, bf16[128,2048]{1,0:T(8,128)(2,1)S(1)}, u32[]{:S(2)}, u32[]{:S(2)}) collective-permute-start(bf16[128,2048]{1,0:T(8,128)(2,1)} %bitcast.37), channel_id=1, source_target_pairs={{0,24},{8,0},{16,8},{24,16},{1,25},{9,1},{17,9},{25,17},{2,26},{10... | collective-permute-start | bytes 1572872 | tf_op jit(solution)/shard_map/ppermute | solution.py:21
  10.4 24.7 %collective-permute-start = (bf16[128,2048]{1,0:T(8,128)(2,1)}, bf16[128,2048]{1,0:T(8,128)(2,1)}, u32[]{:S(2)}, u32[]{:S(2)}) collective-permute-start(bf16[128,2048]{1,0:T(8,128)(2,1)} %bitcast.38), channel_id=1, source_target_pairs={{0,8},{8,16},{16,24},{24,0},{1,9},{9,17},{17,25},{25,1},{2,10},{10... | collective-permute-start | bytes 1572872 | tf_op jit(solution)/shard_map/ppermute | solution.py:21
  10.4 1.0 copy-start.3
  13.7 16.0 %collective-permute-start.2 = (bf16[264,512]{1,0:T(8,128)(2,1)S(1)}, bf16[264,512]{1,0:T(8,128)(2,1)S(1)}, u32[]{:S(2)}, u32[]{:S(2)}) collective-permute-start(bf16[264,512]{1,0:T(8,128)(2,1)S(1)} %get-tuple-element.29), channel_id=1, source_target_pairs={{0,4},{1,5},{2,6},{3,7},{4,0},{5,1},{6,2},{7,3},{8,12},{9,13},{10,... | collective-permute-start | bytes 811016 | tf_op jit(solution)/shard_map/ppermute | solution.py:21
  16.3 14.1 %collective-permute-start.3 = (bf16[264,512]{1,0:T(8,128)(2,1)S(1)}, bf16[264,512]{1,0:T(8,128)(2,1)S(1)}, u32[]{:S(2)}, u32[]{:S(2)}) collective-permute-start(bf16[264,512]{1,0:T(8,128)(2,1)S(1)} %get-tuple-element.26.refs_0_), channel_id=1, source_target_pairs={{0,2},{1,3},{2,0},{3,1},{4,6},{5,7},{6,4},{7,5},{8,10},{9,11},{10,... | collective-permute-start | bytes 811016 | tf_op jit(solution)/shard_map/ppermute | solution.py:26
  17.9 45.9 %collective-permute-start.8 = (bf16[192,2048]{1,0:T(8,128)(2,1)}, bf16[192,2048]{1,0:T(8,128)(2,1)S(1)}, u32[]{:S(2)}, u32[]{:S(2)}) collective-permute-start(bf16[192,2048]{1,0:T(8,128)(2,1)} %bitcast.20), channel_id=1, source_target_pairs={{0,1},{1,0},{2,3},{3,2},{4,5},{5,4},{6,7},{7,6},{8,9},{9,8},{10,11... | collective-permute-start | bytes 2359304 | tf_op jit(solution)/shard_map/ppermute | solution.py:26
  23.8 47.7 %collective-permute-start.9 = (bf16[192,2048]{1,0:T(8,128)(2,1)}, bf16[192,2048]{1,0:T(8,128)(2,1)S(1)}, u32[]{:S(2)}, u32[]{:S(2)}) collective-permute-start(bf16[192,2048]{1,0:T(8,128)(2,1)} %bitcast.23), channel_id=1, source_target_pairs={{0,1},{1,0},{2,3},{3,2},{4,5},{5,4},{6,7},{7,6},{8,9},{9,8},{10,11... | collective-permute-start | bytes 2359304 | tf_op jit(solution)/shard_map/ppermute | solution.py:26
  25.2 1.0 copy-start.6
  29.7 15.1 %collective-permute-start.5 = (bf16[264,512]{1,0:T(8,128)(2,1)S(1)}, bf16[264,512]{1,0:T(8,128)(2,1)}, u32[]{:S(2)}, u32[]{:S(2)}) collective-permute-start(bf16[264,512]{1,0:T(8,128)(2,1)S(1)} %get-tuple-element.33), channel_id=1, source_target_pairs={{0,4},{1,5},{2,6},{3,7},{4,0},{5,1},{6,2},{7,3},{8,12},{9,13},{10,... | collective-permute-start | bytes 811016 | tf_op jit(solution)/shard_map/ppermute | solution.py:21
  31.2 15.1 %collective-permute-start.6 = (bf16[264,512]{1,0:T(8,128)(2,1)S(1)}, bf16[264,512]{1,0:T(8,128)(2,1)S(1)}, u32[]{:S(2)}, u32[]{:S(2)}) collective-permute-start(bf16[264,512]{1,0:T(8,128)(2,1)S(1)} %get-tuple-element.34.refs_4_), channel_id=1, source_target_pairs={{0,2},{1,3},{2,0},{3,1},{4,6},{5,7},{6,4},{7,5},{8,10},{9,11},{10,... | collective-permute-start | bytes 811016 | tf_op jit(solution)/shard_map/ppermute | solution.py:26
  35.1 21.1 %collective-permute-start.4 = (bf16[264,512]{1,0:T(8,128)(2,1)S(1)}, bf16[264,512]{1,0:T(8,128)(2,1)S(1)}, u32[]{:S(2)}, u32[]{:S(2)}) collective-permute-start(bf16[264,512]{1,0:T(8,128)(2,1)S(1)} %collective-permute-done.2.refs_1_), channel_id=1, source_target_pairs={{0,2},{1,3},{2,0},{3,1},{4,6},{5,7},{6,4},{7,5},{8,10},{9,11},{10,... | collective-permute-start | bytes 811016 | tf_op jit(solution)/shard_map/ppermute | solution.py:26
  44.8 14.5 %collective-permute-start.10 = (bf16[264,512]{1,0:T(8,128)(2,1)}, bf16[264,512]{1,0:T(8,128)(2,1)}, u32[]{:S(2)}, u32[]{:S(2)}) collective-permute-start(bf16[264,512]{1,0:T(8,128)(2,1)} %get-tuple-element.38), channel_id=1, source_target_pairs={{0,4},{1,5},{2,6},{3,7},{4,0},{5,1},{6,2},{7,3},{8,12},{9,13},{10,... | collective-permute-start | bytes 811016 | tf_op jit(solution)/shard_map/ppermute | solution.py:21
  47.1 16.8 %collective-permute-start.11 = (bf16[264,512]{1,0:T(8,128)(2,1)}, bf16[264,512]{1,0:T(8,128)(2,1)}, u32[]{:S(2)}, u32[]{:S(2)}) collective-permute-start(bf16[264,512]{1,0:T(8,128)(2,1)} %get-tuple-element.39.refs_0_), channel_id=1, source_target_pairs={{0,2},{1,3},{2,0},{3,1},{4,6},{5,7},{6,4},{7,5},{8,10},{9,11},{10,... | collective-permute-start | bytes 811016 | tf_op jit(solution)/shard_map/ppermute | solution.py:26
  56.9 14.6 %collective-permute-start.7 = (bf16[264,512]{1,0:T(8,128)(2,1)}, bf16[264,512]{1,0:T(8,128)(2,1)}, u32[]{:S(2)}, u32[]{:S(2)}) collective-permute-start(bf16[264,512]{1,0:T(8,128)(2,1)} %collective-permute-done.5.refs_5_), channel_id=1, source_target_pairs={{0,2},{1,3},{2,0},{3,1},{4,6},{5,7},{6,4},{7,5},{8,10},{9,11},{10,... | collective-permute-start | bytes 811016 | tf_op jit(solution)/shard_map/ppermute | solution.py:26
  63.8 19.0 %collective-permute-start.12 = (bf16[264,512]{1,0:T(8,128)(2,1)}, bf16[264,512]{1,0:T(8,128)(2,1)}, u32[]{:S(2)}, u32[]{:S(2)}) collective-permute-start(bf16[264,512]{1,0:T(8,128)(2,1)} %collective-permute-done.10.refs_1_), channel_id=1, source_target_pairs={{0,2},{1,3},{2,0},{3,1},{4,6},{5,7},{6,4},{7,5},{8,10},{9,11},{10,... | collective-permute-start | bytes 811016 | tf_op jit(solution)/shard_map/ppermute | solution.py:26
  71.5 1.4 %copy-start = (bf16[1,384,2048]{2,1,0:T(8,128)(2,1)S(1)}, bf16[1,384,2048]{2,1,0:T(8,128)(2,1)}, u32[]{:S(2)}) copy-start(bf16[1,384,2048]{2,1,0:T(8,128)(2,1)} %all-gather.3.cloned.1.call-done) | copy-start | bytes 4718596
  82.3 9.5 %collective-permute-start.14 = (bf16[264,512]{1,0:T(8,128)(2,1)S(1)}, bf16[264,512]{1,0:T(8,128)(2,1)S(1)}, u32[]{:S(2)}, u32[]{:S(2)}) collective-permute-start(bf16[264,512]{1,0:T(8,128)(2,1)S(1)} %get-tuple-element.47), channel_id=1, source_target_pairs={{0,2},{1,3},{2,0},{3,1},{4,6},{5,7},{6,4},{7,5},{8,10},{9,11},{10,... | collective-permute-start | bytes 811016 | tf_op jit(solution)/shard_map/ppermute | solution.py:26
  86.3 21.4 %copy-start.4 = (bf16[1,128,2048]{2,1,0:T(8,128)(2,1)S(1)}, bf16[1,128,2048]{2,1,0:T(8,128)(2,1)}, u32[]{:S(2)}) copy-start(bf16[1,128,2048]{2,1,0:T(8,128)(2,1)} %param.12) | copy-start | bytes 1572868
  86.3 21.4 %copy-start.7 = (bf16[128,2048]{1,0:T(8,128)(2,1)S(1)}, bf16[128,2048]{1,0:T(8,128)(2,1)}, u32[]{:S(2)}) copy-start(bf16[128,2048]{1,0:T(8,128)(2,1)} %copy-done.5) | copy-start | bytes 1572868
  86.3 21.4 %copy-start.20 = (f32[1,2048]{1,0:T(1,128)S(1)}, f32[1,2048]{1,0:T(1,128)}, u32[]{:S(2)}) copy-start(f32[1,2048]{1,0:T(1,128)} %gain_ref.5) | copy-start | bytes 24580
  86.3 21.4 %copy-start.23 = (s32[1,128,1]{1,2,0:T(1,128)S(1)}, s32[1,128,1]{1,2,0:T(1,128)}, u32[]{:S(2)}) copy-start(s32[1,128,1]{1,2,0:T(1,128)} %param.20) | copy-start | bytes 1540
  86.4 21.4 %copy-start.27 = (f32[1,128,1]{1,2,0:T(1,128)S(1)}, f32[1,128,1]{1,2,0:T(1,128)}, u32[]{:S(2)}) copy-start(f32[1,128,1]{1,2,0:T(1,128)} %param.21) | copy-start | bytes 1540
  86.4 17.0 %collective-permute-start.13 = (bf16[264,512]{1,0:T(8,128)(2,1)S(1)}, bf16[264,512]{1,0:T(8,128)(2,1)S(1)}, u32[]{:S(2)}, u32[]{:S(2)}) collective-permute-start(bf16[264,512]{1,0:T(8,128)(2,1)S(1)} %get-tuple-element.44), channel_id=1, source_target_pairs={{0,2},{1,3},{2,0},{3,1},{4,6},{5,7},{6,4},{7,5},{8,10},{9,11},{10,... | collective-permute-start | bytes 811016 | tf_op jit(solution)/shard_map/ppermute | solution.py:26
  91.9 15.8 %collective-permute-start.15 = (bf16[264,512]{1,0:T(8,128)(2,1)S(1)}, bf16[264,512]{1,0:T(8,128)(2,1)S(1)}, u32[]{:S(2)}, u32[]{:S(2)}) collective-permute-start(bf16[264,512]{1,0:T(8,128)(2,1)S(1)} %get-tuple-element.48), channel_id=1, source_target_pairs={{0,2},{1,3},{2,0},{3,1},{4,6},{5,7},{6,4},{7,5},{8,10},{9,11},{10,... | collective-permute-start | bytes 811016 | tf_op jit(solution)/shard_map/ppermute | solution.py:26
  92.0 15.8 %collective-permute-start.18 = (bf16[264,512]{1,0:T(8,128)(2,1)S(1)}, bf16[264,512]{1,0:T(8,128)(2,1)S(1)}, u32[]{:S(2)}, u32[]{:S(2)}) collective-permute-start(bf16[264,512]{1,0:T(8,128)(2,1)S(1)} %add_convert_fusion), channel_id=1, source_target_pairs={{0,4},{1,5},{2,6},{3,7},{4,0},{5,1},{6,2},{7,3},{8,12},{9,13},{10,... | collective-permute-start | bytes 811016 | tf_op jit(solution)/shard_map/ppermute | solution.py:21
  103.5 16.8 %copy-start.25 = (s32[1,128,1]{1,2,0:T(1,128)S(1)}, s32[1,128,1]{1,2,0:T(1,128)}, u32[]{:S(2)}) copy-start(s32[1,128,1]{1,2,0:T(1,128)} %param.18) | copy-start | bytes 1540
  103.5 16.8 %copy-start.26 = (f32[1,128,1]{1,2,0:T(1,128)S(1)}, f32[1,128,1]{1,2,0:T(1,128)}, u32[]{:S(2)}) copy-start(f32[1,128,1]{1,2,0:T(1,128)} %param.19) | copy-start | bytes 1540
  103.5 15.6 %collective-permute-start.17 = (bf16[264,512]{1,0:T(8,128)(2,1)S(1)}, bf16[264,512]{1,0:T(8,128)(2,1)S(1)}, u32[]{:S(2)}, u32[]{:S(2)}) collective-permute-start(bf16[264,512]{1,0:T(8,128)(2,1)S(1)} %add_convert_fusion.1), channel_id=1, source_target_pairs={{0,4},{1,5},{2,6},{3,7},{4,0},{5,1},{6,2},{7,3},{8,12},{9,13},{10,... | collective-permute-start | bytes 811016 | tf_op jit(solution)/shard_map/ppermute | solution.py:21
  107.7 12.6 %collective-permute-start.16 = (bf16[264,512]{1,0:T(8,128)(2,1)S(1)}, bf16[264,512]{1,0:T(8,128)(2,1)S(1)}, u32[]{:S(2)}, u32[]{:S(2)}) collective-permute-start(bf16[264,512]{1,0:T(8,128)(2,1)S(1)} %get-tuple-element.49), channel_id=1, source_target_pairs={{0,2},{1,3},{2,0},{3,1},{4,6},{5,7},{6,4},{7,5},{8,10},{9,11},{10,... | collective-permute-start | bytes 811016 | tf_op jit(solution)/shard_map/ppermute | solution.py:26
  (16 other events, 12.5 us)
Sparse Core Ops, SparseCore 0:
  9.6 46.6 all-gather.2

commit v8 on v4

--- a/solution.py
+++ b/solution.py
@@ -97,16 +97,24 @@
     pack(normed(x_ref, gain_ref), own_ref, routes_ref, outs)
 
 
-def first_body(own_ref, routes_ref, gain_ref, x_ref, *refs):
-    parts, joined, outs, sems = refs[:3], refs[3], refs[4:-1], refs[-1]
+def first_body(own_ref, *refs):
+    args, parts, joined = refs[:3], refs[3:6], refs[6]
+    outs, held, stage, sems = refs[7:-5], refs[-5:-2], refs[-2], refs[-1]
     units = parts[0].shape[0]
-    copies = [
-        pltpu.make_async_copy(part, joined.at[pl.ds(i * units, units), :], sems.at[i]) for i, part in enumerate(parts)
-    ]
-    for copy in copies:
+    rows = [pl.ds(i * units, units) for i in range(3)]
+    fetch = [pltpu.make_async_copy(arg, to, sems.at[i]) for i, (arg, to) in enumerate(zip(args, held))]
+    load = [pltpu.make_async_copy(part, stage.at[rows[i], :], sems.at[3 + i]) for i, part in enumerate(parts)]
+    store = [pltpu.make_async_copy(stage.at[rows[i], :], joined.at[rows[i], :], sems.at[6 + i]) for i in range(3)]
+    for copy in fetch + load:
         copy.start()
+    for copy in fetch:
+        copy.wait()
+    routes_ref, gain_ref, x_ref = held
     pack(normed(x_ref, gain_ref), own_ref, routes_ref, outs)
-    for copy in copies:
+    for i in range(3):
+        load[i].wait()
+        store[i].start()
+    for copy in store:
         copy.wait()
 
 
@@ -128,31 +136,31 @@
         ref[...] = jnp.concatenate(pieces, axis=0).astype(ref.dtype)
 
 
-def third(shares, i):
-    units = shares[0].shape[0] // 3
-    return jnp.concatenate([share[pl.ds(i * units, units), :] for share in shares], axis=0)
+def joined(shares, i):
+    units = shares[i].shape[0]
+    return jnp.concatenate([shares[i][...], shares[3][pl.ds(i * units, units), :]], axis=0)
 
 
 def forward_body(count, rows, *refs):
-    row_refs, shares, outs, wide_ref = refs[:count], refs[count:count + 2], refs[count + 2:-1], refs[-1]
+    row_refs, shares, outs, wide_ref = refs[:count], refs[count:count + 4], refs[count + 4:-1], refs[-1]
     x = unpack(row_refs, wide_ref, rows)
-    gate_pre = lax.dot_general(x, third(shares, 0), CONTRACT, preferred_element_type=F32)
-    up_pre = lax.dot_general(x, third(shares, 1), CONTRACT, preferred_element_type=F32)
+    gate_pre = lax.dot_general(x, joined(shares, 0), CONTRACT, preferred_element_type=F32)
+    up_pre = lax.dot_general(x, joined(shares, 1), CONTRACT, preferred_element_type=F32)
     hidden = (silu_parts(gate_pre)[0] * up_pre).astype(BF16)
-    total = jnp.dot(hidden, third(shares, 2), preferred_element_type=F32)
+    total = jnp.dot(hidden, joined(shares, 2), preferred_element_type=F32)
     spread_out(total, outs, x.shape[0] // count, rows)
 
 
 def backward_body(count, rows, *refs):
-    row_refs, grad_refs, shares = refs[:count], refs[count:2 * count], refs[2 * count:2 * count + 2]
-    outs, wide_ref, grad_wide_ref = refs[2 * count + 2:-2], refs[-2], refs[-1]
+    row_refs, grad_refs, shares = refs[:count], refs[count:2 * count], refs[2 * count:2 * count + 4]
+    outs, wide_ref, grad_wide_ref = refs[2 * count + 4:-2], refs[-2], refs[-1]
     x = unpack(row_refs, wide_ref, rows)
-    gate, up = third(shares, 0), third(shares, 1)
+    gate, up = joined(shares, 0), joined(shares, 1)
     gate_pre = lax.dot_general(x, gate, CONTRACT, preferred_element_type=F32)
     up_pre = lax.dot_general(x, up, CONTRACT, preferred_element_type=F32)
     activation, derivative = silu_parts(gate_pre)
     grads = unpack(grad_refs, grad_wide_ref, rows)
-    d_hidden = lax.dot_general(grads, third(shares, 2), CONTRACT, preferred_element_type=F32)
+    d_hidden = lax.dot_general(grads, joined(shares, 2), CONTRACT, preferred_element_type=F32)
     d_gate = (d_hidden * up_pre * derivative).astype(BF16)
     d_up = (d_hidden * activation).astype(BF16)
     total = jnp.dot(d_gate, gate, preferred_element_type=F32) + jnp.dot(d_up, up, preferred_element_type=F32)
@@ -224,6 +232,7 @@
     pitch = -(-rows // 16) * 16
     scalar = pl.BlockSpec(memory_space=pltpu.SMEM)
     whole = pl.BlockSpec(memory_space=pltpu.VMEM)
+    anywhere = pl.BlockSpec(memory_space=pl.ANY)
 
     shape = (pieces * rows, width // pieces)
     packed = [jax.ShapeDtypeStruct(shape, BF16)] * experts
@@ -241,12 +250,19 @@
     own_share, *packed_b = local_call(
         first_body,
         [jax.ShapeDtypeStruct((3 * w_down.shape[1], width), BF16)] + packed,
-        in_specs=[scalar] + [whole] * 3 + [pl.BlockSpec(memory_space=pltpu.HBM)] * 3,
-        out_specs=[pl.BlockSpec(memory_space=pl.ANY)] + [whole] * experts,
-        scratch=[pltpu.SemaphoreType.DMA((3,))],
+        in_specs=[scalar] + [anywhere] * 6,
+        out_specs=[anywhere] + [whole] * experts,
+        scratch=[
+            pltpu.VMEM((1, tok_count), jnp.int32),
+            pltpu.VMEM((1, width), F32),
+            pltpu.VMEM((tok_count, width), BF16),
+            pltpu.VMEM((3 * w_down.shape[1], width), BF16),
+            pltpu.SemaphoreType.DMA((9,)),
+        ],
+        vmem_mib=56,
         name="join_weights_pack_saved",
     )(own, r_bwd, norm_gain, saved_in[0], w_gate[0].T, w_up[0].T, w_down[0])
-    shares = (own_share, swapped(own_share, "expert", 1))
+    shares = (w_gate[0].T, w_up[0].T, w_down[0], swapped(own_share, "expert", 1))
 
     rows_b = crossed(packed_b)
     swap_b = partners(rows_b[:1])
@@ -282,7 +298,7 @@
     totals_b, home_b = crossing_home(partial_b)
     totals_f, home_f = crossing_home(partial_f)
     back_b = [partial_b[0]] + partners(partial_b[experts:experts + 1], *totals_b) + home_b
-    back_f = [partial_f[0]] + partners(partial_f[experts:experts + 1], *totals_f) + home_f
+    back_f = [partial_f[0]] + partners(partial_f[experts:experts + 1], *totals_f, back_b[1]) + home_f
 
     grad_out = local_call(
         functools.partial(backward_home_body, experts, rows),

time: 107 us -> 106 us (level)
  local copies, waits for them, and re-layouts: 5.82 us -> 0.99 us
  Pallas kernels: 12.6 us -> 15.8 us
  starting transfers between devices: 27.1 us -> 29.2 us
  waiting for transfers between devices: 60.2 us -> 58.6 us
    ppermute x11, waiting for transfers between devices: 44 us -> 37.9 us  [swapped(): return lax.ppermute(value, axis, [(i, i ^ bit) for i in range(count)])]
    ppermute x7, starting transfers between devices: 12.6 us -> 17.9 us  [shifted(): lax.ppermute(value, axis, [(i, (i + steps) % count) for i in range(count)])]
    unnamed x28 -> x22, local copies, waits for them, and re-layouts: 5.82 us -> 0.99 us
    ppermute x7, waiting for transfers between devices: 16.2 us -> 20.7 us  [shifted(): lax.ppermute(value, axis, [(i, (i + steps) % count) for i in range(count)])]
    pallas_call x1, Pallas kernels: 1.1 us -> 4.43 us  [per_device(): local_call(first_body, [jax.ShapeDtypeStruct((3 * w_down.shape[1], width)...]
    ppermute x11, starting transfers between devices: 14.5 us -> 11.3 us  [swapped(): return lax.ppermute(value, axis, [(i, i ^ bit) for i in range(count)])]
  transfers between devices with their start and end apart: 18 -> 18, of which waited for: 12 -> 14; matrix products, arithmetic and copies ran while one was open for 0% -> 0% of each run, Pallas kernels for 9% -> 9%
where the time goes in v8:
time: 106 us
  waiting for transfers between devices  58.6 us (55%)
  starting transfers between devices  29.2 us (28%)
  Pallas kernels  15.8 us (15%)
    ppermute x11, waiting for transfers between devices, swapped(): return lax.ppermute(value, axis, [(i, i ^ bit) for i in range(count)])  37.9 us
    ppermute x7, waiting for transfers between devices, shifted(): lax.ppermute(value, axis, [(i, (i + steps) % count) for i in range(count)])  20.7 us
    ppermute x7, starting transfers between devices, shifted(): lax.ppermute(value, axis, [(i, (i + steps) % count) for i in range(count)])  17.9 us
    ppermute x11, starting transfers between devices, swapped(): return lax.ppermute(value, axis, [(i, i ^ bit) for i in range(count)])  11.3 us
    pallas_call x1, Pallas kernels, per_device(): local_call(first_body, [jax.ShapeDtypeStruct((3 * w_down.shape[1], width)...  4.43 us
    pallas_call x1, Pallas kernels, per_device(): local_call(functools.partial(backward_body, count, rows), partial, scratc...  3.63 us
    pallas_call x1, Pallas kernels, per_device(): local_call(functools.partial(forward_body, count, rows), partial, scratch...  2.25 us
  transfers between devices with their start and end apart: 18, of which 14 were waited for; matrix products, arithmetic and copies ran while one was open for 0% of the time, Pallas kernels for 9%

profile of v8, /device:TPU:0, one launch (start us, length us, event | category | flops | bytes accessed | tf_op | source)
XLA Modules:
  0.0 105.6 jit_solution(10035232757924440027)
XLA Ops:
  0.7 4.4 %join_weights_pack_saved.1 = (bf16[576,2048]{1,0:T(8,128)(2,1)}, bf16[264,512]{1,0:T(8,128)(2,1)}, bf16[264,512]{1,0:T(8,128)(2,1)}) custom-call(s32[1]{0:T(128)} %bitcast.own_ref, s32[1,128]{1,0:T(1,128)} %bitcast.28, f32[1,2048]{1,0:T(1,128)} %gain_ref.3, bf16[128,2048]{1,0:T(8,128)(2,1)} %bitcast.26, bf16[192,2048]{1,0:T(8,128)(2,1)} %bitcast.17, ...), custom_call_target="tpu_custom_call" | custom-call | flops 1000 | bytes 1000 | tf_op jit(solution)/shard_map/join_weights_pack_saved/pallas_call | solution.py:250
  5.2 3.0 %collective-permute-start.8 = (bf16[576,2048]{1,0:T(8,128)(2,1)}, bf16[576,2048]{1,0:T(8,128)(2,1)S(1)}, u32[]{:S(2)}, u32[]{:S(2)}) collective-permute-start(bf16[576,2048]{1,0:T(8,128)(2,1)} %get-tuple-element.37), channel_id=1, source_target_pairs={{0,1},{1,0},{2,3},{3,2},{4,5},{5,4},{6,7},{7,6},{8,9},{9,8},{10,11... | collective-permute-start | bytes 7077896 | tf_op jit(solution)/shard_map/ppermute | solution.py:26
  8.9 2.6 %collective-permute-start.2 = (bf16[264,512]{1,0:T(8,128)(2,1)}, bf16[264,512]{1,0:T(8,128)(2,1)S(1)}, u32[]{:S(2)}, u32[]{:S(2)}) collective-permute-start(bf16[264,512]{1,0:T(8,128)(2,1)} %get-tuple-element.30), channel_id=1, source_target_pairs={{0,4},{1,5},{2,6},{3,7},{4,0},{5,1},{6,2},{7,3},{8,12},{9,13},{10,... | collective-permute-start | bytes 811016 | tf_op jit(solution)/shard_map/ppermute | solution.py:21
  11.4 1.6 %collective-permute-start.3 = (bf16[264,512]{1,0:T(8,128)(2,1)}, bf16[264,512]{1,0:T(8,128)(2,1)S(1)}, u32[]{:S(2)}, u32[]{:S(2)}) collective-permute-start(bf16[264,512]{1,0:T(8,128)(2,1)} %get-tuple-element.27.refs_0_), channel_id=1, source_target_pairs={{0,2},{1,3},{2,0},{3,1},{4,6},{5,7},{6,4},{7,5},{8,10},{9,11},{10,... | collective-permute-start | bytes 811016 | tf_op jit(solution)/shard_map/ppermute | solution.py:26
  13.0 5.0 %collective-permute-done.1.x_ref.up_ref = bf16[128,2048]{1,0:T(8,128)(2,1)S(1)} collective-permute-done((bf16[128,2048]{1,0:T(8,128)(2,1)S(1)}, bf16[128,2048]{1,0:T(8,128)(2,1)S(1)}, u32[]{:S(2)}, u32[]{:S(2)}) %collective-permute-start.1) | collective-permute-done | bytes 524320 | tf_op jit(solution)/shard_map/ppermute | solution.py:21
  18.9 5.0 %collective-permute-start.5 = (bf16[264,512]{1,0:T(8,128)(2,1)S(1)}, bf16[264,512]{1,0:T(8,128)(2,1)S(1)}, u32[]{:S(2)}, u32[]{:S(2)}) collective-permute-start(bf16[264,512]{1,0:T(8,128)(2,1)S(1)} %get-tuple-element.34), channel_id=1, source_target_pairs={{0,4},{1,5},{2,6},{3,7},{4,0},{5,1},{6,2},{7,3},{8,12},{9,13},{10,... | collective-permute-start | bytes 811016 | tf_op jit(solution)/shard_map/ppermute | solution.py:21
  24.1 1.4 %collective-permute-start.6 = (bf16[264,512]{1,0:T(8,128)(2,1)S(1)}, bf16[264,512]{1,0:T(8,128)(2,1)S(1)}, u32[]{:S(2)}, u32[]{:S(2)}) collective-permute-start(bf16[264,512]{1,0:T(8,128)(2,1)S(1)} %get-tuple-element.35.refs_4_), channel_id=1, source_target_pairs={{0,2},{1,3},{2,0},{3,1},{4,6},{5,7},{6,4},{7,5},{8,10},{9,11},{10,... | collective-permute-start | bytes 811016 | tf_op jit(solution)/shard_map/ppermute | solution.py:26
  25.5 1.3 %collective-permute-done.3.refs_2_ = bf16[264,512]{1,0:T(8,128)(2,1)S(1)} collective-permute-done((bf16[264,512]{1,0:T(8,128)(2,1)}, bf16[264,512]{1,0:T(8,128)(2,1)S(1)}, u32[]{:S(2)}, u32[]{:S(2)}) %collective-permute-start.3) | collective-permute-done | bytes 270368 | tf_op jit(solution)/shard_map/ppermute | solution.py:26
  27.7 2.0 %collective-permute-start.9 = (bf16[264,512]{1,0:T(8,128)(2,1)S(1)}, bf16[264,512]{1,0:T(8,128)(2,1)S(1)}, u32[]{:S(2)}, u32[]{:S(2)}) collective-permute-start(bf16[264,512]{1,0:T(8,128)(2,1)S(1)} %get-tuple-element.40), channel_id=1, source_target_pairs={{0,4},{1,5},{2,6},{3,7},{4,0},{5,1},{6,2},{7,3},{8,12},{9,13},{10,... | collective-permute-start | bytes 811016 | tf_op jit(solution)/shard_map/ppermute | solution.py:21
  29.6 7.2 %collective-permute-done.5.refs_5_ = bf16[264,512]{1,0:T(8,128)(2,1)S(1)} collective-permute-done((bf16[264,512]{1,0:T(8,128)(2,1)S(1)}, bf16[264,512]{1,0:T(8,128)(2,1)S(1)}, u32[]{:S(2)}, u32[]{:S(2)}) %collective-permute-start.5) | collective-permute-done | bytes 270368 | tf_op jit(solution)/shard_map/ppermute | solution.py:21
  36.8 1.2 %collective-permute-start.10 = (bf16[264,512]{1,0:T(8,128)(2,1)S(1)}, bf16[264,512]{1,0:T(8,128)(2,1)S(1)}, u32[]{:S(2)}, u32[]{:S(2)}) collective-permute-start(bf16[264,512]{1,0:T(8,128)(2,1)S(1)} %get-tuple-element.41.refs_0_), channel_id=1, source_target_pairs={{0,2},{1,3},{2,0},{3,1},{4,6},{5,7},{6,4},{7,5},{8,10},{9,11},{10,... | collective-permute-start | bytes 811016 | tf_op jit(solution)/shard_map/ppermute | solution.py:26
  38.1 5.8 %collective-permute-done.6.refs_6_ = bf16[264,512]{1,0:T(8,128)(2,1)S(1)} collective-permute-done((bf16[264,512]{1,0:T(8,128)(2,1)S(1)}, bf16[264,512]{1,0:T(8,128)(2,1)S(1)}, u32[]{:S(2)}, u32[]{:S(2)}) %collective-permute-start.6) | collective-permute-done | bytes 270368 | tf_op jit(solution)/shard_map/ppermute | solution.py:26
  43.9 5.8 %collective-permute-done.4.refs_3_ = bf16[264,512]{1,0:T(8,128)(2,1)S(1)} collective-permute-done((bf16[264,512]{1,0:T(8,128)(2,1)S(1)}, bf16[264,512]{1,0:T(8,128)(2,1)S(1)}, u32[]{:S(2)}, u32[]{:S(2)}) %collective-permute-start.4) | collective-permute-done | bytes 270368 | tf_op jit(solution)/shard_map/ppermute | solution.py:26
  49.7 5.8 %collective-permute-done.10.refs_2_ = bf16[264,512]{1,0:T(8,128)(2,1)S(1)} collective-permute-done((bf16[264,512]{1,0:T(8,128)(2,1)S(1)}, bf16[264,512]{1,0:T(8,128)(2,1)S(1)}, u32[]{:S(2)}, u32[]{:S(2)}) %collective-permute-start.10) | collective-permute-done | bytes 270368 | tf_op jit(solution)/shard_map/ppermute | solution.py:26
  55.4 1.0 collective-permute-start.11
  56.4 4.8 %collective-permute-done.7.refs_7_ = bf16[264,512]{1,0:T(8,128)(2,1)S(1)} collective-permute-done((bf16[264,512]{1,0:T(8,128)(2,1)S(1)}, bf16[264,512]{1,0:T(8,128)(2,1)S(1)}, u32[]{:S(2)}, u32[]{:S(2)}) %collective-permute-start.7) | collective-permute-done | bytes 270368 | tf_op jit(solution)/shard_map/ppermute | solution.py:26
  61.3 0.9 copy-done.4
  62.2 3.6 %experts_bwd.1 = (f32[264,512]{1,0:T(8,128)S(1)}, f32[264,512]{1,0:T(8,128)S(1)}, bf16[264,512]{1,0:T(8,128)(2,1)S(1)}, bf16[264,512]{1,0:T(8,128)(2,1)S(1)}) custom-call(bf16[264,512]{1,0:T(8,128)(2,1)S(1)} %copy-done.4, bf16[264,512]{1,0:T(8,128)(2,1)S(1)} %collective-permute-done.2.refs_1_, bf16[264,512]{1,0:T(8,128)(2,1)S(1)} %collective-permute-done.3.refs_2_, ...), custom_call_target="tpu_custom_call" | custom-call | flops 1000 | bytes 1000 | tf_op jit(solution)/shard_map/experts_bwd/pallas_call | solution.py:292
  65.9 1.0 collective-permute-start.13
  66.9 2.3 %experts_fwd.1 = (f32[264,512]{1,0:T(8,128)S(1)}, f32[264,512]{1,0:T(8,128)S(1)}, bf16[264,512]{1,0:T(8,128)(2,1)S(1)}, bf16[264,512]{1,0:T(8,128)(2,1)S(1)}) custom-call(bf16[264,512]{1,0:T(8,128)(2,1)S(1)} %get-tuple-element.41.refs_0_, bf16[264,512]{1,0:T(8,128)(2,1)S(1)} %collective-permute-done.9.refs_1_, ...), custom_call_target="tpu_custom_call" | custom-call | flops 1000 | bytes 1000 | tf_op jit(solution)/shard_map/experts_fwd/pallas_call | solution.py:295
  69.2 1.2 %collective-permute-start.12 = (bf16[264,512]{1,0:T(8,128)(2,1)S(1)}, bf16[264,512]{1,0:T(8,128)(2,1)S(1)}, u32[]{:S(2)}, u32[]{:S(2)}) collective-permute-start(bf16[264,512]{1,0:T(8,128)(2,1)S(1)} %get-tuple-element.46), channel_id=1, source_target_pairs={{0,2},{1,3},{2,0},{3,1},{4,6},{5,7},{6,4},{7,5},{8,10},{9,11},{10,... | collective-permute-start | bytes 811016 | tf_op jit(solution)/shard_map/ppermute | solution.py:26
  70.3 5.0 %collective-permute-done.13 = bf16[264,512]{1,0:T(8,128)(2,1)S(1)} collective-permute-done((bf16[264,512]{1,0:T(8,128)(2,1)S(1)}, bf16[264,512]{1,0:T(8,128)(2,1)S(1)}, u32[]{:S(2)}, u32[]{:S(2)}) %collective-permute-start.13) | collective-permute-done | bytes 270368 | tf_op jit(solution)/shard_map/ppermute | solution.py:26
  75.4 0.9 collective-permute-start.14
  76.3 6.6 %collective-permute-start.17 = (bf16[264,512]{1,0:T(8,128)(2,1)S(1)}, bf16[264,512]{1,0:T(8,128)(2,1)S(1)}, u32[]{:S(2)}, u32[]{:S(2)}) collective-permute-start(bf16[264,512]{1,0:T(8,128)(2,1)S(1)} %add_convert_fusion), channel_id=1, source_target_pairs={{0,4},{1,5},{2,6},{3,7},{4,0},{5,1},{6,2},{7,3},{8,12},{9,13},{10,... | collective-permute-start | bytes 811016 | tf_op jit(solution)/shard_map/ppermute | solution.py:21
  83.0 3.9 %collective-permute-done.12 = bf16[264,512]{1,0:T(8,128)(2,1)S(1)} collective-permute-done((bf16[264,512]{1,0:T(8,128)(2,1)S(1)}, bf16[264,512]{1,0:T(8,128)(2,1)S(1)}, u32[]{:S(2)}, u32[]{:S(2)}) %collective-permute-start.12) | collective-permute-done | bytes 270368 | tf_op jit(solution)/shard_map/ppermute | solution.py:26
  87.0 1.1 %collective-permute-start.16 = (bf16[264,512]{1,0:T(8,128)(2,1)S(1)}, bf16[264,512]{1,0:T(8,128)(2,1)S(1)}, u32[]{:S(2)}, u32[]{:S(2)}) collective-permute-start(bf16[264,512]{1,0:T(8,128)(2,1)S(1)} %add_convert_fusion.1), channel_id=1, source_target_pairs={{0,4},{1,5},{2,6},{3,7},{4,0},{5,1},{6,2},{7,3},{8,12},{9,13},{10,... | collective-permute-start | bytes 811016 | tf_op jit(solution)/shard_map/ppermute | solution.py:21
  88.0 4.6 %collective-permute-done.14.refs_1_ = bf16[264,512]{1,0:T(8,128)(2,1)S(1)} collective-permute-done((bf16[264,512]{1,0:T(8,128)(2,1)S(1)}, bf16[264,512]{1,0:T(8,128)(2,1)S(1)}, u32[]{:S(2)}, u32[]{:S(2)}) %collective-permute-start.14) | collective-permute-done | bytes 270368 | tf_op jit(solution)/shard_map/ppermute | solution.py:26
  92.6 5.8 %collective-permute-done.17.refs_2_ = bf16[264,512]{1,0:T(8,128)(2,1)S(1)} collective-permute-done((bf16[264,512]{1,0:T(8,128)(2,1)S(1)}, bf16[264,512]{1,0:T(8,128)(2,1)S(1)}, u32[]{:S(2)}, u32[]{:S(2)}) %collective-permute-start.17) | collective-permute-done | bytes 270368 | tf_op jit(solution)/shard_map/ppermute | solution.py:21
  98.4 2.0 %home_bwd.1 = bf16[128,2048]{1,0:T(8,128)(2,1)} custom-call(s32[1]{0:T(128)} %bitcast.own_ref, s32[1,128]{1,0:T(1,128)S(1)} %bitcast.30, f32[1,128]{1,0:T(1,128)S(1)} %bitcast.34, f32[1,2048]{1,0:T(1,128)S(1)} %copy-done.5, bf16[128,2048]{1,0:T(8,128)(2,1)S(1)} %bitcast.27, bf16[128,2048]{1,0:T(8,128)(2,1)S(1)} %collective-permute-done.1.x_ref.up_ref, ...), custom_call_target="tpu_custom_call" | custom-call | flops 1000 | bytes 1000 | tf_op jit(solution)/shard_map/home_bwd/pallas_call | solution.py:303
  100.4 2.5 %collective-permute-done.16.refs_2_ = bf16[264,512]{1,0:T(8,128)(2,1)S(1)} collective-permute-done((bf16[264,512]{1,0:T(8,128)(2,1)S(1)}, bf16[264,512]{1,0:T(8,128)(2,1)S(1)}, u32[]{:S(2)}, u32[]{:S(2)}) %collective-permute-start.16) | collective-permute-done | bytes 270368 | tf_op jit(solution)/shard_map/ppermute | solution.py:21
  102.9 1.0 collective-permute-done.15.refs_1_
  103.9 1.7 %home_fwd.1 = bf16[128,2048]{1,0:T(8,128)(2,1)} custom-call(s32[1]{0:T(128)} %bitcast.own_ref, s32[1,128]{1,0:T(1,128)S(1)} %bitcast.32, f32[1,128]{1,0:T(1,128)S(1)} %bitcast.33, bf16[128,2048]{1,0:T(8,128)(2,1)S(1)} %collective-permute-done.x_ref, f32[264,512]{1,0:T(8,128)S(1)} %get-tuple-element.43.refs_0_, ...), custom_call_target="tpu_custom_call" | custom-call | flops 1000 | bytes 1000 | tf_op jit(solution)/shard_map/home_fwd/pallas_call | solution.py:310
  (35 shorter events, 2.9 us)
Async XLA Ops:
  0.6 60.6 %copy-start.1 = (bf16[1,2048,192]{1,2,0:T(8,128)(2,1)S(1)}, bf16[1,2048,192]{1,2,0:T(8,128)(2,1)}, u32[]{:S(2)}) copy-start(bf16[1,2048,192]{1,2,0:T(8,128)(2,1)} %param.16) | copy-start | bytes 2359300
  0.6 60.6 %copy-start.2 = (bf16[1,192,2048]{2,1,0:T(8,128)(2,1)S(1)}, bf16[1,192,2048]{2,1,0:T(8,128)(2,1)}, u32[]{:S(2)}) copy-start(bf16[1,192,2048]{2,1,0:T(8,128)(2,1)} %param.17) | copy-start | bytes 2359300
  0.7 17.4 %copy-start.6 = (s32[1,128,1]{1,2,0:T(1,128)S(1)}, s32[1,128,1]{1,2,0:T(1,128)}, u32[]{:S(2)}) copy-start(s32[1,128,1]{1,2,0:T(1,128)} %param.20) | copy-start | bytes 1540
  0.7 60.6 %copy-start = (bf16[1,2048,192]{1,2,0:T(8,128)(2,1)S(1)}, bf16[1,2048,192]{1,2,0:T(8,128)(2,1)}, u32[]{:S(2)}) copy-start(bf16[1,2048,192]{1,2,0:T(8,128)(2,1)} %param.15) | copy-start | bytes 2359300
  0.7 26.1 %copy-start.5 = (f32[1,2048]{1,0:T(1,128)S(1)}, f32[1,2048]{1,0:T(1,128)}, u32[]{:S(2)}) copy-start(f32[1,2048]{1,0:T(1,128)} %gain_ref.3) | copy-start | bytes 24580
  0.7 7.5 %copy-start.10 = (bf16[1,128,2048]{2,1,0:T(8,128)(2,1)S(1)}, bf16[1,128,2048]{2,1,0:T(8,128)(2,1)}, u32[]{:S(2)}) copy-start(bf16[1,128,2048]{2,1,0:T(8,128)(2,1)} %param.13) | copy-start | bytes 1572868
  0.7 26.1 %copy-start.7 = (s32[1,128,1]{1,2,0:T(1,128)S(1)}, s32[1,128,1]{1,2,0:T(1,128)}, u32[]{:S(2)}) copy-start(s32[1,128,1]{1,2,0:T(1,128)} %param.18) | copy-start | bytes 1540
  5.2 56.1 %collective-permute-start.8 = (bf16[576,2048]{1,0:T(8,128)(2,1)}, bf16[576,2048]{1,0:T(8,128)(2,1)S(1)}, u32[]{:S(2)}, u32[]{:S(2)}) collective-permute-start(bf16[576,2048]{1,0:T(8,128)(2,1)} %get-tuple-element.37), channel_id=1, source_target_pairs={{0,1},{1,0},{2,3},{3,2},{4,5},{5,4},{6,7},{7,6},{8,9},{9,8},{10,11... | collective-permute-start | bytes 7077896 | tf_op jit(solution)/shard_map/ppermute | solution.py:26
  8.2 9.9 %collective-permute-start.1 = (bf16[128,2048]{1,0:T(8,128)(2,1)S(1)}, bf16[128,2048]{1,0:T(8,128)(2,1)S(1)}, u32[]{:S(2)}, u32[]{:S(2)}) collective-permute-start(bf16[128,2048]{1,0:T(8,128)(2,1)S(1)} %bitcast.37), channel_id=1, source_target_pairs={{0,24},{8,0},{16,8},{24,16},{1,25},{9,1},{17,9},{25,17},{2,26},{10... | collective-permute-start | bytes 1572872 | tf_op jit(solution)/shard_map/ppermute | solution.py:21
  8.9 15.2 %collective-permute-start.2 = (bf16[264,512]{1,0:T(8,128)(2,1)}, bf16[264,512]{1,0:T(8,128)(2,1)S(1)}, u32[]{:S(2)}, u32[]{:S(2)}) collective-permute-start(bf16[264,512]{1,0:T(8,128)(2,1)} %get-tuple-element.30), channel_id=1, source_target_pairs={{0,4},{1,5},{2,6},{3,7},{4,0},{5,1},{6,2},{7,3},{8,12},{9,13},{10,... | collective-permute-start | bytes 811016 | tf_op jit(solution)/shard_map/ppermute | solution.py:21
  11.4 15.3 %collective-permute-start = (bf16[128,2048]{1,0:T(8,128)(2,1)}, bf16[128,2048]{1,0:T(8,128)(2,1)S(1)}, u32[]{:S(2)}, u32[]{:S(2)}) collective-permute-start(bf16[128,2048]{1,0:T(8,128)(2,1)} %bitcast.38), channel_id=1, source_target_pairs={{0,8},{8,16},{16,24},{24,0},{1,9},{9,17},{17,25},{25,1},{2,10},{10... | collective-permute-start | bytes 1572872 | tf_op jit(solution)/shard_map/ppermute | solution.py:21
  11.4 15.3 %collective-permute-start.3 = (bf16[264,512]{1,0:T(8,128)(2,1)}, bf16[264,512]{1,0:T(8,128)(2,1)S(1)}, u32[]{:S(2)}, u32[]{:S(2)}) collective-permute-start(bf16[264,512]{1,0:T(8,128)(2,1)} %get-tuple-element.27.refs_0_), channel_id=1, source_target_pairs={{0,2},{1,3},{2,0},{3,1},{4,6},{5,7},{6,4},{7,5},{8,10},{9,11},{10,... | collective-permute-start | bytes 811016 | tf_op jit(solution)/shard_map/ppermute | solution.py:26
  18.9 17.9 %collective-permute-start.5 = (bf16[264,512]{1,0:T(8,128)(2,1)S(1)}, bf16[264,512]{1,0:T(8,128)(2,1)S(1)}, u32[]{:S(2)}, u32[]{:S(2)}) collective-permute-start(bf16[264,512]{1,0:T(8,128)(2,1)S(1)} %get-tuple-element.34), channel_id=1, source_target_pairs={{0,4},{1,5},{2,6},{3,7},{4,0},{5,1},{6,2},{7,3},{8,12},{9,13},{10,... | collective-permute-start | bytes 811016 | tf_op jit(solution)/shard_map/ppermute | solution.py:21
  24.1 19.8 %collective-permute-start.6 = (bf16[264,512]{1,0:T(8,128)(2,1)S(1)}, bf16[264,512]{1,0:T(8,128)(2,1)S(1)}, u32[]{:S(2)}, u32[]{:S(2)}) collective-permute-start(bf16[264,512]{1,0:T(8,128)(2,1)S(1)} %get-tuple-element.35.refs_4_), channel_id=1, source_target_pairs={{0,2},{1,3},{2,0},{3,1},{4,6},{5,7},{6,4},{7,5},{8,10},{9,11},{10,... | collective-permute-start | bytes 811016 | tf_op jit(solution)/shard_map/ppermute | solution.py:26
  26.7 22.9 %collective-permute-start.4 = (bf16[264,512]{1,0:T(8,128)(2,1)S(1)}, bf16[264,512]{1,0:T(8,128)(2,1)S(1)}, u32[]{:S(2)}, u32[]{:S(2)}) collective-permute-start(bf16[264,512]{1,0:T(8,128)(2,1)S(1)} %collective-permute-done.2.refs_1_), channel_id=1, source_target_pairs={{0,2},{1,3},{2,0},{3,1},{4,6},{5,7},{6,4},{7,5},{8,10},{9,11},{10,... | collective-permute-start | bytes 811016 | tf_op jit(solution)/shard_map/ppermute | solution.py:26
  27.7 22.0 %collective-permute-start.9 = (bf16[264,512]{1,0:T(8,128)(2,1)S(1)}, bf16[264,512]{1,0:T(8,128)(2,1)S(1)}, u32[]{:S(2)}, u32[]{:S(2)}) collective-permute-start(bf16[264,512]{1,0:T(8,128)(2,1)S(1)} %get-tuple-element.40), channel_id=1, source_target_pairs={{0,4},{1,5},{2,6},{3,7},{4,0},{5,1},{6,2},{7,3},{8,12},{9,13},{10,... | collective-permute-start | bytes 811016 | tf_op jit(solution)/shard_map/ppermute | solution.py:21
  36.8 18.6 %collective-permute-start.10 = (bf16[264,512]{1,0:T(8,128)(2,1)S(1)}, bf16[264,512]{1,0:T(8,128)(2,1)S(1)}, u32[]{:S(2)}, u32[]{:S(2)}) collective-permute-start(bf16[264,512]{1,0:T(8,128)(2,1)S(1)} %get-tuple-element.41.refs_0_), channel_id=1, source_target_pairs={{0,2},{1,3},{2,0},{3,1},{4,6},{5,7},{6,4},{7,5},{8,10},{9,11},{10,... | collective-permute-start | bytes 811016 | tf_op jit(solution)/shard_map/ppermute | solution.py:26
  43.9 17.4 %collective-permute-start.7 = (bf16[264,512]{1,0:T(8,128)(2,1)S(1)}, bf16[264,512]{1,0:T(8,128)(2,1)S(1)}, u32[]{:S(2)}, u32[]{:S(2)}) collective-permute-start(bf16[264,512]{1,0:T(8,128)(2,1)S(1)} %collective-permute-done.5.refs_5_), channel_id=1, source_target_pairs={{0,2},{1,3},{2,0},{3,1},{4,6},{5,7},{6,4},{7,5},{8,10},{9,11},{10,... | collective-permute-start | bytes 811016 | tf_op jit(solution)/shard_map/ppermute | solution.py:26
  55.4 11.4 %collective-permute-start.11 = (bf16[264,512]{1,0:T(8,128)(2,1)S(1)}, bf16[264,512]{1,0:T(8,128)(2,1)S(1)}, u32[]{:S(2)}, u32[]{:S(2)}) collective-permute-start(bf16[264,512]{1,0:T(8,128)(2,1)S(1)} %collective-permute-done.9.refs_1_), channel_id=1, source_target_pairs={{0,2},{1,3},{2,0},{3,1},{4,6},{5,7},{6,4},{7,5},{8,10},{9,11},{10,... | collective-permute-start | bytes 811016 | tf_op jit(solution)/shard_map/ppermute | solution.py:26
  61.3 1.0 copy-start.4
  65.9 9.5 %collective-permute-start.13 = (bf16[264,512]{1,0:T(8,128)(2,1)S(1)}, bf16[264,512]{1,0:T(8,128)(2,1)S(1)}, u32[]{:S(2)}, u32[]{:S(2)}) collective-permute-start(bf16[264,512]{1,0:T(8,128)(2,1)S(1)} %get-tuple-element.49), channel_id=1, source_target_pairs={{0,2},{1,3},{2,0},{3,1},{4,6},{5,7},{6,4},{7,5},{8,10},{9,11},{10,... | collective-permute-start | bytes 811016 | tf_op jit(solution)/shard_map/ppermute | solution.py:26
  66.9 31.5 %copy-start.9 = (f32[1,128,1]{1,2,0:T(1,128)S(1)}, f32[1,128,1]{1,2,0:T(1,128)}, u32[]{:S(2)}) copy-start(f32[1,128,1]{1,2,0:T(1,128)} %param.21) | copy-start | bytes 1540
  69.2 29.2 %copy-start.3 = (bf16[1,128,2048]{2,1,0:T(8,128)(2,1)S(1)}, bf16[1,128,2048]{2,1,0:T(8,128)(2,1)}, u32[]{:S(2)}) copy-start(bf16[1,128,2048]{2,1,0:T(8,128)(2,1)} %param.12) | copy-start | bytes 1572868
  69.2 17.7 %collective-permute-start.12 = (bf16[264,512]{1,0:T(8,128)(2,1)S(1)}, bf16[264,512]{1,0:T(8,128)(2,1)S(1)}, u32[]{:S(2)}, u32[]{:S(2)}) collective-permute-start(bf16[264,512]{1,0:T(8,128)(2,1)S(1)} %get-tuple-element.46), channel_id=1, source_target_pairs={{0,2},{1,3},{2,0},{3,1},{4,6},{5,7},{6,4},{7,5},{8,10},{9,11},{10,... | collective-permute-start | bytes 811016 | tf_op jit(solution)/shard_map/ppermute | solution.py:26
  75.3 28.6 %copy-start.8 = (f32[1,128,1]{1,2,0:T(1,128)S(1)}, f32[1,128,1]{1,2,0:T(1,128)}, u32[]{:S(2)}) copy-start(f32[1,128,1]{1,2,0:T(1,128)} %param.19) | copy-start | bytes 1540
  75.4 17.2 %collective-permute-start.14 = (bf16[264,512]{1,0:T(8,128)(2,1)S(1)}, bf16[264,512]{1,0:T(8,128)(2,1)S(1)}, u32[]{:S(2)}, u32[]{:S(2)}) collective-permute-start(bf16[264,512]{1,0:T(8,128)(2,1)S(1)} %get-tuple-element.50), channel_id=1, source_target_pairs={{0,2},{1,3},{2,0},{3,1},{4,6},{5,7},{6,4},{7,5},{8,10},{9,11},{10,... | collective-permute-start | bytes 811016 | tf_op jit(solution)/shard_map/ppermute | solution.py:26
  76.3 22.0 %collective-permute-start.17 = (bf16[264,512]{1,0:T(8,128)(2,1)S(1)}, bf16[264,512]{1,0:T(8,128)(2,1)S(1)}, u32[]{:S(2)}, u32[]{:S(2)}) collective-permute-start(bf16[264,512]{1,0:T(8,128)(2,1)S(1)} %add_convert_fusion), channel_id=1, source_target_pairs={{0,4},{1,5},{2,6},{3,7},{4,0},{5,1},{6,2},{7,3},{8,12},{9,13},{10,... | collective-permute-start | bytes 811016 | tf_op jit(solution)/shard_map/ppermute | solution.py:21
  87.0 16.0 %collective-permute-start.16 = (bf16[264,512]{1,0:T(8,128)(2,1)S(1)}, bf16[264,512]{1,0:T(8,128)(2,1)S(1)}, u32[]{:S(2)}, u32[]{:S(2)}) collective-permute-start(bf16[264,512]{1,0:T(8,128)(2,1)S(1)} %add_convert_fusion.1), channel_id=1, source_target_pairs={{0,4},{1,5},{2,6},{3,7},{4,0},{5,1},{6,2},{7,3},{8,12},{9,13},{10,... | collective-permute-start | bytes 811016 | tf_op jit(solution)/shard_map/ppermute | solution.py:21
  92.6 11.3 %collective-permute-start.15 = (bf16[264,512]{1,0:T(8,128)(2,1)S(1)}, bf16[264,512]{1,0:T(8,128)(2,1)S(1)}, u32[]{:S(2)}, u32[]{:S(2)}) collective-permute-start(bf16[264,512]{1,0:T(8,128)(2,1)S(1)} %get-tuple-element.51), channel_id=1, source_target_pairs={{0,2},{1,3},{2,0},{3,1},{4,6},{5,7},{6,4},{7,5},{8,10},{9,11},{10,... | collective-permute-start | bytes 811016 | tf_op jit(solution)/shard_map/ppermute | solution.py:26

commit v9 on v8

--- a/solution.py
+++ b/solution.py
@@ -110,10 +110,10 @@
     for copy in fetch:
         copy.wait()
     routes_ref, gain_ref, x_ref = held
-    pack(normed(x_ref, gain_ref), own_ref, routes_ref, outs)
     for i in range(3):
         load[i].wait()
         store[i].start()
+    pack(normed(x_ref, gain_ref), own_ref, routes_ref, outs)
     for copy in store:
         copy.wait()
 
@@ -212,13 +212,15 @@
     return [swapped(after(block, *others), "expert", 2) for block in blocks]
 
 
-def crossing_home(partial):
+def totals_to_cross(partial, *others):
     experts = len(partial) // 2
     mine, theirs = partial[:experts], partial[experts:]
-    totals = [
-        (mine[j] + swapped(theirs[j], "expert", 2).astype(F32)).astype(BF16) for j in range(1, experts)
-    ]
-    return totals, [shifted(totals[j - 1], "expert", -SPLIT * j) for j in range(1, experts)]
+    swaps = partners(theirs[1:], *others)
+    return [(mine[j] + swaps[j - 1].astype(F32)).astype(BF16) for j in range(1, experts)]
+
+
+def crossed_home(totals, *others):
+    return [shifted(after(total, *others), "expert", -SPLIT * (j + 1)) for j, total in enumerate(totals)]
 
 
 def per_device(act_in, saved_in, grad_in, norm_gain, w_gate, w_up, w_down, routes_fwd, gates_fwd, routes_bwd, gates_bwd):
@@ -295,9 +297,11 @@
     partial_f = local_call(
         functools.partial(forward_body, count, rows), partial, scratch=[wide], vmem_mib=32, name="experts_fwd"
     )(after(rows_f[0], partial_b[0]), *rows_f[1:], *shares)
-    totals_b, home_b = crossing_home(partial_b)
-    totals_f, home_f = crossing_home(partial_f)
-    back_b = [partial_b[0]] + partners(partial_b[experts:experts + 1], *totals_b) + home_b
+    totals_b = totals_to_cross(partial_b)
+    home_b = crossed_home(totals_b)
+    totals_f = totals_to_cross(partial_f, *totals_b)
+    home_f = crossed_home(totals_f, *home_b)
+    back_b = [partial_b[0]] + partners(partial_b[experts:experts + 1], *totals_f) + home_b
     back_f = [partial_f[0]] + partners(partial_f[experts:experts + 1], *totals_f, back_b[1]) + home_f
 
     grad_out = local_call(

time: 106 us -> 107 us (level)
  waiting for transfers between devices: 58.6 us -> 61.2 us
  starting transfers between devices: 29.2 us -> 27.9 us
    ppermute x7, starting transfers between devices: 17.9 us -> 14.4 us  [shifted(): lax.ppermute(value, axis, [(i, (i + steps) % count) for i in range(count)])]
    ppermute x11, starting transfers between devices: 11.3 us -> 13.5 us  [swapped(): return lax.ppermute(value, axis, [(i, i ^ bit) for i in range(count)])]
    ppermute x7, waiting for transfers between devices: 20.7 us -> 22.3 us  [shifted(): lax.ppermute(value, axis, [(i, (i + steps) % count) for i in range(count)])]
where the time goes in v9:
time: 107 us; the launch traced here: 106 us
  waiting for transfers between devices  61.2 us (57%)
  starting transfers between devices  27.9 us (26%)
  Pallas kernels  15.2 us (14%)
    ppermute x11, waiting for transfers between devices, swapped(): return lax.ppermute(value, axis, [(i, i ^ bit) for i in range(count)])  38.9 us
    ppermute x7, waiting for transfers between devices, shifted(): lax.ppermute(value, axis, [(i, (i + steps) % count) for i in range(count)])  22.3 us
    ppermute x7, starting transfers between devices, shifted(): lax.ppermute(value, axis, [(i, (i + steps) % count) for i in range(count)])  14.4 us
    ppermute x11, starting transfers between devices, swapped(): return lax.ppermute(value, axis, [(i, i ^ bit) for i in range(count)])  13.5 us
    pallas_call x1, Pallas kernels, per_device(): local_call(first_body, [jax.ShapeDtypeStruct((3 * w_down.shape[1], width)...  3.76 us
    pallas_call x1, Pallas kernels, per_device(): local_call(functools.partial(backward_body, count, rows), partial, scratc...  3.63 us
    pallas_call x1, Pallas kernels, per_device(): local_call(functools.partial(forward_body, count, rows), partial, scratch...  2.25 us
  transfers between devices with their start and end apart: 18, of which 14 were waited for; matrix products, arithmetic and copies ran while one was open for 0% of the time, Pallas kernels for 9%

profile of v9, /device:TPU:0, one launch (start us, length us, event | category | flops | bytes accessed | tf_op | source)
XLA Modules:
  0.0 106.2 jit_solution(11404917998084271292)
XLA Ops:
  0.7 3.8 %join_weights_pack_saved.1 = (bf16[576,2048]{1,0:T(8,128)(2,1)}, bf16[264,512]{1,0:T(8,128)(2,1)}, bf16[264,512]{1,0:T(8,128)(2,1)}) custom-call(s32[1]{0:T(128)} %bitcast.own_ref, s32[1,128]{1,0:T(1,128)} %bitcast.28, f32[1,2048]{1,0:T(1,128)} %gain_ref.3, bf16[128,2048]{1,0:T(8,128)(2,1)} %bitcast.26, bf16[192,2048]{1,0:T(8,128)(2,1)} %bitcast.17, ...), custom_call_target="tpu_custom_call" | custom-call | flops 1000 | bytes 1000 | tf_op jit(solution)/shard_map/join_weights_pack_saved/pallas_call | solution.py:252
  4.5 3.0 %collective-permute-start.8 = (bf16[576,2048]{1,0:T(8,128)(2,1)}, bf16[576,2048]{1,0:T(8,128)(2,1)S(1)}, u32[]{:S(2)}, u32[]{:S(2)}) collective-permute-start(bf16[576,2048]{1,0:T(8,128)(2,1)} %get-tuple-element.39), channel_id=1, source_target_pairs={{0,1},{1,0},{2,3},{3,2},{4,5},{5,4},{6,7},{7,6},{8,9},{9,8},{10,11... | collective-permute-start | bytes 7077896 | tf_op jit(solution)/shard_map/ppermute | solution.py:26
  8.2 2.6 %collective-permute-start.2 = (bf16[264,512]{1,0:T(8,128)(2,1)}, bf16[264,512]{1,0:T(8,128)(2,1)S(1)}, u32[]{:S(2)}, u32[]{:S(2)}) collective-permute-start(bf16[264,512]{1,0:T(8,128)(2,1)} %get-tuple-element.32), channel_id=1, source_target_pairs={{0,4},{1,5},{2,6},{3,7},{4,0},{5,1},{6,2},{7,3},{8,12},{9,13},{10,... | collective-permute-start | bytes 811016 | tf_op jit(solution)/shard_map/ppermute | solution.py:21
  10.8 1.6 %collective-permute-start.3 = (bf16[264,512]{1,0:T(8,128)(2,1)}, bf16[264,512]{1,0:T(8,128)(2,1)S(1)}, u32[]{:S(2)}, u32[]{:S(2)}) collective-permute-start(bf16[264,512]{1,0:T(8,128)(2,1)} %get-tuple-element.29.refs_0_), channel_id=1, source_target_pairs={{0,2},{1,3},{2,0},{3,1},{4,6},{5,7},{6,4},{7,5},{8,10},{9,11},{10,... | collective-permute-start | bytes 811016 | tf_op jit(solution)/shard_map/ppermute | solution.py:26
  12.3 5.0 %collective-permute-done.1.x_ref.up_ref = bf16[128,2048]{1,0:T(8,128)(2,1)S(1)} collective-permute-done((bf16[128,2048]{1,0:T(8,128)(2,1)S(1)}, bf16[128,2048]{1,0:T(8,128)(2,1)S(1)}, u32[]{:S(2)}, u32[]{:S(2)}) %collective-permute-start.1) | collective-permute-done | bytes 524320 | tf_op jit(solution)/shard_map/ppermute | solution.py:21
  18.2 5.0 %collective-permute-start.5 = (bf16[264,512]{1,0:T(8,128)(2,1)S(1)}, bf16[264,512]{1,0:T(8,128)(2,1)S(1)}, u32[]{:S(2)}, u32[]{:S(2)}) collective-permute-start(bf16[264,512]{1,0:T(8,128)(2,1)S(1)} %get-tuple-element.36), channel_id=1, source_target_pairs={{0,4},{1,5},{2,6},{3,7},{4,0},{5,1},{6,2},{7,3},{8,12},{9,13},{10,... | collective-permute-start | bytes 811016 | tf_op jit(solution)/shard_map/ppermute | solution.py:21
  23.4 1.4 %collective-permute-start.6 = (bf16[264,512]{1,0:T(8,128)(2,1)S(1)}, bf16[264,512]{1,0:T(8,128)(2,1)S(1)}, u32[]{:S(2)}, u32[]{:S(2)}) collective-permute-start(bf16[264,512]{1,0:T(8,128)(2,1)S(1)} %get-tuple-element.37.refs_4_), channel_id=1, source_target_pairs={{0,2},{1,3},{2,0},{3,1},{4,6},{5,7},{6,4},{7,5},{8,10},{9,11},{10,... | collective-permute-start | bytes 811016 | tf_op jit(solution)/shard_map/ppermute | solution.py:26
  24.8 1.2 %collective-permute-done.3.refs_2_ = bf16[264,512]{1,0:T(8,128)(2,1)S(1)} collective-permute-done((bf16[264,512]{1,0:T(8,128)(2,1)}, bf16[264,512]{1,0:T(8,128)(2,1)S(1)}, u32[]{:S(2)}, u32[]{:S(2)}) %collective-permute-start.3) | collective-permute-done | bytes 270368 | tf_op jit(solution)/shard_map/ppermute | solution.py:26
  27.0 2.0 %collective-permute-start.9 = (bf16[264,512]{1,0:T(8,128)(2,1)S(1)}, bf16[264,512]{1,0:T(8,128)(2,1)S(1)}, u32[]{:S(2)}, u32[]{:S(2)}) collective-permute-start(bf16[264,512]{1,0:T(8,128)(2,1)S(1)} %get-tuple-element.42), channel_id=1, source_target_pairs={{0,4},{1,5},{2,6},{3,7},{4,0},{5,1},{6,2},{7,3},{8,12},{9,13},{10,... | collective-permute-start | bytes 811016 | tf_op jit(solution)/shard_map/ppermute | solution.py:21
  29.0 7.2 %collective-permute-done.5.refs_5_ = bf16[264,512]{1,0:T(8,128)(2,1)S(1)} collective-permute-done((bf16[264,512]{1,0:T(8,128)(2,1)S(1)}, bf16[264,512]{1,0:T(8,128)(2,1)S(1)}, u32[]{:S(2)}, u32[]{:S(2)}) %collective-permute-start.5) | collective-permute-done | bytes 270368 | tf_op jit(solution)/shard_map/ppermute | solution.py:21
  36.2 1.2 %collective-permute-start.10 = (bf16[264,512]{1,0:T(8,128)(2,1)S(1)}, bf16[264,512]{1,0:T(8,128)(2,1)S(1)}, u32[]{:S(2)}, u32[]{:S(2)}) collective-permute-start(bf16[264,512]{1,0:T(8,128)(2,1)S(1)} %get-tuple-element.43.refs_0_), channel_id=1, source_target_pairs={{0,2},{1,3},{2,0},{3,1},{4,6},{5,7},{6,4},{7,5},{8,10},{9,11},{10,... | collective-permute-start | bytes 811016 | tf_op jit(solution)/shard_map/ppermute | solution.py:26
  37.4 5.8 %collective-permute-done.6.refs_6_ = bf16[264,512]{1,0:T(8,128)(2,1)S(1)} collective-permute-done((bf16[264,512]{1,0:T(8,128)(2,1)S(1)}, bf16[264,512]{1,0:T(8,128)(2,1)S(1)}, u32[]{:S(2)}, u32[]{:S(2)}) %collective-permute-start.6) | collective-permute-done | bytes 270368 | tf_op jit(solution)/shard_map/ppermute | solution.py:26
  43.2 5.8 %collective-permute-done.4.refs_3_ = bf16[264,512]{1,0:T(8,128)(2,1)S(1)} collective-permute-done((bf16[264,512]{1,0:T(8,128)(2,1)S(1)}, bf16[264,512]{1,0:T(8,128)(2,1)S(1)}, u32[]{:S(2)}, u32[]{:S(2)}) %collective-permute-start.4) | collective-permute-done | bytes 270368 | tf_op jit(solution)/shard_map/ppermute | solution.py:26
  49.0 5.8 %collective-permute-done.10.refs_2_ = bf16[264,512]{1,0:T(8,128)(2,1)S(1)} collective-permute-done((bf16[264,512]{1,0:T(8,128)(2,1)S(1)}, bf16[264,512]{1,0:T(8,128)(2,1)S(1)}, u32[]{:S(2)}, u32[]{:S(2)}) %collective-permute-start.10) | collective-permute-done | bytes 270368 | tf_op jit(solution)/shard_map/ppermute | solution.py:26
  54.8 1.0 collective-permute-start.11
  55.8 4.8 %collective-permute-done.7.refs_7_ = bf16[264,512]{1,0:T(8,128)(2,1)S(1)} collective-permute-done((bf16[264,512]{1,0:T(8,128)(2,1)S(1)}, bf16[264,512]{1,0:T(8,128)(2,1)S(1)}, u32[]{:S(2)}, u32[]{:S(2)}) %collective-permute-start.7) | collective-permute-done | bytes 270368 | tf_op jit(solution)/shard_map/ppermute | solution.py:26
  60.6 0.9 copy-done.4
  61.5 3.6 %experts_bwd.1 = (f32[264,512]{1,0:T(8,128)S(1)}, f32[264,512]{1,0:T(8,128)S(1)}, bf16[264,512]{1,0:T(8,128)(2,1)S(1)}, bf16[264,512]{1,0:T(8,128)(2,1)S(1)}) custom-call(bf16[264,512]{1,0:T(8,128)(2,1)S(1)} %copy-done.4, bf16[264,512]{1,0:T(8,128)(2,1)S(1)} %collective-permute-done.2.refs_1_, bf16[264,512]{1,0:T(8,128)(2,1)S(1)} %collective-permute-done.3.refs_2_, ...), custom_call_target="tpu_custom_call" | custom-call | flops 1000 | bytes 1000 | tf_op jit(solution)/shard_map/experts_bwd/pallas_call | solution.py:294
  65.2 1.0 collective-permute-start.12
  66.2 2.3 %experts_fwd.1 = (f32[264,512]{1,0:T(8,128)S(1)}, f32[264,512]{1,0:T(8,128)S(1)}, bf16[264,512]{1,0:T(8,128)(2,1)S(1)}, bf16[264,512]{1,0:T(8,128)(2,1)S(1)}) custom-call(bf16[264,512]{1,0:T(8,128)(2,1)S(1)} %get-tuple-element.43.refs_0_, bf16[264,512]{1,0:T(8,128)(2,1)S(1)} %collective-permute-done.9.refs_1_, ...), custom_call_target="tpu_custom_call" | custom-call | flops 1000 | bytes 1000 | tf_op jit(solution)/shard_map/experts_fwd/pallas_call | solution.py:297
  68.5 4.6 %collective-permute-done.12 = bf16[264,512]{1,0:T(8,128)(2,1)S(1)} collective-permute-done((bf16[264,512]{1,0:T(8,128)(2,1)S(1)}, bf16[264,512]{1,0:T(8,128)(2,1)S(1)}, u32[]{:S(2)}, u32[]{:S(2)}) %collective-permute-start.12) | collective-permute-done | bytes 270368 | tf_op jit(solution)/shard_map/ppermute | solution.py:26
  73.2 1.7 %collective-permute-start.13 = (bf16[264,512]{1,0:T(8,128)(2,1)S(1)}, bf16[264,512]{1,0:T(8,128)(2,1)S(1)}, u32[]{:S(2)}, u32[]{:S(2)}) collective-permute-start(bf16[264,512]{1,0:T(8,128)(2,1)S(1)} %get-tuple-element.51), channel_id=1, source_target_pairs={{0,2},{1,3},{2,0},{3,1},{4,6},{5,7},{6,4},{7,5},{8,10},{9,11},{10,... | collective-permute-start | bytes 811016 | tf_op jit(solution)/shard_map/ppermute | solution.py:26
  75.0 2.3 %collective-permute-start.16 = (bf16[264,512]{1,0:T(8,128)(2,1)S(1)}, bf16[264,512]{1,0:T(8,128)(2,1)S(1)}, u32[]{:S(2)}, u32[]{:S(2)}) collective-permute-start(bf16[264,512]{1,0:T(8,128)(2,1)S(1)} %add_convert_fusion.1), channel_id=1, source_target_pairs={{0,4},{1,5},{2,6},{3,7},{4,0},{5,1},{6,2},{7,3},{8,12},{9,13},{10,... | collective-permute-start | bytes 811016 | tf_op jit(solution)/shard_map/ppermute | solution.py:21
  77.3 7.2 %collective-permute-done.13 = bf16[264,512]{1,0:T(8,128)(2,1)S(1)} collective-permute-done((bf16[264,512]{1,0:T(8,128)(2,1)S(1)}, bf16[264,512]{1,0:T(8,128)(2,1)S(1)}, u32[]{:S(2)}, u32[]{:S(2)}) %collective-permute-start.13) | collective-permute-done | bytes 270368 | tf_op jit(solution)/shard_map/ppermute | solution.py:26
  84.7 4.6 %collective-permute-done.16.refs_2_ = bf16[264,512]{1,0:T(8,128)(2,1)S(1)} collective-permute-done((bf16[264,512]{1,0:T(8,128)(2,1)S(1)}, bf16[264,512]{1,0:T(8,128)(2,1)S(1)}, u32[]{:S(2)}, u32[]{:S(2)}) %collective-permute-start.16) | collective-permute-done | bytes 270368 | tf_op jit(solution)/shard_map/ppermute | solution.py:21
  89.3 1.8 %collective-permute-start.17 = (bf16[264,512]{1,0:T(8,128)(2,1)S(1)}, bf16[264,512]{1,0:T(8,128)(2,1)S(1)}, u32[]{:S(2)}, u32[]{:S(2)}) collective-permute-start(bf16[264,512]{1,0:T(8,128)(2,1)S(1)} %add_convert_fusion), channel_id=1, source_target_pairs={{0,4},{1,5},{2,6},{3,7},{4,0},{5,1},{6,2},{7,3},{8,12},{9,13},{10,... | collective-permute-start | bytes 811016 | tf_op jit(solution)/shard_map/ppermute | solution.py:21
  91.1 2.4 %collective-permute-done.14.refs_1_ = bf16[264,512]{1,0:T(8,128)(2,1)S(1)} collective-permute-done((bf16[264,512]{1,0:T(8,128)(2,1)S(1)}, bf16[264,512]{1,0:T(8,128)(2,1)S(1)}, u32[]{:S(2)}, u32[]{:S(2)}) %collective-permute-start.14) | collective-permute-done | bytes 270368 | tf_op jit(solution)/shard_map/ppermute | solution.py:26
  93.5 2.5 %collective-permute-start.15 = (bf16[264,512]{1,0:T(8,128)(2,1)S(1)}, bf16[264,512]{1,0:T(8,128)(2,1)S(1)}, u32[]{:S(2)}, u32[]{:S(2)}) collective-permute-start(bf16[264,512]{1,0:T(8,128)(2,1)S(1)} %get-tuple-element.54), channel_id=1, source_target_pairs={{0,2},{1,3},{2,0},{3,1},{4,6},{5,7},{6,4},{7,5},{8,10},{9,11},{10,... | collective-permute-start | bytes 811016 | tf_op jit(solution)/shard_map/ppermute | solution.py:26
  96.0 2.0 %home_bwd.1 = bf16[128,2048]{1,0:T(8,128)(2,1)} custom-call(s32[1]{0:T(128)} %bitcast.own_ref, s32[1,128]{1,0:T(1,128)S(1)} %bitcast.30, f32[1,128]{1,0:T(1,128)S(1)} %bitcast.34, f32[1,2048]{1,0:T(1,128)S(1)} %copy-done.5, bf16[128,2048]{1,0:T(8,128)(2,1)S(1)} %bitcast.27, bf16[128,2048]{1,0:T(8,128)(2,1)S(1)} %collective-permute-done.1.x_ref.up_ref, ...), custom_call_target="tpu_custom_call" | custom-call | flops 1000 | bytes 1000 | tf_op jit(solution)/shard_map/home_bwd/pallas_call | solution.py:307
  98.0 5.3 %collective-permute-done.17.refs_2_ = bf16[264,512]{1,0:T(8,128)(2,1)S(1)} collective-permute-done((bf16[264,512]{1,0:T(8,128)(2,1)S(1)}, bf16[264,512]{1,0:T(8,128)(2,1)S(1)}, u32[]{:S(2)}, u32[]{:S(2)}) %collective-permute-start.17) | collective-permute-done | bytes 270368 | tf_op jit(solution)/shard_map/ppermute | solution.py:21
  103.3 1.2 %collective-permute-done.15.refs_1_ = bf16[264,512]{1,0:T(8,128)(2,1)S(1)} collective-permute-done((bf16[264,512]{1,0:T(8,128)(2,1)S(1)}, bf16[264,512]{1,0:T(8,128)(2,1)S(1)}, u32[]{:S(2)}, u32[]{:S(2)}) %collective-permute-start.15) | collective-permute-done | bytes 270368 | tf_op jit(solution)/shard_map/ppermute | solution.py:26
  104.5 1.7 %home_fwd.1 = bf16[128,2048]{1,0:T(8,128)(2,1)} custom-call(s32[1]{0:T(128)} %bitcast.own_ref, s32[1,128]{1,0:T(1,128)S(1)} %bitcast.32, f32[1,128]{1,0:T(1,128)S(1)} %bitcast.33, bf16[128,2048]{1,0:T(8,128)(2,1)S(1)} %collective-permute-done.x_ref, f32[264,512]{1,0:T(8,128)S(1)} %get-tuple-element.45.refs_0_, ...), custom_call_target="tpu_custom_call" | custom-call | flops 1000 | bytes 1000 | tf_op jit(solution)/shard_map/home_fwd/pallas_call | solution.py:314
  (35 shorter events, 2.9 us)
Async XLA Ops:
  0.6 59.9 %copy-start.1 = (bf16[1,2048,192]{1,2,0:T(8,128)(2,1)S(1)}, bf16[1,2048,192]{1,2,0:T(8,128)(2,1)}, u32[]{:S(2)}) copy-start(bf16[1,2048,192]{1,2,0:T(8,128)(2,1)} %param.16) | copy-start | bytes 2359300
  0.6 59.9 %copy-start.2 = (bf16[1,192,2048]{2,1,0:T(8,128)(2,1)S(1)}, bf16[1,192,2048]{2,1,0:T(8,128)(2,1)}, u32[]{:S(2)}) copy-start(bf16[1,192,2048]{2,1,0:T(8,128)(2,1)} %param.17) | copy-start | bytes 2359300
  0.7 16.7 %copy-start.6 = (s32[1,128,1]{1,2,0:T(1,128)S(1)}, s32[1,128,1]{1,2,0:T(1,128)}, u32[]{:S(2)}) copy-start(s32[1,128,1]{1,2,0:T(1,128)} %param.20) | copy-start | bytes 1540
  0.7 59.9 %copy-start = (bf16[1,2048,192]{1,2,0:T(8,128)(2,1)S(1)}, bf16[1,2048,192]{1,2,0:T(8,128)(2,1)}, u32[]{:S(2)}) copy-start(bf16[1,2048,192]{1,2,0:T(8,128)(2,1)} %param.15) | copy-start | bytes 2359300
  0.7 25.4 %copy-start.5 = (f32[1,2048]{1,0:T(1,128)S(1)}, f32[1,2048]{1,0:T(1,128)}, u32[]{:S(2)}) copy-start(f32[1,2048]{1,0:T(1,128)} %gain_ref.3) | copy-start | bytes 24580
  0.7 6.8 %copy-start.10 = (bf16[1,128,2048]{2,1,0:T(8,128)(2,1)S(1)}, bf16[1,128,2048]{2,1,0:T(8,128)(2,1)}, u32[]{:S(2)}) copy-start(bf16[1,128,2048]{2,1,0:T(8,128)(2,1)} %param.13) | copy-start | bytes 1572868
  0.7 25.4 %copy-start.7 = (s32[1,128,1]{1,2,0:T(1,128)S(1)}, s32[1,128,1]{1,2,0:T(1,128)}, u32[]{:S(2)}) copy-start(s32[1,128,1]{1,2,0:T(1,128)} %param.18) | copy-start | bytes 1540
  4.5 56.1 %collective-permute-start.8 = (bf16[576,2048]{1,0:T(8,128)(2,1)}, bf16[576,2048]{1,0:T(8,128)(2,1)S(1)}, u32[]{:S(2)}, u32[]{:S(2)}) collective-permute-start(bf16[576,2048]{1,0:T(8,128)(2,1)} %get-tuple-element.39), channel_id=1, source_target_pairs={{0,1},{1,0},{2,3},{3,2},{4,5},{5,4},{6,7},{7,6},{8,9},{9,8},{10,11... | collective-permute-start | bytes 7077896 | tf_op jit(solution)/shard_map/ppermute | solution.py:26
  7.5 9.9 %collective-permute-start.1 = (bf16[128,2048]{1,0:T(8,128)(2,1)S(1)}, bf16[128,2048]{1,0:T(8,128)(2,1)S(1)}, u32[]{:S(2)}, u32[]{:S(2)}) collective-permute-start(bf16[128,2048]{1,0:T(8,128)(2,1)S(1)} %bitcast.37), channel_id=1, source_target_pairs={{0,24},{8,0},{16,8},{24,16},{1,25},{9,1},{17,9},{25,17},{2,26},{10... | collective-permute-start | bytes 1572872 | tf_op jit(solution)/shard_map/ppermute | solution.py:21
  8.2 15.2 %collective-permute-start.2 = (bf16[264,512]{1,0:T(8,128)(2,1)}, bf16[264,512]{1,0:T(8,128)(2,1)S(1)}, u32[]{:S(2)}, u32[]{:S(2)}) collective-permute-start(bf16[264,512]{1,0:T(8,128)(2,1)} %get-tuple-element.32), channel_id=1, source_target_pairs={{0,4},{1,5},{2,6},{3,7},{4,0},{5,1},{6,2},{7,3},{8,12},{9,13},{10,... | collective-permute-start | bytes 811016 | tf_op jit(solution)/shard_map/ppermute | solution.py:21
  10.8 15.3 %collective-permute-start = (bf16[128,2048]{1,0:T(8,128)(2,1)}, bf16[128,2048]{1,0:T(8,128)(2,1)S(1)}, u32[]{:S(2)}, u32[]{:S(2)}) collective-permute-start(bf16[128,2048]{1,0:T(8,128)(2,1)} %bitcast.38), channel_id=1, source_target_pairs={{0,8},{8,16},{16,24},{24,0},{1,9},{9,17},{17,25},{25,1},{2,10},{10... | collective-permute-start | bytes 1572872 | tf_op jit(solution)/shard_map/ppermute | solution.py:21
  10.8 15.3 %collective-permute-start.3 = (bf16[264,512]{1,0:T(8,128)(2,1)}, bf16[264,512]{1,0:T(8,128)(2,1)S(1)}, u32[]{:S(2)}, u32[]{:S(2)}) collective-permute-start(bf16[264,512]{1,0:T(8,128)(2,1)} %get-tuple-element.29.refs_0_), channel_id=1, source_target_pairs={{0,2},{1,3},{2,0},{3,1},{4,6},{5,7},{6,4},{7,5},{8,10},{9,11},{10,... | collective-permute-start | bytes 811016 | tf_op jit(solution)/shard_map/ppermute | solution.py:26
  18.2 17.9 %collective-permute-start.5 = (bf16[264,512]{1,0:T(8,128)(2,1)S(1)}, bf16[264,512]{1,0:T(8,128)(2,1)S(1)}, u32[]{:S(2)}, u32[]{:S(2)}) collective-permute-start(bf16[264,512]{1,0:T(8,128)(2,1)S(1)} %get-tuple-element.36), channel_id=1, source_target_pairs={{0,4},{1,5},{2,6},{3,7},{4,0},{5,1},{6,2},{7,3},{8,12},{9,13},{10,... | collective-permute-start | bytes 811016 | tf_op jit(solution)/shard_map/ppermute | solution.py:21
  23.4 19.8 %collective-permute-start.6 = (bf16[264,512]{1,0:T(8,128)(2,1)S(1)}, bf16[264,512]{1,0:T(8,128)(2,1)S(1)}, u32[]{:S(2)}, u32[]{:S(2)}) collective-permute-start(bf16[264,512]{1,0:T(8,128)(2,1)S(1)} %get-tuple-element.37.refs_4_), channel_id=1, source_target_pairs={{0,2},{1,3},{2,0},{3,1},{4,6},{5,7},{6,4},{7,5},{8,10},{9,11},{10,... | collective-permute-start | bytes 811016 | tf_op jit(solution)/shard_map/ppermute | solution.py:26
  26.1 22.9 %collective-permute-start.4 = (bf16[264,512]{1,0:T(8,128)(2,1)S(1)}, bf16[264,512]{1,0:T(8,128)(2,1)S(1)}, u32[]{:S(2)}, u32[]{:S(2)}) collective-permute-start(bf16[264,512]{1,0:T(8,128)(2,1)S(1)} %collective-permute-done.2.refs_1_), channel_id=1, source_target_pairs={{0,2},{1,3},{2,0},{3,1},{4,6},{5,7},{6,4},{7,5},{8,10},{9,11},{10,... | collective-permute-start | bytes 811016 | tf_op jit(solution)/shard_map/ppermute | solution.py:26
  27.0 22.0 %collective-permute-start.9 = (bf16[264,512]{1,0:T(8,128)(2,1)S(1)}, bf16[264,512]{1,0:T(8,128)(2,1)S(1)}, u32[]{:S(2)}, u32[]{:S(2)}) collective-permute-start(bf16[264,512]{1,0:T(8,128)(2,1)S(1)} %get-tuple-element.42), channel_id=1, source_target_pairs={{0,4},{1,5},{2,6},{3,7},{4,0},{5,1},{6,2},{7,3},{8,12},{9,13},{10,... | collective-permute-start | bytes 811016 | tf_op jit(solution)/shard_map/ppermute | solution.py:21
  36.2 18.6 %collective-permute-start.10 = (bf16[264,512]{1,0:T(8,128)(2,1)S(1)}, bf16[264,512]{1,0:T(8,128)(2,1)S(1)}, u32[]{:S(2)}, u32[]{:S(2)}) collective-permute-start(bf16[264,512]{1,0:T(8,128)(2,1)S(1)} %get-tuple-element.43.refs_0_), channel_id=1, source_target_pairs={{0,2},{1,3},{2,0},{3,1},{4,6},{5,7},{6,4},{7,5},{8,10},{9,11},{10,... | collective-permute-start | bytes 811016 | tf_op jit(solution)/shard_map/ppermute | solution.py:26
  43.2 17.4 %collective-permute-start.7 = (bf16[264,512]{1,0:T(8,128)(2,1)S(1)}, bf16[264,512]{1,0:T(8,128)(2,1)S(1)}, u32[]{:S(2)}, u32[]{:S(2)}) collective-permute-start(bf16[264,512]{1,0:T(8,128)(2,1)S(1)} %collective-permute-done.5.refs_5_), channel_id=1, source_target_pairs={{0,2},{1,3},{2,0},{3,1},{4,6},{5,7},{6,4},{7,5},{8,10},{9,11},{10,... | collective-permute-start | bytes 811016 | tf_op jit(solution)/shard_map/ppermute | solution.py:26
  54.8 11.5 %collective-permute-start.11 = (bf16[264,512]{1,0:T(8,128)(2,1)S(1)}, bf16[264,512]{1,0:T(8,128)(2,1)S(1)}, u32[]{:S(2)}, u32[]{:S(2)}) collective-permute-start(bf16[264,512]{1,0:T(8,128)(2,1)S(1)} %collective-permute-done.9.refs_1_), channel_id=1, source_target_pairs={{0,2},{1,3},{2,0},{3,1},{4,6},{5,7},{6,4},{7,5},{8,10},{9,11},{10,... | collective-permute-start | bytes 811016 | tf_op jit(solution)/shard_map/ppermute | solution.py:26
  60.6 1.0 copy-start.4
  65.2 8.0 %collective-permute-start.12 = (bf16[264,512]{1,0:T(8,128)(2,1)S(1)}, bf16[264,512]{1,0:T(8,128)(2,1)S(1)}, u32[]{:S(2)}, u32[]{:S(2)}) collective-permute-start(bf16[264,512]{1,0:T(8,128)(2,1)S(1)} %get-tuple-element.50), channel_id=1, source_target_pairs={{0,2},{1,3},{2,0},{3,1},{4,6},{5,7},{6,4},{7,5},{8,10},{9,11},{10,... | collective-permute-start | bytes 811016 | tf_op jit(solution)/shard_map/ppermute | solution.py:26
  66.2 29.8 %copy-start.9 = (f32[1,128,1]{1,2,0:T(1,128)S(1)}, f32[1,128,1]{1,2,0:T(1,128)}, u32[]{:S(2)}) copy-start(f32[1,128,1]{1,2,0:T(1,128)} %param.21) | copy-start | bytes 1540
  68.5 27.5 %copy-start.3 = (bf16[1,128,2048]{2,1,0:T(8,128)(2,1)S(1)}, bf16[1,128,2048]{2,1,0:T(8,128)(2,1)}, u32[]{:S(2)}) copy-start(bf16[1,128,2048]{2,1,0:T(8,128)(2,1)} %param.12) | copy-start | bytes 1572868
  73.2 31.3 %copy-start.8 = (f32[1,128,1]{1,2,0:T(1,128)S(1)}, f32[1,128,1]{1,2,0:T(1,128)}, u32[]{:S(2)}) copy-start(f32[1,128,1]{1,2,0:T(1,128)} %param.19) | copy-start | bytes 1540
  73.2 11.3 %collective-permute-start.13 = (bf16[264,512]{1,0:T(8,128)(2,1)S(1)}, bf16[264,512]{1,0:T(8,128)(2,1)S(1)}, u32[]{:S(2)}, u32[]{:S(2)}) collective-permute-start(bf16[264,512]{1,0:T(8,128)(2,1)S(1)} %get-tuple-element.51), channel_id=1, source_target_pairs={{0,2},{1,3},{2,0},{3,1},{4,6},{5,7},{6,4},{7,5},{8,10},{9,11},{10,... | collective-permute-start | bytes 811016 | tf_op jit(solution)/shard_map/ppermute | solution.py:26
  75.0 14.3 %collective-permute-start.16 = (bf16[264,512]{1,0:T(8,128)(2,1)S(1)}, bf16[264,512]{1,0:T(8,128)(2,1)S(1)}, u32[]{:S(2)}, u32[]{:S(2)}) collective-permute-start(bf16[264,512]{1,0:T(8,128)(2,1)S(1)} %add_convert_fusion.1), channel_id=1, source_target_pairs={{0,4},{1,5},{2,6},{3,7},{4,0},{5,1},{6,2},{7,3},{8,12},{9,13},{10,... | collective-permute-start | bytes 811016 | tf_op jit(solution)/shard_map/ppermute | solution.py:21
  84.6 8.9 %collective-permute-start.14 = (bf16[264,512]{1,0:T(8,128)(2,1)S(1)}, bf16[264,512]{1,0:T(8,128)(2,1)S(1)}, u32[]{:S(2)}, u32[]{:S(2)}) collective-permute-start(bf16[264,512]{1,0:T(8,128)(2,1)S(1)} %get-tuple-element.53), channel_id=1, source_target_pairs={{0,2},{1,3},{2,0},{3,1},{4,6},{5,7},{6,4},{7,5},{8,10},{9,11},{10,... | collective-permute-start | bytes 811016 | tf_op jit(solution)/shard_map/ppermute | solution.py:26
  89.3 14.0 %collective-permute-start.17 = (bf16[264,512]{1,0:T(8,128)(2,1)S(1)}, bf16[264,512]{1,0:T(8,128)(2,1)S(1)}, u32[]{:S(2)}, u32[]{:S(2)}) collective-permute-start(bf16[264,512]{1,0:T(8,128)(2,1)S(1)} %add_convert_fusion), channel_id=1, source_target_pairs={{0,4},{1,5},{2,6},{3,7},{4,0},{5,1},{6,2},{7,3},{8,12},{9,13},{10,... | collective-permute-start | bytes 811016 | tf_op jit(solution)/shard_map/ppermute | solution.py:21
  93.5 11.0 %collective-permute-start.15 = (bf16[264,512]{1,0:T(8,128)(2,1)S(1)}, bf16[264,512]{1,0:T(8,128)(2,1)S(1)}, u32[]{:S(2)}, u32[]{:S(2)}) collective-permute-start(bf16[264,512]{1,0:T(8,128)(2,1)S(1)} %get-tuple-element.54), channel_id=1, source_target_pairs={{0,2},{1,3},{2,0},{3,1},{4,6},{5,7},{6,4},{7,5},{8,10},{9,11},{10,... | collective-permute-start | bytes 811016 | tf_op jit(solution)/shard_map/ppermute | solution.py:26

commit v10 on v9

--- a/solution.py
+++ b/solution.py
@@ -89,12 +89,10 @@
     return (values * inverse_rms(values) * gain_ref[...]).astype(BF16)
 
 
-def pack_grad_body(own_ref, routes_ref, x_ref, *outs):
-    pack(x_ref[...], own_ref, routes_ref, outs)
-
-
-def pack_act_body(own_ref, routes_ref, gain_ref, x_ref, *outs):
-    pack(normed(x_ref, gain_ref), own_ref, routes_ref, outs)
+def pack_two_body(own_ref, routes_b_ref, routes_f_ref, gain_ref, grad_ref, x_ref, *outs):
+    half = outs[0].shape[0] // 2
+    pack(grad_ref[...], own_ref, routes_b_ref, [out.at[pl.ds(0, half), :] for out in outs])
+    pack(normed(x_ref, gain_ref), own_ref, routes_f_ref, [out.at[pl.ds(half, half), :] for out in outs])
 
 
 def first_body(own_ref, *refs):
@@ -118,22 +116,16 @@
         copy.wait()
 
 
-def unpack(refs, wide_ref, rows):
-    pitch = wide_ref.shape[0] // len(refs)
-    pieces = refs[0].shape[0] // rows
-    for i, ref in enumerate(refs):
-        value = ref[...].astype(F32)
-        whole = jnp.concatenate([value[p * rows:(p + 1) * rows] for p in range(pieces)], axis=1)
-        wide_ref[pl.ds(i * pitch, rows), :] = whole.astype(BF16)
-    return wide_ref[...]
-
-
-def spread_out(total, refs, pitch, rows):
-    for i, ref in enumerate(refs):
-        cols = ref.shape[1]
-        whole = total[i * pitch:i * pitch + rows]
-        pieces = [whole[:, p * cols:(p + 1) * cols] for p in range(ref.shape[0] // rows)]
-        ref[...] = jnp.concatenate(pieces, axis=0).astype(ref.dtype)
+def unpack(blocks, wide_ref, first, pitch, rows):
+    for i, block in enumerate(blocks):
+        value = block.astype(F32)
+        whole = jnp.concatenate([value[p * rows:(p + 1) * rows] for p in range(value.shape[0] // rows)], axis=1)
+        wide_ref[pl.ds(first + i * pitch, rows), :] = whole.astype(BF16)
+
+
+def pieces_of(total, i, pitch, rows, cols):
+    whole = total[i * pitch:i * pitch + rows]
+    return [whole[:, p:p + cols] for p in range(0, whole.shape[1], cols)]
 
 
 def joined(shares, i):
@@ -141,36 +133,35 @@
     return jnp.concatenate([shares[i][...], shares[3][pl.ds(i * units, units), :]], axis=0)
 
 
-def forward_body(count, rows, *refs):
-    row_refs, shares, outs, wide_ref = refs[:count], refs[count:count + 4], refs[count + 4:-1], refs[-1]
-    x = unpack(row_refs, wide_ref, rows)
-    gate_pre = lax.dot_general(x, joined(shares, 0), CONTRACT, preferred_element_type=F32)
-    up_pre = lax.dot_general(x, joined(shares, 1), CONTRACT, preferred_element_type=F32)
-    hidden = (silu_parts(gate_pre)[0] * up_pre).astype(BF16)
-    total = jnp.dot(hidden, joined(shares, 2), preferred_element_type=F32)
-    spread_out(total, outs, x.shape[0] // count, rows)
-
-
-def backward_body(count, rows, *refs):
-    row_refs, grad_refs, shares = refs[:count], refs[count:2 * count], refs[2 * count:2 * count + 4]
-    outs, wide_ref, grad_wide_ref = refs[2 * count + 4:-2], refs[-2], refs[-1]
-    x = unpack(row_refs, wide_ref, rows)
-    gate, up = joined(shares, 0), joined(shares, 1)
+def experts_body(count, rows, *refs):
+    saved_refs, two_refs, shares = refs[:count], refs[count:2 * count], refs[2 * count:2 * count + 4]
+    outs, x_ref, grads_ref = refs[2 * count + 4:-2], refs[-2], refs[-1]
+    pitch = grads_ref.shape[0] // count
+    half = two_refs[0].shape[0] // 2
+    cols = two_refs[0].shape[1]
+    split = count * pitch
+    two = [ref[...] for ref in two_refs]
+    unpack([ref[...] for ref in saved_refs], x_ref, 0, pitch, rows)
+    unpack([value[half:] for value in two], x_ref, split, pitch, rows)
+    unpack([value[:half] for value in two], grads_ref, 0, pitch, rows)
+    gate, up, down = joined(shares, 0), joined(shares, 1), joined(shares, 2)
+    x = x_ref[...]
     gate_pre = lax.dot_general(x, gate, CONTRACT, preferred_element_type=F32)
     up_pre = lax.dot_general(x, up, CONTRACT, preferred_element_type=F32)
+    d_hidden = lax.dot_general(grads_ref[...], down, CONTRACT, preferred_element_type=F32)
     activation, derivative = silu_parts(gate_pre)
-    grads = unpack(grad_refs, grad_wide_ref, rows)
-    d_hidden = lax.dot_general(grads, joined(shares, 2), CONTRACT, preferred_element_type=F32)
-    d_gate = (d_hidden * up_pre * derivative).astype(BF16)
-    d_up = (d_hidden * activation).astype(BF16)
-    total = jnp.dot(d_gate, gate, preferred_element_type=F32) + jnp.dot(d_up, up, preferred_element_type=F32)
-    spread_out(total, outs, x.shape[0] // count, rows)
-
-
-def routed_sum(experts, rows, own_ref, routes_ref, gates_ref, home_refs):
+    d_gate = (d_hidden * up_pre[:split] * derivative[:split]).astype(BF16)
+    d_up = (d_hidden * activation[:split]).astype(BF16)
+    hidden = (activation[split:] * up_pre[split:]).astype(BF16)
+    total_b = jnp.dot(d_gate, gate, preferred_element_type=F32) + jnp.dot(d_up, up, preferred_element_type=F32)
+    total_f = jnp.dot(hidden, down, preferred_element_type=F32)
+    for i, out in enumerate(outs):
+        parts = pieces_of(total_b, i, pitch, rows, cols) + pieces_of(total_f, i, pitch, rows, cols)
+        out[...] = jnp.concatenate(parts, axis=0).astype(out.dtype)
+
+
+def routed_sum(experts, rows, own_ref, routes_ref, gates_ref, blocks):
     block, slot = slots_of(routes_ref[...], own_ref[0], experts)
-    mine, theirs, *crossed_refs = home_refs
-    blocks = [(mine[...] + theirs[...].astype(F32)).astype(BF16)] + [ref[...] for ref in crossed_refs]
     height = blocks[0].shape[0]
     columns = []
     for p in range(height // rows):
@@ -188,20 +179,21 @@
     return jnp.concatenate(columns, axis=1) * gates
 
 
-def forward_home_body(experts, rows, own_ref, routes_ref, gates_ref, x_ref, *refs):
-    mixed = routed_sum(experts, rows, own_ref, routes_ref, gates_ref, refs[:-1])
-    refs[-1][...] = (x_ref[...].astype(F32) + mixed).astype(BF16)
-
-
-def backward_home_body(experts, rows, own_ref, routes_ref, gates_ref, gain_ref, saved_ref, up_ref, *refs):
-    d_norm = routed_sum(experts, rows, own_ref, routes_ref, gates_ref, refs[:-1])
+def home_body(experts, rows, own_ref, routes_b, gates_b, routes_f, gates_f, gain_ref, saved_ref, up_ref, x_ref, *refs):
+    mine, theirs, *crossed_refs = refs[:-2]
+    act_out, grad_out = refs[-2:]
+    half = mine.shape[0] // 2
+    blocks = [(mine[...] + theirs[...].astype(F32)).astype(BF16)] + [ref[...] for ref in crossed_refs]
+    mixed = routed_sum(experts, rows, own_ref, routes_f, gates_f, [value[half:] for value in blocks])
+    act_out[...] = (x_ref[...].astype(F32) + mixed).astype(BF16)
+    d_norm = routed_sum(experts, rows, own_ref, routes_b, gates_b, [value[:half] for value in blocks])
     base = saved_ref[...].astype(F32)
     inv_scale = inverse_rms(base)
     scaled = d_norm * gain_ref[...]
     d_input = inv_scale * (
         scaled - base * inv_scale * inv_scale * jnp.mean(scaled * base, axis=-1, keepdims=True)
     )
-    refs[-1][...] = (up_ref[...].astype(F32) + d_input).astype(BF16)
+    grad_out[...] = (up_ref[...].astype(F32) + d_input).astype(BF16)
 
 
 def crossed(blocks):
@@ -210,17 +202,6 @@
 
 def partners(blocks, *others):
     return [swapped(after(block, *others), "expert", 2) for block in blocks]
-
-
-def totals_to_cross(partial, *others):
-    experts = len(partial) // 2
-    mine, theirs = partial[:experts], partial[experts:]
-    swaps = partners(theirs[1:], *others)
-    return [(mine[j] + swaps[j - 1].astype(F32)).astype(BF16) for j in range(1, experts)]
-
-
-def crossed_home(totals, *others):
-    return [shifted(after(total, *others), "expert", -SPLIT * (j + 1)) for j, total in enumerate(totals)]
 
 
 def per_device(act_in, saved_in, grad_in, norm_gain, w_gate, w_up, w_down, routes_fwd, gates_fwd, routes_bwd, gates_bwd):
@@ -238,9 +219,8 @@
 
     shape = (pieces * rows, width // pieces)
     packed = [jax.ShapeDtypeStruct(shape, BF16)] * experts
-    partial = [jax.ShapeDtypeStruct(shape, F32)] * experts + packed
+    double = (2 * shape[0], shape[1])
     tokens = jax.ShapeDtypeStruct((tok_count, width), BF16)
-    wide = pltpu.VMEM((2 * experts * pitch, width), BF16)
 
     incoming = shifted(act_in[0], "section", 1)
     upstream = shifted(grad_in[0], "section", -1)
@@ -268,56 +248,43 @@
 
     rows_b = crossed(packed_b)
     swap_b = partners(rows_b[:1])
-    packed_g = local_call(
-        pack_grad_body,
-        packed,
-        in_specs=[scalar] + [whole] * 2,
+    packed_two = local_call(
+        pack_two_body,
+        [jax.ShapeDtypeStruct(double, BF16)] * experts,
+        in_specs=[scalar] + [whole] * 5,
         out_specs=[whole] * experts,
-        name="pack_grad",
-    )(own, r_bwd, after(upstream, packed_b[0]))
-    rows_g = crossed(packed_g)
-    packed_f = local_call(
-        pack_act_body,
-        packed,
-        in_specs=[scalar] + [whole] * 3,
-        out_specs=[whole] * experts,
-        name="pack_act",
-    )(own, r_fwd, norm_gain, after(incoming, packed_g[0], rows_b[-1]))
-    rows_f = crossed(packed_f)
-    swap_g = partners(rows_g[:1], rows_b[-1])
-    swap_f = partners(rows_f[:1], rows_g[-1])
-    rows_b = rows_b + swap_b + partners(rows_b[1:], swap_b[0])
-    rows_g = rows_g + swap_g + partners(rows_g[1:], swap_g[0])
-    rows_f = rows_f + swap_f + partners(rows_f[1:], swap_f[0], rows_b[-1])
-
-    count = 2 * experts
-    partial_b = local_call(
-        functools.partial(backward_body, count, rows), partial, scratch=[wide, wide], vmem_mib=40, name="experts_bwd"
-    )(*rows_b, *rows_g, *shares)
-    partial_f = local_call(
-        functools.partial(forward_body, count, rows), partial, scratch=[wide], vmem_mib=32, name="experts_fwd"
-    )(after(rows_f[0], partial_b[0]), *rows_f[1:], *shares)
-    totals_b = totals_to_cross(partial_b)
-    home_b = crossed_home(totals_b)
-    totals_f = totals_to_cross(partial_f, *totals_b)
-    home_f = crossed_home(totals_f, *home_b)
-    back_b = [partial_b[0]] + partners(partial_b[experts:experts + 1], *totals_f) + home_b
-    back_f = [partial_f[0]] + partners(partial_f[experts:experts + 1], *totals_f, back_b[1]) + home_f
-
-    grad_out = local_call(
-        functools.partial(backward_home_body, experts, rows),
-        tokens,
-        in_specs=[scalar] + [whole] * (6 + experts),
-        out_specs=whole,
-        name="home_bwd",
-    )(own, r_bwd, g_bwd, norm_gain, saved_in[0], upstream, *back_b)
-    act_out = local_call(
-        functools.partial(forward_home_body, experts, rows),
-        tokens,
-        in_specs=[scalar] + [whole] * (4 + experts),
-        out_specs=whole,
-        name="home_fwd",
-    )(own, r_fwd, g_fwd, incoming, *back_f)
+        name="pack_grad_and_act",
+    )(own, r_bwd, r_fwd, norm_gain, after(upstream, packed_b[0]), incoming)
+    rows_two = crossed(packed_two)
+    swap_two = partners(rows_two[:1], rows_b[-1])
+    far_b = partners(rows_b[1:], swap_b[0], packed_two[0])
+    far_two = partners(rows_two[1:], *far_b)
+
+    def run_experts(name, rows_saved, rows_double, kinds):
+        count = len(rows_saved)
+        return local_call(
+            functools.partial(experts_body, count, rows),
+            [jax.ShapeDtypeStruct(double, kind) for kind in kinds],
+            in_specs=[whole] * (2 * count + 4),
+            out_specs=[whole] * count,
+            scratch=[pltpu.VMEM((2 * count * pitch, width), BF16), pltpu.VMEM((count * pitch, width), BF16)],
+            vmem_mib=32,
+            name=name,
+        )(*rows_saved, *rows_double, *shares)
+
+    near = run_experts("experts_near", rows_b + swap_b, rows_two + swap_two, [F32] * experts + [BF16])
+    far = run_experts("experts_far", far_b, [after(far_two[0], near[0])] + far_two[1:], [BF16] * (experts - 1))
+    totals = [(near[j] + part.astype(F32)).astype(BF16) for j, part in enumerate(partners(far), 1)]
+    home = [shifted(total, "expert", -SPLIT * j) for j, total in enumerate(totals, 1)]
+    theirs = partners(near[experts:], *totals)
+
+    act_out, grad_out = local_call(
+        functools.partial(home_body, experts, rows),
+        [tokens, tokens],
+        in_specs=[scalar] + [whole] * (9 + experts),
+        out_specs=[whole] * 2,
+        name="home",
+    )(own, r_bwd, g_bwd, r_fwd, g_fwd, norm_gain, saved_in[0], upstream, incoming, near[0], theirs[0], *home)
     return (act_out[None], grad_out[None])
 
 

time: 107 us -> 111 us (1.037)
  waiting for transfers between devices: 61.2 us -> 73 us
  starting transfers between devices: 27.9 us -> 20 us
    ppermute x11 -> x7, waiting for transfers between devices: 38.9 us -> 58.4 us  [swapped(): return lax.ppermute(value, axis, [(i, i ^ bit) for i in range(count)])]
    ppermute x7 -> x5, waiting for transfers between devices: 22.3 us -> 14.6 us  [shifted(): lax.ppermute(value, axis, [(i, (i + steps) % count) for i in range(count)])]
    ppermute x7 -> x5, starting transfers between devices: 14.4 us -> 9.52 us  [shifted(): lax.ppermute(value, axis, [(i, (i + steps) % count) for i in range(count)])]
    ppermute x11 -> x7, starting transfers between devices: 13.5 us -> 10.5 us  [swapped(): return lax.ppermute(value, axis, [(i, i ^ bit) for i in range(count)])]
    pallas_call x6 -> x4, Pallas kernels: 11.4 us -> 11.6 us  [the longest x2 7.1 us: run_experts(): local_call(functools.partial(experts_body, count, rows), [jax.ShapeDtypeS...]
  transfers between devices with their start and end apart: 18 -> 12, of which waited for: 14 -> 9; matrix products, arithmetic and copies ran while one was open for 0% -> 0% of each run, Pallas kernels for 9% -> 5%
where the time goes in v10:
time: 111 us; the launch traced here: 109 us
  waiting for transfers between devices  73 us (66%)
  starting transfers between devices  20 us (18%)
  Pallas kernels  15.4 us (14%)
    ppermute x7, waiting for transfers between devices, swapped(): return lax.ppermute(value, axis, [(i, i ^ bit) for i in range(count)])  58.4 us
    ppermute x5, waiting for transfers between devices, shifted(): lax.ppermute(value, axis, [(i, (i + steps) % count) for i in range(count)])  14.6 us
    ppermute x7, starting transfers between devices, swapped(): return lax.ppermute(value, axis, [(i, i ^ bit) for i in range(count)])  10.5 us
    ppermute x5, starting transfers between devices, shifted(): lax.ppermute(value, axis, [(i, (i + steps) % count) for i in range(count)])  9.52 us
    pallas_call x2, Pallas kernels, run_experts(): local_call(functools.partial(experts_body, count, rows), [jax.ShapeDtypeS...  7.1 us
    pallas_call x1, Pallas kernels, per_device(): local_call(first_body, [jax.ShapeDtypeStruct((3 * w_down.shape[1], width)...  3.77 us
    pallas_call x1, Pallas kernels, per_device(): local_call(functools.partial(home_body, experts, rows), [tokens, tokens],...  2.98 us
  transfers between devices with their start and end apart: 12, of which 9 were waited for; matrix products, arithmetic and copies ran while one was open for 0% of the time, Pallas kernels for 5%

profile of v10, /device:TPU:0, one launch (start us, length us, event | category | flops | bytes accessed | tf_op | source)
XLA Modules:
  0.0 109.5 jit_solution(13300470362581510169)
XLA Ops:
  0.7 3.8 %join_weights_pack_saved.1 = (bf16[576,2048]{1,0:T(8,128)(2,1)}, bf16[264,512]{1,0:T(8,128)(2,1)}, bf16[264,512]{1,0:T(8,128)(2,1)}) custom-call(s32[1]{0:T(128)} %bitcast.own_ref, s32[1,128]{1,0:T(1,128)} %bitcast.28, f32[1,2048]{1,0:T(1,128)} %gain_ref.3, bf16[128,2048]{1,0:T(8,128)(2,1)} %bitcast.26, bf16[192,2048]{1,0:T(8,128)(2,1)} %bitcast.17, ...), custom_call_target="tpu_custom_call" | custom-call | flops 1000 | bytes 1000 | tf_op jit(solution)/shard_map/join_weights_pack_saved/pallas_call | solution.py:232
  4.5 0.0 copy-start
  4.5 0.0 copy-start.4
  4.5 3.0 %collective-permute-start.6 = (bf16[576,2048]{1,0:T(8,128)(2,1)}, bf16[576,2048]{1,0:T(8,128)(2,1)S(1)}, u32[]{:S(2)}, u32[]{:S(2)}) collective-permute-start(bf16[576,2048]{1,0:T(8,128)(2,1)} %get-tuple-element.24), channel_id=1, source_target_pairs={{0,1},{1,0},{2,3},{3,2},{4,5},{5,4},{6,7},{7,6},{8,9},{9,8},{10,11... | collective-permute-start | bytes 7077896 | tf_op jit(solution)/shard_map/ppermute | solution.py:26
  7.5 0.7 collective-permute-start
  8.2 0.0 collective-permute-start.1
  8.2 2.6 %collective-permute-start.2 = (bf16[264,512]{1,0:T(8,128)(2,1)}, bf16[264,512]{1,0:T(8,128)(2,1)S(1)}, u32[]{:S(2)}, u32[]{:S(2)}) collective-permute-start(bf16[264,512]{1,0:T(8,128)(2,1)} %get-tuple-element.19), channel_id=1, source_target_pairs={{0,4},{1,5},{2,6},{3,7},{4,0},{5,1},{6,2},{7,3},{8,12},{9,13},{10,... | collective-permute-start | bytes 811016 | tf_op jit(solution)/shard_map/ppermute | solution.py:21
  10.8 1.6 %collective-permute-start.3 = (bf16[264,512]{1,0:T(8,128)(2,1)}, bf16[264,512]{1,0:T(8,128)(2,1)S(1)}, u32[]{:S(2)}, u32[]{:S(2)}) collective-permute-start(bf16[264,512]{1,0:T(8,128)(2,1)} %get-tuple-element.18.refs_0_), channel_id=1, source_target_pairs={{0,2},{1,3},{2,0},{3,1},{4,6},{5,7},{6,4},{7,5},{8,10},{9,11},{10,... | collective-permute-start | bytes 811016 | tf_op jit(solution)/shard_map/ppermute | solution.py:26
  12.4 7.8 %collective-permute-done.grad_ref.up_ref = bf16[128,2048]{1,0:T(8,128)(2,1)S(1)} collective-permute-done((bf16[128,2048]{1,0:T(8,128)(2,1)S(1)}, bf16[128,2048]{1,0:T(8,128)(2,1)S(1)}, u32[]{:S(2)}, u32[]{:S(2)}) %collective-permute-start) | collective-permute-done | bytes 524320 | tf_op jit(solution)/shard_map/ppermute | solution.py:21
  20.2 1.6 %collective-permute-done.1.x_ref = bf16[128,2048]{1,0:T(8,128)(2,1)S(1)} collective-permute-done((bf16[128,2048]{1,0:T(8,128)(2,1)S(1)}, bf16[128,2048]{1,0:T(8,128)(2,1)S(1)}, u32[]{:S(2)}, u32[]{:S(2)}) %collective-permute-start.1) | collective-permute-done | bytes 524320 | tf_op jit(solution)/shard_map/ppermute | solution.py:21
  21.8 1.6 %pack_grad_and_act.1 = (bf16[528,512]{1,0:T(8,128)(2,1)S(1)}, bf16[528,512]{1,0:T(8,128)(2,1)S(1)}) custom-call(s32[1]{0:T(128)} %bitcast.own_ref, s32[1,128]{1,0:T(1,128)S(1)} %bitcast.29, s32[1,128]{1,0:T(1,128)S(1)} %bitcast.31, f32[1,2048]{1,0:T(1,128)S(1)} %copy-done.5, bf16[128,2048]{1,0:T(8,128)(2,1)S(1)} %collective-permute-done.grad_ref.up_ref, ...), custom_call_target="tpu_custom_call" | custom-call | flops 1000 | bytes 1000 | tf_op jit(solution)/shard_map/pack_grad_and_act/pallas_call | solution.py:251
  23.4 2.7 %collective-permute-start.4 = (bf16[528,512]{1,0:T(8,128)(2,1)S(1)}, bf16[528,512]{1,0:T(8,128)(2,1)S(1)}, u32[]{:S(2)}, u32[]{:S(2)}) collective-permute-start(bf16[528,512]{1,0:T(8,128)(2,1)S(1)} %get-tuple-element.22), channel_id=1, source_target_pairs={{0,4},{1,5},{2,6},{3,7},{4,0},{5,1},{6,2},{7,3},{8,12},{9,13},{10,... | collective-permute-start | bytes 1622024 | tf_op jit(solution)/shard_map/ppermute | solution.py:21
  26.1 0.0 collective-permute-done.2.refs_1_
  26.1 0.0 collective-permute-done.3.refs_2_
  26.1 1.6 %collective-permute-start.7 = (bf16[264,512]{1,0:T(8,128)(2,1)S(1)}, bf16[264,512]{1,0:T(8,128)(2,1)S(1)}, u32[]{:S(2)}, u32[]{:S(2)}) collective-permute-start(bf16[264,512]{1,0:T(8,128)(2,1)S(1)} %collective-permute-done.2.refs_1_), channel_id=1, source_target_pairs={{0,2},{1,3},{2,0},{3,1},{4,6},{5,7},{6,4},{7,5},{8,10},{9,11},{10,... | collective-permute-start | bytes 811016 | tf_op jit(solution)/shard_map/ppermute | solution.py:26
  27.6 0.4 collective-permute-start.5
  28.1 16.5 %collective-permute-done.7.refs_0_ = bf16[264,512]{1,0:T(8,128)(2,1)S(1)} collective-permute-done((bf16[264,512]{1,0:T(8,128)(2,1)S(1)}, bf16[264,512]{1,0:T(8,128)(2,1)S(1)}, u32[]{:S(2)}, u32[]{:S(2)}) %collective-permute-start.7) | collective-permute-done | bytes 270368 | tf_op jit(solution)/shard_map/ppermute | solution.py:26
  44.6 5.2 %collective-permute-done.4.refs_4_ = bf16[528,512]{1,0:T(8,128)(2,1)S(1)} collective-permute-done((bf16[528,512]{1,0:T(8,128)(2,1)S(1)}, bf16[528,512]{1,0:T(8,128)(2,1)S(1)}, u32[]{:S(2)}, u32[]{:S(2)}) %collective-permute-start.4) | collective-permute-done | bytes 540704 | tf_op jit(solution)/shard_map/ppermute | solution.py:21
  49.8 0.6 collective-permute-start.8
  50.4 7.1 %collective-permute-done.5.refs_5_ = bf16[528,512]{1,0:T(8,128)(2,1)S(1)} collective-permute-done((bf16[528,512]{1,0:T(8,128)(2,1)S(1)}, bf16[528,512]{1,0:T(8,128)(2,1)S(1)}, u32[]{:S(2)}, u32[]{:S(2)}) %collective-permute-start.5) | collective-permute-done | bytes 540704 | tf_op jit(solution)/shard_map/ppermute | solution.py:26
  57.5 1.4 %collective-permute-done.6.refs_9_.refs_5_ = bf16[576,2048]{1,0:T(8,128)(2,1)S(1)} collective-permute-done((bf16[576,2048]{1,0:T(8,128)(2,1)}, bf16[576,2048]{1,0:T(8,128)(2,1)S(1)}, u32[]{:S(2)}, u32[]{:S(2)}) %collective-permute-start.6) | collective-permute-done | bytes 2359328 | tf_op jit(solution)/shard_map/ppermute | solution.py:26
  59.0 4.4 %experts_near.1 = (f32[528,512]{1,0:T(8,128)S(1)}, f32[528,512]{1,0:T(8,128)S(1)}, bf16[528,512]{1,0:T(8,128)(2,1)S(1)}) custom-call(bf16[264,512]{1,0:T(8,128)(2,1)S(1)} %copy-done.4, bf16[264,512]{1,0:T(8,128)(2,1)S(1)} %collective-permute-done.2.refs_1_, bf16[264,512]{1,0:T(8,128)(2,1)S(1)} %collective-permute-done.3.refs_2_, ...), custom_call_target="tpu_custom_call" | custom-call | flops 1000 | bytes 1000 | tf_op jit(solution)/shard_map/experts_near/pallas_call | solution.py:265
  63.4 4.0 %collective-permute-done.8.refs_1_ = bf16[528,512]{1,0:T(8,128)(2,1)S(1)} collective-permute-done((bf16[528,512]{1,0:T(8,128)(2,1)S(1)}, bf16[528,512]{1,0:T(8,128)(2,1)S(1)}, u32[]{:S(2)}, u32[]{:S(2)}) %collective-permute-start.8) | collective-permute-done | bytes 540704 | tf_op jit(solution)/shard_map/ppermute | solution.py:26
  67.4 2.7 %experts_far.1 = bf16[528,512]{1,0:T(8,128)(2,1)S(1)} custom-call(bf16[264,512]{1,0:T(8,128)(2,1)S(1)} %collective-permute-done.7.refs_0_, bf16[528,512]{1,0:T(8,128)(2,1)S(1)} %collective-permute-done.8.refs_1_, bf16[192,2048]{1,0:T(8,128)(2,1)S(1)} %bitcast.19, bf16[192,2048]{1,0:T(8,128)(2,1)S(1)} %bitcast.22, bf16[192,2048]{1,0:T(8,128)(2,1)S(1)} %bitcast.25, ...), custom_call_target="tpu_custom_call" | custom-call | flops 1000 | bytes 1000 | tf_op jit(solution)/shard_map/experts_far/pallas_call | solution.py:265
  70.1 1.5 %collective-permute-start.9 = (bf16[528,512]{1,0:T(8,128)(2,1)S(1)}, bf16[528,512]{1,0:T(8,128)(2,1)S(1)}, u32[]{:S(2)}, u32[]{:S(2)}) collective-permute-start(bf16[528,512]{1,0:T(8,128)(2,1)S(1)} %experts_far.1), channel_id=1, source_target_pairs={{0,2},{1,3},{2,0},{3,1},{4,6},{5,7},{6,4},{7,5},{8,10},{9,11},{10,... | collective-permute-start | bytes 1622024 | tf_op jit(solution)/shard_map/ppermute | solution.py:26
  71.6 11.1 %collective-permute-done.9 = bf16[528,512]{1,0:T(8,128)(2,1)S(1)} collective-permute-done((bf16[528,512]{1,0:T(8,128)(2,1)S(1)}, bf16[528,512]{1,0:T(8,128)(2,1)S(1)}, u32[]{:S(2)}, u32[]{:S(2)}) %collective-permute-start.9) | collective-permute-done | bytes 540704 | tf_op jit(solution)/shard_map/ppermute | solution.py:26
  82.7 0.2 add_convert_fusion
  82.9 1.8 %collective-permute-start.10 = (bf16[528,512]{1,0:T(8,128)(2,1)S(1)}, bf16[528,512]{1,0:T(8,128)(2,1)S(1)}, u32[]{:S(2)}, u32[]{:S(2)}) collective-permute-start(bf16[528,512]{1,0:T(8,128)(2,1)S(1)} %get-tuple-element.31), channel_id=1, source_target_pairs={{0,2},{1,3},{2,0},{3,1},{4,6},{5,7},{6,4},{7,5},{8,10},{9,11},{10,... | collective-permute-start | bytes 1622024 | tf_op jit(solution)/shard_map/ppermute | solution.py:26
  84.7 3.6 %collective-permute-start.11 = (bf16[528,512]{1,0:T(8,128)(2,1)S(1)}, bf16[528,512]{1,0:T(8,128)(2,1)S(1)}, u32[]{:S(2)}, u32[]{:S(2)}) collective-permute-start(bf16[528,512]{1,0:T(8,128)(2,1)S(1)} %add_convert_fusion), channel_id=1, source_target_pairs={{0,4},{1,5},{2,6},{3,7},{4,0},{5,1},{6,2},{7,3},{8,12},{9,13},{10,... | collective-permute-start | bytes 1622024 | tf_op jit(solution)/shard_map/ppermute | solution.py:21
  88.3 18.2 %collective-permute-done.10.refs_1_ = bf16[528,512]{1,0:T(8,128)(2,1)S(1)} collective-permute-done((bf16[528,512]{1,0:T(8,128)(2,1)S(1)}, bf16[528,512]{1,0:T(8,128)(2,1)S(1)}, u32[]{:S(2)}, u32[]{:S(2)}) %collective-permute-start.10) | collective-permute-done | bytes 540704 | tf_op jit(solution)/shard_map/ppermute | solution.py:26
  106.5 0.0 collective-permute-done.11.refs_2_
  106.5 3.0 %home.1 = (bf16[128,2048]{1,0:T(8,128)(2,1)}, bf16[128,2048]{1,0:T(8,128)(2,1)}) custom-call(s32[1]{0:T(128)} %bitcast.own_ref, s32[1,128]{1,0:T(1,128)S(1)} %bitcast.30, f32[1,128]{1,0:T(1,128)S(1)} %bitcast.33, s32[1,128]{1,0:T(1,128)S(1)} %bitcast.32, f32[1,128]{1,0:T(1,128)S(1)} %bitcast.34, f32[1,2048]{1,0:T(1,128)S(1)} %copy-done.5, ...), custom_call_target="tpu_custom_call" | custom-call | flops 1000 | bytes 1000 | tf_op jit(solution)/shard_map/home/pallas_call | solution.py:281
  (22 shorter events, 0.0 us)
Async XLA Ops:
  0.6 6.9 %copy-start.10 = (bf16[1,128,2048]{2,1,0:T(8,128)(2,1)S(1)}, bf16[1,128,2048]{2,1,0:T(8,128)(2,1)}, u32[]{:S(2)}) copy-start(bf16[1,128,2048]{2,1,0:T(8,128)(2,1)} %param.13) | copy-start | bytes 1572868
  0.7 7.6 %copy-start.11 = (bf16[1,128,2048]{2,1,0:T(8,128)(2,1)S(1)}, bf16[1,128,2048]{2,1,0:T(8,128)(2,1)}, u32[]{:S(2)}) copy-start(bf16[1,128,2048]{2,1,0:T(8,128)(2,1)} %param.11) | copy-start | bytes 1572868
  0.7 21.2 %copy-start.5 = (f32[1,2048]{1,0:T(1,128)S(1)}, f32[1,2048]{1,0:T(1,128)}, u32[]{:S(2)}) copy-start(f32[1,2048]{1,0:T(1,128)} %gain_ref.3) | copy-start | bytes 24580
  0.7 21.2 %copy-start.6 = (s32[1,128,1]{1,2,0:T(1,128)S(1)}, s32[1,128,1]{1,2,0:T(1,128)}, u32[]{:S(2)}) copy-start(s32[1,128,1]{1,2,0:T(1,128)} %param.20) | copy-start | bytes 1540
  0.7 21.1 %copy-start.7 = (s32[1,128,1]{1,2,0:T(1,128)S(1)}, s32[1,128,1]{1,2,0:T(1,128)}, u32[]{:S(2)}) copy-start(s32[1,128,1]{1,2,0:T(1,128)} %param.18) | copy-start | bytes 1540
  0.7 58.3 %copy-start.1 = (bf16[1,2048,192]{1,2,0:T(8,128)(2,1)S(1)}, bf16[1,2048,192]{1,2,0:T(8,128)(2,1)}, u32[]{:S(2)}) copy-start(bf16[1,2048,192]{1,2,0:T(8,128)(2,1)} %param.16) | copy-start | bytes 2359300
  0.7 58.3 %copy-start.2 = (bf16[1,192,2048]{2,1,0:T(8,128)(2,1)S(1)}, bf16[1,192,2048]{2,1,0:T(8,128)(2,1)}, u32[]{:S(2)}) copy-start(bf16[1,192,2048]{2,1,0:T(8,128)(2,1)} %param.17) | copy-start | bytes 2359300
  4.5 54.5 %copy-start = (bf16[1,2048,192]{1,2,0:T(8,128)(2,1)S(1)}, bf16[1,2048,192]{1,2,0:T(8,128)(2,1)}, u32[]{:S(2)}) copy-start(bf16[1,2048,192]{1,2,0:T(8,128)(2,1)} %param.15) | copy-start | bytes 2359300
  4.5 54.5 %copy-start.4 = (bf16[264,512]{1,0:T(8,128)(2,1)S(1)}, bf16[264,512]{1,0:T(8,128)(2,1)}, u32[]{:S(2)}) copy-start(bf16[264,512]{1,0:T(8,128)(2,1)} %get-tuple-element.18.refs_0_) | copy-start | bytes 811012
  4.5 54.5 %collective-permute-start.6 = (bf16[576,2048]{1,0:T(8,128)(2,1)}, bf16[576,2048]{1,0:T(8,128)(2,1)S(1)}, u32[]{:S(2)}, u32[]{:S(2)}) collective-permute-start(bf16[576,2048]{1,0:T(8,128)(2,1)} %get-tuple-element.24), channel_id=1, source_target_pairs={{0,1},{1,0},{2,3},{3,2},{4,5},{5,4},{6,7},{7,6},{8,9},{9,8},{10,11... | collective-permute-start | bytes 7077896 | tf_op jit(solution)/shard_map/ppermute | solution.py:26
  7.5 12.7 %collective-permute-start = (bf16[128,2048]{1,0:T(8,128)(2,1)S(1)}, bf16[128,2048]{1,0:T(8,128)(2,1)S(1)}, u32[]{:S(2)}, u32[]{:S(2)}) collective-permute-start(bf16[128,2048]{1,0:T(8,128)(2,1)S(1)} %bitcast.35), channel_id=1, source_target_pairs={{0,24},{8,0},{16,8},{24,16},{1,25},{9,1},{17,9},{25,17},{2,26},{10... | collective-permute-start | bytes 1572872 | tf_op jit(solution)/shard_map/ppermute | solution.py:21
  8.2 13.6 %collective-permute-start.1 = (bf16[128,2048]{1,0:T(8,128)(2,1)S(1)}, bf16[128,2048]{1,0:T(8,128)(2,1)S(1)}, u32[]{:S(2)}, u32[]{:S(2)}) collective-permute-start(bf16[128,2048]{1,0:T(8,128)(2,1)S(1)} %bitcast.36), channel_id=1, source_target_pairs={{0,8},{8,16},{16,24},{24,0},{1,9},{9,17},{17,25},{25,1},{2,10},{10... | collective-permute-start | bytes 1572872 | tf_op jit(solution)/shard_map/ppermute | solution.py:21
  8.2 17.8 %collective-permute-start.2 = (bf16[264,512]{1,0:T(8,128)(2,1)}, bf16[264,512]{1,0:T(8,128)(2,1)S(1)}, u32[]{:S(2)}, u32[]{:S(2)}) collective-permute-start(bf16[264,512]{1,0:T(8,128)(2,1)} %get-tuple-element.19), channel_id=1, source_target_pairs={{0,4},{1,5},{2,6},{3,7},{4,0},{5,1},{6,2},{7,3},{8,12},{9,13},{10,... | collective-permute-start | bytes 811016 | tf_op jit(solution)/shard_map/ppermute | solution.py:21
  10.8 15.3 %collective-permute-start.3 = (bf16[264,512]{1,0:T(8,128)(2,1)}, bf16[264,512]{1,0:T(8,128)(2,1)S(1)}, u32[]{:S(2)}, u32[]{:S(2)}) collective-permute-start(bf16[264,512]{1,0:T(8,128)(2,1)} %get-tuple-element.18.refs_0_), channel_id=1, source_target_pairs={{0,2},{1,3},{2,0},{3,1},{4,6},{5,7},{6,4},{7,5},{8,10},{9,11},{10,... | collective-permute-start | bytes 811016 | tf_op jit(solution)/shard_map/ppermute | solution.py:26
  23.4 26.4 %collective-permute-start.4 = (bf16[528,512]{1,0:T(8,128)(2,1)S(1)}, bf16[528,512]{1,0:T(8,128)(2,1)S(1)}, u32[]{:S(2)}, u32[]{:S(2)}) collective-permute-start(bf16[528,512]{1,0:T(8,128)(2,1)S(1)} %get-tuple-element.22), channel_id=1, source_target_pairs={{0,4},{1,5},{2,6},{3,7},{4,0},{5,1},{6,2},{7,3},{8,12},{9,13},{10,... | collective-permute-start | bytes 1622024 | tf_op jit(solution)/shard_map/ppermute | solution.py:21
  26.1 18.5 %collective-permute-start.7 = (bf16[264,512]{1,0:T(8,128)(2,1)S(1)}, bf16[264,512]{1,0:T(8,128)(2,1)S(1)}, u32[]{:S(2)}, u32[]{:S(2)}) collective-permute-start(bf16[264,512]{1,0:T(8,128)(2,1)S(1)} %collective-permute-done.2.refs_1_), channel_id=1, source_target_pairs={{0,2},{1,3},{2,0},{3,1},{4,6},{5,7},{6,4},{7,5},{8,10},{9,11},{10,... | collective-permute-start | bytes 811016 | tf_op jit(solution)/shard_map/ppermute | solution.py:26
  27.6 29.9 %collective-permute-start.5 = (bf16[528,512]{1,0:T(8,128)(2,1)S(1)}, bf16[528,512]{1,0:T(8,128)(2,1)S(1)}, u32[]{:S(2)}, u32[]{:S(2)}) collective-permute-start(bf16[528,512]{1,0:T(8,128)(2,1)S(1)} %get-tuple-element.23.refs_3_), channel_id=1, source_target_pairs={{0,2},{1,3},{2,0},{3,1},{4,6},{5,7},{6,4},{7,5},{8,10},{9,11},{10,... | collective-permute-start | bytes 1622024 | tf_op jit(solution)/shard_map/ppermute | solution.py:26
  49.8 17.6 %collective-permute-start.8 = (bf16[528,512]{1,0:T(8,128)(2,1)S(1)}, bf16[528,512]{1,0:T(8,128)(2,1)S(1)}, u32[]{:S(2)}, u32[]{:S(2)}) collective-permute-start(bf16[528,512]{1,0:T(8,128)(2,1)S(1)} %collective-permute-done.4.refs_4_), channel_id=1, source_target_pairs={{0,2},{1,3},{2,0},{3,1},{4,6},{5,7},{6,4},{7,5},{8,10},{9,11},{10,... | collective-permute-start | bytes 1622024 | tf_op jit(solution)/shard_map/ppermute | solution.py:26
  70.1 12.6 %collective-permute-start.9 = (bf16[528,512]{1,0:T(8,128)(2,1)S(1)}, bf16[528,512]{1,0:T(8,128)(2,1)S(1)}, u32[]{:S(2)}, u32[]{:S(2)}) collective-permute-start(bf16[528,512]{1,0:T(8,128)(2,1)S(1)} %experts_far.1), channel_id=1, source_target_pairs={{0,2},{1,3},{2,0},{3,1},{4,6},{5,7},{6,4},{7,5},{8,10},{9,11},{10,... | collective-permute-start | bytes 1622024 | tf_op jit(solution)/shard_map/ppermute | solution.py:26
  82.7 23.7 %copy-start.3 = (bf16[1,128,2048]{2,1,0:T(8,128)(2,1)S(1)}, bf16[1,128,2048]{2,1,0:T(8,128)(2,1)}, u32[]{:S(2)}) copy-start(bf16[1,128,2048]{2,1,0:T(8,128)(2,1)} %param.12) | copy-start | bytes 1572868
  82.7 23.7 %copy-start.8 = (f32[1,128,1]{1,2,0:T(1,128)S(1)}, f32[1,128,1]{1,2,0:T(1,128)}, u32[]{:S(2)}) copy-start(f32[1,128,1]{1,2,0:T(1,128)} %param.21) | copy-start | bytes 1540
  82.7 23.7 %copy-start.9 = (f32[1,128,1]{1,2,0:T(1,128)S(1)}, f32[1,128,1]{1,2,0:T(1,128)}, u32[]{:S(2)}) copy-start(f32[1,128,1]{1,2,0:T(1,128)} %param.19) | copy-start | bytes 1540
  82.9 23.5 %collective-permute-start.10 = (bf16[528,512]{1,0:T(8,128)(2,1)S(1)}, bf16[528,512]{1,0:T(8,128)(2,1)S(1)}, u32[]{:S(2)}, u32[]{:S(2)}) collective-permute-start(bf16[528,512]{1,0:T(8,128)(2,1)S(1)} %get-tuple-element.31), channel_id=1, source_target_pairs={{0,2},{1,3},{2,0},{3,1},{4,6},{5,7},{6,4},{7,5},{8,10},{9,11},{10,... | collective-permute-start | bytes 1622024 | tf_op jit(solution)/shard_map/ppermute | solution.py:26
  84.7 21.8 %collective-permute-start.11 = (bf16[528,512]{1,0:T(8,128)(2,1)S(1)}, bf16[528,512]{1,0:T(8,128)(2,1)S(1)}, u32[]{:S(2)}, u32[]{:S(2)}) collective-permute-start(bf16[528,512]{1,0:T(8,128)(2,1)S(1)} %add_convert_fusion), channel_id=1, source_target_pairs={{0,4},{1,5},{2,6},{3,7},{4,0},{5,1},{6,2},{7,3},{8,12},{9,13},{10,... | collective-permute-start | bytes 1622024 | tf_op jit(solution)/shard_map/ppermute | solution.py:21

commit v11 on v8

--- a/solution.py
+++ b/solution.py
@@ -93,8 +93,9 @@
     pack(x_ref[...], own_ref, routes_ref, outs)
 
 
-def pack_act_body(own_ref, routes_ref, gain_ref, x_ref, *outs):
-    pack(normed(x_ref, gain_ref), own_ref, routes_ref, outs)
+def pack_act_body(own_ref, routes_ref, gain_ref, x_ref, kept_ref, *outs):
+    pack(normed(x_ref, gain_ref), own_ref, routes_ref, outs[:-1])
+    outs[-1][...] = kept_ref[...]
 
 
 def first_body(own_ref, *refs):
@@ -110,10 +111,10 @@
     for copy in fetch:
         copy.wait()
     routes_ref, gain_ref, x_ref = held
-    pack(normed(x_ref, gain_ref), own_ref, routes_ref, outs)
     for i in range(3):
         load[i].wait()
         store[i].start()
+    pack(normed(x_ref, gain_ref), own_ref, routes_ref, outs)
     for copy in store:
         copy.wait()
 
@@ -274,19 +275,18 @@
         name="pack_grad",
     )(own, r_bwd, after(upstream, packed_b[0]))
     rows_g = crossed(packed_g)
-    packed_f = local_call(
+    *packed_f, kept_b = local_call(
         pack_act_body,
-        packed,
-        in_specs=[scalar] + [whole] * 3,
-        out_specs=[whole] * experts,
+        packed + packed[:1],
+        in_specs=[scalar] + [whole] * 4,
+        out_specs=[whole] * (experts + 1),
         name="pack_act",
-    )(own, r_fwd, norm_gain, after(incoming, packed_g[0], rows_b[-1]))
+    )(own, r_fwd, norm_gain, after(incoming, packed_g[0], rows_b[-1]), packed_b[0])
     rows_f = crossed(packed_f)
     swap_g = partners(rows_g[:1], rows_b[-1])
-    swap_f = partners(rows_f[:1], rows_g[-1])
-    rows_b = rows_b + swap_b + partners(rows_b[1:], swap_b[0])
-    rows_g = rows_g + swap_g + partners(rows_g[1:], swap_g[0])
-    rows_f = rows_f + swap_f + partners(rows_f[1:], swap_f[0], rows_b[-1])
+    rows_b = [kept_b] + rows_b[1:] + swap_b + partners(rows_b[1:], swap_b[0])
+    rows_g = rows_g + swap_g + partners(rows_g[1:])
+    rows_f = rows_f + partners(rows_f, rows_g[-1], rows_b[-1])
 
     count = 2 * experts
     partial_b = local_call(

time: 106 us -> 106 us (level)
  waiting for transfers between devices: 58.6 us -> 60.6 us
    ppermute x7, waiting for transfers between devices: 20.7 us -> 35 us  [shifted(): lax.ppermute(value, axis, [(i, (i + steps) % count) for i in range(count)])]
    ppermute x11, waiting for transfers between devices: 37.9 us -> 25.5 us  [swapped(): return lax.ppermute(value, axis, [(i, i ^ bit) for i in range(count)])]
    ppermute x7, starting transfers between devices: 17.9 us -> 16.1 us  [shifted(): lax.ppermute(value, axis, [(i, (i + steps) % count) for i in range(count)])]
where the time goes in v11:
time: 106 us
  waiting for transfers between devices  60.6 us (57%)
  starting transfers between devices  28.3 us (27%)
  Pallas kernels  15.2 us (14%)
    ppermute x7, waiting for transfers between devices, shifted(): lax.ppermute(value, axis, [(i, (i + steps) % count) for i in range(count)])  35 us
    ppermute x11, waiting for transfers between devices, swapped(): return lax.ppermute(value, axis, [(i, i ^ bit) for i in range(count)])  25.5 us
    ppermute x7, starting transfers between devices, shifted(): lax.ppermute(value, axis, [(i, (i + steps) % count) for i in range(count)])  16.1 us
    ppermute x11, starting transfers between devices, swapped(): return lax.ppermute(value, axis, [(i, i ^ bit) for i in range(count)])  12.1 us
    pallas_call x1, Pallas kernels, per_device(): local_call(first_body, [jax.ShapeDtypeStruct((3 * w_down.shape[1], width)...  3.76 us
    pallas_call x1, Pallas kernels, per_device(): local_call(functools.partial(backward_body, count, rows), partial, scratc...  3.64 us
    pallas_call x1, Pallas kernels, per_device(): local_call(functools.partial(forward_body, count, rows), partial, scratch...  2.25 us
  transfers between devices with their start and end apart: 18, of which 14 were waited for; matrix products, arithmetic and copies ran while one was open for 0% of the time, Pallas kernels for 9%

profile of v11, /device:TPU:0, one launch (start us, length us, event | category | flops | bytes accessed | tf_op | source)
XLA Modules:
  0.0 106.0 jit_solution(7534976514934441082)
XLA Ops:
  0.7 3.8 %join_weights_pack_saved.1 = (bf16[576,2048]{1,0:T(8,128)(2,1)}, bf16[264,512]{1,0:T(8,128)(2,1)}, bf16[264,512]{1,0:T(8,128)(2,1)}) custom-call(s32[1]{0:T(128)} %bitcast.own_ref, s32[1,128]{1,0:T(1,128)} %bitcast.28, f32[1,2048]{1,0:T(1,128)} %gain_ref.3, bf16[128,2048]{1,0:T(8,128)(2,1)} %bitcast.26, bf16[192,2048]{1,0:T(8,128)(2,1)} %bitcast.17, ...), custom_call_target="tpu_custom_call" | custom-call | flops 1000 | bytes 1000 | tf_op jit(solution)/shard_map/join_weights_pack_saved/pallas_call | solution.py:251
  4.5 3.0 %collective-permute-start.8 = (bf16[576,2048]{1,0:T(8,128)(2,1)}, bf16[576,2048]{1,0:T(8,128)(2,1)S(1)}, u32[]{:S(2)}, u32[]{:S(2)}) collective-permute-start(bf16[576,2048]{1,0:T(8,128)(2,1)} %get-tuple-element.37), channel_id=1, source_target_pairs={{0,1},{1,0},{2,3},{3,2},{4,5},{5,4},{6,7},{7,6},{8,9},{9,8},{10,11... | collective-permute-start | bytes 7077896 | tf_op jit(solution)/shard_map/ppermute | solution.py:26
  8.2 2.6 %collective-permute-start.2 = (bf16[264,512]{1,0:T(8,128)(2,1)}, bf16[264,512]{1,0:T(8,128)(2,1)S(1)}, u32[]{:S(2)}, u32[]{:S(2)}) collective-permute-start(bf16[264,512]{1,0:T(8,128)(2,1)} %get-tuple-element.30), channel_id=1, source_target_pairs={{0,4},{1,5},{2,6},{3,7},{4,0},{5,1},{6,2},{7,3},{8,12},{9,13},{10,... | collective-permute-start | bytes 811016 | tf_op jit(solution)/shard_map/ppermute | solution.py:21
  10.8 1.6 %collective-permute-start.3 = (bf16[264,512]{1,0:T(8,128)(2,1)}, bf16[264,512]{1,0:T(8,128)(2,1)S(1)}, u32[]{:S(2)}, u32[]{:S(2)}) collective-permute-start(bf16[264,512]{1,0:T(8,128)(2,1)} %get-tuple-element.27.kept_ref), channel_id=1, source_target_pairs={{0,2},{1,3},{2,0},{3,1},{4,6},{5,7},{6,4},{7,5},{8,10},{9,11},{10,... | collective-permute-start | bytes 811016 | tf_op jit(solution)/shard_map/ppermute | solution.py:26
  12.3 7.7 %collective-permute-done.1.x_ref.up_ref = bf16[128,2048]{1,0:T(8,128)(2,1)S(1)} collective-permute-done((bf16[128,2048]{1,0:T(8,128)(2,1)S(1)}, bf16[128,2048]{1,0:T(8,128)(2,1)S(1)}, u32[]{:S(2)}, u32[]{:S(2)}) %collective-permute-start.1) | collective-permute-done | bytes 524320 | tf_op jit(solution)/shard_map/ppermute | solution.py:21
  20.1 0.9 pack_grad.1
  21.0 2.6 %collective-permute-start.5 = (bf16[264,512]{1,0:T(8,128)(2,1)S(1)}, bf16[264,512]{1,0:T(8,128)(2,1)S(1)}, u32[]{:S(2)}, u32[]{:S(2)}) collective-permute-start(bf16[264,512]{1,0:T(8,128)(2,1)S(1)} %get-tuple-element.35), channel_id=1, source_target_pairs={{0,4},{1,5},{2,6},{3,7},{4,0},{5,1},{6,2},{7,3},{8,12},{9,13},{10,... | collective-permute-start | bytes 811016 | tf_op jit(solution)/shard_map/ppermute | solution.py:21
  23.6 0.9 collective-permute-done.2.refs_1_
  24.7 1.4 %collective-permute-start.4 = (bf16[264,512]{1,0:T(8,128)(2,1)S(1)}, bf16[264,512]{1,0:T(8,128)(2,1)S(1)}, u32[]{:S(2)}, u32[]{:S(2)}) collective-permute-start(bf16[264,512]{1,0:T(8,128)(2,1)S(1)} %collective-permute-done.2.refs_1_), channel_id=1, source_target_pairs={{0,2},{1,3},{2,0},{3,1},{4,6},{5,7},{6,4},{7,5},{8,10},{9,11},{10,... | collective-permute-start | bytes 811016 | tf_op jit(solution)/shard_map/ppermute | solution.py:26
  26.2 0.9 copy-done.4
  27.1 0.9 pack_act.1
  28.0 2.4 %collective-permute-start.9 = (bf16[264,512]{1,0:T(8,128)(2,1)S(1)}, bf16[264,512]{1,0:T(8,128)(2,1)S(1)}, u32[]{:S(2)}, u32[]{:S(2)}) collective-permute-start(bf16[264,512]{1,0:T(8,128)(2,1)S(1)} %get-tuple-element.40), channel_id=1, source_target_pairs={{0,4},{1,5},{2,6},{3,7},{4,0},{5,1},{6,2},{7,3},{8,12},{9,13},{10,... | collective-permute-start | bytes 811016 | tf_op jit(solution)/shard_map/ppermute | solution.py:21
  30.4 6.7 %collective-permute-done.5.refs_5_ = bf16[264,512]{1,0:T(8,128)(2,1)S(1)} collective-permute-done((bf16[264,512]{1,0:T(8,128)(2,1)S(1)}, bf16[264,512]{1,0:T(8,128)(2,1)S(1)}, u32[]{:S(2)}, u32[]{:S(2)}) %collective-permute-start.5) | collective-permute-done | bytes 270368 | tf_op jit(solution)/shard_map/ppermute | solution.py:21
  37.8 1.4 %collective-permute-start.6 = (bf16[264,512]{1,0:T(8,128)(2,1)S(1)}, bf16[264,512]{1,0:T(8,128)(2,1)S(1)}, u32[]{:S(2)}, u32[]{:S(2)}) collective-permute-start(bf16[264,512]{1,0:T(8,128)(2,1)S(1)} %get-tuple-element.36.refs_4_), channel_id=1, source_target_pairs={{0,2},{1,3},{2,0},{3,1},{4,6},{5,7},{6,4},{7,5},{8,10},{9,11},{10,... | collective-permute-start | bytes 811016 | tf_op jit(solution)/shard_map/ppermute | solution.py:26
  39.1 9.6 %collective-permute-done.9.refs_1_ = bf16[264,512]{1,0:T(8,128)(2,1)S(1)} collective-permute-done((bf16[264,512]{1,0:T(8,128)(2,1)S(1)}, bf16[264,512]{1,0:T(8,128)(2,1)S(1)}, u32[]{:S(2)}, u32[]{:S(2)}) %collective-permute-start.9) | collective-permute-done | bytes 270368 | tf_op jit(solution)/shard_map/ppermute | solution.py:21
  48.8 2.4 %collective-permute-done.7.refs_7_ = bf16[264,512]{1,0:T(8,128)(2,1)S(1)} collective-permute-done((bf16[264,512]{1,0:T(8,128)(2,1)S(1)}, bf16[264,512]{1,0:T(8,128)(2,1)S(1)}, u32[]{:S(2)}, u32[]{:S(2)}) %collective-permute-start.7) | collective-permute-done | bytes 270368 | tf_op jit(solution)/shard_map/ppermute | solution.py:26
  51.1 2.0 %collective-permute-start.10 = (bf16[264,512]{1,0:T(8,128)(2,1)S(1)}, bf16[264,512]{1,0:T(8,128)(2,1)S(1)}, u32[]{:S(2)}, u32[]{:S(2)}) collective-permute-start(bf16[264,512]{1,0:T(8,128)(2,1)S(1)} %get-tuple-element.41.refs_0_), channel_id=1, source_target_pairs={{0,2},{1,3},{2,0},{3,1},{4,6},{5,7},{6,4},{7,5},{8,10},{9,11},{10,... | collective-permute-start | bytes 811016 | tf_op jit(solution)/shard_map/ppermute | solution.py:26
  53.1 3.8 %collective-permute-done.6.refs_6_ = bf16[264,512]{1,0:T(8,128)(2,1)S(1)} collective-permute-done((bf16[264,512]{1,0:T(8,128)(2,1)S(1)}, bf16[264,512]{1,0:T(8,128)(2,1)S(1)}, u32[]{:S(2)}, u32[]{:S(2)}) %collective-permute-start.6) | collective-permute-done | bytes 270368 | tf_op jit(solution)/shard_map/ppermute | solution.py:26
  56.9 2.0 %collective-permute-done.8.refs_11_.refs_7_ = bf16[576,2048]{1,0:T(8,128)(2,1)S(1)} collective-permute-done((bf16[576,2048]{1,0:T(8,128)(2,1)}, bf16[576,2048]{1,0:T(8,128)(2,1)S(1)}, u32[]{:S(2)}, u32[]{:S(2)}) %collective-permute-start.8) | collective-permute-done | bytes 2359328 | tf_op jit(solution)/shard_map/ppermute | solution.py:26
  59.0 3.6 %experts_bwd.1 = (f32[264,512]{1,0:T(8,128)S(1)}, f32[264,512]{1,0:T(8,128)S(1)}, bf16[264,512]{1,0:T(8,128)(2,1)S(1)}, bf16[264,512]{1,0:T(8,128)(2,1)S(1)}) custom-call(bf16[264,512]{1,0:T(8,128)(2,1)S(1)} %get-tuple-element.33.refs_0_, bf16[264,512]{1,0:T(8,128)(2,1)S(1)} %collective-permute-done.2.refs_1_, ...), custom_call_target="tpu_custom_call" | custom-call | flops 1000 | bytes 1000 | tf_op jit(solution)/shard_map/experts_bwd/pallas_call | solution.py:292
  62.6 1.9 %collective-permute-start.13 = (bf16[264,512]{1,0:T(8,128)(2,1)S(1)}, bf16[264,512]{1,0:T(8,128)(2,1)S(1)}, u32[]{:S(2)}, u32[]{:S(2)}) collective-permute-start(bf16[264,512]{1,0:T(8,128)(2,1)S(1)} %get-tuple-element.49), channel_id=1, source_target_pairs={{0,2},{1,3},{2,0},{3,1},{4,6},{5,7},{6,4},{7,5},{8,10},{9,11},{10,... | collective-permute-start | bytes 811016 | tf_op jit(solution)/shard_map/ppermute | solution.py:26
  64.5 4.0 %collective-permute-done.10.refs_2_ = bf16[264,512]{1,0:T(8,128)(2,1)S(1)} collective-permute-done((bf16[264,512]{1,0:T(8,128)(2,1)S(1)}, bf16[264,512]{1,0:T(8,128)(2,1)S(1)}, u32[]{:S(2)}, u32[]{:S(2)}) %collective-permute-start.10) | collective-permute-done | bytes 270368 | tf_op jit(solution)/shard_map/ppermute | solution.py:26
  68.5 2.3 %experts_fwd.1 = (f32[264,512]{1,0:T(8,128)S(1)}, f32[264,512]{1,0:T(8,128)S(1)}, bf16[264,512]{1,0:T(8,128)(2,1)S(1)}, bf16[264,512]{1,0:T(8,128)(2,1)S(1)}) custom-call(bf16[264,512]{1,0:T(8,128)(2,1)S(1)} %get-tuple-element.41.refs_0_, bf16[264,512]{1,0:T(8,128)(2,1)S(1)} %collective-permute-done.9.refs_1_, ...), custom_call_target="tpu_custom_call" | custom-call | flops 1000 | bytes 1000 | tf_op jit(solution)/shard_map/experts_fwd/pallas_call | solution.py:295
  70.9 3.4 %collective-permute-done.13 = bf16[264,512]{1,0:T(8,128)(2,1)S(1)} collective-permute-done((bf16[264,512]{1,0:T(8,128)(2,1)S(1)}, bf16[264,512]{1,0:T(8,128)(2,1)S(1)}, u32[]{:S(2)}, u32[]{:S(2)}) %collective-permute-start.13) | collective-permute-done | bytes 270368 | tf_op jit(solution)/shard_map/ppermute | solution.py:26
  74.5 5.1 %collective-permute-start.17 = (bf16[264,512]{1,0:T(8,128)(2,1)S(1)}, bf16[264,512]{1,0:T(8,128)(2,1)S(1)}, u32[]{:S(2)}, u32[]{:S(2)}) collective-permute-start(bf16[264,512]{1,0:T(8,128)(2,1)S(1)} %add_convert_fusion), channel_id=1, source_target_pairs={{0,4},{1,5},{2,6},{3,7},{4,0},{5,1},{6,2},{7,3},{8,12},{9,13},{10,... | collective-permute-start | bytes 811016 | tf_op jit(solution)/shard_map/ppermute | solution.py:21
  79.6 6.5 %collective-permute-done.12 = bf16[264,512]{1,0:T(8,128)(2,1)S(1)} collective-permute-done((bf16[264,512]{1,0:T(8,128)(2,1)S(1)}, bf16[264,512]{1,0:T(8,128)(2,1)S(1)}, u32[]{:S(2)}, u32[]{:S(2)}) %collective-permute-start.12) | collective-permute-done | bytes 270368 | tf_op jit(solution)/shard_map/ppermute | solution.py:26
  86.1 2.7 %collective-permute-start.16 = (bf16[264,512]{1,0:T(8,128)(2,1)S(1)}, bf16[264,512]{1,0:T(8,128)(2,1)S(1)}, u32[]{:S(2)}, u32[]{:S(2)}) collective-permute-start(bf16[264,512]{1,0:T(8,128)(2,1)S(1)} %add_convert_fusion.1), channel_id=1, source_target_pairs={{0,4},{1,5},{2,6},{3,7},{4,0},{5,1},{6,2},{7,3},{8,12},{9,13},{10,... | collective-permute-start | bytes 811016 | tf_op jit(solution)/shard_map/ppermute | solution.py:21
  88.9 2.5 %collective-permute-done.14.refs_1_ = bf16[264,512]{1,0:T(8,128)(2,1)S(1)} collective-permute-done((bf16[264,512]{1,0:T(8,128)(2,1)S(1)}, bf16[264,512]{1,0:T(8,128)(2,1)S(1)}, u32[]{:S(2)}, u32[]{:S(2)}) %collective-permute-start.14) | collective-permute-done | bytes 270368 | tf_op jit(solution)/shard_map/ppermute | solution.py:26
  91.4 2.0 %home_bwd.1 = bf16[128,2048]{1,0:T(8,128)(2,1)} custom-call(s32[1]{0:T(128)} %bitcast.own_ref, s32[1,128]{1,0:T(1,128)S(1)} %bitcast.30, f32[1,128]{1,0:T(1,128)S(1)} %bitcast.34, f32[1,2048]{1,0:T(1,128)S(1)} %copy-done.5, bf16[128,2048]{1,0:T(8,128)(2,1)S(1)} %bitcast.27, bf16[128,2048]{1,0:T(8,128)(2,1)S(1)} %collective-permute-done.1.x_ref.up_ref, ...), custom_call_target="tpu_custom_call" | custom-call | flops 1000 | bytes 1000 | tf_op jit(solution)/shard_map/home_bwd/pallas_call | solution.py:303
  93.4 10.1 %collective-permute-done.16.refs_2_ = bf16[264,512]{1,0:T(8,128)(2,1)S(1)} collective-permute-done((bf16[264,512]{1,0:T(8,128)(2,1)S(1)}, bf16[264,512]{1,0:T(8,128)(2,1)S(1)}, u32[]{:S(2)}, u32[]{:S(2)}) %collective-permute-start.16) | collective-permute-done | bytes 270368 | tf_op jit(solution)/shard_map/ppermute | solution.py:21
  103.5 0.8 collective-permute-done.15.refs_1_
  104.3 1.7 %home_fwd.1 = bf16[128,2048]{1,0:T(8,128)(2,1)} custom-call(s32[1]{0:T(128)} %bitcast.own_ref, s32[1,128]{1,0:T(1,128)S(1)} %bitcast.32, f32[1,128]{1,0:T(1,128)S(1)} %bitcast.33, bf16[128,2048]{1,0:T(8,128)(2,1)S(1)} %collective-permute-done.x_ref, f32[264,512]{1,0:T(8,128)S(1)} %get-tuple-element.43.refs_0_, ...), custom_call_target="tpu_custom_call" | custom-call | flops 1000 | bytes 1000 | tf_op jit(solution)/shard_map/home_fwd/pallas_call | solution.py:310
  (35 shorter events, 1.9 us)
Async XLA Ops:
  0.6 58.3 %copy-start.1 = (bf16[1,2048,192]{1,2,0:T(8,128)(2,1)S(1)}, bf16[1,2048,192]{1,2,0:T(8,128)(2,1)}, u32[]{:S(2)}) copy-start(bf16[1,2048,192]{1,2,0:T(8,128)(2,1)} %param.16) | copy-start | bytes 2359300
  0.6 58.3 %copy-start.2 = (bf16[1,192,2048]{2,1,0:T(8,128)(2,1)S(1)}, bf16[1,192,2048]{2,1,0:T(8,128)(2,1)}, u32[]{:S(2)}) copy-start(bf16[1,192,2048]{2,1,0:T(8,128)(2,1)} %param.17) | copy-start | bytes 2359300
  0.7 19.4 %copy-start.6 = (s32[1,128,1]{1,2,0:T(1,128)S(1)}, s32[1,128,1]{1,2,0:T(1,128)}, u32[]{:S(2)}) copy-start(s32[1,128,1]{1,2,0:T(1,128)} %param.20) | copy-start | bytes 1540
  0.7 58.3 %copy-start = (bf16[1,2048,192]{1,2,0:T(8,128)(2,1)S(1)}, bf16[1,2048,192]{1,2,0:T(8,128)(2,1)}, u32[]{:S(2)}) copy-start(bf16[1,2048,192]{1,2,0:T(8,128)(2,1)} %param.15) | copy-start | bytes 2359300
  0.7 25.5 %copy-start.5 = (f32[1,2048]{1,0:T(1,128)S(1)}, f32[1,2048]{1,0:T(1,128)}, u32[]{:S(2)}) copy-start(f32[1,2048]{1,0:T(1,128)} %gain_ref.3) | copy-start | bytes 24580
  0.7 6.8 %copy-start.10 = (bf16[1,128,2048]{2,1,0:T(8,128)(2,1)S(1)}, bf16[1,128,2048]{2,1,0:T(8,128)(2,1)}, u32[]{:S(2)}) copy-start(bf16[1,128,2048]{2,1,0:T(8,128)(2,1)} %param.13) | copy-start | bytes 1572868
  0.7 25.5 %copy-start.7 = (s32[1,128,1]{1,2,0:T(1,128)S(1)}, s32[1,128,1]{1,2,0:T(1,128)}, u32[]{:S(2)}) copy-start(s32[1,128,1]{1,2,0:T(1,128)} %param.18) | copy-start | bytes 1540
  4.5 54.5 %collective-permute-start.8 = (bf16[576,2048]{1,0:T(8,128)(2,1)}, bf16[576,2048]{1,0:T(8,128)(2,1)S(1)}, u32[]{:S(2)}, u32[]{:S(2)}) collective-permute-start(bf16[576,2048]{1,0:T(8,128)(2,1)} %get-tuple-element.37), channel_id=1, source_target_pairs={{0,1},{1,0},{2,3},{3,2},{4,5},{5,4},{6,7},{7,6},{8,9},{9,8},{10,11... | collective-permute-start | bytes 7077896 | tf_op jit(solution)/shard_map/ppermute | solution.py:26
  7.5 12.6 %collective-permute-start.1 = (bf16[128,2048]{1,0:T(8,128)(2,1)S(1)}, bf16[128,2048]{1,0:T(8,128)(2,1)S(1)}, u32[]{:S(2)}, u32[]{:S(2)}) collective-permute-start(bf16[128,2048]{1,0:T(8,128)(2,1)S(1)} %bitcast.37), channel_id=1, source_target_pairs={{0,24},{8,0},{16,8},{24,16},{1,25},{9,1},{17,9},{25,17},{2,26},{10... | collective-permute-start | bytes 1572872 | tf_op jit(solution)/shard_map/ppermute | solution.py:21
  8.2 18.0 %collective-permute-start = (bf16[128,2048]{1,0:T(8,128)(2,1)}, bf16[128,2048]{1,0:T(8,128)(2,1)S(1)}, u32[]{:S(2)}, u32[]{:S(2)}) collective-permute-start(bf16[128,2048]{1,0:T(8,128)(2,1)} %bitcast.38), channel_id=1, source_target_pairs={{0,8},{8,16},{16,24},{24,0},{1,9},{9,17},{17,25},{25,1},{2,10},{10... | collective-permute-start | bytes 1572872 | tf_op jit(solution)/shard_map/ppermute | solution.py:21
  8.2 16.4 %collective-permute-start.2 = (bf16[264,512]{1,0:T(8,128)(2,1)}, bf16[264,512]{1,0:T(8,128)(2,1)S(1)}, u32[]{:S(2)}, u32[]{:S(2)}) collective-permute-start(bf16[264,512]{1,0:T(8,128)(2,1)} %get-tuple-element.30), channel_id=1, source_target_pairs={{0,4},{1,5},{2,6},{3,7},{4,0},{5,1},{6,2},{7,3},{8,12},{9,13},{10,... | collective-permute-start | bytes 811016 | tf_op jit(solution)/shard_map/ppermute | solution.py:21
  10.8 14.0 %collective-permute-start.3 = (bf16[264,512]{1,0:T(8,128)(2,1)}, bf16[264,512]{1,0:T(8,128)(2,1)S(1)}, u32[]{:S(2)}, u32[]{:S(2)}) collective-permute-start(bf16[264,512]{1,0:T(8,128)(2,1)} %get-tuple-element.27.kept_ref), channel_id=1, source_target_pairs={{0,2},{1,3},{2,0},{3,1},{4,6},{5,7},{6,4},{7,5},{8,10},{9,11},{10,... | collective-permute-start | bytes 811016 | tf_op jit(solution)/shard_map/ppermute | solution.py:26
  21.0 16.2 %collective-permute-start.5 = (bf16[264,512]{1,0:T(8,128)(2,1)S(1)}, bf16[264,512]{1,0:T(8,128)(2,1)S(1)}, u32[]{:S(2)}, u32[]{:S(2)}) collective-permute-start(bf16[264,512]{1,0:T(8,128)(2,1)S(1)} %get-tuple-element.35), channel_id=1, source_target_pairs={{0,4},{1,5},{2,6},{3,7},{4,0},{5,1},{6,2},{7,3},{8,12},{9,13},{10,... | collective-permute-start | bytes 811016 | tf_op jit(solution)/shard_map/ppermute | solution.py:21
  24.7 14.4 %collective-permute-start.4 = (bf16[264,512]{1,0:T(8,128)(2,1)S(1)}, bf16[264,512]{1,0:T(8,128)(2,1)S(1)}, u32[]{:S(2)}, u32[]{:S(2)}) collective-permute-start(bf16[264,512]{1,0:T(8,128)(2,1)S(1)} %collective-permute-done.2.refs_1_), channel_id=1, source_target_pairs={{0,2},{1,3},{2,0},{3,1},{4,6},{5,7},{6,4},{7,5},{8,10},{9,11},{10,... | collective-permute-start | bytes 811016 | tf_op jit(solution)/shard_map/ppermute | solution.py:26
  26.2 1.0 copy-start.4
  28.0 20.7 %collective-permute-start.9 = (bf16[264,512]{1,0:T(8,128)(2,1)S(1)}, bf16[264,512]{1,0:T(8,128)(2,1)S(1)}, u32[]{:S(2)}, u32[]{:S(2)}) collective-permute-start(bf16[264,512]{1,0:T(8,128)(2,1)S(1)} %get-tuple-element.40), channel_id=1, source_target_pairs={{0,4},{1,5},{2,6},{3,7},{4,0},{5,1},{6,2},{7,3},{8,12},{9,13},{10,... | collective-permute-start | bytes 811016 | tf_op jit(solution)/shard_map/ppermute | solution.py:21
  37.1 14.0 %collective-permute-start.7 = (bf16[264,512]{1,0:T(8,128)(2,1)S(1)}, bf16[264,512]{1,0:T(8,128)(2,1)S(1)}, u32[]{:S(2)}, u32[]{:S(2)}) collective-permute-start(bf16[264,512]{1,0:T(8,128)(2,1)S(1)} %collective-permute-done.5.refs_5_), channel_id=1, source_target_pairs={{0,2},{1,3},{2,0},{3,1},{4,6},{5,7},{6,4},{7,5},{8,10},{9,11},{10,... | collective-permute-start | bytes 811016 | tf_op jit(solution)/shard_map/ppermute | solution.py:26
  37.8 19.1 %collective-permute-start.6 = (bf16[264,512]{1,0:T(8,128)(2,1)S(1)}, bf16[264,512]{1,0:T(8,128)(2,1)S(1)}, u32[]{:S(2)}, u32[]{:S(2)}) collective-permute-start(bf16[264,512]{1,0:T(8,128)(2,1)S(1)} %get-tuple-element.36.refs_4_), channel_id=1, source_target_pairs={{0,2},{1,3},{2,0},{3,1},{4,6},{5,7},{6,4},{7,5},{8,10},{9,11},{10,... | collective-permute-start | bytes 811016 | tf_op jit(solution)/shard_map/ppermute | solution.py:26
  51.1 13.4 %collective-permute-start.11 = (bf16[264,512]{1,0:T(8,128)(2,1)S(1)}, bf16[264,512]{1,0:T(8,128)(2,1)S(1)}, u32[]{:S(2)}, u32[]{:S(2)}) collective-permute-start(bf16[264,512]{1,0:T(8,128)(2,1)S(1)} %collective-permute-done.9.refs_1_), channel_id=1, source_target_pairs={{0,2},{1,3},{2,0},{3,1},{4,6},{5,7},{6,4},{7,5},{8,10},{9,11},{10,... | collective-permute-start | bytes 811016 | tf_op jit(solution)/shard_map/ppermute | solution.py:26
  51.1 17.4 %collective-permute-start.10 = (bf16[264,512]{1,0:T(8,128)(2,1)S(1)}, bf16[264,512]{1,0:T(8,128)(2,1)S(1)}, u32[]{:S(2)}, u32[]{:S(2)}) collective-permute-start(bf16[264,512]{1,0:T(8,128)(2,1)S(1)} %get-tuple-element.41.refs_0_), channel_id=1, source_target_pairs={{0,2},{1,3},{2,0},{3,1},{4,6},{5,7},{6,4},{7,5},{8,10},{9,11},{10,... | collective-permute-start | bytes 811016 | tf_op jit(solution)/shard_map/ppermute | solution.py:26
  62.6 11.7 %collective-permute-start.13 = (bf16[264,512]{1,0:T(8,128)(2,1)S(1)}, bf16[264,512]{1,0:T(8,128)(2,1)S(1)}, u32[]{:S(2)}, u32[]{:S(2)}) collective-permute-start(bf16[264,512]{1,0:T(8,128)(2,1)S(1)} %get-tuple-element.49), channel_id=1, source_target_pairs={{0,2},{1,3},{2,0},{3,1},{4,6},{5,7},{6,4},{7,5},{8,10},{9,11},{10,... | collective-permute-start | bytes 811016 | tf_op jit(solution)/shard_map/ppermute | solution.py:26
  64.5 26.9 %copy-start.9 = (f32[1,128,1]{1,2,0:T(1,128)S(1)}, f32[1,128,1]{1,2,0:T(1,128)}, u32[]{:S(2)}) copy-start(f32[1,128,1]{1,2,0:T(1,128)} %param.21) | copy-start | bytes 1540
  70.8 20.6 %copy-start.3 = (bf16[1,128,2048]{2,1,0:T(8,128)(2,1)S(1)}, bf16[1,128,2048]{2,1,0:T(8,128)(2,1)}, u32[]{:S(2)}) copy-start(bf16[1,128,2048]{2,1,0:T(8,128)(2,1)} %param.12) | copy-start | bytes 1572868
  70.8 15.3 %collective-permute-start.12 = (bf16[264,512]{1,0:T(8,128)(2,1)S(1)}, bf16[264,512]{1,0:T(8,128)(2,1)S(1)}, u32[]{:S(2)}, u32[]{:S(2)}) collective-permute-start(bf16[264,512]{1,0:T(8,128)(2,1)S(1)} %get-tuple-element.46), channel_id=1, source_target_pairs={{0,2},{1,3},{2,0},{3,1},{4,6},{5,7},{6,4},{7,5},{8,10},{9,11},{10,... | collective-permute-start | bytes 811016 | tf_op jit(solution)/shard_map/ppermute | solution.py:26
  74.3 30.0 %copy-start.8 = (f32[1,128,1]{1,2,0:T(1,128)S(1)}, f32[1,128,1]{1,2,0:T(1,128)}, u32[]{:S(2)}) copy-start(f32[1,128,1]{1,2,0:T(1,128)} %param.19) | copy-start | bytes 1540
  74.4 16.9 %collective-permute-start.14 = (bf16[264,512]{1,0:T(8,128)(2,1)S(1)}, bf16[264,512]{1,0:T(8,128)(2,1)S(1)}, u32[]{:S(2)}, u32[]{:S(2)}) collective-permute-start(bf16[264,512]{1,0:T(8,128)(2,1)S(1)} %get-tuple-element.50), channel_id=1, source_target_pairs={{0,2},{1,3},{2,0},{3,1},{4,6},{5,7},{6,4},{7,5},{8,10},{9,11},{10,... | collective-permute-start | bytes 811016 | tf_op jit(solution)/shard_map/ppermute | solution.py:26
  74.5 16.9 %collective-permute-start.17 = (bf16[264,512]{1,0:T(8,128)(2,1)S(1)}, bf16[264,512]{1,0:T(8,128)(2,1)S(1)}, u32[]{:S(2)}, u32[]{:S(2)}) collective-permute-start(bf16[264,512]{1,0:T(8,128)(2,1)S(1)} %add_convert_fusion), channel_id=1, source_target_pairs={{0,4},{1,5},{2,6},{3,7},{4,0},{5,1},{6,2},{7,3},{8,12},{9,13},{10,... | collective-permute-start | bytes 811016 | tf_op jit(solution)/shard_map/ppermute | solution.py:21
  86.1 17.3 %collective-permute-start.16 = (bf16[264,512]{1,0:T(8,128)(2,1)S(1)}, bf16[264,512]{1,0:T(8,128)(2,1)S(1)}, u32[]{:S(2)}, u32[]{:S(2)}) collective-permute-start(bf16[264,512]{1,0:T(8,128)(2,1)S(1)} %add_convert_fusion.1), channel_id=1, source_target_pairs={{0,4},{1,5},{2,6},{3,7},{4,0},{5,1},{6,2},{7,3},{8,12},{9,13},{10,... | collective-permute-start | bytes 811016 | tf_op jit(solution)/shard_map/ppermute | solution.py:21
  91.3 13.0 %collective-permute-start.15 = (bf16[264,512]{1,0:T(8,128)(2,1)S(1)}, bf16[264,512]{1,0:T(8,128)(2,1)S(1)}, u32[]{:S(2)}, u32[]{:S(2)}) collective-permute-start(bf16[264,512]{1,0:T(8,128)(2,1)S(1)} %get-tuple-element.51), channel_id=1, source_target_pairs={{0,2},{1,3},{2,0},{3,1},{4,6},{5,7},{6,4},{7,5},{8,10},{9,11},{10,... | collective-permute-start | bytes 811016 | tf_op jit(solution)/shard_map/ppermute | solution.py:26

commit v12 on v11

--- a/solution.py
+++ b/solution.py
@@ -284,9 +284,10 @@
     )(own, r_fwd, norm_gain, after(incoming, packed_g[0], rows_b[-1]), packed_b[0])
     rows_f = crossed(packed_f)
     swap_g = partners(rows_g[:1], rows_b[-1])
+    swap_f = partners(rows_f[:1], rows_g[-1])
     rows_b = [kept_b] + rows_b[1:] + swap_b + partners(rows_b[1:], swap_b[0])
-    rows_g = rows_g + swap_g + partners(rows_g[1:])
-    rows_f = rows_f + partners(rows_f, rows_g[-1], rows_b[-1])
+    rows_g = rows_g + swap_g + partners(rows_g[1:], swap_g[0])
+    rows_f = rows_f + swap_f + partners(rows_f[1:], swap_f[0], rows_b[-1])
 
     count = 2 * experts
     partial_b = local_call(

time: 106 us -> 104 us (0.981)
  waiting for transfers between devices: 60.6 us -> 55.8 us
  starting transfers between devices: 28.3 us -> 31.3 us
    ppermute x7, waiting for transfers between devices: 35 us -> 21.6 us  [shifted(): lax.ppermute(value, axis, [(i, (i + steps) % count) for i in range(count)])]
    ppermute x11, waiting for transfers between devices: 25.5 us -> 34.2 us  [swapped(): return lax.ppermute(value, axis, [(i, i ^ bit) for i in range(count)])]
    ppermute x7, starting transfers between devices: 16.1 us -> 19.6 us  [shifted(): lax.ppermute(value, axis, [(i, (i + steps) % count) for i in range(count)])]
  transfers between devices with their start and end apart: 18 -> 18, of which waited for: 14 -> 15; matrix products, arithmetic and copies ran while one was open for 0% -> 0% of each run, Pallas kernels for 9% -> 9%
where the time goes in v12:
time: 104 us
  waiting for transfers between devices  55.8 us (54%)
  starting transfers between devices  31.3 us (30%)
  Pallas kernels  15.2 us (15%)
    ppermute x11, waiting for transfers between devices, swapped(): return lax.ppermute(value, axis, [(i, i ^ bit) for i in range(count)])  34.2 us
    ppermute x7, waiting for transfers between devices, shifted(): lax.ppermute(value, axis, [(i, (i + steps) % count) for i in range(count)])  21.6 us
    ppermute x7, starting transfers between devices, shifted(): lax.ppermute(value, axis, [(i, (i + steps) % count) for i in range(count)])  19.6 us
    ppermute x11, starting transfers between devices, swapped(): return lax.ppermute(value, axis, [(i, i ^ bit) for i in range(count)])  11.7 us
    pallas_call x1, Pallas kernels, per_device(): local_call(first_body, [jax.ShapeDtypeStruct((3 * w_down.shape[1], width)...  3.76 us
    pallas_call x1, Pallas kernels, per_device(): local_call(functools.partial(backward_body, count, rows), partial, scratc...  3.64 us
    pallas_call x1, Pallas kernels, per_device(): local_call(functools.partial(forward_body, count, rows), partial, scratch...  2.25 us
  transfers between devices with their start and end apart: 18, of which 15 were waited for; matrix products, arithmetic and copies ran while one was open for 0% of the time, Pallas kernels for 9%

profile of v12, /device:TPU:0, one launch (start us, length us, event | category | flops | bytes accessed | tf_op | source)
XLA Modules:
  0.0 104.3 jit_solution(4479027392340334010)
XLA Ops:
  0.7 3.8 %join_weights_pack_saved.1 = (bf16[576,2048]{1,0:T(8,128)(2,1)}, bf16[264,512]{1,0:T(8,128)(2,1)}, bf16[264,512]{1,0:T(8,128)(2,1)}) custom-call(s32[1]{0:T(128)} %bitcast.own_ref, s32[1,128]{1,0:T(1,128)} %bitcast.28, f32[1,2048]{1,0:T(1,128)} %gain_ref.3, bf16[128,2048]{1,0:T(8,128)(2,1)} %bitcast.26, bf16[192,2048]{1,0:T(8,128)(2,1)} %bitcast.17, ...), custom_call_target="tpu_custom_call" | custom-call | flops 1000 | bytes 1000 | tf_op jit(solution)/shard_map/join_weights_pack_saved/pallas_call | solution.py:251
  4.5 3.0 %collective-permute-start.8 = (bf16[576,2048]{1,0:T(8,128)(2,1)}, bf16[576,2048]{1,0:T(8,128)(2,1)S(1)}, u32[]{:S(2)}, u32[]{:S(2)}) collective-permute-start(bf16[576,2048]{1,0:T(8,128)(2,1)} %get-tuple-element.39), channel_id=1, source_target_pairs={{0,1},{1,0},{2,3},{3,2},{4,5},{5,4},{6,7},{7,6},{8,9},{9,8},{10,11... | collective-permute-start | bytes 7077896 | tf_op jit(solution)/shard_map/ppermute | solution.py:26
  8.2 2.6 %collective-permute-start.2 = (bf16[264,512]{1,0:T(8,128)(2,1)}, bf16[264,512]{1,0:T(8,128)(2,1)S(1)}, u32[]{:S(2)}, u32[]{:S(2)}) collective-permute-start(bf16[264,512]{1,0:T(8,128)(2,1)} %get-tuple-element.31), channel_id=1, source_target_pairs={{0,4},{1,5},{2,6},{3,7},{4,0},{5,1},{6,2},{7,3},{8,12},{9,13},{10,... | collective-permute-start | bytes 811016 | tf_op jit(solution)/shard_map/ppermute | solution.py:21
  10.8 1.6 %collective-permute-start.3 = (bf16[264,512]{1,0:T(8,128)(2,1)}, bf16[264,512]{1,0:T(8,128)(2,1)S(1)}, u32[]{:S(2)}, u32[]{:S(2)}) collective-permute-start(bf16[264,512]{1,0:T(8,128)(2,1)} %get-tuple-element.28.kept_ref), channel_id=1, source_target_pairs={{0,2},{1,3},{2,0},{3,1},{4,6},{5,7},{6,4},{7,5},{8,10},{9,11},{10,... | collective-permute-start | bytes 811016 | tf_op jit(solution)/shard_map/ppermute | solution.py:26
  12.3 5.0 %collective-permute-done.1.x_ref.up_ref = bf16[128,2048]{1,0:T(8,128)(2,1)S(1)} collective-permute-done((bf16[128,2048]{1,0:T(8,128)(2,1)S(1)}, bf16[128,2048]{1,0:T(8,128)(2,1)S(1)}, u32[]{:S(2)}, u32[]{:S(2)}) %collective-permute-start.1) | collective-permute-done | bytes 524320 | tf_op jit(solution)/shard_map/ppermute | solution.py:21
  18.2 5.0 %collective-permute-start.5 = (bf16[264,512]{1,0:T(8,128)(2,1)S(1)}, bf16[264,512]{1,0:T(8,128)(2,1)S(1)}, u32[]{:S(2)}, u32[]{:S(2)}) collective-permute-start(bf16[264,512]{1,0:T(8,128)(2,1)S(1)} %get-tuple-element.36), channel_id=1, source_target_pairs={{0,4},{1,5},{2,6},{3,7},{4,0},{5,1},{6,2},{7,3},{8,12},{9,13},{10,... | collective-permute-start | bytes 811016 | tf_op jit(solution)/shard_map/ppermute | solution.py:21
  23.4 1.4 %collective-permute-start.6 = (bf16[264,512]{1,0:T(8,128)(2,1)S(1)}, bf16[264,512]{1,0:T(8,128)(2,1)S(1)}, u32[]{:S(2)}, u32[]{:S(2)}) collective-permute-start(bf16[264,512]{1,0:T(8,128)(2,1)S(1)} %get-tuple-element.37.refs_4_), channel_id=1, source_target_pairs={{0,2},{1,3},{2,0},{3,1},{4,6},{5,7},{6,4},{7,5},{8,10},{9,11},{10,... | collective-permute-start | bytes 811016 | tf_op jit(solution)/shard_map/ppermute | solution.py:26
  24.8 1.2 %collective-permute-done.3.refs_2_ = bf16[264,512]{1,0:T(8,128)(2,1)S(1)} collective-permute-done((bf16[264,512]{1,0:T(8,128)(2,1)}, bf16[264,512]{1,0:T(8,128)(2,1)S(1)}, u32[]{:S(2)}, u32[]{:S(2)}) %collective-permute-start.3) | collective-permute-done | bytes 270368 | tf_op jit(solution)/shard_map/ppermute | solution.py:26
  26.1 0.9 copy-done.4
  27.0 0.9 pack_act.1
  28.0 2.0 %collective-permute-start.9 = (bf16[264,512]{1,0:T(8,128)(2,1)S(1)}, bf16[264,512]{1,0:T(8,128)(2,1)S(1)}, u32[]{:S(2)}, u32[]{:S(2)}) collective-permute-start(bf16[264,512]{1,0:T(8,128)(2,1)S(1)} %get-tuple-element.42), channel_id=1, source_target_pairs={{0,4},{1,5},{2,6},{3,7},{4,0},{5,1},{6,2},{7,3},{8,12},{9,13},{10,... | collective-permute-start | bytes 811016 | tf_op jit(solution)/shard_map/ppermute | solution.py:21
  29.9 6.2 %collective-permute-done.5.refs_5_ = bf16[264,512]{1,0:T(8,128)(2,1)S(1)} collective-permute-done((bf16[264,512]{1,0:T(8,128)(2,1)S(1)}, bf16[264,512]{1,0:T(8,128)(2,1)S(1)}, u32[]{:S(2)}, u32[]{:S(2)}) %collective-permute-start.5) | collective-permute-done | bytes 270368 | tf_op jit(solution)/shard_map/ppermute | solution.py:21
  36.2 1.2 %collective-permute-start.10 = (bf16[264,512]{1,0:T(8,128)(2,1)S(1)}, bf16[264,512]{1,0:T(8,128)(2,1)S(1)}, u32[]{:S(2)}, u32[]{:S(2)}) collective-permute-start(bf16[264,512]{1,0:T(8,128)(2,1)S(1)} %get-tuple-element.43.refs_0_), channel_id=1, source_target_pairs={{0,2},{1,3},{2,0},{3,1},{4,6},{5,7},{6,4},{7,5},{8,10},{9,11},{10,... | collective-permute-start | bytes 811016 | tf_op jit(solution)/shard_map/ppermute | solution.py:26
  37.4 5.8 %collective-permute-done.6.refs_6_ = bf16[264,512]{1,0:T(8,128)(2,1)S(1)} collective-permute-done((bf16[264,512]{1,0:T(8,128)(2,1)S(1)}, bf16[264,512]{1,0:T(8,128)(2,1)S(1)}, u32[]{:S(2)}, u32[]{:S(2)}) %collective-permute-start.6) | collective-permute-done | bytes 270368 | tf_op jit(solution)/shard_map/ppermute | solution.py:26
  43.2 5.8 %collective-permute-done.4.refs_3_ = bf16[264,512]{1,0:T(8,128)(2,1)S(1)} collective-permute-done((bf16[264,512]{1,0:T(8,128)(2,1)S(1)}, bf16[264,512]{1,0:T(8,128)(2,1)S(1)}, u32[]{:S(2)}, u32[]{:S(2)}) %collective-permute-start.4) | collective-permute-done | bytes 270368 | tf_op jit(solution)/shard_map/ppermute | solution.py:26
  49.0 5.8 %collective-permute-done.10.refs_2_ = bf16[264,512]{1,0:T(8,128)(2,1)S(1)} collective-permute-done((bf16[264,512]{1,0:T(8,128)(2,1)S(1)}, bf16[264,512]{1,0:T(8,128)(2,1)S(1)}, u32[]{:S(2)}, u32[]{:S(2)}) %collective-permute-start.10) | collective-permute-done | bytes 270368 | tf_op jit(solution)/shard_map/ppermute | solution.py:26
  54.8 1.0 collective-permute-start.11
  55.8 4.8 %collective-permute-done.7.refs_7_ = bf16[264,512]{1,0:T(8,128)(2,1)S(1)} collective-permute-done((bf16[264,512]{1,0:T(8,128)(2,1)S(1)}, bf16[264,512]{1,0:T(8,128)(2,1)S(1)}, u32[]{:S(2)}, u32[]{:S(2)}) %collective-permute-start.7) | collective-permute-done | bytes 270368 | tf_op jit(solution)/shard_map/ppermute | solution.py:26
  60.6 3.6 %experts_bwd.1 = (f32[264,512]{1,0:T(8,128)S(1)}, f32[264,512]{1,0:T(8,128)S(1)}, bf16[264,512]{1,0:T(8,128)(2,1)S(1)}, bf16[264,512]{1,0:T(8,128)(2,1)S(1)}) custom-call(bf16[264,512]{1,0:T(8,128)(2,1)S(1)} %get-tuple-element.34.refs_0_, bf16[264,512]{1,0:T(8,128)(2,1)S(1)} %collective-permute-done.2.refs_1_, ...), custom_call_target="tpu_custom_call" | custom-call | flops 1000 | bytes 1000 | tf_op jit(solution)/shard_map/experts_bwd/pallas_call | solution.py:293
  64.2 1.0 %collective-permute-start.13 = (bf16[264,512]{1,0:T(8,128)(2,1)S(1)}, bf16[264,512]{1,0:T(8,128)(2,1)S(1)}, u32[]{:S(2)}, u32[]{:S(2)}) collective-permute-start(bf16[264,512]{1,0:T(8,128)(2,1)S(1)} %get-tuple-element.51), channel_id=1, source_target_pairs={{0,2},{1,3},{2,0},{3,1},{4,6},{5,7},{6,4},{7,5},{8,10},{9,11},{10,... | collective-permute-start | bytes 811016 | tf_op jit(solution)/shard_map/ppermute | solution.py:26
  66.1 2.3 %experts_fwd.1 = (f32[264,512]{1,0:T(8,128)S(1)}, f32[264,512]{1,0:T(8,128)S(1)}, bf16[264,512]{1,0:T(8,128)(2,1)S(1)}, bf16[264,512]{1,0:T(8,128)(2,1)S(1)}) custom-call(bf16[264,512]{1,0:T(8,128)(2,1)S(1)} %get-tuple-element.43.refs_0_, bf16[264,512]{1,0:T(8,128)(2,1)S(1)} %collective-permute-done.9.refs_1_, ...), custom_call_target="tpu_custom_call" | custom-call | flops 1000 | bytes 1000 | tf_op jit(solution)/shard_map/experts_fwd/pallas_call | solution.py:296
  68.3 1.3 %collective-permute-start.12 = (bf16[264,512]{1,0:T(8,128)(2,1)S(1)}, bf16[264,512]{1,0:T(8,128)(2,1)S(1)}, u32[]{:S(2)}, u32[]{:S(2)}) collective-permute-start(bf16[264,512]{1,0:T(8,128)(2,1)S(1)} %get-tuple-element.48), channel_id=1, source_target_pairs={{0,2},{1,3},{2,0},{3,1},{4,6},{5,7},{6,4},{7,5},{8,10},{9,11},{10,... | collective-permute-start | bytes 811016 | tf_op jit(solution)/shard_map/ppermute | solution.py:26
  69.7 3.9 %collective-permute-done.13 = bf16[264,512]{1,0:T(8,128)(2,1)S(1)} collective-permute-done((bf16[264,512]{1,0:T(8,128)(2,1)S(1)}, bf16[264,512]{1,0:T(8,128)(2,1)S(1)}, u32[]{:S(2)}, u32[]{:S(2)}) %collective-permute-start.13) | collective-permute-done | bytes 270368 | tf_op jit(solution)/shard_map/ppermute | solution.py:26
  73.6 1.1 %collective-permute-start.14 = (bf16[264,512]{1,0:T(8,128)(2,1)S(1)}, bf16[264,512]{1,0:T(8,128)(2,1)S(1)}, u32[]{:S(2)}, u32[]{:S(2)}) collective-permute-start(bf16[264,512]{1,0:T(8,128)(2,1)S(1)} %get-tuple-element.52), channel_id=1, source_target_pairs={{0,2},{1,3},{2,0},{3,1},{4,6},{5,7},{6,4},{7,5},{8,10},{9,11},{10,... | collective-permute-start | bytes 811016 | tf_op jit(solution)/shard_map/ppermute | solution.py:26
  74.7 6.2 %collective-permute-start.17 = (bf16[264,512]{1,0:T(8,128)(2,1)S(1)}, bf16[264,512]{1,0:T(8,128)(2,1)S(1)}, u32[]{:S(2)}, u32[]{:S(2)}) collective-permute-start(bf16[264,512]{1,0:T(8,128)(2,1)S(1)} %add_convert_fusion), channel_id=1, source_target_pairs={{0,4},{1,5},{2,6},{3,7},{4,0},{5,1},{6,2},{7,3},{8,12},{9,13},{10,... | collective-permute-start | bytes 811016 | tf_op jit(solution)/shard_map/ppermute | solution.py:21
  81.0 2.2 %collective-permute-done.12 = bf16[264,512]{1,0:T(8,128)(2,1)S(1)} collective-permute-done((bf16[264,512]{1,0:T(8,128)(2,1)S(1)}, bf16[264,512]{1,0:T(8,128)(2,1)S(1)}, u32[]{:S(2)}, u32[]{:S(2)}) %collective-permute-start.12) | collective-permute-done | bytes 270368 | tf_op jit(solution)/shard_map/ppermute | solution.py:26
  83.3 3.1 %collective-permute-start.16 = (bf16[264,512]{1,0:T(8,128)(2,1)S(1)}, bf16[264,512]{1,0:T(8,128)(2,1)S(1)}, u32[]{:S(2)}, u32[]{:S(2)}) collective-permute-start(bf16[264,512]{1,0:T(8,128)(2,1)S(1)} %add_convert_fusion.1), channel_id=1, source_target_pairs={{0,4},{1,5},{2,6},{3,7},{4,0},{5,1},{6,2},{7,3},{8,12},{9,13},{10,... | collective-permute-start | bytes 811016 | tf_op jit(solution)/shard_map/ppermute | solution.py:21
  86.4 3.7 %collective-permute-done.14.refs_1_ = bf16[264,512]{1,0:T(8,128)(2,1)S(1)} collective-permute-done((bf16[264,512]{1,0:T(8,128)(2,1)S(1)}, bf16[264,512]{1,0:T(8,128)(2,1)S(1)}, u32[]{:S(2)}, u32[]{:S(2)}) %collective-permute-start.14) | collective-permute-done | bytes 270368 | tf_op jit(solution)/shard_map/ppermute | solution.py:26
  90.1 9.1 %collective-permute-done.17.refs_2_ = bf16[264,512]{1,0:T(8,128)(2,1)S(1)} collective-permute-done((bf16[264,512]{1,0:T(8,128)(2,1)S(1)}, bf16[264,512]{1,0:T(8,128)(2,1)S(1)}, u32[]{:S(2)}, u32[]{:S(2)}) %collective-permute-start.17) | collective-permute-done | bytes 270368 | tf_op jit(solution)/shard_map/ppermute | solution.py:21
  99.2 2.0 %home_bwd.1 = bf16[128,2048]{1,0:T(8,128)(2,1)} custom-call(s32[1]{0:T(128)} %bitcast.own_ref, s32[1,128]{1,0:T(1,128)S(1)} %bitcast.30, f32[1,128]{1,0:T(1,128)S(1)} %bitcast.34, f32[1,2048]{1,0:T(1,128)S(1)} %copy-done.5, bf16[128,2048]{1,0:T(8,128)(2,1)S(1)} %bitcast.27, bf16[128,2048]{1,0:T(8,128)(2,1)S(1)} %collective-permute-done.1.x_ref.up_ref, ...), custom_call_target="tpu_custom_call" | custom-call | flops 1000 | bytes 1000 | tf_op jit(solution)/shard_map/home_bwd/pallas_call | solution.py:304
  101.2 1.1 %collective-permute-done.16.refs_2_ = bf16[264,512]{1,0:T(8,128)(2,1)S(1)} collective-permute-done((bf16[264,512]{1,0:T(8,128)(2,1)S(1)}, bf16[264,512]{1,0:T(8,128)(2,1)S(1)}, u32[]{:S(2)}, u32[]{:S(2)}) %collective-permute-start.16) | collective-permute-done | bytes 270368 | tf_op jit(solution)/shard_map/ppermute | solution.py:21
  102.5 1.7 %home_fwd.1 = bf16[128,2048]{1,0:T(8,128)(2,1)} custom-call(s32[1]{0:T(128)} %bitcast.own_ref, s32[1,128]{1,0:T(1,128)S(1)} %bitcast.32, f32[1,128]{1,0:T(1,128)S(1)} %bitcast.33, bf16[128,2048]{1,0:T(8,128)(2,1)S(1)} %collective-permute-done.x_ref, f32[264,512]{1,0:T(8,128)S(1)} %get-tuple-element.45.refs_0_, ...), custom_call_target="tpu_custom_call" | custom-call | flops 1000 | bytes 1000 | tf_op jit(solution)/shard_map/home_fwd/pallas_call | solution.py:311
  (35 shorter events, 3.0 us)
Async XLA Ops:
  0.6 59.9 %copy-start.1 = (bf16[1,2048,192]{1,2,0:T(8,128)(2,1)S(1)}, bf16[1,2048,192]{1,2,0:T(8,128)(2,1)}, u32[]{:S(2)}) copy-start(bf16[1,2048,192]{1,2,0:T(8,128)(2,1)} %param.16) | copy-start | bytes 2359300
  0.6 59.9 %copy-start.2 = (bf16[1,192,2048]{2,1,0:T(8,128)(2,1)S(1)}, bf16[1,192,2048]{2,1,0:T(8,128)(2,1)}, u32[]{:S(2)}) copy-start(bf16[1,192,2048]{2,1,0:T(8,128)(2,1)} %param.17) | copy-start | bytes 2359300
  0.7 16.7 %copy-start.6 = (s32[1,128,1]{1,2,0:T(1,128)S(1)}, s32[1,128,1]{1,2,0:T(1,128)}, u32[]{:S(2)}) copy-start(s32[1,128,1]{1,2,0:T(1,128)} %param.20) | copy-start | bytes 1540
  0.7 59.9 %copy-start = (bf16[1,2048,192]{1,2,0:T(8,128)(2,1)S(1)}, bf16[1,2048,192]{1,2,0:T(8,128)(2,1)}, u32[]{:S(2)}) copy-start(bf16[1,2048,192]{1,2,0:T(8,128)(2,1)} %param.15) | copy-start | bytes 2359300
  0.7 25.4 %copy-start.5 = (f32[1,2048]{1,0:T(1,128)S(1)}, f32[1,2048]{1,0:T(1,128)}, u32[]{:S(2)}) copy-start(f32[1,2048]{1,0:T(1,128)} %gain_ref.3) | copy-start | bytes 24580
  0.7 6.8 %copy-start.10 = (bf16[1,128,2048]{2,1,0:T(8,128)(2,1)S(1)}, bf16[1,128,2048]{2,1,0:T(8,128)(2,1)}, u32[]{:S(2)}) copy-start(bf16[1,128,2048]{2,1,0:T(8,128)(2,1)} %param.13) | copy-start | bytes 1572868
  0.7 25.4 %copy-start.7 = (s32[1,128,1]{1,2,0:T(1,128)S(1)}, s32[1,128,1]{1,2,0:T(1,128)}, u32[]{:S(2)}) copy-start(s32[1,128,1]{1,2,0:T(1,128)} %param.18) | copy-start | bytes 1540
  4.5 56.1 %collective-permute-start.8 = (bf16[576,2048]{1,0:T(8,128)(2,1)}, bf16[576,2048]{1,0:T(8,128)(2,1)S(1)}, u32[]{:S(2)}, u32[]{:S(2)}) collective-permute-start(bf16[576,2048]{1,0:T(8,128)(2,1)} %get-tuple-element.39), channel_id=1, source_target_pairs={{0,1},{1,0},{2,3},{3,2},{4,5},{5,4},{6,7},{7,6},{8,9},{9,8},{10,11... | collective-permute-start | bytes 7077896 | tf_op jit(solution)/shard_map/ppermute | solution.py:26
  7.5 9.9 %collective-permute-start.1 = (bf16[128,2048]{1,0:T(8,128)(2,1)S(1)}, bf16[128,2048]{1,0:T(8,128)(2,1)S(1)}, u32[]{:S(2)}, u32[]{:S(2)}) collective-permute-start(bf16[128,2048]{1,0:T(8,128)(2,1)S(1)} %bitcast.37), channel_id=1, source_target_pairs={{0,24},{8,0},{16,8},{24,16},{1,25},{9,1},{17,9},{25,17},{2,26},{10... | collective-permute-start | bytes 1572872 | tf_op jit(solution)/shard_map/ppermute | solution.py:21
  8.2 15.2 %collective-permute-start.2 = (bf16[264,512]{1,0:T(8,128)(2,1)}, bf16[264,512]{1,0:T(8,128)(2,1)S(1)}, u32[]{:S(2)}, u32[]{:S(2)}) collective-permute-start(bf16[264,512]{1,0:T(8,128)(2,1)} %get-tuple-element.31), channel_id=1, source_target_pairs={{0,4},{1,5},{2,6},{3,7},{4,0},{5,1},{6,2},{7,3},{8,12},{9,13},{10,... | collective-permute-start | bytes 811016 | tf_op jit(solution)/shard_map/ppermute | solution.py:21
  10.8 15.3 %collective-permute-start = (bf16[128,2048]{1,0:T(8,128)(2,1)}, bf16[128,2048]{1,0:T(8,128)(2,1)S(1)}, u32[]{:S(2)}, u32[]{:S(2)}) collective-permute-start(bf16[128,2048]{1,0:T(8,128)(2,1)} %bitcast.38), channel_id=1, source_target_pairs={{0,8},{8,16},{16,24},{24,0},{1,9},{9,17},{17,25},{25,1},{2,10},{10... | collective-permute-start | bytes 1572872 | tf_op jit(solution)/shard_map/ppermute | solution.py:21
  10.8 15.3 %collective-permute-start.3 = (bf16[264,512]{1,0:T(8,128)(2,1)}, bf16[264,512]{1,0:T(8,128)(2,1)S(1)}, u32[]{:S(2)}, u32[]{:S(2)}) collective-permute-start(bf16[264,512]{1,0:T(8,128)(2,1)} %get-tuple-element.28.kept_ref), channel_id=1, source_target_pairs={{0,2},{1,3},{2,0},{3,1},{4,6},{5,7},{6,4},{7,5},{8,10},{9,11},{10,... | collective-permute-start | bytes 811016 | tf_op jit(solution)/shard_map/ppermute | solution.py:26
  18.2 17.9 %collective-permute-start.5 = (bf16[264,512]{1,0:T(8,128)(2,1)S(1)}, bf16[264,512]{1,0:T(8,128)(2,1)S(1)}, u32[]{:S(2)}, u32[]{:S(2)}) collective-permute-start(bf16[264,512]{1,0:T(8,128)(2,1)S(1)} %get-tuple-element.36), channel_id=1, source_target_pairs={{0,4},{1,5},{2,6},{3,7},{4,0},{5,1},{6,2},{7,3},{8,12},{9,13},{10,... | collective-permute-start | bytes 811016 | tf_op jit(solution)/shard_map/ppermute | solution.py:21
  23.4 19.8 %collective-permute-start.6 = (bf16[264,512]{1,0:T(8,128)(2,1)S(1)}, bf16[264,512]{1,0:T(8,128)(2,1)S(1)}, u32[]{:S(2)}, u32[]{:S(2)}) collective-permute-start(bf16[264,512]{1,0:T(8,128)(2,1)S(1)} %get-tuple-element.37.refs_4_), channel_id=1, source_target_pairs={{0,2},{1,3},{2,0},{3,1},{4,6},{5,7},{6,4},{7,5},{8,10},{9,11},{10,... | collective-permute-start | bytes 811016 | tf_op jit(solution)/shard_map/ppermute | solution.py:26
  26.1 22.9 %collective-permute-start.4 = (bf16[264,512]{1,0:T(8,128)(2,1)S(1)}, bf16[264,512]{1,0:T(8,128)(2,1)S(1)}, u32[]{:S(2)}, u32[]{:S(2)}) collective-permute-start(bf16[264,512]{1,0:T(8,128)(2,1)S(1)} %collective-permute-done.2.refs_1_), channel_id=1, source_target_pairs={{0,2},{1,3},{2,0},{3,1},{4,6},{5,7},{6,4},{7,5},{8,10},{9,11},{10,... | collective-permute-start | bytes 811016 | tf_op jit(solution)/shard_map/ppermute | solution.py:26
  26.1 1.0 copy-start.4
  28.0 21.0 %collective-permute-start.9 = (bf16[264,512]{1,0:T(8,128)(2,1)S(1)}, bf16[264,512]{1,0:T(8,128)(2,1)S(1)}, u32[]{:S(2)}, u32[]{:S(2)}) collective-permute-start(bf16[264,512]{1,0:T(8,128)(2,1)S(1)} %get-tuple-element.42), channel_id=1, source_target_pairs={{0,4},{1,5},{2,6},{3,7},{4,0},{5,1},{6,2},{7,3},{8,12},{9,13},{10,... | collective-permute-start | bytes 811016 | tf_op jit(solution)/shard_map/ppermute | solution.py:21
  36.2 18.6 %collective-permute-start.10 = (bf16[264,512]{1,0:T(8,128)(2,1)S(1)}, bf16[264,512]{1,0:T(8,128)(2,1)S(1)}, u32[]{:S(2)}, u32[]{:S(2)}) collective-permute-start(bf16[264,512]{1,0:T(8,128)(2,1)S(1)} %get-tuple-element.43.refs_0_), channel_id=1, source_target_pairs={{0,2},{1,3},{2,0},{3,1},{4,6},{5,7},{6,4},{7,5},{8,10},{9,11},{10,... | collective-permute-start | bytes 811016 | tf_op jit(solution)/shard_map/ppermute | solution.py:26
  43.2 17.4 %collective-permute-start.7 = (bf16[264,512]{1,0:T(8,128)(2,1)S(1)}, bf16[264,512]{1,0:T(8,128)(2,1)S(1)}, u32[]{:S(2)}, u32[]{:S(2)}) collective-permute-start(bf16[264,512]{1,0:T(8,128)(2,1)S(1)} %collective-permute-done.5.refs_5_), channel_id=1, source_target_pairs={{0,2},{1,3},{2,0},{3,1},{4,6},{5,7},{6,4},{7,5},{8,10},{9,11},{10,... | collective-permute-start | bytes 811016 | tf_op jit(solution)/shard_map/ppermute | solution.py:26
  54.8 11.3 %collective-permute-start.11 = (bf16[264,512]{1,0:T(8,128)(2,1)S(1)}, bf16[264,512]{1,0:T(8,128)(2,1)S(1)}, u32[]{:S(2)}, u32[]{:S(2)}) collective-permute-start(bf16[264,512]{1,0:T(8,128)(2,1)S(1)} %collective-permute-done.9.refs_1_), channel_id=1, source_target_pairs={{0,2},{1,3},{2,0},{3,1},{4,6},{5,7},{6,4},{7,5},{8,10},{9,11},{10,... | collective-permute-start | bytes 811016 | tf_op jit(solution)/shard_map/ppermute | solution.py:26
  64.2 9.3 %collective-permute-start.13 = (bf16[264,512]{1,0:T(8,128)(2,1)S(1)}, bf16[264,512]{1,0:T(8,128)(2,1)S(1)}, u32[]{:S(2)}, u32[]{:S(2)}) collective-permute-start(bf16[264,512]{1,0:T(8,128)(2,1)S(1)} %get-tuple-element.51), channel_id=1, source_target_pairs={{0,2},{1,3},{2,0},{3,1},{4,6},{5,7},{6,4},{7,5},{8,10},{9,11},{10,... | collective-permute-start | bytes 811016 | tf_op jit(solution)/shard_map/ppermute | solution.py:26
  65.3 33.9 %copy-start.9 = (f32[1,128,1]{1,2,0:T(1,128)S(1)}, f32[1,128,1]{1,2,0:T(1,128)}, u32[]{:S(2)}) copy-start(f32[1,128,1]{1,2,0:T(1,128)} %param.21) | copy-start | bytes 1540
  68.3 30.8 %copy-start.3 = (bf16[1,128,2048]{2,1,0:T(8,128)(2,1)S(1)}, bf16[1,128,2048]{2,1,0:T(8,128)(2,1)}, u32[]{:S(2)}) copy-start(bf16[1,128,2048]{2,1,0:T(8,128)(2,1)} %param.12) | copy-start | bytes 1572868
  68.3 14.8 %collective-permute-start.12 = (bf16[264,512]{1,0:T(8,128)(2,1)S(1)}, bf16[264,512]{1,0:T(8,128)(2,1)S(1)}, u32[]{:S(2)}, u32[]{:S(2)}) collective-permute-start(bf16[264,512]{1,0:T(8,128)(2,1)S(1)} %get-tuple-element.48), channel_id=1, source_target_pairs={{0,2},{1,3},{2,0},{3,1},{4,6},{5,7},{6,4},{7,5},{8,10},{9,11},{10,... | collective-permute-start | bytes 811016 | tf_op jit(solution)/shard_map/ppermute | solution.py:26
  73.5 29.0 %copy-start.8 = (f32[1,128,1]{1,2,0:T(1,128)S(1)}, f32[1,128,1]{1,2,0:T(1,128)}, u32[]{:S(2)}) copy-start(f32[1,128,1]{1,2,0:T(1,128)} %param.19) | copy-start | bytes 1540
  73.6 16.5 %collective-permute-start.14 = (bf16[264,512]{1,0:T(8,128)(2,1)S(1)}, bf16[264,512]{1,0:T(8,128)(2,1)S(1)}, u32[]{:S(2)}, u32[]{:S(2)}) collective-permute-start(bf16[264,512]{1,0:T(8,128)(2,1)S(1)} %get-tuple-element.52), channel_id=1, source_target_pairs={{0,2},{1,3},{2,0},{3,1},{4,6},{5,7},{6,4},{7,5},{8,10},{9,11},{10,... | collective-permute-start | bytes 811016 | tf_op jit(solution)/shard_map/ppermute | solution.py:26
  74.7 24.4 %collective-permute-start.17 = (bf16[264,512]{1,0:T(8,128)(2,1)S(1)}, bf16[264,512]{1,0:T(8,128)(2,1)S(1)}, u32[]{:S(2)}, u32[]{:S(2)}) collective-permute-start(bf16[264,512]{1,0:T(8,128)(2,1)S(1)} %add_convert_fusion), channel_id=1, source_target_pairs={{0,4},{1,5},{2,6},{3,7},{4,0},{5,1},{6,2},{7,3},{8,12},{9,13},{10,... | collective-permute-start | bytes 811016 | tf_op jit(solution)/shard_map/ppermute | solution.py:21
  83.3 19.1 %collective-permute-start.16 = (bf16[264,512]{1,0:T(8,128)(2,1)S(1)}, bf16[264,512]{1,0:T(8,128)(2,1)S(1)}, u32[]{:S(2)}, u32[]{:S(2)}) collective-permute-start(bf16[264,512]{1,0:T(8,128)(2,1)S(1)} %add_convert_fusion.1), channel_id=1, source_target_pairs={{0,4},{1,5},{2,6},{3,7},{4,0},{5,1},{6,2},{7,3},{8,12},{9,13},{10,... | collective-permute-start | bytes 811016 | tf_op jit(solution)/shard_map/ppermute | solution.py:21
  90.1 12.5 %collective-permute-start.15 = (bf16[264,512]{1,0:T(8,128)(2,1)S(1)}, bf16[264,512]{1,0:T(8,128)(2,1)S(1)}, u32[]{:S(2)}, u32[]{:S(2)}) collective-permute-start(bf16[264,512]{1,0:T(8,128)(2,1)S(1)} %get-tuple-element.53), channel_id=1, source_target_pairs={{0,2},{1,3},{2,0},{3,1},{4,6},{5,7},{6,4},{7,5},{8,10},{9,11},{10,... | collective-permute-start | bytes 811016 | tf_op jit(solution)/shard_map/ppermute | solution.py:26

commit v13 on v12

--- a/solution.py
+++ b/solution.py
@@ -299,7 +299,7 @@
     totals_b, home_b = crossing_home(partial_b)
     totals_f, home_f = crossing_home(partial_f)
     back_b = [partial_b[0]] + partners(partial_b[experts:experts + 1], *totals_b) + home_b
-    back_f = [partial_f[0]] + partners(partial_f[experts:experts + 1], *totals_f, back_b[1]) + home_f
+    back_f = [partial_f[0]] + partners(partial_f[experts:experts + 1], *totals_f, *home_b) + home_f
 
     grad_out = local_call(
         functools.partial(backward_home_body, experts, rows),

time: 104 us -> 103 us (level)
  waiting for transfers between devices: 55.8 us -> 54 us
    ppermute x7, waiting for transfers between devices: 21.6 us -> 13.7 us  [shifted(): lax.ppermute(value, axis, [(i, (i + steps) % count) for i in range(count)])]
    ppermute x11, starting transfers between devices: 11.7 us -> 19.4 us  [swapped(): return lax.ppermute(value, axis, [(i, i ^ bit) for i in range(count)])]
    ppermute x7, starting transfers between devices: 19.6 us -> 12.4 us  [shifted(): lax.ppermute(value, axis, [(i, (i + steps) % count) for i in range(count)])]
    ppermute x11, waiting for transfers between devices: 34.2 us -> 40.3 us  [swapped(): return lax.ppermute(value, axis, [(i, i ^ bit) for i in range(count)])]
  transfers between devices with their start and end apart: 18 -> 18, of which waited for: 15 -> 14; matrix products, arithmetic and copies ran while one was open for 0% -> 0% of each run, Pallas kernels for 9% -> 9%
where the time goes in v13:
time: 103 us
  waiting for transfers between devices  54 us (52%)
  starting transfers between devices  31.8 us (31%)
  Pallas kernels  15.2 us (15%)
    ppermute x11, waiting for transfers between devices, swapped(): return lax.ppermute(value, axis, [(i, i ^ bit) for i in range(count)])  40.3 us
    ppermute x11, starting transfers between devices, swapped(): return lax.ppermute(value, axis, [(i, i ^ bit) for i in range(count)])  19.4 us
    ppermute x7, waiting for transfers between devices, shifted(): lax.ppermute(value, axis, [(i, (i + steps) % count) for i in range(count)])  13.7 us
    ppermute x7, starting transfers between devices, shifted(): lax.ppermute(value, axis, [(i, (i + steps) % count) for i in range(count)])  12.4 us
    pallas_call x1, Pallas kernels, per_device(): local_call(first_body, [jax.ShapeDtypeStruct((3 * w_down.shape[1], width)...  3.76 us
    pallas_call x1, Pallas kernels, per_device(): local_call(functools.partial(backward_body, count, rows), partial, scratc...  3.64 us
    pallas_call x1, Pallas kernels, per_device(): local_call(functools.partial(forward_body, count, rows), partial, scratch...  2.25 us
  transfers between devices with their start and end apart: 18, of which 14 were waited for; matrix products, arithmetic and copies ran while one was open for 0% of the time, Pallas kernels for 9%

profile of v13, /device:TPU:0, one launch (start us, length us, event | category | flops | bytes accessed | tf_op | source)
XLA Modules:
  0.0 102.9 jit_solution(4932116788637903851)
XLA Ops:
  0.7 3.8 %join_weights_pack_saved.1 = (bf16[576,2048]{1,0:T(8,128)(2,1)}, bf16[264,512]{1,0:T(8,128)(2,1)}, bf16[264,512]{1,0:T(8,128)(2,1)}) custom-call(s32[1]{0:T(128)} %bitcast.own_ref, s32[1,128]{1,0:T(1,128)} %bitcast.28, f32[1,2048]{1,0:T(1,128)} %gain_ref.3, bf16[128,2048]{1,0:T(8,128)(2,1)} %bitcast.26, bf16[192,2048]{1,0:T(8,128)(2,1)} %bitcast.17, ...), custom_call_target="tpu_custom_call" | custom-call | flops 1000 | bytes 1000 | tf_op jit(solution)/shard_map/join_weights_pack_saved/pallas_call | solution.py:251
  4.5 3.0 %collective-permute-start.8 = (bf16[576,2048]{1,0:T(8,128)(2,1)}, bf16[576,2048]{1,0:T(8,128)(2,1)S(1)}, u32[]{:S(2)}, u32[]{:S(2)}) collective-permute-start(bf16[576,2048]{1,0:T(8,128)(2,1)} %get-tuple-element.39), channel_id=1, source_target_pairs={{0,1},{1,0},{2,3},{3,2},{4,5},{5,4},{6,7},{7,6},{8,9},{9,8},{10,11... | collective-permute-start | bytes 7077896 | tf_op jit(solution)/shard_map/ppermute | solution.py:26
  8.2 2.6 %collective-permute-start.2 = (bf16[264,512]{1,0:T(8,128)(2,1)}, bf16[264,512]{1,0:T(8,128)(2,1)S(1)}, u32[]{:S(2)}, u32[]{:S(2)}) collective-permute-start(bf16[264,512]{1,0:T(8,128)(2,1)} %get-tuple-element.31), channel_id=1, source_target_pairs={{0,4},{1,5},{2,6},{3,7},{4,0},{5,1},{6,2},{7,3},{8,12},{9,13},{10,... | collective-permute-start | bytes 811016 | tf_op jit(solution)/shard_map/ppermute | solution.py:21
  10.8 1.6 %collective-permute-start.3 = (bf16[264,512]{1,0:T(8,128)(2,1)}, bf16[264,512]{1,0:T(8,128)(2,1)S(1)}, u32[]{:S(2)}, u32[]{:S(2)}) collective-permute-start(bf16[264,512]{1,0:T(8,128)(2,1)} %get-tuple-element.28.kept_ref), channel_id=1, source_target_pairs={{0,2},{1,3},{2,0},{3,1},{4,6},{5,7},{6,4},{7,5},{8,10},{9,11},{10,... | collective-permute-start | bytes 811016 | tf_op jit(solution)/shard_map/ppermute | solution.py:26
  12.3 5.0 %collective-permute-done.1.x_ref.up_ref = bf16[128,2048]{1,0:T(8,128)(2,1)S(1)} collective-permute-done((bf16[128,2048]{1,0:T(8,128)(2,1)S(1)}, bf16[128,2048]{1,0:T(8,128)(2,1)S(1)}, u32[]{:S(2)}, u32[]{:S(2)}) %collective-permute-start.1) | collective-permute-done | bytes 524320 | tf_op jit(solution)/shard_map/ppermute | solution.py:21
  18.2 5.0 %collective-permute-start.5 = (bf16[264,512]{1,0:T(8,128)(2,1)S(1)}, bf16[264,512]{1,0:T(8,128)(2,1)S(1)}, u32[]{:S(2)}, u32[]{:S(2)}) collective-permute-start(bf16[264,512]{1,0:T(8,128)(2,1)S(1)} %get-tuple-element.36), channel_id=1, source_target_pairs={{0,4},{1,5},{2,6},{3,7},{4,0},{5,1},{6,2},{7,3},{8,12},{9,13},{10,... | collective-permute-start | bytes 811016 | tf_op jit(solution)/shard_map/ppermute | solution.py:21
  23.4 1.4 %collective-permute-start.6 = (bf16[264,512]{1,0:T(8,128)(2,1)S(1)}, bf16[264,512]{1,0:T(8,128)(2,1)S(1)}, u32[]{:S(2)}, u32[]{:S(2)}) collective-permute-start(bf16[264,512]{1,0:T(8,128)(2,1)S(1)} %get-tuple-element.37.refs_4_), channel_id=1, source_target_pairs={{0,2},{1,3},{2,0},{3,1},{4,6},{5,7},{6,4},{7,5},{8,10},{9,11},{10,... | collective-permute-start | bytes 811016 | tf_op jit(solution)/shard_map/ppermute | solution.py:26
  24.8 1.2 %collective-permute-done.3.refs_2_ = bf16[264,512]{1,0:T(8,128)(2,1)S(1)} collective-permute-done((bf16[264,512]{1,0:T(8,128)(2,1)}, bf16[264,512]{1,0:T(8,128)(2,1)S(1)}, u32[]{:S(2)}, u32[]{:S(2)}) %collective-permute-start.3) | collective-permute-done | bytes 270368 | tf_op jit(solution)/shard_map/ppermute | solution.py:26
  26.1 0.9 copy-done.4
  27.0 0.9 pack_act.1
  28.0 2.0 %collective-permute-start.9 = (bf16[264,512]{1,0:T(8,128)(2,1)S(1)}, bf16[264,512]{1,0:T(8,128)(2,1)S(1)}, u32[]{:S(2)}, u32[]{:S(2)}) collective-permute-start(bf16[264,512]{1,0:T(8,128)(2,1)S(1)} %get-tuple-element.42), channel_id=1, source_target_pairs={{0,4},{1,5},{2,6},{3,7},{4,0},{5,1},{6,2},{7,3},{8,12},{9,13},{10,... | collective-permute-start | bytes 811016 | tf_op jit(solution)/shard_map/ppermute | solution.py:21
  29.9 6.2 %collective-permute-done.5.refs_5_ = bf16[264,512]{1,0:T(8,128)(2,1)S(1)} collective-permute-done((bf16[264,512]{1,0:T(8,128)(2,1)S(1)}, bf16[264,512]{1,0:T(8,128)(2,1)S(1)}, u32[]{:S(2)}, u32[]{:S(2)}) %collective-permute-start.5) | collective-permute-done | bytes 270368 | tf_op jit(solution)/shard_map/ppermute | solution.py:21
  36.2 1.2 %collective-permute-start.10 = (bf16[264,512]{1,0:T(8,128)(2,1)S(1)}, bf16[264,512]{1,0:T(8,128)(2,1)S(1)}, u32[]{:S(2)}, u32[]{:S(2)}) collective-permute-start(bf16[264,512]{1,0:T(8,128)(2,1)S(1)} %get-tuple-element.43.refs_0_), channel_id=1, source_target_pairs={{0,2},{1,3},{2,0},{3,1},{4,6},{5,7},{6,4},{7,5},{8,10},{9,11},{10,... | collective-permute-start | bytes 811016 | tf_op jit(solution)/shard_map/ppermute | solution.py:26
  37.4 5.8 %collective-permute-done.6.refs_6_ = bf16[264,512]{1,0:T(8,128)(2,1)S(1)} collective-permute-done((bf16[264,512]{1,0:T(8,128)(2,1)S(1)}, bf16[264,512]{1,0:T(8,128)(2,1)S(1)}, u32[]{:S(2)}, u32[]{:S(2)}) %collective-permute-start.6) | collective-permute-done | bytes 270368 | tf_op jit(solution)/shard_map/ppermute | solution.py:26
  43.2 5.8 %collective-permute-done.4.refs_3_ = bf16[264,512]{1,0:T(8,128)(2,1)S(1)} collective-permute-done((bf16[264,512]{1,0:T(8,128)(2,1)S(1)}, bf16[264,512]{1,0:T(8,128)(2,1)S(1)}, u32[]{:S(2)}, u32[]{:S(2)}) %collective-permute-start.4) | collective-permute-done | bytes 270368 | tf_op jit(solution)/shard_map/ppermute | solution.py:26
  49.0 5.8 %collective-permute-done.10.refs_2_ = bf16[264,512]{1,0:T(8,128)(2,1)S(1)} collective-permute-done((bf16[264,512]{1,0:T(8,128)(2,1)S(1)}, bf16[264,512]{1,0:T(8,128)(2,1)S(1)}, u32[]{:S(2)}, u32[]{:S(2)}) %collective-permute-start.10) | collective-permute-done | bytes 270368 | tf_op jit(solution)/shard_map/ppermute | solution.py:26
  54.8 1.0 collective-permute-start.11
  55.8 4.8 %collective-permute-done.7.refs_7_ = bf16[264,512]{1,0:T(8,128)(2,1)S(1)} collective-permute-done((bf16[264,512]{1,0:T(8,128)(2,1)S(1)}, bf16[264,512]{1,0:T(8,128)(2,1)S(1)}, u32[]{:S(2)}, u32[]{:S(2)}) %collective-permute-start.7) | collective-permute-done | bytes 270368 | tf_op jit(solution)/shard_map/ppermute | solution.py:26
  60.6 3.6 %experts_bwd.1 = (f32[264,512]{1,0:T(8,128)S(1)}, f32[264,512]{1,0:T(8,128)S(1)}, bf16[264,512]{1,0:T(8,128)(2,1)S(1)}, bf16[264,512]{1,0:T(8,128)(2,1)S(1)}) custom-call(bf16[264,512]{1,0:T(8,128)(2,1)S(1)} %get-tuple-element.34.refs_0_, bf16[264,512]{1,0:T(8,128)(2,1)S(1)} %collective-permute-done.2.refs_1_, ...), custom_call_target="tpu_custom_call" | custom-call | flops 1000 | bytes 1000 | tf_op jit(solution)/shard_map/experts_bwd/pallas_call | solution.py:293
  64.2 1.0 %collective-permute-start.13 = (bf16[264,512]{1,0:T(8,128)(2,1)S(1)}, bf16[264,512]{1,0:T(8,128)(2,1)S(1)}, u32[]{:S(2)}, u32[]{:S(2)}) collective-permute-start(bf16[264,512]{1,0:T(8,128)(2,1)S(1)} %get-tuple-element.50), channel_id=1, source_target_pairs={{0,2},{1,3},{2,0},{3,1},{4,6},{5,7},{6,4},{7,5},{8,10},{9,11},{10,... | collective-permute-start | bytes 811016 | tf_op jit(solution)/shard_map/ppermute | solution.py:26
  66.1 2.3 %experts_fwd.1 = (f32[264,512]{1,0:T(8,128)S(1)}, f32[264,512]{1,0:T(8,128)S(1)}, bf16[264,512]{1,0:T(8,128)(2,1)S(1)}, bf16[264,512]{1,0:T(8,128)(2,1)S(1)}) custom-call(bf16[264,512]{1,0:T(8,128)(2,1)S(1)} %get-tuple-element.43.refs_0_, bf16[264,512]{1,0:T(8,128)(2,1)S(1)} %collective-permute-done.9.refs_1_, ...), custom_call_target="tpu_custom_call" | custom-call | flops 1000 | bytes 1000 | tf_op jit(solution)/shard_map/experts_fwd/pallas_call | solution.py:296
  68.3 1.3 %collective-permute-start.12 = (bf16[264,512]{1,0:T(8,128)(2,1)S(1)}, bf16[264,512]{1,0:T(8,128)(2,1)S(1)}, u32[]{:S(2)}, u32[]{:S(2)}) collective-permute-start(bf16[264,512]{1,0:T(8,128)(2,1)S(1)} %get-tuple-element.48), channel_id=1, source_target_pairs={{0,2},{1,3},{2,0},{3,1},{4,6},{5,7},{6,4},{7,5},{8,10},{9,11},{10,... | collective-permute-start | bytes 811016 | tf_op jit(solution)/shard_map/ppermute | solution.py:26
  69.7 3.9 %collective-permute-done.13 = bf16[264,512]{1,0:T(8,128)(2,1)S(1)} collective-permute-done((bf16[264,512]{1,0:T(8,128)(2,1)S(1)}, bf16[264,512]{1,0:T(8,128)(2,1)S(1)}, u32[]{:S(2)}, u32[]{:S(2)}) %collective-permute-start.13) | collective-permute-done | bytes 270368 | tf_op jit(solution)/shard_map/ppermute | solution.py:26
  73.6 2.1 %collective-permute-start.14 = (bf16[264,512]{1,0:T(8,128)(2,1)S(1)}, bf16[264,512]{1,0:T(8,128)(2,1)S(1)}, u32[]{:S(2)}, u32[]{:S(2)}) collective-permute-start(bf16[264,512]{1,0:T(8,128)(2,1)S(1)} %add_convert_fusion), channel_id=1, source_target_pairs={{0,4},{1,5},{2,6},{3,7},{4,0},{5,1},{6,2},{7,3},{8,12},{9,13},{10,... | collective-permute-start | bytes 811016 | tf_op jit(solution)/shard_map/ppermute | solution.py:21
  75.7 5.3 %collective-permute-start.17 = (bf16[264,512]{1,0:T(8,128)(2,1)S(1)}, bf16[264,512]{1,0:T(8,128)(2,1)S(1)}, u32[]{:S(2)}, u32[]{:S(2)}) collective-permute-start(bf16[264,512]{1,0:T(8,128)(2,1)S(1)} %get-tuple-element.53), channel_id=1, source_target_pairs={{0,2},{1,3},{2,0},{3,1},{4,6},{5,7},{6,4},{7,5},{8,10},{9,11},{10,... | collective-permute-start | bytes 811016 | tf_op jit(solution)/shard_map/ppermute | solution.py:26
  81.0 3.4 %collective-permute-done.12 = bf16[264,512]{1,0:T(8,128)(2,1)S(1)} collective-permute-done((bf16[264,512]{1,0:T(8,128)(2,1)S(1)}, bf16[264,512]{1,0:T(8,128)(2,1)S(1)}, u32[]{:S(2)}, u32[]{:S(2)}) %collective-permute-start.12) | collective-permute-done | bytes 270368 | tf_op jit(solution)/shard_map/ppermute | solution.py:26
  84.6 2.3 %collective-permute-done.14.refs_2_ = bf16[264,512]{1,0:T(8,128)(2,1)S(1)} collective-permute-done((bf16[264,512]{1,0:T(8,128)(2,1)S(1)}, bf16[264,512]{1,0:T(8,128)(2,1)S(1)}, u32[]{:S(2)}, u32[]{:S(2)}) %collective-permute-start.14) | collective-permute-done | bytes 270368 | tf_op jit(solution)/shard_map/ppermute | solution.py:21
  86.8 3.5 %collective-permute-start.15 = (bf16[264,512]{1,0:T(8,128)(2,1)S(1)}, bf16[264,512]{1,0:T(8,128)(2,1)S(1)}, u32[]{:S(2)}, u32[]{:S(2)}) collective-permute-start(bf16[264,512]{1,0:T(8,128)(2,1)S(1)} %get-tuple-element.51), channel_id=1, source_target_pairs={{0,2},{1,3},{2,0},{3,1},{4,6},{5,7},{6,4},{7,5},{8,10},{9,11},{10,... | collective-permute-start | bytes 811016 | tf_op jit(solution)/shard_map/ppermute | solution.py:26
  90.3 5.7 %collective-permute-done.17.refs_1_ = bf16[264,512]{1,0:T(8,128)(2,1)S(1)} collective-permute-done((bf16[264,512]{1,0:T(8,128)(2,1)S(1)}, bf16[264,512]{1,0:T(8,128)(2,1)S(1)}, u32[]{:S(2)}, u32[]{:S(2)}) %collective-permute-start.17) | collective-permute-done | bytes 270368 | tf_op jit(solution)/shard_map/ppermute | solution.py:26
  96.0 2.0 %home_bwd.1 = bf16[128,2048]{1,0:T(8,128)(2,1)} custom-call(s32[1]{0:T(128)} %bitcast.own_ref, s32[1,128]{1,0:T(1,128)S(1)} %bitcast.30, f32[1,128]{1,0:T(1,128)S(1)} %bitcast.34, f32[1,2048]{1,0:T(1,128)S(1)} %copy-done.5, bf16[128,2048]{1,0:T(8,128)(2,1)S(1)} %bitcast.27, bf16[128,2048]{1,0:T(8,128)(2,1)S(1)} %collective-permute-done.1.x_ref.up_ref, ...), custom_call_target="tpu_custom_call" | custom-call | flops 1000 | bytes 1000 | tf_op jit(solution)/shard_map/home_bwd/pallas_call | solution.py:304
  98.0 3.1 %collective-permute-done.15.refs_1_ = bf16[264,512]{1,0:T(8,128)(2,1)S(1)} collective-permute-done((bf16[264,512]{1,0:T(8,128)(2,1)S(1)}, bf16[264,512]{1,0:T(8,128)(2,1)S(1)}, u32[]{:S(2)}, u32[]{:S(2)}) %collective-permute-start.15) | collective-permute-done | bytes 270368 | tf_op jit(solution)/shard_map/ppermute | solution.py:26
  101.2 1.7 %home_fwd.1 = bf16[128,2048]{1,0:T(8,128)(2,1)} custom-call(s32[1]{0:T(128)} %bitcast.own_ref, s32[1,128]{1,0:T(1,128)S(1)} %bitcast.32, f32[1,128]{1,0:T(1,128)S(1)} %bitcast.33, bf16[128,2048]{1,0:T(8,128)(2,1)S(1)} %collective-permute-done.x_ref, f32[264,512]{1,0:T(8,128)S(1)} %get-tuple-element.45.refs_0_, ...), custom_call_target="tpu_custom_call" | custom-call | flops 1000 | bytes 1000 | tf_op jit(solution)/shard_map/home_fwd/pallas_call | solution.py:311
  (35 shorter events, 2.8 us)
Async XLA Ops:
  0.6 59.9 %copy-start.1 = (bf16[1,2048,192]{1,2,0:T(8,128)(2,1)S(1)}, bf16[1,2048,192]{1,2,0:T(8,128)(2,1)}, u32[]{:S(2)}) copy-start(bf16[1,2048,192]{1,2,0:T(8,128)(2,1)} %param.16) | copy-start | bytes 2359300
  0.6 59.9 %copy-start.2 = (bf16[1,192,2048]{2,1,0:T(8,128)(2,1)S(1)}, bf16[1,192,2048]{2,1,0:T(8,128)(2,1)}, u32[]{:S(2)}) copy-start(bf16[1,192,2048]{2,1,0:T(8,128)(2,1)} %param.17) | copy-start | bytes 2359300
  0.7 16.7 %copy-start.6 = (s32[1,128,1]{1,2,0:T(1,128)S(1)}, s32[1,128,1]{1,2,0:T(1,128)}, u32[]{:S(2)}) copy-start(s32[1,128,1]{1,2,0:T(1,128)} %param.20) | copy-start | bytes 1540
  0.7 59.9 %copy-start = (bf16[1,2048,192]{1,2,0:T(8,128)(2,1)S(1)}, bf16[1,2048,192]{1,2,0:T(8,128)(2,1)}, u32[]{:S(2)}) copy-start(bf16[1,2048,192]{1,2,0:T(8,128)(2,1)} %param.15) | copy-start | bytes 2359300
  0.7 25.4 %copy-start.5 = (f32[1,2048]{1,0:T(1,128)S(1)}, f32[1,2048]{1,0:T(1,128)}, u32[]{:S(2)}) copy-start(f32[1,2048]{1,0:T(1,128)} %gain_ref.3) | copy-start | bytes 24580
  0.7 6.8 %copy-start.10 = (bf16[1,128,2048]{2,1,0:T(8,128)(2,1)S(1)}, bf16[1,128,2048]{2,1,0:T(8,128)(2,1)}, u32[]{:S(2)}) copy-start(bf16[1,128,2048]{2,1,0:T(8,128)(2,1)} %param.13) | copy-start | bytes 1572868
  0.7 25.4 %copy-start.7 = (s32[1,128,1]{1,2,0:T(1,128)S(1)}, s32[1,128,1]{1,2,0:T(1,128)}, u32[]{:S(2)}) copy-start(s32[1,128,1]{1,2,0:T(1,128)} %param.18) | copy-start | bytes 1540
  4.5 56.1 %collective-permute-start.8 = (bf16[576,2048]{1,0:T(8,128)(2,1)}, bf16[576,2048]{1,0:T(8,128)(2,1)S(1)}, u32[]{:S(2)}, u32[]{:S(2)}) collective-permute-start(bf16[576,2048]{1,0:T(8,128)(2,1)} %get-tuple-element.39), channel_id=1, source_target_pairs={{0,1},{1,0},{2,3},{3,2},{4,5},{5,4},{6,7},{7,6},{8,9},{9,8},{10,11... | collective-permute-start | bytes 7077896 | tf_op jit(solution)/shard_map/ppermute | solution.py:26
  7.5 9.9 %collective-permute-start.1 = (bf16[128,2048]{1,0:T(8,128)(2,1)S(1)}, bf16[128,2048]{1,0:T(8,128)(2,1)S(1)}, u32[]{:S(2)}, u32[]{:S(2)}) collective-permute-start(bf16[128,2048]{1,0:T(8,128)(2,1)S(1)} %bitcast.37), channel_id=1, source_target_pairs={{0,24},{8,0},{16,8},{24,16},{1,25},{9,1},{17,9},{25,17},{2,26},{10... | collective-permute-start | bytes 1572872 | tf_op jit(solution)/shard_map/ppermute | solution.py:21
  8.2 15.2 %collective-permute-start.2 = (bf16[264,512]{1,0:T(8,128)(2,1)}, bf16[264,512]{1,0:T(8,128)(2,1)S(1)}, u32[]{:S(2)}, u32[]{:S(2)}) collective-permute-start(bf16[264,512]{1,0:T(8,128)(2,1)} %get-tuple-element.31), channel_id=1, source_target_pairs={{0,4},{1,5},{2,6},{3,7},{4,0},{5,1},{6,2},{7,3},{8,12},{9,13},{10,... | collective-permute-start | bytes 811016 | tf_op jit(solution)/shard_map/ppermute | solution.py:21
  10.8 15.3 %collective-permute-start = (bf16[128,2048]{1,0:T(8,128)(2,1)}, bf16[128,2048]{1,0:T(8,128)(2,1)S(1)}, u32[]{:S(2)}, u32[]{:S(2)}) collective-permute-start(bf16[128,2048]{1,0:T(8,128)(2,1)} %bitcast.38), channel_id=1, source_target_pairs={{0,8},{8,16},{16,24},{24,0},{1,9},{9,17},{17,25},{25,1},{2,10},{10... | collective-permute-start | bytes 1572872 | tf_op jit(solution)/shard_map/ppermute | solution.py:21
  10.8 15.3 %collective-permute-start.3 = (bf16[264,512]{1,0:T(8,128)(2,1)}, bf16[264,512]{1,0:T(8,128)(2,1)S(1)}, u32[]{:S(2)}, u32[]{:S(2)}) collective-permute-start(bf16[264,512]{1,0:T(8,128)(2,1)} %get-tuple-element.28.kept_ref), channel_id=1, source_target_pairs={{0,2},{1,3},{2,0},{3,1},{4,6},{5,7},{6,4},{7,5},{8,10},{9,11},{10,... | collective-permute-start | bytes 811016 | tf_op jit(solution)/shard_map/ppermute | solution.py:26
  18.2 17.9 %collective-permute-start.5 = (bf16[264,512]{1,0:T(8,128)(2,1)S(1)}, bf16[264,512]{1,0:T(8,128)(2,1)S(1)}, u32[]{:S(2)}, u32[]{:S(2)}) collective-permute-start(bf16[264,512]{1,0:T(8,128)(2,1)S(1)} %get-tuple-element.36), channel_id=1, source_target_pairs={{0,4},{1,5},{2,6},{3,7},{4,0},{5,1},{6,2},{7,3},{8,12},{9,13},{10,... | collective-permute-start | bytes 811016 | tf_op jit(solution)/shard_map/ppermute | solution.py:21
  23.4 19.8 %collective-permute-start.6 = (bf16[264,512]{1,0:T(8,128)(2,1)S(1)}, bf16[264,512]{1,0:T(8,128)(2,1)S(1)}, u32[]{:S(2)}, u32[]{:S(2)}) collective-permute-start(bf16[264,512]{1,0:T(8,128)(2,1)S(1)} %get-tuple-element.37.refs_4_), channel_id=1, source_target_pairs={{0,2},{1,3},{2,0},{3,1},{4,6},{5,7},{6,4},{7,5},{8,10},{9,11},{10,... | collective-permute-start | bytes 811016 | tf_op jit(solution)/shard_map/ppermute | solution.py:26
  26.1 22.9 %collective-permute-start.4 = (bf16[264,512]{1,0:T(8,128)(2,1)S(1)}, bf16[264,512]{1,0:T(8,128)(2,1)S(1)}, u32[]{:S(2)}, u32[]{:S(2)}) collective-permute-start(bf16[264,512]{1,0:T(8,128)(2,1)S(1)} %collective-permute-done.2.refs_1_), channel_id=1, source_target_pairs={{0,2},{1,3},{2,0},{3,1},{4,6},{5,7},{6,4},{7,5},{8,10},{9,11},{10,... | collective-permute-start | bytes 811016 | tf_op jit(solution)/shard_map/ppermute | solution.py:26
  26.1 1.0 copy-start.4
  28.0 21.0 %collective-permute-start.9 = (bf16[264,512]{1,0:T(8,128)(2,1)S(1)}, bf16[264,512]{1,0:T(8,128)(2,1)S(1)}, u32[]{:S(2)}, u32[]{:S(2)}) collective-permute-start(bf16[264,512]{1,0:T(8,128)(2,1)S(1)} %get-tuple-element.42), channel_id=1, source_target_pairs={{0,4},{1,5},{2,6},{3,7},{4,0},{5,1},{6,2},{7,3},{8,12},{9,13},{10,... | collective-permute-start | bytes 811016 | tf_op jit(solution)/shard_map/ppermute | solution.py:21
  36.2 18.6 %collective-permute-start.10 = (bf16[264,512]{1,0:T(8,128)(2,1)S(1)}, bf16[264,512]{1,0:T(8,128)(2,1)S(1)}, u32[]{:S(2)}, u32[]{:S(2)}) collective-permute-start(bf16[264,512]{1,0:T(8,128)(2,1)S(1)} %get-tuple-element.43.refs_0_), channel_id=1, source_target_pairs={{0,2},{1,3},{2,0},{3,1},{4,6},{5,7},{6,4},{7,5},{8,10},{9,11},{10,... | collective-permute-start | bytes 811016 | tf_op jit(solution)/shard_map/ppermute | solution.py:26
  43.2 17.4 %collective-permute-start.7 = (bf16[264,512]{1,0:T(8,128)(2,1)S(1)}, bf16[264,512]{1,0:T(8,128)(2,1)S(1)}, u32[]{:S(2)}, u32[]{:S(2)}) collective-permute-start(bf16[264,512]{1,0:T(8,128)(2,1)S(1)} %collective-permute-done.5.refs_5_), channel_id=1, source_target_pairs={{0,2},{1,3},{2,0},{3,1},{4,6},{5,7},{6,4},{7,5},{8,10},{9,11},{10,... | collective-permute-start | bytes 811016 | tf_op jit(solution)/shard_map/ppermute | solution.py:26
  54.8 11.3 %collective-permute-start.11 = (bf16[264,512]{1,0:T(8,128)(2,1)S(1)}, bf16[264,512]{1,0:T(8,128)(2,1)S(1)}, u32[]{:S(2)}, u32[]{:S(2)}) collective-permute-start(bf16[264,512]{1,0:T(8,128)(2,1)S(1)} %collective-permute-done.9.refs_1_), channel_id=1, source_target_pairs={{0,2},{1,3},{2,0},{3,1},{4,6},{5,7},{6,4},{7,5},{8,10},{9,11},{10,... | collective-permute-start | bytes 811016 | tf_op jit(solution)/shard_map/ppermute | solution.py:26
  64.2 9.3 %collective-permute-start.13 = (bf16[264,512]{1,0:T(8,128)(2,1)S(1)}, bf16[264,512]{1,0:T(8,128)(2,1)S(1)}, u32[]{:S(2)}, u32[]{:S(2)}) collective-permute-start(bf16[264,512]{1,0:T(8,128)(2,1)S(1)} %get-tuple-element.50), channel_id=1, source_target_pairs={{0,2},{1,3},{2,0},{3,1},{4,6},{5,7},{6,4},{7,5},{8,10},{9,11},{10,... | collective-permute-start | bytes 811016 | tf_op jit(solution)/shard_map/ppermute | solution.py:26
  65.3 30.7 %copy-start.9 = (f32[1,128,1]{1,2,0:T(1,128)S(1)}, f32[1,128,1]{1,2,0:T(1,128)}, u32[]{:S(2)}) copy-start(f32[1,128,1]{1,2,0:T(1,128)} %param.21) | copy-start | bytes 1540
  68.3 27.7 %copy-start.3 = (bf16[1,128,2048]{2,1,0:T(8,128)(2,1)S(1)}, bf16[1,128,2048]{2,1,0:T(8,128)(2,1)}, u32[]{:S(2)}) copy-start(bf16[1,128,2048]{2,1,0:T(8,128)(2,1)} %param.12) | copy-start | bytes 1572868
  68.3 16.1 %collective-permute-start.12 = (bf16[264,512]{1,0:T(8,128)(2,1)S(1)}, bf16[264,512]{1,0:T(8,128)(2,1)S(1)}, u32[]{:S(2)}, u32[]{:S(2)}) collective-permute-start(bf16[264,512]{1,0:T(8,128)(2,1)S(1)} %get-tuple-element.48), channel_id=1, source_target_pairs={{0,2},{1,3},{2,0},{3,1},{4,6},{5,7},{6,4},{7,5},{8,10},{9,11},{10,... | collective-permute-start | bytes 811016 | tf_op jit(solution)/shard_map/ppermute | solution.py:26
  73.5 27.6 %copy-start.8 = (f32[1,128,1]{1,2,0:T(1,128)S(1)}, f32[1,128,1]{1,2,0:T(1,128)}, u32[]{:S(2)}) copy-start(f32[1,128,1]{1,2,0:T(1,128)} %param.19) | copy-start | bytes 1540
  73.6 13.2 %collective-permute-start.14 = (bf16[264,512]{1,0:T(8,128)(2,1)S(1)}, bf16[264,512]{1,0:T(8,128)(2,1)S(1)}, u32[]{:S(2)}, u32[]{:S(2)}) collective-permute-start(bf16[264,512]{1,0:T(8,128)(2,1)S(1)} %add_convert_fusion), channel_id=1, source_target_pairs={{0,4},{1,5},{2,6},{3,7},{4,0},{5,1},{6,2},{7,3},{8,12},{9,13},{10,... | collective-permute-start | bytes 811016 | tf_op jit(solution)/shard_map/ppermute | solution.py:21
  75.7 20.3 %collective-permute-start.17 = (bf16[264,512]{1,0:T(8,128)(2,1)S(1)}, bf16[264,512]{1,0:T(8,128)(2,1)S(1)}, u32[]{:S(2)}, u32[]{:S(2)}) collective-permute-start(bf16[264,512]{1,0:T(8,128)(2,1)S(1)} %get-tuple-element.53), channel_id=1, source_target_pairs={{0,2},{1,3},{2,0},{3,1},{4,6},{5,7},{6,4},{7,5},{8,10},{9,11},{10,... | collective-permute-start | bytes 811016 | tf_op jit(solution)/shard_map/ppermute | solution.py:26
  84.5 13.5 %collective-permute-start.16 = (bf16[264,512]{1,0:T(8,128)(2,1)S(1)}, bf16[264,512]{1,0:T(8,128)(2,1)S(1)}, u32[]{:S(2)}, u32[]{:S(2)}) collective-permute-start(bf16[264,512]{1,0:T(8,128)(2,1)S(1)} %add_convert_fusion.1), channel_id=1, source_target_pairs={{0,4},{1,5},{2,6},{3,7},{4,0},{5,1},{6,2},{7,3},{8,12},{9,13},{10,... | collective-permute-start | bytes 811016 | tf_op jit(solution)/shard_map/ppermute | solution.py:21
  86.8 14.3 %collective-permute-start.15 = (bf16[264,512]{1,0:T(8,128)(2,1)S(1)}, bf16[264,512]{1,0:T(8,128)(2,1)S(1)}, u32[]{:S(2)}, u32[]{:S(2)}) collective-permute-start(bf16[264,512]{1,0:T(8,128)(2,1)S(1)} %get-tuple-element.51), channel_id=1, source_target_pairs={{0,2},{1,3},{2,0},{3,1},{4,6},{5,7},{6,4},{7,5},{8,10},{9,11},{10,... | collective-permute-start | bytes 811016 | tf_op jit(solution)/shard_map/ppermute | solution.py:26

commit v14 on v13

--- a/solution.py
+++ b/solution.py
@@ -239,7 +239,6 @@
     packed = [jax.ShapeDtypeStruct(shape, BF16)] * experts
     partial = [jax.ShapeDtypeStruct(shape, F32)] * experts + packed
     tokens = jax.ShapeDtypeStruct((tok_count, width), BF16)
-    wide = pltpu.VMEM((2 * experts * pitch, width), BF16)
 
     incoming = shifted(act_in[0], "section", 1)
     upstream = shifted(grad_in[0], "section", -1)
@@ -289,13 +288,20 @@
     rows_g = rows_g + swap_g + partners(rows_g[1:], swap_g[0])
     rows_f = rows_f + swap_f + partners(rows_f[1:], swap_f[0], rows_b[-1])
 
-    count = 2 * experts
-    partial_b = local_call(
-        functools.partial(backward_body, count, rows), partial, scratch=[wide, wide], vmem_mib=40, name="experts_bwd"
-    )(*rows_b, *rows_g, *shares)
-    partial_f = local_call(
-        functools.partial(forward_body, count, rows), partial, scratch=[wide], vmem_mib=32, name="experts_fwd"
-    )(after(rows_f[0], partial_b[0]), *rows_f[1:], *shares)
+    def run_experts(body, name, inputs, count, out_shape):
+        wides = [pltpu.VMEM((count * pitch, width), BF16)] * (len(inputs) // count)
+        return local_call(
+            functools.partial(body, count, rows), out_shape, scratch=wides, vmem_mib=40, name=name
+        )(*inputs, *shares)
+
+    near = experts + 1
+    partial_b = run_experts(backward_body, "experts_bwd_near", rows_b[:near] + rows_g[:near], near, partial[:near])
+    far_g = [after(rows_g[near], partial_b[0])] + rows_g[near + 1:]
+    partial_b = partial_b + run_experts(
+        backward_body, "experts_bwd_far", rows_b[near:] + far_g, experts - 1, partial[near:]
+    )
+    rows_f = [after(rows_f[0], partial_b[-1])] + rows_f[1:]
+    partial_f = run_experts(forward_body, "experts_fwd", rows_f, 2 * experts, partial)
     totals_b, home_b = crossing_home(partial_b)
     totals_f, home_f = crossing_home(partial_f)
     back_b = [partial_b[0]] + partners(partial_b[experts:experts + 1], *totals_b) + home_b

time: 103 us -> 103 us (level)
  starting transfers between devices: 31.8 us -> 28.4 us
  Pallas kernels: 15.2 us -> 16.9 us
  waiting for transfers between devices: 54 us -> 55.5 us
    ppermute x11, starting transfers between devices: 19.4 us -> 14.6 us  [swapped(): return lax.ppermute(value, axis, [(i, i ^ bit) for i in range(count)])]
    pallas_call x2 -> x3, Pallas kernels: 5.89 us -> 7.63 us  [run_experts(): local_call(functools.partial(body, count, rows), out_shape, scratch=wides...]
    ppermute x7, starting transfers between devices: 12.4 us -> 13.8 us  [shifted(): lax.ppermute(value, axis, [(i, (i + steps) % count) for i in range(count)])]
  transfers between devices with their start and end apart: 18 -> 18, of which waited for: 14 -> 14; matrix products, arithmetic and copies ran while one was open for 0% -> 0% of each run, Pallas kernels for 9% -> 11%
where the time goes in v14:
time: 103 us
  waiting for transfers between devices  55.5 us (54%)
  starting transfers between devices  28.4 us (28%)
  Pallas kernels  16.9 us (16%)
    ppermute x11, waiting for transfers between devices, swapped(): return lax.ppermute(value, axis, [(i, i ^ bit) for i in range(count)])  41 us
    ppermute x11, starting transfers between devices, swapped(): return lax.ppermute(value, axis, [(i, i ^ bit) for i in range(count)])  14.6 us
    ppermute x7, waiting for transfers between devices, shifted(): lax.ppermute(value, axis, [(i, (i + steps) % count) for i in range(count)])  14.5 us
    ppermute x7, starting transfers between devices, shifted(): lax.ppermute(value, axis, [(i, (i + steps) % count) for i in range(count)])  13.8 us
    pallas_call x3, Pallas kernels, run_experts(): local_call(functools.partial(body, count, rows), out_shape, scratch=wides...  7.63 us
    pallas_call x1, Pallas kernels, per_device(): local_call(first_body, [jax.ShapeDtypeStruct((3 * w_down.shape[1], width)...  3.76 us
  transfers between devices with their start and end apart: 18, of which 14 were waited for; matrix products, arithmetic and copies ran while one was open for 0% of the time, Pallas kernels for 11%

profile of v14, /device:TPU:0, one launch (start us, length us, event | category | flops | bytes accessed | tf_op | source)
XLA Modules:
  0.0 102.8 jit_solution(4357099617463882742)
XLA Ops:
  0.7 3.8 %join_weights_pack_saved.1 = (bf16[576,2048]{1,0:T(8,128)(2,1)}, bf16[264,512]{1,0:T(8,128)(2,1)}, bf16[264,512]{1,0:T(8,128)(2,1)}) custom-call(s32[1]{0:T(128)} %bitcast.own_ref, s32[1,128]{1,0:T(1,128)} %bitcast.31, f32[1,2048]{1,0:T(1,128)} %gain_ref.3, bf16[128,2048]{1,0:T(8,128)(2,1)} %bitcast.29, bf16[192,2048]{1,0:T(8,128)(2,1)} %bitcast.17, ...), custom_call_target="tpu_custom_call" | custom-call | flops 1000 | bytes 1000 | tf_op jit(solution)/shard_map/join_weights_pack_saved/pallas_call | solution.py:250
  4.5 3.0 %collective-permute-start.8 = (bf16[576,2048]{1,0:T(8,128)(2,1)}, bf16[576,2048]{1,0:T(8,128)(2,1)S(1)}, u32[]{:S(2)}, u32[]{:S(2)}) collective-permute-start(bf16[576,2048]{1,0:T(8,128)(2,1)} %get-tuple-element.39), channel_id=1, source_target_pairs={{0,1},{1,0},{2,3},{3,2},{4,5},{5,4},{6,7},{7,6},{8,9},{9,8},{10,11... | collective-permute-start | bytes 7077896 | tf_op jit(solution)/shard_map/ppermute | solution.py:26
  8.2 2.6 %collective-permute-start.2 = (bf16[264,512]{1,0:T(8,128)(2,1)}, bf16[264,512]{1,0:T(8,128)(2,1)S(1)}, u32[]{:S(2)}, u32[]{:S(2)}) collective-permute-start(bf16[264,512]{1,0:T(8,128)(2,1)} %get-tuple-element.31), channel_id=1, source_target_pairs={{0,4},{1,5},{2,6},{3,7},{4,0},{5,1},{6,2},{7,3},{8,12},{9,13},{10,... | collective-permute-start | bytes 811016 | tf_op jit(solution)/shard_map/ppermute | solution.py:21
  10.8 1.6 %collective-permute-start.3 = (bf16[264,512]{1,0:T(8,128)(2,1)}, bf16[264,512]{1,0:T(8,128)(2,1)S(1)}, u32[]{:S(2)}, u32[]{:S(2)}) collective-permute-start(bf16[264,512]{1,0:T(8,128)(2,1)} %get-tuple-element.28.kept_ref), channel_id=1, source_target_pairs={{0,2},{1,3},{2,0},{3,1},{4,6},{5,7},{6,4},{7,5},{8,10},{9,11},{10,... | collective-permute-start | bytes 811016 | tf_op jit(solution)/shard_map/ppermute | solution.py:26
  12.3 5.0 %collective-permute-done.1.x_ref.up_ref = bf16[128,2048]{1,0:T(8,128)(2,1)S(1)} collective-permute-done((bf16[128,2048]{1,0:T(8,128)(2,1)S(1)}, bf16[128,2048]{1,0:T(8,128)(2,1)S(1)}, u32[]{:S(2)}, u32[]{:S(2)}) %collective-permute-start.1) | collective-permute-done | bytes 524320 | tf_op jit(solution)/shard_map/ppermute | solution.py:21
  18.2 5.0 %collective-permute-start.5 = (bf16[264,512]{1,0:T(8,128)(2,1)S(1)}, bf16[264,512]{1,0:T(8,128)(2,1)S(1)}, u32[]{:S(2)}, u32[]{:S(2)}) collective-permute-start(bf16[264,512]{1,0:T(8,128)(2,1)S(1)} %get-tuple-element.35), channel_id=1, source_target_pairs={{0,4},{1,5},{2,6},{3,7},{4,0},{5,1},{6,2},{7,3},{8,12},{9,13},{10,... | collective-permute-start | bytes 811016 | tf_op jit(solution)/shard_map/ppermute | solution.py:21
  23.4 1.4 %collective-permute-start.6 = (bf16[264,512]{1,0:T(8,128)(2,1)S(1)}, bf16[264,512]{1,0:T(8,128)(2,1)S(1)}, u32[]{:S(2)}, u32[]{:S(2)}) collective-permute-start(bf16[264,512]{1,0:T(8,128)(2,1)S(1)} %get-tuple-element.36.refs_3_), channel_id=1, source_target_pairs={{0,2},{1,3},{2,0},{3,1},{4,6},{5,7},{6,4},{7,5},{8,10},{9,11},{10,... | collective-permute-start | bytes 811016 | tf_op jit(solution)/shard_map/ppermute | solution.py:26
  24.8 1.2 %collective-permute-done.3.refs_2_ = bf16[264,512]{1,0:T(8,128)(2,1)S(1)} collective-permute-done((bf16[264,512]{1,0:T(8,128)(2,1)}, bf16[264,512]{1,0:T(8,128)(2,1)S(1)}, u32[]{:S(2)}, u32[]{:S(2)}) %collective-permute-start.3) | collective-permute-done | bytes 270368 | tf_op jit(solution)/shard_map/ppermute | solution.py:26
  26.1 0.9 copy-done.4
  28.0 2.0 %collective-permute-start.9 = (bf16[264,512]{1,0:T(8,128)(2,1)S(1)}, bf16[264,512]{1,0:T(8,128)(2,1)S(1)}, u32[]{:S(2)}, u32[]{:S(2)}) collective-permute-start(bf16[264,512]{1,0:T(8,128)(2,1)S(1)} %get-tuple-element.43), channel_id=1, source_target_pairs={{0,4},{1,5},{2,6},{3,7},{4,0},{5,1},{6,2},{7,3},{8,12},{9,13},{10,... | collective-permute-start | bytes 811016 | tf_op jit(solution)/shard_map/ppermute | solution.py:21
  29.9 6.2 %collective-permute-done.5.refs_4_ = bf16[264,512]{1,0:T(8,128)(2,1)S(1)} collective-permute-done((bf16[264,512]{1,0:T(8,128)(2,1)S(1)}, bf16[264,512]{1,0:T(8,128)(2,1)S(1)}, u32[]{:S(2)}, u32[]{:S(2)}) %collective-permute-start.5) | collective-permute-done | bytes 270368 | tf_op jit(solution)/shard_map/ppermute | solution.py:21
  36.2 1.2 %collective-permute-start.10 = (bf16[264,512]{1,0:T(8,128)(2,1)S(1)}, bf16[264,512]{1,0:T(8,128)(2,1)S(1)}, u32[]{:S(2)}, u32[]{:S(2)}) collective-permute-start(bf16[264,512]{1,0:T(8,128)(2,1)S(1)} %get-tuple-element.44.refs_0_), channel_id=1, source_target_pairs={{0,2},{1,3},{2,0},{3,1},{4,6},{5,7},{6,4},{7,5},{8,10},{9,11},{10,... | collective-permute-start | bytes 811016 | tf_op jit(solution)/shard_map/ppermute | solution.py:26
  37.4 5.8 %collective-permute-done.6.refs_5_ = bf16[264,512]{1,0:T(8,128)(2,1)S(1)} collective-permute-done((bf16[264,512]{1,0:T(8,128)(2,1)S(1)}, bf16[264,512]{1,0:T(8,128)(2,1)S(1)}, u32[]{:S(2)}, u32[]{:S(2)}) %collective-permute-start.6) | collective-permute-done | bytes 270368 | tf_op jit(solution)/shard_map/ppermute | solution.py:26
  43.2 5.8 %collective-permute-done.4.refs_0_ = bf16[264,512]{1,0:T(8,128)(2,1)S(1)} collective-permute-done((bf16[264,512]{1,0:T(8,128)(2,1)S(1)}, bf16[264,512]{1,0:T(8,128)(2,1)S(1)}, u32[]{:S(2)}, u32[]{:S(2)}) %collective-permute-start.4) | collective-permute-done | bytes 270368 | tf_op jit(solution)/shard_map/ppermute | solution.py:26
  49.0 5.8 %collective-permute-done.10.refs_2_ = bf16[264,512]{1,0:T(8,128)(2,1)S(1)} collective-permute-done((bf16[264,512]{1,0:T(8,128)(2,1)S(1)}, bf16[264,512]{1,0:T(8,128)(2,1)S(1)}, u32[]{:S(2)}, u32[]{:S(2)}) %collective-permute-start.10) | collective-permute-done | bytes 270368 | tf_op jit(solution)/shard_map/ppermute | solution.py:26
  54.8 1.0 collective-permute-start.11
  55.8 3.2 %collective-permute-done.8.refs_9_.refs_5_.refs_7_ = bf16[576,2048]{1,0:T(8,128)(2,1)S(1)} collective-permute-done((bf16[576,2048]{1,0:T(8,128)(2,1)}, bf16[576,2048]{1,0:T(8,128)(2,1)S(1)}, u32[]{:S(2)}, u32[]{:S(2)}) %collective-permute-start.8) | collective-permute-done | bytes 2359328 | tf_op jit(solution)/shard_map/ppermute | solution.py:26
  59.0 2.9 %experts_bwd_near.1 = (f32[264,512]{1,0:T(8,128)S(1)}, f32[264,512]{1,0:T(8,128)S(1)}, bf16[264,512]{1,0:T(8,128)(2,1)S(1)}) custom-call(bf16[264,512]{1,0:T(8,128)(2,1)S(1)} %get-tuple-element.38.refs_0_, bf16[264,512]{1,0:T(8,128)(2,1)S(1)} %collective-permute-done.2.refs_1_, bf16[264,512]{1,0:T(8,128)(2,1)S(1)} %collective-permute-done.3.refs_2_, ...), custom_call_target="tpu_custom_call" | custom-call | flops 1000 | bytes 1000 | tf_op jit(solution)/shard_map/experts_bwd_near/pallas_call | solution.py:293
  61.8 2.5 %experts_bwd_far.1 = bf16[264,512]{1,0:T(8,128)(2,1)S(1)} custom-call(bf16[264,512]{1,0:T(8,128)(2,1)S(1)} %collective-permute-done.4.refs_0_, bf16[264,512]{1,0:T(8,128)(2,1)S(1)} %collective-permute-done.7.refs_1_, bf16[192,2048]{1,0:T(8,128)(2,1)S(1)} %bitcast.19, bf16[192,2048]{1,0:T(8,128)(2,1)S(1)} %bitcast.23, bf16[192,2048]{1,0:T(8,128)(2,1)S(1)} %bitcast.27, ...), custom_call_target="tpu_custom_call" | custom-call | flops 1000 | bytes 1000 | tf_op jit(solution)/shard_map/experts_bwd_far/pallas_call | solution.py:293
  64.4 1.9 %collective-permute-start.13 = (bf16[264,512]{1,0:T(8,128)(2,1)S(1)}, bf16[264,512]{1,0:T(8,128)(2,1)S(1)}, u32[]{:S(2)}, u32[]{:S(2)}) collective-permute-start(bf16[264,512]{1,0:T(8,128)(2,1)S(1)} %experts_bwd_far.1), channel_id=1, source_target_pairs={{0,2},{1,3},{2,0},{3,1},{4,6},{5,7},{6,4},{7,5},{8,10},{9,11},{10,... | collective-permute-start | bytes 811016 | tf_op jit(solution)/shard_map/ppermute | solution.py:26
  66.3 2.3 %experts_fwd.1 = (f32[264,512]{1,0:T(8,128)S(1)}, f32[264,512]{1,0:T(8,128)S(1)}, bf16[264,512]{1,0:T(8,128)(2,1)S(1)}, bf16[264,512]{1,0:T(8,128)(2,1)S(1)}) custom-call(bf16[264,512]{1,0:T(8,128)(2,1)S(1)} %get-tuple-element.44.refs_0_, bf16[264,512]{1,0:T(8,128)(2,1)S(1)} %collective-permute-done.9.refs_1_, ...), custom_call_target="tpu_custom_call" | custom-call | flops 1000 | bytes 1000 | tf_op jit(solution)/shard_map/experts_fwd/pallas_call | solution.py:293
  68.5 1.1 %collective-permute-start.12 = (bf16[264,512]{1,0:T(8,128)(2,1)S(1)}, bf16[264,512]{1,0:T(8,128)(2,1)S(1)}, u32[]{:S(2)}, u32[]{:S(2)}) collective-permute-start(bf16[264,512]{1,0:T(8,128)(2,1)S(1)} %get-tuple-element.49), channel_id=1, source_target_pairs={{0,2},{1,3},{2,0},{3,1},{4,6},{5,7},{6,4},{7,5},{8,10},{9,11},{10,... | collective-permute-start | bytes 811016 | tf_op jit(solution)/shard_map/ppermute | solution.py:26
  69.7 3.7 %collective-permute-done.13 = bf16[264,512]{1,0:T(8,128)(2,1)S(1)} collective-permute-done((bf16[264,512]{1,0:T(8,128)(2,1)S(1)}, bf16[264,512]{1,0:T(8,128)(2,1)S(1)}, u32[]{:S(2)}, u32[]{:S(2)}) %collective-permute-start.13) | collective-permute-done | bytes 270368 | tf_op jit(solution)/shard_map/ppermute | solution.py:26
  73.4 3.1 %collective-permute-start.14 = (bf16[264,512]{1,0:T(8,128)(2,1)S(1)}, bf16[264,512]{1,0:T(8,128)(2,1)S(1)}, u32[]{:S(2)}, u32[]{:S(2)}) collective-permute-start(bf16[264,512]{1,0:T(8,128)(2,1)S(1)} %add_convert_fusion), channel_id=1, source_target_pairs={{0,4},{1,5},{2,6},{3,7},{4,0},{5,1},{6,2},{7,3},{8,12},{9,13},{10,... | collective-permute-start | bytes 811016 | tf_op jit(solution)/shard_map/ppermute | solution.py:21
  76.5 1.5 %collective-permute-start.17 = (bf16[264,512]{1,0:T(8,128)(2,1)S(1)}, bf16[264,512]{1,0:T(8,128)(2,1)S(1)}, u32[]{:S(2)}, u32[]{:S(2)}) collective-permute-start(bf16[264,512]{1,0:T(8,128)(2,1)S(1)} %get-tuple-element.53), channel_id=1, source_target_pairs={{0,2},{1,3},{2,0},{3,1},{4,6},{5,7},{6,4},{7,5},{8,10},{9,11},{10,... | collective-permute-start | bytes 811016 | tf_op jit(solution)/shard_map/ppermute | solution.py:26
  78.1 5.8 %collective-permute-done.12 = bf16[264,512]{1,0:T(8,128)(2,1)S(1)} collective-permute-done((bf16[264,512]{1,0:T(8,128)(2,1)S(1)}, bf16[264,512]{1,0:T(8,128)(2,1)S(1)}, u32[]{:S(2)}, u32[]{:S(2)}) %collective-permute-start.12) | collective-permute-done | bytes 270368 | tf_op jit(solution)/shard_map/ppermute | solution.py:26
  84.5 2.8 %collective-permute-done.14.refs_2_ = bf16[264,512]{1,0:T(8,128)(2,1)S(1)} collective-permute-done((bf16[264,512]{1,0:T(8,128)(2,1)S(1)}, bf16[264,512]{1,0:T(8,128)(2,1)S(1)}, u32[]{:S(2)}, u32[]{:S(2)}) %collective-permute-start.14) | collective-permute-done | bytes 270368 | tf_op jit(solution)/shard_map/ppermute | solution.py:21
  87.3 1.8 %collective-permute-start.15 = (bf16[264,512]{1,0:T(8,128)(2,1)S(1)}, bf16[264,512]{1,0:T(8,128)(2,1)S(1)}, u32[]{:S(2)}, u32[]{:S(2)}) collective-permute-start(bf16[264,512]{1,0:T(8,128)(2,1)S(1)} %get-tuple-element.51), channel_id=1, source_target_pairs={{0,2},{1,3},{2,0},{3,1},{4,6},{5,7},{6,4},{7,5},{8,10},{9,11},{10,... | collective-permute-start | bytes 811016 | tf_op jit(solution)/shard_map/ppermute | solution.py:26
  89.1 6.4 %collective-permute-done.17.refs_1_ = bf16[264,512]{1,0:T(8,128)(2,1)S(1)} collective-permute-done((bf16[264,512]{1,0:T(8,128)(2,1)S(1)}, bf16[264,512]{1,0:T(8,128)(2,1)S(1)}, u32[]{:S(2)}, u32[]{:S(2)}) %collective-permute-start.17) | collective-permute-done | bytes 270368 | tf_op jit(solution)/shard_map/ppermute | solution.py:26
  95.5 2.0 %home_bwd.1 = bf16[128,2048]{1,0:T(8,128)(2,1)} custom-call(s32[1]{0:T(128)} %bitcast.own_ref, s32[1,128]{1,0:T(1,128)S(1)} %bitcast.33, f32[1,128]{1,0:T(1,128)S(1)} %bitcast.37, f32[1,2048]{1,0:T(1,128)S(1)} %copy-done.5, bf16[128,2048]{1,0:T(8,128)(2,1)S(1)} %bitcast.30, bf16[128,2048]{1,0:T(8,128)(2,1)S(1)} %collective-permute-done.1.x_ref.up_ref, ...), custom_call_target="tpu_custom_call" | custom-call | flops 1000 | bytes 1000 | tf_op jit(solution)/shard_map/home_bwd/pallas_call | solution.py:310
  97.7 3.3 %collective-permute-done.15.refs_1_ = bf16[264,512]{1,0:T(8,128)(2,1)S(1)} collective-permute-done((bf16[264,512]{1,0:T(8,128)(2,1)S(1)}, bf16[264,512]{1,0:T(8,128)(2,1)S(1)}, u32[]{:S(2)}, u32[]{:S(2)}) %collective-permute-start.15) | collective-permute-done | bytes 270368 | tf_op jit(solution)/shard_map/ppermute | solution.py:26
  101.1 1.7 %home_fwd.1 = bf16[128,2048]{1,0:T(8,128)(2,1)} custom-call(s32[1]{0:T(128)} %bitcast.own_ref, s32[1,128]{1,0:T(1,128)S(1)} %bitcast.35, f32[1,128]{1,0:T(1,128)S(1)} %bitcast.36, bf16[128,2048]{1,0:T(8,128)(2,1)S(1)} %collective-permute-done.x_ref, f32[264,512]{1,0:T(8,128)S(1)} %get-tuple-element.46.refs_0_, ...), custom_call_target="tpu_custom_call" | custom-call | flops 1000 | bytes 1000 | tf_op jit(solution)/shard_map/home_fwd/pallas_call | solution.py:317
  (36 shorter events, 3.5 us)
Async XLA Ops:
  0.6 58.3 %copy-start.1 = (bf16[1,2048,192]{1,2,0:T(8,128)(2,1)S(1)}, bf16[1,2048,192]{1,2,0:T(8,128)(2,1)}, u32[]{:S(2)}) copy-start(bf16[1,2048,192]{1,2,0:T(8,128)(2,1)} %param.16) | copy-start | bytes 2359300
  0.6 58.3 %copy-start.2 = (bf16[1,192,2048]{2,1,0:T(8,128)(2,1)S(1)}, bf16[1,192,2048]{2,1,0:T(8,128)(2,1)}, u32[]{:S(2)}) copy-start(bf16[1,192,2048]{2,1,0:T(8,128)(2,1)} %param.17) | copy-start | bytes 2359300
  0.7 58.3 %copy-start = (bf16[1,2048,192]{1,2,0:T(8,128)(2,1)S(1)}, bf16[1,2048,192]{1,2,0:T(8,128)(2,1)}, u32[]{:S(2)}) copy-start(bf16[1,2048,192]{1,2,0:T(8,128)(2,1)} %param.15) | copy-start | bytes 2359300
  0.7 16.7 %copy-start.6 = (s32[1,128,1]{1,2,0:T(1,128)S(1)}, s32[1,128,1]{1,2,0:T(1,128)}, u32[]{:S(2)}) copy-start(s32[1,128,1]{1,2,0:T(1,128)} %param.20) | copy-start | bytes 1540
  0.7 25.4 %copy-start.5 = (f32[1,2048]{1,0:T(1,128)S(1)}, f32[1,2048]{1,0:T(1,128)}, u32[]{:S(2)}) copy-start(f32[1,2048]{1,0:T(1,128)} %gain_ref.3) | copy-start | bytes 24580
  0.7 6.8 %copy-start.10 = (bf16[1,128,2048]{2,1,0:T(8,128)(2,1)S(1)}, bf16[1,128,2048]{2,1,0:T(8,128)(2,1)}, u32[]{:S(2)}) copy-start(bf16[1,128,2048]{2,1,0:T(8,128)(2,1)} %param.13) | copy-start | bytes 1572868
  0.7 25.4 %copy-start.7 = (s32[1,128,1]{1,2,0:T(1,128)S(1)}, s32[1,128,1]{1,2,0:T(1,128)}, u32[]{:S(2)}) copy-start(s32[1,128,1]{1,2,0:T(1,128)} %param.18) | copy-start | bytes 1540
  4.5 54.5 %collective-permute-start.8 = (bf16[576,2048]{1,0:T(8,128)(2,1)}, bf16[576,2048]{1,0:T(8,128)(2,1)S(1)}, u32[]{:S(2)}, u32[]{:S(2)}) collective-permute-start(bf16[576,2048]{1,0:T(8,128)(2,1)} %get-tuple-element.39), channel_id=1, source_target_pairs={{0,1},{1,0},{2,3},{3,2},{4,5},{5,4},{6,7},{7,6},{8,9},{9,8},{10,11... | collective-permute-start | bytes 7077896 | tf_op jit(solution)/shard_map/ppermute | solution.py:26
  7.5 9.9 %collective-permute-start.1 = (bf16[128,2048]{1,0:T(8,128)(2,1)S(1)}, bf16[128,2048]{1,0:T(8,128)(2,1)S(1)}, u32[]{:S(2)}, u32[]{:S(2)}) collective-permute-start(bf16[128,2048]{1,0:T(8,128)(2,1)S(1)} %bitcast.40), channel_id=1, source_target_pairs={{0,24},{8,0},{16,8},{24,16},{1,25},{9,1},{17,9},{25,17},{2,26},{10... | collective-permute-start | bytes 1572872 | tf_op jit(solution)/shard_map/ppermute | solution.py:21
  8.2 15.2 %collective-permute-start.2 = (bf16[264,512]{1,0:T(8,128)(2,1)}, bf16[264,512]{1,0:T(8,128)(2,1)S(1)}, u32[]{:S(2)}, u32[]{:S(2)}) collective-permute-start(bf16[264,512]{1,0:T(8,128)(2,1)} %get-tuple-element.31), channel_id=1, source_target_pairs={{0,4},{1,5},{2,6},{3,7},{4,0},{5,1},{6,2},{7,3},{8,12},{9,13},{10,... | collective-permute-start | bytes 811016 | tf_op jit(solution)/shard_map/ppermute | solution.py:21
  10.8 15.3 %collective-permute-start = (bf16[128,2048]{1,0:T(8,128)(2,1)}, bf16[128,2048]{1,0:T(8,128)(2,1)S(1)}, u32[]{:S(2)}, u32[]{:S(2)}) collective-permute-start(bf16[128,2048]{1,0:T(8,128)(2,1)} %bitcast.41), channel_id=1, source_target_pairs={{0,8},{8,16},{16,24},{24,0},{1,9},{9,17},{17,25},{25,1},{2,10},{10... | collective-permute-start | bytes 1572872 | tf_op jit(solution)/shard_map/ppermute | solution.py:21
  10.8 15.3 %collective-permute-start.3 = (bf16[264,512]{1,0:T(8,128)(2,1)}, bf16[264,512]{1,0:T(8,128)(2,1)S(1)}, u32[]{:S(2)}, u32[]{:S(2)}) collective-permute-start(bf16[264,512]{1,0:T(8,128)(2,1)} %get-tuple-element.28.kept_ref), channel_id=1, source_target_pairs={{0,2},{1,3},{2,0},{3,1},{4,6},{5,7},{6,4},{7,5},{8,10},{9,11},{10,... | collective-permute-start | bytes 811016 | tf_op jit(solution)/shard_map/ppermute | solution.py:26
  18.2 17.9 %collective-permute-start.5 = (bf16[264,512]{1,0:T(8,128)(2,1)S(1)}, bf16[264,512]{1,0:T(8,128)(2,1)S(1)}, u32[]{:S(2)}, u32[]{:S(2)}) collective-permute-start(bf16[264,512]{1,0:T(8,128)(2,1)S(1)} %get-tuple-element.35), channel_id=1, source_target_pairs={{0,4},{1,5},{2,6},{3,7},{4,0},{5,1},{6,2},{7,3},{8,12},{9,13},{10,... | collective-permute-start | bytes 811016 | tf_op jit(solution)/shard_map/ppermute | solution.py:21
  23.4 19.8 %collective-permute-start.6 = (bf16[264,512]{1,0:T(8,128)(2,1)S(1)}, bf16[264,512]{1,0:T(8,128)(2,1)S(1)}, u32[]{:S(2)}, u32[]{:S(2)}) collective-permute-start(bf16[264,512]{1,0:T(8,128)(2,1)S(1)} %get-tuple-element.36.refs_3_), channel_id=1, source_target_pairs={{0,2},{1,3},{2,0},{3,1},{4,6},{5,7},{6,4},{7,5},{8,10},{9,11},{10,... | collective-permute-start | bytes 811016 | tf_op jit(solution)/shard_map/ppermute | solution.py:26
  26.1 22.9 %collective-permute-start.4 = (bf16[264,512]{1,0:T(8,128)(2,1)S(1)}, bf16[264,512]{1,0:T(8,128)(2,1)S(1)}, u32[]{:S(2)}, u32[]{:S(2)}) collective-permute-start(bf16[264,512]{1,0:T(8,128)(2,1)S(1)} %collective-permute-done.2.refs_1_), channel_id=1, source_target_pairs={{0,2},{1,3},{2,0},{3,1},{4,6},{5,7},{6,4},{7,5},{8,10},{9,11},{10,... | collective-permute-start | bytes 811016 | tf_op jit(solution)/shard_map/ppermute | solution.py:26
  26.1 1.0 copy-start.4
  28.0 21.0 %collective-permute-start.9 = (bf16[264,512]{1,0:T(8,128)(2,1)S(1)}, bf16[264,512]{1,0:T(8,128)(2,1)S(1)}, u32[]{:S(2)}, u32[]{:S(2)}) collective-permute-start(bf16[264,512]{1,0:T(8,128)(2,1)S(1)} %get-tuple-element.43), channel_id=1, source_target_pairs={{0,4},{1,5},{2,6},{3,7},{4,0},{5,1},{6,2},{7,3},{8,12},{9,13},{10,... | collective-permute-start | bytes 811016 | tf_op jit(solution)/shard_map/ppermute | solution.py:21
  36.2 18.6 %collective-permute-start.10 = (bf16[264,512]{1,0:T(8,128)(2,1)S(1)}, bf16[264,512]{1,0:T(8,128)(2,1)S(1)}, u32[]{:S(2)}, u32[]{:S(2)}) collective-permute-start(bf16[264,512]{1,0:T(8,128)(2,1)S(1)} %get-tuple-element.44.refs_0_), channel_id=1, source_target_pairs={{0,2},{1,3},{2,0},{3,1},{4,6},{5,7},{6,4},{7,5},{8,10},{9,11},{10,... | collective-permute-start | bytes 811016 | tf_op jit(solution)/shard_map/ppermute | solution.py:26
  43.2 18.6 %collective-permute-start.7 = (bf16[264,512]{1,0:T(8,128)(2,1)S(1)}, bf16[264,512]{1,0:T(8,128)(2,1)S(1)}, u32[]{:S(2)}, u32[]{:S(2)}) collective-permute-start(bf16[264,512]{1,0:T(8,128)(2,1)S(1)} %collective-permute-done.5.refs_4_), channel_id=1, source_target_pairs={{0,2},{1,3},{2,0},{3,1},{4,6},{5,7},{6,4},{7,5},{8,10},{9,11},{10,... | collective-permute-start | bytes 811016 | tf_op jit(solution)/shard_map/ppermute | solution.py:26
  54.8 11.5 %collective-permute-start.11 = (bf16[264,512]{1,0:T(8,128)(2,1)S(1)}, bf16[264,512]{1,0:T(8,128)(2,1)S(1)}, u32[]{:S(2)}, u32[]{:S(2)}) collective-permute-start(bf16[264,512]{1,0:T(8,128)(2,1)S(1)} %collective-permute-done.9.refs_1_), channel_id=1, source_target_pairs={{0,2},{1,3},{2,0},{3,1},{4,6},{5,7},{6,4},{7,5},{8,10},{9,11},{10,... | collective-permute-start | bytes 811016 | tf_op jit(solution)/shard_map/ppermute | solution.py:26
  64.4 31.1 %copy-start.9 = (f32[1,128,1]{1,2,0:T(1,128)S(1)}, f32[1,128,1]{1,2,0:T(1,128)}, u32[]{:S(2)}) copy-start(f32[1,128,1]{1,2,0:T(1,128)} %param.21) | copy-start | bytes 1540
  64.4 9.0 %collective-permute-start.13 = (bf16[264,512]{1,0:T(8,128)(2,1)S(1)}, bf16[264,512]{1,0:T(8,128)(2,1)S(1)}, u32[]{:S(2)}, u32[]{:S(2)}) collective-permute-start(bf16[264,512]{1,0:T(8,128)(2,1)S(1)} %experts_bwd_far.1), channel_id=1, source_target_pairs={{0,2},{1,3},{2,0},{3,1},{4,6},{5,7},{6,4},{7,5},{8,10},{9,11},{10,... | collective-permute-start | bytes 811016 | tf_op jit(solution)/shard_map/ppermute | solution.py:26
  68.5 27.0 %copy-start.3 = (bf16[1,128,2048]{2,1,0:T(8,128)(2,1)S(1)}, bf16[1,128,2048]{2,1,0:T(8,128)(2,1)}, u32[]{:S(2)}) copy-start(bf16[1,128,2048]{2,1,0:T(8,128)(2,1)} %param.12) | copy-start | bytes 1572868
  68.5 15.4 %collective-permute-start.12 = (bf16[264,512]{1,0:T(8,128)(2,1)S(1)}, bf16[264,512]{1,0:T(8,128)(2,1)S(1)}, u32[]{:S(2)}, u32[]{:S(2)}) collective-permute-start(bf16[264,512]{1,0:T(8,128)(2,1)S(1)} %get-tuple-element.49), channel_id=1, source_target_pairs={{0,2},{1,3},{2,0},{3,1},{4,6},{5,7},{6,4},{7,5},{8,10},{9,11},{10,... | collective-permute-start | bytes 811016 | tf_op jit(solution)/shard_map/ppermute | solution.py:26
  73.3 27.7 %copy-start.8 = (f32[1,128,1]{1,2,0:T(1,128)S(1)}, f32[1,128,1]{1,2,0:T(1,128)}, u32[]{:S(2)}) copy-start(f32[1,128,1]{1,2,0:T(1,128)} %param.19) | copy-start | bytes 1540
  73.4 13.9 %collective-permute-start.14 = (bf16[264,512]{1,0:T(8,128)(2,1)S(1)}, bf16[264,512]{1,0:T(8,128)(2,1)S(1)}, u32[]{:S(2)}, u32[]{:S(2)}) collective-permute-start(bf16[264,512]{1,0:T(8,128)(2,1)S(1)} %add_convert_fusion), channel_id=1, source_target_pairs={{0,4},{1,5},{2,6},{3,7},{4,0},{5,1},{6,2},{7,3},{8,12},{9,13},{10,... | collective-permute-start | bytes 811016 | tf_op jit(solution)/shard_map/ppermute | solution.py:21
  76.5 18.9 %collective-permute-start.17 = (bf16[264,512]{1,0:T(8,128)(2,1)S(1)}, bf16[264,512]{1,0:T(8,128)(2,1)S(1)}, u32[]{:S(2)}, u32[]{:S(2)}) collective-permute-start(bf16[264,512]{1,0:T(8,128)(2,1)S(1)} %get-tuple-element.53), channel_id=1, source_target_pairs={{0,2},{1,3},{2,0},{3,1},{4,6},{5,7},{6,4},{7,5},{8,10},{9,11},{10,... | collective-permute-start | bytes 811016 | tf_op jit(solution)/shard_map/ppermute | solution.py:26
  84.0 13.7 %collective-permute-start.16 = (bf16[264,512]{1,0:T(8,128)(2,1)S(1)}, bf16[264,512]{1,0:T(8,128)(2,1)S(1)}, u32[]{:S(2)}, u32[]{:S(2)}) collective-permute-start(bf16[264,512]{1,0:T(8,128)(2,1)S(1)} %add_convert_fusion.1), channel_id=1, source_target_pairs={{0,4},{1,5},{2,6},{3,7},{4,0},{5,1},{6,2},{7,3},{8,12},{9,13},{10,... | collective-permute-start | bytes 811016 | tf_op jit(solution)/shard_map/ppermute | solution.py:21
  87.3 13.8 %collective-permute-start.15 = (bf16[264,512]{1,0:T(8,128)(2,1)S(1)}, bf16[264,512]{1,0:T(8,128)(2,1)S(1)}, u32[]{:S(2)}, u32[]{:S(2)}) collective-permute-start(bf16[264,512]{1,0:T(8,128)(2,1)S(1)} %get-tuple-element.51), channel_id=1, source_target_pairs={{0,2},{1,3},{2,0},{3,1},{4,6},{5,7},{6,4},{7,5},{8,10},{9,11},{10,... | collective-permute-start | bytes 811016 | tf_op jit(solution)/shard_map/ppermute | solution.py:26

commit v15 on v14

--- a/solution.py
+++ b/solution.py
@@ -102,16 +102,20 @@
     args, parts, joined = refs[:3], refs[3:6], refs[6]
     outs, held, stage, sems = refs[7:-5], refs[-5:-2], refs[-2], refs[-1]
     units = parts[0].shape[0]
-    rows = [pl.ds(i * units, units) for i in range(3)]
+    piece = units // 2
     fetch = [pltpu.make_async_copy(arg, to, sems.at[i]) for i, (arg, to) in enumerate(zip(args, held))]
-    load = [pltpu.make_async_copy(part, stage.at[rows[i], :], sems.at[3 + i]) for i, part in enumerate(parts)]
-    store = [pltpu.make_async_copy(stage.at[rows[i], :], joined.at[rows[i], :], sems.at[6 + i]) for i in range(3)]
+    load, store = [], []
+    for i in range(6):
+        rows = pl.ds(i * piece, piece)
+        source = parts[i // 2].at[pl.ds(i % 2 * piece, piece), :]
+        load.append(pltpu.make_async_copy(source, stage.at[rows, :], sems.at[3 + i]))
+        store.append(pltpu.make_async_copy(stage.at[rows, :], joined.at[rows, :], sems.at[9 + i]))
     for copy in fetch + load:
         copy.start()
     for copy in fetch:
         copy.wait()
     routes_ref, gain_ref, x_ref = held
-    for i in range(3):
+    for i in range(6):
         load[i].wait()
         store[i].start()
     pack(normed(x_ref, gain_ref), own_ref, routes_ref, outs)
@@ -257,7 +261,7 @@
             pltpu.VMEM((1, width), F32),
             pltpu.VMEM((tok_count, width), BF16),
             pltpu.VMEM((3 * w_down.shape[1], width), BF16),
-            pltpu.SemaphoreType.DMA((9,)),
+            pltpu.SemaphoreType.DMA((15,)),
         ],
         vmem_mib=56,
         name="join_weights_pack_saved",

time: 103 us -> 103 us (level)
  no operation moved by 1% of the time
where the time goes in v15:
time: 103 us
  waiting for transfers between devices  55.3 us (54%)
  starting transfers between devices  28.6 us (28%)
  Pallas kernels  17 us (17%)
    ppermute x11, waiting for transfers between devices, swapped(): return lax.ppermute(value, axis, [(i, i ^ bit) for i in range(count)])  40.9 us
    ppermute x11, starting transfers between devices, swapped(): return lax.ppermute(value, axis, [(i, i ^ bit) for i in range(count)])  14.8 us
    ppermute x7, waiting for transfers between devices, shifted(): lax.ppermute(value, axis, [(i, (i + steps) % count) for i in range(count)])  14.4 us
    ppermute x7, starting transfers between devices, shifted(): lax.ppermute(value, axis, [(i, (i + steps) % count) for i in range(count)])  13.9 us
    pallas_call x3, Pallas kernels, run_experts(): local_call(functools.partial(body, count, rows), out_shape, scratch=wides...  7.64 us
    pallas_call x1, Pallas kernels, per_device(): local_call(first_body, [jax.ShapeDtypeStruct((3 * w_down.shape[1], width)...  3.79 us
  transfers between devices with their start and end apart: 18, of which 14 were waited for; matrix products, arithmetic and copies ran while one was open for 0% of the time, Pallas kernels for 11%

profile of v15, /device:TPU:0, one launch (start us, length us, event | category | flops | bytes accessed | tf_op | source)
XLA Modules:
  0.0 102.8 jit_solution(4722605161413538326)
XLA Ops:
  0.7 3.8 %join_weights_pack_saved.1 = (bf16[576,2048]{1,0:T(8,128)(2,1)}, bf16[264,512]{1,0:T(8,128)(2,1)}, bf16[264,512]{1,0:T(8,128)(2,1)}) custom-call(s32[1]{0:T(128)} %bitcast.own_ref, s32[1,128]{1,0:T(1,128)} %bitcast.31, f32[1,2048]{1,0:T(1,128)} %gain_ref.3, bf16[128,2048]{1,0:T(8,128)(2,1)} %bitcast.29, bf16[192,2048]{1,0:T(8,128)(2,1)} %bitcast.17, ...), custom_call_target="tpu_custom_call" | custom-call | flops 1000 | bytes 1000 | tf_op jit(solution)/shard_map/join_weights_pack_saved/pallas_call | solution.py:254
  4.5 3.0 %collective-permute-start.8 = (bf16[576,2048]{1,0:T(8,128)(2,1)}, bf16[576,2048]{1,0:T(8,128)(2,1)S(1)}, u32[]{:S(2)}, u32[]{:S(2)}) collective-permute-start(bf16[576,2048]{1,0:T(8,128)(2,1)} %get-tuple-element.39), channel_id=1, source_target_pairs={{0,1},{1,0},{2,3},{3,2},{4,5},{5,4},{6,7},{7,6},{8,9},{9,8},{10,11... | collective-permute-start | bytes 7077896 | tf_op jit(solution)/shard_map/ppermute | solution.py:26
  8.2 2.6 %collective-permute-start.2 = (bf16[264,512]{1,0:T(8,128)(2,1)}, bf16[264,512]{1,0:T(8,128)(2,1)S(1)}, u32[]{:S(2)}, u32[]{:S(2)}) collective-permute-start(bf16[264,512]{1,0:T(8,128)(2,1)} %get-tuple-element.31), channel_id=1, source_target_pairs={{0,4},{1,5},{2,6},{3,7},{4,0},{5,1},{6,2},{7,3},{8,12},{9,13},{10,... | collective-permute-start | bytes 811016 | tf_op jit(solution)/shard_map/ppermute | solution.py:21
  10.8 1.6 %collective-permute-start.3 = (bf16[264,512]{1,0:T(8,128)(2,1)}, bf16[264,512]{1,0:T(8,128)(2,1)S(1)}, u32[]{:S(2)}, u32[]{:S(2)}) collective-permute-start(bf16[264,512]{1,0:T(8,128)(2,1)} %get-tuple-element.28.kept_ref), channel_id=1, source_target_pairs={{0,2},{1,3},{2,0},{3,1},{4,6},{5,7},{6,4},{7,5},{8,10},{9,11},{10,... | collective-permute-start | bytes 811016 | tf_op jit(solution)/shard_map/ppermute | solution.py:26
  12.4 5.0 %collective-permute-done.1.x_ref.up_ref = bf16[128,2048]{1,0:T(8,128)(2,1)S(1)} collective-permute-done((bf16[128,2048]{1,0:T(8,128)(2,1)S(1)}, bf16[128,2048]{1,0:T(8,128)(2,1)S(1)}, u32[]{:S(2)}, u32[]{:S(2)}) %collective-permute-start.1) | collective-permute-done | bytes 524320 | tf_op jit(solution)/shard_map/ppermute | solution.py:21
  18.3 5.0 %collective-permute-start.5 = (bf16[264,512]{1,0:T(8,128)(2,1)S(1)}, bf16[264,512]{1,0:T(8,128)(2,1)S(1)}, u32[]{:S(2)}, u32[]{:S(2)}) collective-permute-start(bf16[264,512]{1,0:T(8,128)(2,1)S(1)} %get-tuple-element.35), channel_id=1, source_target_pairs={{0,4},{1,5},{2,6},{3,7},{4,0},{5,1},{6,2},{7,3},{8,12},{9,13},{10,... | collective-permute-start | bytes 811016 | tf_op jit(solution)/shard_map/ppermute | solution.py:21
  23.4 1.4 %collective-permute-start.6 = (bf16[264,512]{1,0:T(8,128)(2,1)S(1)}, bf16[264,512]{1,0:T(8,128)(2,1)S(1)}, u32[]{:S(2)}, u32[]{:S(2)}) collective-permute-start(bf16[264,512]{1,0:T(8,128)(2,1)S(1)} %get-tuple-element.36.refs_3_), channel_id=1, source_target_pairs={{0,2},{1,3},{2,0},{3,1},{4,6},{5,7},{6,4},{7,5},{8,10},{9,11},{10,... | collective-permute-start | bytes 811016 | tf_op jit(solution)/shard_map/ppermute | solution.py:26
  24.8 1.3 %collective-permute-done.3.refs_2_ = bf16[264,512]{1,0:T(8,128)(2,1)S(1)} collective-permute-done((bf16[264,512]{1,0:T(8,128)(2,1)}, bf16[264,512]{1,0:T(8,128)(2,1)S(1)}, u32[]{:S(2)}, u32[]{:S(2)}) %collective-permute-start.3) | collective-permute-done | bytes 270368 | tf_op jit(solution)/shard_map/ppermute | solution.py:26
  26.1 0.9 copy-done.4
  28.0 2.0 %collective-permute-start.9 = (bf16[264,512]{1,0:T(8,128)(2,1)S(1)}, bf16[264,512]{1,0:T(8,128)(2,1)S(1)}, u32[]{:S(2)}, u32[]{:S(2)}) collective-permute-start(bf16[264,512]{1,0:T(8,128)(2,1)S(1)} %get-tuple-element.43), channel_id=1, source_target_pairs={{0,4},{1,5},{2,6},{3,7},{4,0},{5,1},{6,2},{7,3},{8,12},{9,13},{10,... | collective-permute-start | bytes 811016 | tf_op jit(solution)/shard_map/ppermute | solution.py:21
  30.0 6.3 %collective-permute-done.5.refs_4_ = bf16[264,512]{1,0:T(8,128)(2,1)S(1)} collective-permute-done((bf16[264,512]{1,0:T(8,128)(2,1)S(1)}, bf16[264,512]{1,0:T(8,128)(2,1)S(1)}, u32[]{:S(2)}, u32[]{:S(2)}) %collective-permute-start.5) | collective-permute-done | bytes 270368 | tf_op jit(solution)/shard_map/ppermute | solution.py:21
  36.2 1.2 %collective-permute-start.10 = (bf16[264,512]{1,0:T(8,128)(2,1)S(1)}, bf16[264,512]{1,0:T(8,128)(2,1)S(1)}, u32[]{:S(2)}, u32[]{:S(2)}) collective-permute-start(bf16[264,512]{1,0:T(8,128)(2,1)S(1)} %get-tuple-element.44.refs_0_), channel_id=1, source_target_pairs={{0,2},{1,3},{2,0},{3,1},{4,6},{5,7},{6,4},{7,5},{8,10},{9,11},{10,... | collective-permute-start | bytes 811016 | tf_op jit(solution)/shard_map/ppermute | solution.py:26
  37.5 5.8 %collective-permute-done.6.refs_5_ = bf16[264,512]{1,0:T(8,128)(2,1)S(1)} collective-permute-done((bf16[264,512]{1,0:T(8,128)(2,1)S(1)}, bf16[264,512]{1,0:T(8,128)(2,1)S(1)}, u32[]{:S(2)}, u32[]{:S(2)}) %collective-permute-start.6) | collective-permute-done | bytes 270368 | tf_op jit(solution)/shard_map/ppermute | solution.py:26
  43.2 5.8 %collective-permute-done.4.refs_0_ = bf16[264,512]{1,0:T(8,128)(2,1)S(1)} collective-permute-done((bf16[264,512]{1,0:T(8,128)(2,1)S(1)}, bf16[264,512]{1,0:T(8,128)(2,1)S(1)}, u32[]{:S(2)}, u32[]{:S(2)}) %collective-permute-start.4) | collective-permute-done | bytes 270368 | tf_op jit(solution)/shard_map/ppermute | solution.py:26
  49.0 5.8 %collective-permute-done.10.refs_2_ = bf16[264,512]{1,0:T(8,128)(2,1)S(1)} collective-permute-done((bf16[264,512]{1,0:T(8,128)(2,1)S(1)}, bf16[264,512]{1,0:T(8,128)(2,1)S(1)}, u32[]{:S(2)}, u32[]{:S(2)}) %collective-permute-start.10) | collective-permute-done | bytes 270368 | tf_op jit(solution)/shard_map/ppermute | solution.py:26
  54.8 1.0 collective-permute-start.11
  55.8 3.2 %collective-permute-done.8.refs_9_.refs_5_.refs_7_ = bf16[576,2048]{1,0:T(8,128)(2,1)S(1)} collective-permute-done((bf16[576,2048]{1,0:T(8,128)(2,1)}, bf16[576,2048]{1,0:T(8,128)(2,1)S(1)}, u32[]{:S(2)}, u32[]{:S(2)}) %collective-permute-start.8) | collective-permute-done | bytes 2359328 | tf_op jit(solution)/shard_map/ppermute | solution.py:26
  59.0 2.9 %experts_bwd_near.1 = (f32[264,512]{1,0:T(8,128)S(1)}, f32[264,512]{1,0:T(8,128)S(1)}, bf16[264,512]{1,0:T(8,128)(2,1)S(1)}) custom-call(bf16[264,512]{1,0:T(8,128)(2,1)S(1)} %get-tuple-element.38.refs_0_, bf16[264,512]{1,0:T(8,128)(2,1)S(1)} %collective-permute-done.2.refs_1_, bf16[264,512]{1,0:T(8,128)(2,1)S(1)} %collective-permute-done.3.refs_2_, ...), custom_call_target="tpu_custom_call" | custom-call | flops 1000 | bytes 1000 | tf_op jit(solution)/shard_map/experts_bwd_near/pallas_call | solution.py:297
  61.9 2.5 %experts_bwd_far.1 = bf16[264,512]{1,0:T(8,128)(2,1)S(1)} custom-call(bf16[264,512]{1,0:T(8,128)(2,1)S(1)} %collective-permute-done.4.refs_0_, bf16[264,512]{1,0:T(8,128)(2,1)S(1)} %collective-permute-done.7.refs_1_, bf16[192,2048]{1,0:T(8,128)(2,1)S(1)} %bitcast.19, bf16[192,2048]{1,0:T(8,128)(2,1)S(1)} %bitcast.23, bf16[192,2048]{1,0:T(8,128)(2,1)S(1)} %bitcast.27, ...), custom_call_target="tpu_custom_call" | custom-call | flops 1000 | bytes 1000 | tf_op jit(solution)/shard_map/experts_bwd_far/pallas_call | solution.py:297
  64.4 1.9 %collective-permute-start.13 = (bf16[264,512]{1,0:T(8,128)(2,1)S(1)}, bf16[264,512]{1,0:T(8,128)(2,1)S(1)}, u32[]{:S(2)}, u32[]{:S(2)}) collective-permute-start(bf16[264,512]{1,0:T(8,128)(2,1)S(1)} %experts_bwd_far.1), channel_id=1, source_target_pairs={{0,2},{1,3},{2,0},{3,1},{4,6},{5,7},{6,4},{7,5},{8,10},{9,11},{10,... | collective-permute-start | bytes 811016 | tf_op jit(solution)/shard_map/ppermute | solution.py:26
  66.3 2.3 %experts_fwd.1 = (f32[264,512]{1,0:T(8,128)S(1)}, f32[264,512]{1,0:T(8,128)S(1)}, bf16[264,512]{1,0:T(8,128)(2,1)S(1)}, bf16[264,512]{1,0:T(8,128)(2,1)S(1)}) custom-call(bf16[264,512]{1,0:T(8,128)(2,1)S(1)} %get-tuple-element.44.refs_0_, bf16[264,512]{1,0:T(8,128)(2,1)S(1)} %collective-permute-done.9.refs_1_, ...), custom_call_target="tpu_custom_call" | custom-call | flops 1000 | bytes 1000 | tf_op jit(solution)/shard_map/experts_fwd/pallas_call | solution.py:297
  68.6 1.2 %collective-permute-start.12 = (bf16[264,512]{1,0:T(8,128)(2,1)S(1)}, bf16[264,512]{1,0:T(8,128)(2,1)S(1)}, u32[]{:S(2)}, u32[]{:S(2)}) collective-permute-start(bf16[264,512]{1,0:T(8,128)(2,1)S(1)} %get-tuple-element.49), channel_id=1, source_target_pairs={{0,2},{1,3},{2,0},{3,1},{4,6},{5,7},{6,4},{7,5},{8,10},{9,11},{10,... | collective-permute-start | bytes 811016 | tf_op jit(solution)/shard_map/ppermute | solution.py:26
  69.7 3.6 %collective-permute-done.13 = bf16[264,512]{1,0:T(8,128)(2,1)S(1)} collective-permute-done((bf16[264,512]{1,0:T(8,128)(2,1)S(1)}, bf16[264,512]{1,0:T(8,128)(2,1)S(1)}, u32[]{:S(2)}, u32[]{:S(2)}) %collective-permute-start.13) | collective-permute-done | bytes 270368 | tf_op jit(solution)/shard_map/ppermute | solution.py:26
  73.5 3.1 %collective-permute-start.14 = (bf16[264,512]{1,0:T(8,128)(2,1)S(1)}, bf16[264,512]{1,0:T(8,128)(2,1)S(1)}, u32[]{:S(2)}, u32[]{:S(2)}) collective-permute-start(bf16[264,512]{1,0:T(8,128)(2,1)S(1)} %add_convert_fusion), channel_id=1, source_target_pairs={{0,4},{1,5},{2,6},{3,7},{4,0},{5,1},{6,2},{7,3},{8,12},{9,13},{10,... | collective-permute-start | bytes 811016 | tf_op jit(solution)/shard_map/ppermute | solution.py:21
  76.6 1.6 %collective-permute-start.17 = (bf16[264,512]{1,0:T(8,128)(2,1)S(1)}, bf16[264,512]{1,0:T(8,128)(2,1)S(1)}, u32[]{:S(2)}, u32[]{:S(2)}) collective-permute-start(bf16[264,512]{1,0:T(8,128)(2,1)S(1)} %get-tuple-element.53), channel_id=1, source_target_pairs={{0,2},{1,3},{2,0},{3,1},{4,6},{5,7},{6,4},{7,5},{8,10},{9,11},{10,... | collective-permute-start | bytes 811016 | tf_op jit(solution)/shard_map/ppermute | solution.py:26
  78.1 5.8 %collective-permute-done.12 = bf16[264,512]{1,0:T(8,128)(2,1)S(1)} collective-permute-done((bf16[264,512]{1,0:T(8,128)(2,1)S(1)}, bf16[264,512]{1,0:T(8,128)(2,1)S(1)}, u32[]{:S(2)}, u32[]{:S(2)}) %collective-permute-start.12) | collective-permute-done | bytes 270368 | tf_op jit(solution)/shard_map/ppermute | solution.py:26
  84.5 2.7 %collective-permute-done.14.refs_2_ = bf16[264,512]{1,0:T(8,128)(2,1)S(1)} collective-permute-done((bf16[264,512]{1,0:T(8,128)(2,1)S(1)}, bf16[264,512]{1,0:T(8,128)(2,1)S(1)}, u32[]{:S(2)}, u32[]{:S(2)}) %collective-permute-start.14) | collective-permute-done | bytes 270368 | tf_op jit(solution)/shard_map/ppermute | solution.py:21
  87.2 1.9 %collective-permute-start.15 = (bf16[264,512]{1,0:T(8,128)(2,1)S(1)}, bf16[264,512]{1,0:T(8,128)(2,1)S(1)}, u32[]{:S(2)}, u32[]{:S(2)}) collective-permute-start(bf16[264,512]{1,0:T(8,128)(2,1)S(1)} %get-tuple-element.51), channel_id=1, source_target_pairs={{0,2},{1,3},{2,0},{3,1},{4,6},{5,7},{6,4},{7,5},{8,10},{9,11},{10,... | collective-permute-start | bytes 811016 | tf_op jit(solution)/shard_map/ppermute | solution.py:26
  89.1 6.4 %collective-permute-done.17.refs_1_ = bf16[264,512]{1,0:T(8,128)(2,1)S(1)} collective-permute-done((bf16[264,512]{1,0:T(8,128)(2,1)S(1)}, bf16[264,512]{1,0:T(8,128)(2,1)S(1)}, u32[]{:S(2)}, u32[]{:S(2)}) %collective-permute-start.17) | collective-permute-done | bytes 270368 | tf_op jit(solution)/shard_map/ppermute | solution.py:26
  95.5 2.0 %home_bwd.1 = bf16[128,2048]{1,0:T(8,128)(2,1)} custom-call(s32[1]{0:T(128)} %bitcast.own_ref, s32[1,128]{1,0:T(1,128)S(1)} %bitcast.33, f32[1,128]{1,0:T(1,128)S(1)} %bitcast.37, f32[1,2048]{1,0:T(1,128)S(1)} %copy-done.5, bf16[128,2048]{1,0:T(8,128)(2,1)S(1)} %bitcast.30, bf16[128,2048]{1,0:T(8,128)(2,1)S(1)} %collective-permute-done.1.x_ref.up_ref, ...), custom_call_target="tpu_custom_call" | custom-call | flops 1000 | bytes 1000 | tf_op jit(solution)/shard_map/home_bwd/pallas_call | solution.py:314
  97.7 3.4 %collective-permute-done.15.refs_1_ = bf16[264,512]{1,0:T(8,128)(2,1)S(1)} collective-permute-done((bf16[264,512]{1,0:T(8,128)(2,1)S(1)}, bf16[264,512]{1,0:T(8,128)(2,1)S(1)}, u32[]{:S(2)}, u32[]{:S(2)}) %collective-permute-start.15) | collective-permute-done | bytes 270368 | tf_op jit(solution)/shard_map/ppermute | solution.py:26
  101.1 1.7 %home_fwd.1 = bf16[128,2048]{1,0:T(8,128)(2,1)} custom-call(s32[1]{0:T(128)} %bitcast.own_ref, s32[1,128]{1,0:T(1,128)S(1)} %bitcast.35, f32[1,128]{1,0:T(1,128)S(1)} %bitcast.36, bf16[128,2048]{1,0:T(8,128)(2,1)S(1)} %collective-permute-done.x_ref, f32[264,512]{1,0:T(8,128)S(1)} %get-tuple-element.46.refs_0_, ...), custom_call_target="tpu_custom_call" | custom-call | flops 1000 | bytes 1000 | tf_op jit(solution)/shard_map/home_fwd/pallas_call | solution.py:321
  (36 shorter events, 3.5 us)
Async XLA Ops:
  0.6 58.3 %copy-start.1 = (bf16[1,2048,192]{1,2,0:T(8,128)(2,1)S(1)}, bf16[1,2048,192]{1,2,0:T(8,128)(2,1)}, u32[]{:S(2)}) copy-start(bf16[1,2048,192]{1,2,0:T(8,128)(2,1)} %param.16) | copy-start | bytes 2359300
  0.6 58.3 %copy-start.2 = (bf16[1,192,2048]{2,1,0:T(8,128)(2,1)S(1)}, bf16[1,192,2048]{2,1,0:T(8,128)(2,1)}, u32[]{:S(2)}) copy-start(bf16[1,192,2048]{2,1,0:T(8,128)(2,1)} %param.17) | copy-start | bytes 2359300
  0.7 58.3 %copy-start = (bf16[1,2048,192]{1,2,0:T(8,128)(2,1)S(1)}, bf16[1,2048,192]{1,2,0:T(8,128)(2,1)}, u32[]{:S(2)}) copy-start(bf16[1,2048,192]{1,2,0:T(8,128)(2,1)} %param.15) | copy-start | bytes 2359300
  0.7 16.7 %copy-start.6 = (s32[1,128,1]{1,2,0:T(1,128)S(1)}, s32[1,128,1]{1,2,0:T(1,128)}, u32[]{:S(2)}) copy-start(s32[1,128,1]{1,2,0:T(1,128)} %param.20) | copy-start | bytes 1540
  0.7 25.4 %copy-start.5 = (f32[1,2048]{1,0:T(1,128)S(1)}, f32[1,2048]{1,0:T(1,128)}, u32[]{:S(2)}) copy-start(f32[1,2048]{1,0:T(1,128)} %gain_ref.3) | copy-start | bytes 24580
  0.7 6.8 %copy-start.10 = (bf16[1,128,2048]{2,1,0:T(8,128)(2,1)S(1)}, bf16[1,128,2048]{2,1,0:T(8,128)(2,1)}, u32[]{:S(2)}) copy-start(bf16[1,128,2048]{2,1,0:T(8,128)(2,1)} %param.13) | copy-start | bytes 1572868
  0.7 25.4 %copy-start.7 = (s32[1,128,1]{1,2,0:T(1,128)S(1)}, s32[1,128,1]{1,2,0:T(1,128)}, u32[]{:S(2)}) copy-start(s32[1,128,1]{1,2,0:T(1,128)} %param.18) | copy-start | bytes 1540
  4.5 54.5 %collective-permute-start.8 = (bf16[576,2048]{1,0:T(8,128)(2,1)}, bf16[576,2048]{1,0:T(8,128)(2,1)S(1)}, u32[]{:S(2)}, u32[]{:S(2)}) collective-permute-start(bf16[576,2048]{1,0:T(8,128)(2,1)} %get-tuple-element.39), channel_id=1, source_target_pairs={{0,1},{1,0},{2,3},{3,2},{4,5},{5,4},{6,7},{7,6},{8,9},{9,8},{10,11... | collective-permute-start | bytes 7077896 | tf_op jit(solution)/shard_map/ppermute | solution.py:26
  7.5 9.9 %collective-permute-start.1 = (bf16[128,2048]{1,0:T(8,128)(2,1)S(1)}, bf16[128,2048]{1,0:T(8,128)(2,1)S(1)}, u32[]{:S(2)}, u32[]{:S(2)}) collective-permute-start(bf16[128,2048]{1,0:T(8,128)(2,1)S(1)} %bitcast.40), channel_id=1, source_target_pairs={{0,24},{8,0},{16,8},{24,16},{1,25},{9,1},{17,9},{25,17},{2,26},{10... | collective-permute-start | bytes 1572872 | tf_op jit(solution)/shard_map/ppermute | solution.py:21
  8.2 15.2 %collective-permute-start.2 = (bf16[264,512]{1,0:T(8,128)(2,1)}, bf16[264,512]{1,0:T(8,128)(2,1)S(1)}, u32[]{:S(2)}, u32[]{:S(2)}) collective-permute-start(bf16[264,512]{1,0:T(8,128)(2,1)} %get-tuple-element.31), channel_id=1, source_target_pairs={{0,4},{1,5},{2,6},{3,7},{4,0},{5,1},{6,2},{7,3},{8,12},{9,13},{10,... | collective-permute-start | bytes 811016 | tf_op jit(solution)/shard_map/ppermute | solution.py:21
  10.8 15.3 %collective-permute-start = (bf16[128,2048]{1,0:T(8,128)(2,1)}, bf16[128,2048]{1,0:T(8,128)(2,1)S(1)}, u32[]{:S(2)}, u32[]{:S(2)}) collective-permute-start(bf16[128,2048]{1,0:T(8,128)(2,1)} %bitcast.41), channel_id=1, source_target_pairs={{0,8},{8,16},{16,24},{24,0},{1,9},{9,17},{17,25},{25,1},{2,10},{10... | collective-permute-start | bytes 1572872 | tf_op jit(solution)/shard_map/ppermute | solution.py:21
  10.8 15.3 %collective-permute-start.3 = (bf16[264,512]{1,0:T(8,128)(2,1)}, bf16[264,512]{1,0:T(8,128)(2,1)S(1)}, u32[]{:S(2)}, u32[]{:S(2)}) collective-permute-start(bf16[264,512]{1,0:T(8,128)(2,1)} %get-tuple-element.28.kept_ref), channel_id=1, source_target_pairs={{0,2},{1,3},{2,0},{3,1},{4,6},{5,7},{6,4},{7,5},{8,10},{9,11},{10,... | collective-permute-start | bytes 811016 | tf_op jit(solution)/shard_map/ppermute | solution.py:26
  18.3 17.9 %collective-permute-start.5 = (bf16[264,512]{1,0:T(8,128)(2,1)S(1)}, bf16[264,512]{1,0:T(8,128)(2,1)S(1)}, u32[]{:S(2)}, u32[]{:S(2)}) collective-permute-start(bf16[264,512]{1,0:T(8,128)(2,1)S(1)} %get-tuple-element.35), channel_id=1, source_target_pairs={{0,4},{1,5},{2,6},{3,7},{4,0},{5,1},{6,2},{7,3},{8,12},{9,13},{10,... | collective-permute-start | bytes 811016 | tf_op jit(solution)/shard_map/ppermute | solution.py:21
  23.4 19.8 %collective-permute-start.6 = (bf16[264,512]{1,0:T(8,128)(2,1)S(1)}, bf16[264,512]{1,0:T(8,128)(2,1)S(1)}, u32[]{:S(2)}, u32[]{:S(2)}) collective-permute-start(bf16[264,512]{1,0:T(8,128)(2,1)S(1)} %get-tuple-element.36.refs_3_), channel_id=1, source_target_pairs={{0,2},{1,3},{2,0},{3,1},{4,6},{5,7},{6,4},{7,5},{8,10},{9,11},{10,... | collective-permute-start | bytes 811016 | tf_op jit(solution)/shard_map/ppermute | solution.py:26
  26.1 22.9 %collective-permute-start.4 = (bf16[264,512]{1,0:T(8,128)(2,1)S(1)}, bf16[264,512]{1,0:T(8,128)(2,1)S(1)}, u32[]{:S(2)}, u32[]{:S(2)}) collective-permute-start(bf16[264,512]{1,0:T(8,128)(2,1)S(1)} %collective-permute-done.2.refs_1_), channel_id=1, source_target_pairs={{0,2},{1,3},{2,0},{3,1},{4,6},{5,7},{6,4},{7,5},{8,10},{9,11},{10,... | collective-permute-start | bytes 811016 | tf_op jit(solution)/shard_map/ppermute | solution.py:26
  26.1 1.0 copy-start.4
  28.0 21.0 %collective-permute-start.9 = (bf16[264,512]{1,0:T(8,128)(2,1)S(1)}, bf16[264,512]{1,0:T(8,128)(2,1)S(1)}, u32[]{:S(2)}, u32[]{:S(2)}) collective-permute-start(bf16[264,512]{1,0:T(8,128)(2,1)S(1)} %get-tuple-element.43), channel_id=1, source_target_pairs={{0,4},{1,5},{2,6},{3,7},{4,0},{5,1},{6,2},{7,3},{8,12},{9,13},{10,... | collective-permute-start | bytes 811016 | tf_op jit(solution)/shard_map/ppermute | solution.py:21
  36.2 18.6 %collective-permute-start.10 = (bf16[264,512]{1,0:T(8,128)(2,1)S(1)}, bf16[264,512]{1,0:T(8,128)(2,1)S(1)}, u32[]{:S(2)}, u32[]{:S(2)}) collective-permute-start(bf16[264,512]{1,0:T(8,128)(2,1)S(1)} %get-tuple-element.44.refs_0_), channel_id=1, source_target_pairs={{0,2},{1,3},{2,0},{3,1},{4,6},{5,7},{6,4},{7,5},{8,10},{9,11},{10,... | collective-permute-start | bytes 811016 | tf_op jit(solution)/shard_map/ppermute | solution.py:26
  43.2 18.7 %collective-permute-start.7 = (bf16[264,512]{1,0:T(8,128)(2,1)S(1)}, bf16[264,512]{1,0:T(8,128)(2,1)S(1)}, u32[]{:S(2)}, u32[]{:S(2)}) collective-permute-start(bf16[264,512]{1,0:T(8,128)(2,1)S(1)} %collective-permute-done.5.refs_4_), channel_id=1, source_target_pairs={{0,2},{1,3},{2,0},{3,1},{4,6},{5,7},{6,4},{7,5},{8,10},{9,11},{10,... | collective-permute-start | bytes 811016 | tf_op jit(solution)/shard_map/ppermute | solution.py:26
  54.8 11.5 %collective-permute-start.11 = (bf16[264,512]{1,0:T(8,128)(2,1)S(1)}, bf16[264,512]{1,0:T(8,128)(2,1)S(1)}, u32[]{:S(2)}, u32[]{:S(2)}) collective-permute-start(bf16[264,512]{1,0:T(8,128)(2,1)S(1)} %collective-permute-done.9.refs_1_), channel_id=1, source_target_pairs={{0,2},{1,3},{2,0},{3,1},{4,6},{5,7},{6,4},{7,5},{8,10},{9,11},{10,... | collective-permute-start | bytes 811016 | tf_op jit(solution)/shard_map/ppermute | solution.py:26
  64.4 31.1 %copy-start.9 = (f32[1,128,1]{1,2,0:T(1,128)S(1)}, f32[1,128,1]{1,2,0:T(1,128)}, u32[]{:S(2)}) copy-start(f32[1,128,1]{1,2,0:T(1,128)} %param.21) | copy-start | bytes 1540
  64.4 9.0 %collective-permute-start.13 = (bf16[264,512]{1,0:T(8,128)(2,1)S(1)}, bf16[264,512]{1,0:T(8,128)(2,1)S(1)}, u32[]{:S(2)}, u32[]{:S(2)}) collective-permute-start(bf16[264,512]{1,0:T(8,128)(2,1)S(1)} %experts_bwd_far.1), channel_id=1, source_target_pairs={{0,2},{1,3},{2,0},{3,1},{4,6},{5,7},{6,4},{7,5},{8,10},{9,11},{10,... | collective-permute-start | bytes 811016 | tf_op jit(solution)/shard_map/ppermute | solution.py:26
  68.6 27.0 %copy-start.3 = (bf16[1,128,2048]{2,1,0:T(8,128)(2,1)S(1)}, bf16[1,128,2048]{2,1,0:T(8,128)(2,1)}, u32[]{:S(2)}) copy-start(bf16[1,128,2048]{2,1,0:T(8,128)(2,1)} %param.12) | copy-start | bytes 1572868
  68.6 15.4 %collective-permute-start.12 = (bf16[264,512]{1,0:T(8,128)(2,1)S(1)}, bf16[264,512]{1,0:T(8,128)(2,1)S(1)}, u32[]{:S(2)}, u32[]{:S(2)}) collective-permute-start(bf16[264,512]{1,0:T(8,128)(2,1)S(1)} %get-tuple-element.49), channel_id=1, source_target_pairs={{0,2},{1,3},{2,0},{3,1},{4,6},{5,7},{6,4},{7,5},{8,10},{9,11},{10,... | collective-permute-start | bytes 811016 | tf_op jit(solution)/shard_map/ppermute | solution.py:26
  73.4 27.7 %copy-start.8 = (f32[1,128,1]{1,2,0:T(1,128)S(1)}, f32[1,128,1]{1,2,0:T(1,128)}, u32[]{:S(2)}) copy-start(f32[1,128,1]{1,2,0:T(1,128)} %param.19) | copy-start | bytes 1540
  73.5 13.8 %collective-permute-start.14 = (bf16[264,512]{1,0:T(8,128)(2,1)S(1)}, bf16[264,512]{1,0:T(8,128)(2,1)S(1)}, u32[]{:S(2)}, u32[]{:S(2)}) collective-permute-start(bf16[264,512]{1,0:T(8,128)(2,1)S(1)} %add_convert_fusion), channel_id=1, source_target_pairs={{0,4},{1,5},{2,6},{3,7},{4,0},{5,1},{6,2},{7,3},{8,12},{9,13},{10,... | collective-permute-start | bytes 811016 | tf_op jit(solution)/shard_map/ppermute | solution.py:21
  76.6 19.0 %collective-permute-start.17 = (bf16[264,512]{1,0:T(8,128)(2,1)S(1)}, bf16[264,512]{1,0:T(8,128)(2,1)S(1)}, u32[]{:S(2)}, u32[]{:S(2)}) collective-permute-start(bf16[264,512]{1,0:T(8,128)(2,1)S(1)} %get-tuple-element.53), channel_id=1, source_target_pairs={{0,2},{1,3},{2,0},{3,1},{4,6},{5,7},{6,4},{7,5},{8,10},{9,11},{10,... | collective-permute-start | bytes 811016 | tf_op jit(solution)/shard_map/ppermute | solution.py:26
  84.0 13.7 %collective-permute-start.16 = (bf16[264,512]{1,0:T(8,128)(2,1)S(1)}, bf16[264,512]{1,0:T(8,128)(2,1)S(1)}, u32[]{:S(2)}, u32[]{:S(2)}) collective-permute-start(bf16[264,512]{1,0:T(8,128)(2,1)S(1)} %add_convert_fusion.1), channel_id=1, source_target_pairs={{0,4},{1,5},{2,6},{3,7},{4,0},{5,1},{6,2},{7,3},{8,12},{9,13},{10,... | collective-permute-start | bytes 811016 | tf_op jit(solution)/shard_map/ppermute | solution.py:21
  87.2 13.9 %collective-permute-start.15 = (bf16[264,512]{1,0:T(8,128)(2,1)S(1)}, bf16[264,512]{1,0:T(8,128)(2,1)S(1)}, u32[]{:S(2)}, u32[]{:S(2)}) collective-permute-start(bf16[264,512]{1,0:T(8,128)(2,1)S(1)} %get-tuple-element.51), channel_id=1, source_target_pairs={{0,2},{1,3},{2,0},{3,1},{4,6},{5,7},{6,4},{7,5},{8,10},{9,11},{10,... | collective-permute-start | bytes 811016 | tf_op jit(solution)/shard_map/ppermute | solution.py:26

commit v16 on v14

--- a/solution.py
+++ b/solution.py
@@ -295,12 +295,10 @@
         )(*inputs, *shares)
 
     near = experts + 1
-    partial_b = run_experts(backward_body, "experts_bwd_near", rows_b[:near] + rows_g[:near], near, partial[:near])
-    far_g = [after(rows_g[near], partial_b[0])] + rows_g[near + 1:]
-    partial_b = partial_b + run_experts(
-        backward_body, "experts_bwd_far", rows_b[near:] + far_g, experts - 1, partial[near:]
-    )
-    rows_f = [after(rows_f[0], partial_b[-1])] + rows_f[1:]
+    far_b = run_experts(backward_body, "experts_bwd_far", rows_b[near:] + rows_g[near:], experts - 1, partial[near:])
+    near_b = [after(rows_b[0], far_b[0])] + rows_b[1:near]
+    partial_b = run_experts(backward_body, "experts_bwd_near", near_b + rows_g[:near], near, partial[:near]) + far_b
+    rows_f = [after(rows_f[0], partial_b[0])] + rows_f[1:]
     partial_f = run_experts(forward_body, "experts_fwd", rows_f, 2 * experts, partial)
     totals_b, home_b = crossing_home(partial_b)
     totals_f, home_f = crossing_home(partial_f)

time: 103 us -> 103 us (level)
  waiting for transfers between devices: 55.5 us -> 53.5 us
  starting transfers between devices: 28.4 us -> 30.2 us
    ppermute x11, starting transfers between devices: 14.6 us -> 16.4 us  [swapped(): return lax.ppermute(value, axis, [(i, i ^ bit) for i in range(count)])]
    ppermute x7, waiting for transfers between devices: 14.5 us -> 13.3 us  [shifted(): lax.ppermute(value, axis, [(i, (i + steps) % count) for i in range(count)])]
  transfers between devices with their start and end apart: 18 -> 18, of which waited for: 14 -> 13; matrix products, arithmetic and copies ran while one was open for 0% -> 0% of each run, Pallas kernels for 11% -> 11%
where the time goes in v16:
time: 103 us
  waiting for transfers between devices  53.5 us (52%)
  starting transfers between devices  30.2 us (29%)
  Pallas kernels  16.9 us (16%)
    ppermute x11, waiting for transfers between devices, swapped(): return lax.ppermute(value, axis, [(i, i ^ bit) for i in range(count)])  40.2 us
    ppermute x11, starting transfers between devices, swapped(): return lax.ppermute(value, axis, [(i, i ^ bit) for i in range(count)])  16.4 us
    ppermute x7, starting transfers between devices, shifted(): lax.ppermute(value, axis, [(i, (i + steps) % count) for i in range(count)])  13.7 us
    ppermute x7, waiting for transfers between devices, shifted(): lax.ppermute(value, axis, [(i, (i + steps) % count) for i in range(count)])  13.3 us
    pallas_call x3, Pallas kernels, run_experts(): local_call(functools.partial(body, count, rows), out_shape, scratch=wides...  7.64 us
    pallas_call x1, Pallas kernels, per_device(): local_call(first_body, [jax.ShapeDtypeStruct((3 * w_down.shape[1], width)...  3.76 us
  transfers between devices with their start and end apart: 18, of which 13 were waited for; matrix products, arithmetic and copies ran while one was open for 0% of the time, Pallas kernels for 11%

profile of v16, /device:TPU:0, one launch (start us, length us, event | category | flops | bytes accessed | tf_op | source)
XLA Modules:
  0.0 102.6 jit_solution(14465022833197619620)
XLA Ops:
  0.7 3.8 %join_weights_pack_saved.1 = (bf16[576,2048]{1,0:T(8,128)(2,1)}, bf16[264,512]{1,0:T(8,128)(2,1)}, bf16[264,512]{1,0:T(8,128)(2,1)}) custom-call(s32[1]{0:T(128)} %bitcast.own_ref, s32[1,128]{1,0:T(1,128)} %bitcast.31, f32[1,2048]{1,0:T(1,128)} %gain_ref.3, bf16[128,2048]{1,0:T(8,128)(2,1)} %bitcast.29, bf16[192,2048]{1,0:T(8,128)(2,1)} %bitcast.17, ...), custom_call_target="tpu_custom_call" | custom-call | flops 1000 | bytes 1000 | tf_op jit(solution)/shard_map/join_weights_pack_saved/pallas_call | solution.py:250
  4.5 3.0 %collective-permute-start.8 = (bf16[576,2048]{1,0:T(8,128)(2,1)}, bf16[576,2048]{1,0:T(8,128)(2,1)S(1)}, u32[]{:S(2)}, u32[]{:S(2)}) collective-permute-start(bf16[576,2048]{1,0:T(8,128)(2,1)} %get-tuple-element.39), channel_id=1, source_target_pairs={{0,1},{1,0},{2,3},{3,2},{4,5},{5,4},{6,7},{7,6},{8,9},{9,8},{10,11... | collective-permute-start | bytes 7077896 | tf_op jit(solution)/shard_map/ppermute | solution.py:26
  8.2 2.6 %collective-permute-start.2 = (bf16[264,512]{1,0:T(8,128)(2,1)}, bf16[264,512]{1,0:T(8,128)(2,1)S(1)}, u32[]{:S(2)}, u32[]{:S(2)}) collective-permute-start(bf16[264,512]{1,0:T(8,128)(2,1)} %get-tuple-element.31), channel_id=1, source_target_pairs={{0,4},{1,5},{2,6},{3,7},{4,0},{5,1},{6,2},{7,3},{8,12},{9,13},{10,... | collective-permute-start | bytes 811016 | tf_op jit(solution)/shard_map/ppermute | solution.py:21
  10.8 1.6 %collective-permute-start.3 = (bf16[264,512]{1,0:T(8,128)(2,1)}, bf16[264,512]{1,0:T(8,128)(2,1)S(1)}, u32[]{:S(2)}, u32[]{:S(2)}) collective-permute-start(bf16[264,512]{1,0:T(8,128)(2,1)} %get-tuple-element.28.kept_ref), channel_id=1, source_target_pairs={{0,2},{1,3},{2,0},{3,1},{4,6},{5,7},{6,4},{7,5},{8,10},{9,11},{10,... | collective-permute-start | bytes 811016 | tf_op jit(solution)/shard_map/ppermute | solution.py:26
  12.3 5.0 %collective-permute-done.1.x_ref.up_ref = bf16[128,2048]{1,0:T(8,128)(2,1)S(1)} collective-permute-done((bf16[128,2048]{1,0:T(8,128)(2,1)S(1)}, bf16[128,2048]{1,0:T(8,128)(2,1)S(1)}, u32[]{:S(2)}, u32[]{:S(2)}) %collective-permute-start.1) | collective-permute-done | bytes 524320 | tf_op jit(solution)/shard_map/ppermute | solution.py:21
  18.2 5.0 %collective-permute-start.5 = (bf16[264,512]{1,0:T(8,128)(2,1)S(1)}, bf16[264,512]{1,0:T(8,128)(2,1)S(1)}, u32[]{:S(2)}, u32[]{:S(2)}) collective-permute-start(bf16[264,512]{1,0:T(8,128)(2,1)S(1)} %get-tuple-element.36), channel_id=1, source_target_pairs={{0,4},{1,5},{2,6},{3,7},{4,0},{5,1},{6,2},{7,3},{8,12},{9,13},{10,... | collective-permute-start | bytes 811016 | tf_op jit(solution)/shard_map/ppermute | solution.py:21
  23.4 1.4 %collective-permute-start.6 = (bf16[264,512]{1,0:T(8,128)(2,1)S(1)}, bf16[264,512]{1,0:T(8,128)(2,1)S(1)}, u32[]{:S(2)}, u32[]{:S(2)}) collective-permute-start(bf16[264,512]{1,0:T(8,128)(2,1)S(1)} %get-tuple-element.37.refs_3_), channel_id=1, source_target_pairs={{0,2},{1,3},{2,0},{3,1},{4,6},{5,7},{6,4},{7,5},{8,10},{9,11},{10,... | collective-permute-start | bytes 811016 | tf_op jit(solution)/shard_map/ppermute | solution.py:26
  24.8 1.2 %collective-permute-done.3.refs_2_ = bf16[264,512]{1,0:T(8,128)(2,1)S(1)} collective-permute-done((bf16[264,512]{1,0:T(8,128)(2,1)}, bf16[264,512]{1,0:T(8,128)(2,1)S(1)}, u32[]{:S(2)}, u32[]{:S(2)}) %collective-permute-start.3) | collective-permute-done | bytes 270368 | tf_op jit(solution)/shard_map/ppermute | solution.py:26
  26.1 0.9 copy-done.4
  28.0 2.0 %collective-permute-start.9 = (bf16[264,512]{1,0:T(8,128)(2,1)S(1)}, bf16[264,512]{1,0:T(8,128)(2,1)S(1)}, u32[]{:S(2)}, u32[]{:S(2)}) collective-permute-start(bf16[264,512]{1,0:T(8,128)(2,1)S(1)} %get-tuple-element.43), channel_id=1, source_target_pairs={{0,4},{1,5},{2,6},{3,7},{4,0},{5,1},{6,2},{7,3},{8,12},{9,13},{10,... | collective-permute-start | bytes 811016 | tf_op jit(solution)/shard_map/ppermute | solution.py:21
  29.9 6.2 %collective-permute-done.5.refs_4_ = bf16[264,512]{1,0:T(8,128)(2,1)S(1)} collective-permute-done((bf16[264,512]{1,0:T(8,128)(2,1)S(1)}, bf16[264,512]{1,0:T(8,128)(2,1)S(1)}, u32[]{:S(2)}, u32[]{:S(2)}) %collective-permute-start.5) | collective-permute-done | bytes 270368 | tf_op jit(solution)/shard_map/ppermute | solution.py:21
  36.2 1.2 %collective-permute-start.10 = (bf16[264,512]{1,0:T(8,128)(2,1)S(1)}, bf16[264,512]{1,0:T(8,128)(2,1)S(1)}, u32[]{:S(2)}, u32[]{:S(2)}) collective-permute-start(bf16[264,512]{1,0:T(8,128)(2,1)S(1)} %get-tuple-element.44.refs_0_), channel_id=1, source_target_pairs={{0,2},{1,3},{2,0},{3,1},{4,6},{5,7},{6,4},{7,5},{8,10},{9,11},{10,... | collective-permute-start | bytes 811016 | tf_op jit(solution)/shard_map/ppermute | solution.py:26
  37.4 5.8 %collective-permute-done.6.refs_5_ = bf16[264,512]{1,0:T(8,128)(2,1)S(1)} collective-permute-done((bf16[264,512]{1,0:T(8,128)(2,1)S(1)}, bf16[264,512]{1,0:T(8,128)(2,1)S(1)}, u32[]{:S(2)}, u32[]{:S(2)}) %collective-permute-start.6) | collective-permute-done | bytes 270368 | tf_op jit(solution)/shard_map/ppermute | solution.py:26
  43.2 5.8 %collective-permute-done.4.refs_0_ = bf16[264,512]{1,0:T(8,128)(2,1)S(1)} collective-permute-done((bf16[264,512]{1,0:T(8,128)(2,1)S(1)}, bf16[264,512]{1,0:T(8,128)(2,1)S(1)}, u32[]{:S(2)}, u32[]{:S(2)}) %collective-permute-start.4) | collective-permute-done | bytes 270368 | tf_op jit(solution)/shard_map/ppermute | solution.py:26
  49.0 5.8 %collective-permute-done.10.refs_2_ = bf16[264,512]{1,0:T(8,128)(2,1)S(1)} collective-permute-done((bf16[264,512]{1,0:T(8,128)(2,1)S(1)}, bf16[264,512]{1,0:T(8,128)(2,1)S(1)}, u32[]{:S(2)}, u32[]{:S(2)}) %collective-permute-start.10) | collective-permute-done | bytes 270368 | tf_op jit(solution)/shard_map/ppermute | solution.py:26
  54.8 1.0 collective-permute-start.11
  55.8 4.8 %collective-permute-done.7.refs_1_ = bf16[264,512]{1,0:T(8,128)(2,1)S(1)} collective-permute-done((bf16[264,512]{1,0:T(8,128)(2,1)S(1)}, bf16[264,512]{1,0:T(8,128)(2,1)S(1)}, u32[]{:S(2)}, u32[]{:S(2)}) %collective-permute-start.7) | collective-permute-done | bytes 270368 | tf_op jit(solution)/shard_map/ppermute | solution.py:26
  60.6 2.5 %experts_bwd_far.1 = bf16[264,512]{1,0:T(8,128)(2,1)S(1)} custom-call(bf16[264,512]{1,0:T(8,128)(2,1)S(1)} %collective-permute-done.4.refs_0_, bf16[264,512]{1,0:T(8,128)(2,1)S(1)} %collective-permute-done.7.refs_1_, bf16[192,2048]{1,0:T(8,128)(2,1)S(1)} %bitcast.18, bf16[192,2048]{1,0:T(8,128)(2,1)S(1)} %bitcast.22, bf16[192,2048]{1,0:T(8,128)(2,1)S(1)} %bitcast.26, ...), custom_call_target="tpu_custom_call" | custom-call | flops 1000 | bytes 1000 | tf_op jit(solution)/shard_map/experts_bwd_far/pallas_call | solution.py:293
  63.1 1.0 %collective-permute-start.13 = (bf16[264,512]{1,0:T(8,128)(2,1)S(1)}, bf16[264,512]{1,0:T(8,128)(2,1)S(1)}, u32[]{:S(2)}, u32[]{:S(2)}) collective-permute-start(bf16[264,512]{1,0:T(8,128)(2,1)S(1)} %experts_bwd_far.1), channel_id=1, source_target_pairs={{0,2},{1,3},{2,0},{3,1},{4,6},{5,7},{6,4},{7,5},{8,10},{9,11},{10,... | collective-permute-start | bytes 811016 | tf_op jit(solution)/shard_map/ppermute | solution.py:26
  64.2 2.9 %experts_bwd_near.1 = (f32[264,512]{1,0:T(8,128)S(1)}, f32[264,512]{1,0:T(8,128)S(1)}, bf16[264,512]{1,0:T(8,128)(2,1)S(1)}) custom-call(bf16[264,512]{1,0:T(8,128)(2,1)S(1)} %get-tuple-element.40.refs_0_, bf16[264,512]{1,0:T(8,128)(2,1)S(1)} %collective-permute-done.2.refs_1_, bf16[264,512]{1,0:T(8,128)(2,1)S(1)} %collective-permute-done.3.refs_2_, ...), custom_call_target="tpu_custom_call" | custom-call | flops 1000 | bytes 1000 | tf_op jit(solution)/shard_map/experts_bwd_near/pallas_call | solution.py:293
  67.1 2.3 %experts_fwd.1 = (f32[264,512]{1,0:T(8,128)S(1)}, f32[264,512]{1,0:T(8,128)S(1)}, bf16[264,512]{1,0:T(8,128)(2,1)S(1)}, bf16[264,512]{1,0:T(8,128)(2,1)S(1)}) custom-call(bf16[264,512]{1,0:T(8,128)(2,1)S(1)} %get-tuple-element.44.refs_0_, bf16[264,512]{1,0:T(8,128)(2,1)S(1)} %collective-permute-done.9.refs_1_, ...), custom_call_target="tpu_custom_call" | custom-call | flops 1000 | bytes 1000 | tf_op jit(solution)/shard_map/experts_fwd/pallas_call | solution.py:293
  69.3 1.1 %collective-permute-start.12 = (bf16[264,512]{1,0:T(8,128)(2,1)S(1)}, bf16[264,512]{1,0:T(8,128)(2,1)S(1)}, u32[]{:S(2)}, u32[]{:S(2)}) collective-permute-start(bf16[264,512]{1,0:T(8,128)(2,1)S(1)} %get-tuple-element.49), channel_id=1, source_target_pairs={{0,2},{1,3},{2,0},{3,1},{4,6},{5,7},{6,4},{7,5},{8,10},{9,11},{10,... | collective-permute-start | bytes 811016 | tf_op jit(solution)/shard_map/ppermute | solution.py:26
  70.4 1.4 %collective-permute-done.13 = bf16[264,512]{1,0:T(8,128)(2,1)S(1)} collective-permute-done((bf16[264,512]{1,0:T(8,128)(2,1)S(1)}, bf16[264,512]{1,0:T(8,128)(2,1)S(1)}, u32[]{:S(2)}, u32[]{:S(2)}) %collective-permute-start.13) | collective-permute-done | bytes 270368 | tf_op jit(solution)/shard_map/ppermute | solution.py:26
  71.9 3.4 %collective-permute-start.14 = (bf16[264,512]{1,0:T(8,128)(2,1)S(1)}, bf16[264,512]{1,0:T(8,128)(2,1)S(1)}, u32[]{:S(2)}, u32[]{:S(2)}) collective-permute-start(bf16[264,512]{1,0:T(8,128)(2,1)S(1)} %add_convert_fusion), channel_id=1, source_target_pairs={{0,4},{1,5},{2,6},{3,7},{4,0},{5,1},{6,2},{7,3},{8,12},{9,13},{10,... | collective-permute-start | bytes 811016 | tf_op jit(solution)/shard_map/ppermute | solution.py:21
  75.4 2.5 %collective-permute-start.17 = (bf16[264,512]{1,0:T(8,128)(2,1)S(1)}, bf16[264,512]{1,0:T(8,128)(2,1)S(1)}, u32[]{:S(2)}, u32[]{:S(2)}) collective-permute-start(bf16[264,512]{1,0:T(8,128)(2,1)S(1)} %get-tuple-element.53), channel_id=1, source_target_pairs={{0,2},{1,3},{2,0},{3,1},{4,6},{5,7},{6,4},{7,5},{8,10},{9,11},{10,... | collective-permute-start | bytes 811016 | tf_op jit(solution)/shard_map/ppermute | solution.py:26
  77.9 6.4 %collective-permute-done.12 = bf16[264,512]{1,0:T(8,128)(2,1)S(1)} collective-permute-done((bf16[264,512]{1,0:T(8,128)(2,1)S(1)}, bf16[264,512]{1,0:T(8,128)(2,1)S(1)}, u32[]{:S(2)}, u32[]{:S(2)}) %collective-permute-start.12) | collective-permute-done | bytes 270368 | tf_op jit(solution)/shard_map/ppermute | solution.py:26
  84.4 1.9 %collective-permute-done.14.refs_2_ = bf16[264,512]{1,0:T(8,128)(2,1)S(1)} collective-permute-done((bf16[264,512]{1,0:T(8,128)(2,1)S(1)}, bf16[264,512]{1,0:T(8,128)(2,1)S(1)}, u32[]{:S(2)}, u32[]{:S(2)}) %collective-permute-start.14) | collective-permute-done | bytes 270368 | tf_op jit(solution)/shard_map/ppermute | solution.py:21
  86.3 3.6 %collective-permute-start.15 = (bf16[264,512]{1,0:T(8,128)(2,1)S(1)}, bf16[264,512]{1,0:T(8,128)(2,1)S(1)}, u32[]{:S(2)}, u32[]{:S(2)}) collective-permute-start(bf16[264,512]{1,0:T(8,128)(2,1)S(1)} %get-tuple-element.51), channel_id=1, source_target_pairs={{0,2},{1,3},{2,0},{3,1},{4,6},{5,7},{6,4},{7,5},{8,10},{9,11},{10,... | collective-permute-start | bytes 811016 | tf_op jit(solution)/shard_map/ppermute | solution.py:26
  89.8 6.0 %collective-permute-done.17.refs_1_ = bf16[264,512]{1,0:T(8,128)(2,1)S(1)} collective-permute-done((bf16[264,512]{1,0:T(8,128)(2,1)S(1)}, bf16[264,512]{1,0:T(8,128)(2,1)S(1)}, u32[]{:S(2)}, u32[]{:S(2)}) %collective-permute-start.17) | collective-permute-done | bytes 270368 | tf_op jit(solution)/shard_map/ppermute | solution.py:26
  95.8 2.0 %home_bwd.1 = bf16[128,2048]{1,0:T(8,128)(2,1)} custom-call(s32[1]{0:T(128)} %bitcast.own_ref, s32[1,128]{1,0:T(1,128)S(1)} %bitcast.33, f32[1,128]{1,0:T(1,128)S(1)} %bitcast.37, f32[1,2048]{1,0:T(1,128)S(1)} %copy-done.5, bf16[128,2048]{1,0:T(8,128)(2,1)S(1)} %bitcast.30, bf16[128,2048]{1,0:T(8,128)(2,1)S(1)} %collective-permute-done.1.x_ref.up_ref, ...), custom_call_target="tpu_custom_call" | custom-call | flops 1000 | bytes 1000 | tf_op jit(solution)/shard_map/home_bwd/pallas_call | solution.py:308
  97.8 3.0 %collective-permute-done.15.refs_1_ = bf16[264,512]{1,0:T(8,128)(2,1)S(1)} collective-permute-done((bf16[264,512]{1,0:T(8,128)(2,1)S(1)}, bf16[264,512]{1,0:T(8,128)(2,1)S(1)}, u32[]{:S(2)}, u32[]{:S(2)}) %collective-permute-start.15) | collective-permute-done | bytes 270368 | tf_op jit(solution)/shard_map/ppermute | solution.py:26
  100.9 1.7 %home_fwd.1 = bf16[128,2048]{1,0:T(8,128)(2,1)} custom-call(s32[1]{0:T(128)} %bitcast.own_ref, s32[1,128]{1,0:T(1,128)S(1)} %bitcast.35, f32[1,128]{1,0:T(1,128)S(1)} %bitcast.36, bf16[128,2048]{1,0:T(8,128)(2,1)S(1)} %collective-permute-done.x_ref, f32[264,512]{1,0:T(8,128)S(1)} %get-tuple-element.46.refs_0_, ...), custom_call_target="tpu_custom_call" | custom-call | flops 1000 | bytes 1000 | tf_op jit(solution)/shard_map/home_fwd/pallas_call | solution.py:315
  (36 shorter events, 2.9 us)
Async XLA Ops:
  0.6 59.9 %copy-start.1 = (bf16[1,2048,192]{1,2,0:T(8,128)(2,1)S(1)}, bf16[1,2048,192]{1,2,0:T(8,128)(2,1)}, u32[]{:S(2)}) copy-start(bf16[1,2048,192]{1,2,0:T(8,128)(2,1)} %param.16) | copy-start | bytes 2359300
  0.6 59.9 %copy-start.2 = (bf16[1,192,2048]{2,1,0:T(8,128)(2,1)S(1)}, bf16[1,192,2048]{2,1,0:T(8,128)(2,1)}, u32[]{:S(2)}) copy-start(bf16[1,192,2048]{2,1,0:T(8,128)(2,1)} %param.17) | copy-start | bytes 2359300
  0.7 59.9 %copy-start = (bf16[1,2048,192]{1,2,0:T(8,128)(2,1)S(1)}, bf16[1,2048,192]{1,2,0:T(8,128)(2,1)}, u32[]{:S(2)}) copy-start(bf16[1,2048,192]{1,2,0:T(8,128)(2,1)} %param.15) | copy-start | bytes 2359300
  0.7 16.7 %copy-start.6 = (s32[1,128,1]{1,2,0:T(1,128)S(1)}, s32[1,128,1]{1,2,0:T(1,128)}, u32[]{:S(2)}) copy-start(s32[1,128,1]{1,2,0:T(1,128)} %param.20) | copy-start | bytes 1540
  0.7 25.4 %copy-start.5 = (f32[1,2048]{1,0:T(1,128)S(1)}, f32[1,2048]{1,0:T(1,128)}, u32[]{:S(2)}) copy-start(f32[1,2048]{1,0:T(1,128)} %gain_ref.3) | copy-start | bytes 24580
  0.7 6.8 %copy-start.10 = (bf16[1,128,2048]{2,1,0:T(8,128)(2,1)S(1)}, bf16[1,128,2048]{2,1,0:T(8,128)(2,1)}, u32[]{:S(2)}) copy-start(bf16[1,128,2048]{2,1,0:T(8,128)(2,1)} %param.13) | copy-start | bytes 1572868
  0.7 25.4 %copy-start.7 = (s32[1,128,1]{1,2,0:T(1,128)S(1)}, s32[1,128,1]{1,2,0:T(1,128)}, u32[]{:S(2)}) copy-start(s32[1,128,1]{1,2,0:T(1,128)} %param.18) | copy-start | bytes 1540
  4.5 56.1 %collective-permute-start.8 = (bf16[576,2048]{1,0:T(8,128)(2,1)}, bf16[576,2048]{1,0:T(8,128)(2,1)S(1)}, u32[]{:S(2)}, u32[]{:S(2)}) collective-permute-start(bf16[576,2048]{1,0:T(8,128)(2,1)} %get-tuple-element.39), channel_id=1, source_target_pairs={{0,1},{1,0},{2,3},{3,2},{4,5},{5,4},{6,7},{7,6},{8,9},{9,8},{10,11... | collective-permute-start | bytes 7077896 | tf_op jit(solution)/shard_map/ppermute | solution.py:26
  7.5 9.9 %collective-permute-start.1 = (bf16[128,2048]{1,0:T(8,128)(2,1)S(1)}, bf16[128,2048]{1,0:T(8,128)(2,1)S(1)}, u32[]{:S(2)}, u32[]{:S(2)}) collective-permute-start(bf16[128,2048]{1,0:T(8,128)(2,1)S(1)} %bitcast.40), channel_id=1, source_target_pairs={{0,24},{8,0},{16,8},{24,16},{1,25},{9,1},{17,9},{25,17},{2,26},{10... | collective-permute-start | bytes 1572872 | tf_op jit(solution)/shard_map/ppermute | solution.py:21
  8.2 15.2 %collective-permute-start.2 = (bf16[264,512]{1,0:T(8,128)(2,1)}, bf16[264,512]{1,0:T(8,128)(2,1)S(1)}, u32[]{:S(2)}, u32[]{:S(2)}) collective-permute-start(bf16[264,512]{1,0:T(8,128)(2,1)} %get-tuple-element.31), channel_id=1, source_target_pairs={{0,4},{1,5},{2,6},{3,7},{4,0},{5,1},{6,2},{7,3},{8,12},{9,13},{10,... | collective-permute-start | bytes 811016 | tf_op jit(solution)/shard_map/ppermute | solution.py:21
  10.8 15.3 %collective-permute-start = (bf16[128,2048]{1,0:T(8,128)(2,1)}, bf16[128,2048]{1,0:T(8,128)(2,1)S(1)}, u32[]{:S(2)}, u32[]{:S(2)}) collective-permute-start(bf16[128,2048]{1,0:T(8,128)(2,1)} %bitcast.41), channel_id=1, source_target_pairs={{0,8},{8,16},{16,24},{24,0},{1,9},{9,17},{17,25},{25,1},{2,10},{10... | collective-permute-start | bytes 1572872 | tf_op jit(solution)/shard_map/ppermute | solution.py:21
  10.8 15.3 %collective-permute-start.3 = (bf16[264,512]{1,0:T(8,128)(2,1)}, bf16[264,512]{1,0:T(8,128)(2,1)S(1)}, u32[]{:S(2)}, u32[]{:S(2)}) collective-permute-start(bf16[264,512]{1,0:T(8,128)(2,1)} %get-tuple-element.28.kept_ref), channel_id=1, source_target_pairs={{0,2},{1,3},{2,0},{3,1},{4,6},{5,7},{6,4},{7,5},{8,10},{9,11},{10,... | collective-permute-start | bytes 811016 | tf_op jit(solution)/shard_map/ppermute | solution.py:26
  18.2 17.9 %collective-permute-start.5 = (bf16[264,512]{1,0:T(8,128)(2,1)S(1)}, bf16[264,512]{1,0:T(8,128)(2,1)S(1)}, u32[]{:S(2)}, u32[]{:S(2)}) collective-permute-start(bf16[264,512]{1,0:T(8,128)(2,1)S(1)} %get-tuple-element.36), channel_id=1, source_target_pairs={{0,4},{1,5},{2,6},{3,7},{4,0},{5,1},{6,2},{7,3},{8,12},{9,13},{10,... | collective-permute-start | bytes 811016 | tf_op jit(solution)/shard_map/ppermute | solution.py:21
  23.4 19.8 %collective-permute-start.6 = (bf16[264,512]{1,0:T(8,128)(2,1)S(1)}, bf16[264,512]{1,0:T(8,128)(2,1)S(1)}, u32[]{:S(2)}, u32[]{:S(2)}) collective-permute-start(bf16[264,512]{1,0:T(8,128)(2,1)S(1)} %get-tuple-element.37.refs_3_), channel_id=1, source_target_pairs={{0,2},{1,3},{2,0},{3,1},{4,6},{5,7},{6,4},{7,5},{8,10},{9,11},{10,... | collective-permute-start | bytes 811016 | tf_op jit(solution)/shard_map/ppermute | solution.py:26
  26.1 22.9 %collective-permute-start.4 = (bf16[264,512]{1,0:T(8,128)(2,1)S(1)}, bf16[264,512]{1,0:T(8,128)(2,1)S(1)}, u32[]{:S(2)}, u32[]{:S(2)}) collective-permute-start(bf16[264,512]{1,0:T(8,128)(2,1)S(1)} %collective-permute-done.2.refs_1_), channel_id=1, source_target_pairs={{0,2},{1,3},{2,0},{3,1},{4,6},{5,7},{6,4},{7,5},{8,10},{9,11},{10,... | collective-permute-start | bytes 811016 | tf_op jit(solution)/shard_map/ppermute | solution.py:26
  26.1 1.0 copy-start.4
  28.0 21.0 %collective-permute-start.9 = (bf16[264,512]{1,0:T(8,128)(2,1)S(1)}, bf16[264,512]{1,0:T(8,128)(2,1)S(1)}, u32[]{:S(2)}, u32[]{:S(2)}) collective-permute-start(bf16[264,512]{1,0:T(8,128)(2,1)S(1)} %get-tuple-element.43), channel_id=1, source_target_pairs={{0,4},{1,5},{2,6},{3,7},{4,0},{5,1},{6,2},{7,3},{8,12},{9,13},{10,... | collective-permute-start | bytes 811016 | tf_op jit(solution)/shard_map/ppermute | solution.py:21
  36.2 18.6 %collective-permute-start.10 = (bf16[264,512]{1,0:T(8,128)(2,1)S(1)}, bf16[264,512]{1,0:T(8,128)(2,1)S(1)}, u32[]{:S(2)}, u32[]{:S(2)}) collective-permute-start(bf16[264,512]{1,0:T(8,128)(2,1)S(1)} %get-tuple-element.44.refs_0_), channel_id=1, source_target_pairs={{0,2},{1,3},{2,0},{3,1},{4,6},{5,7},{6,4},{7,5},{8,10},{9,11},{10,... | collective-permute-start | bytes 811016 | tf_op jit(solution)/shard_map/ppermute | solution.py:26
  43.2 17.4 %collective-permute-start.7 = (bf16[264,512]{1,0:T(8,128)(2,1)S(1)}, bf16[264,512]{1,0:T(8,128)(2,1)S(1)}, u32[]{:S(2)}, u32[]{:S(2)}) collective-permute-start(bf16[264,512]{1,0:T(8,128)(2,1)S(1)} %collective-permute-done.5.refs_4_), channel_id=1, source_target_pairs={{0,2},{1,3},{2,0},{3,1},{4,6},{5,7},{6,4},{7,5},{8,10},{9,11},{10,... | collective-permute-start | bytes 811016 | tf_op jit(solution)/shard_map/ppermute | solution.py:26
  54.8 12.3 %collective-permute-start.11 = (bf16[264,512]{1,0:T(8,128)(2,1)S(1)}, bf16[264,512]{1,0:T(8,128)(2,1)S(1)}, u32[]{:S(2)}, u32[]{:S(2)}) collective-permute-start(bf16[264,512]{1,0:T(8,128)(2,1)S(1)} %collective-permute-done.9.refs_1_), channel_id=1, source_target_pairs={{0,2},{1,3},{2,0},{3,1},{4,6},{5,7},{6,4},{7,5},{8,10},{9,11},{10,... | collective-permute-start | bytes 811016 | tf_op jit(solution)/shard_map/ppermute | solution.py:26
  63.1 8.7 %collective-permute-start.13 = (bf16[264,512]{1,0:T(8,128)(2,1)S(1)}, bf16[264,512]{1,0:T(8,128)(2,1)S(1)}, u32[]{:S(2)}, u32[]{:S(2)}) collective-permute-start(bf16[264,512]{1,0:T(8,128)(2,1)S(1)} %experts_bwd_far.1), channel_id=1, source_target_pairs={{0,2},{1,3},{2,0},{3,1},{4,6},{5,7},{6,4},{7,5},{8,10},{9,11},{10,... | collective-permute-start | bytes 811016 | tf_op jit(solution)/shard_map/ppermute | solution.py:26
  67.0 28.8 %copy-start.9 = (f32[1,128,1]{1,2,0:T(1,128)S(1)}, f32[1,128,1]{1,2,0:T(1,128)}, u32[]{:S(2)}) copy-start(f32[1,128,1]{1,2,0:T(1,128)} %param.21) | copy-start | bytes 1540
  69.3 26.5 %copy-start.3 = (bf16[1,128,2048]{2,1,0:T(8,128)(2,1)S(1)}, bf16[1,128,2048]{2,1,0:T(8,128)(2,1)}, u32[]{:S(2)}) copy-start(bf16[1,128,2048]{2,1,0:T(8,128)(2,1)} %param.12) | copy-start | bytes 1572868
  69.3 14.9 %collective-permute-start.12 = (bf16[264,512]{1,0:T(8,128)(2,1)S(1)}, bf16[264,512]{1,0:T(8,128)(2,1)S(1)}, u32[]{:S(2)}, u32[]{:S(2)}) collective-permute-start(bf16[264,512]{1,0:T(8,128)(2,1)S(1)} %get-tuple-element.49), channel_id=1, source_target_pairs={{0,2},{1,3},{2,0},{3,1},{4,6},{5,7},{6,4},{7,5},{8,10},{9,11},{10,... | collective-permute-start | bytes 811016 | tf_op jit(solution)/shard_map/ppermute | solution.py:26
  71.9 29.0 %copy-start.8 = (f32[1,128,1]{1,2,0:T(1,128)S(1)}, f32[1,128,1]{1,2,0:T(1,128)}, u32[]{:S(2)}) copy-start(f32[1,128,1]{1,2,0:T(1,128)} %param.19) | copy-start | bytes 1540
  71.9 14.3 %collective-permute-start.14 = (bf16[264,512]{1,0:T(8,128)(2,1)S(1)}, bf16[264,512]{1,0:T(8,128)(2,1)S(1)}, u32[]{:S(2)}, u32[]{:S(2)}) collective-permute-start(bf16[264,512]{1,0:T(8,128)(2,1)S(1)} %add_convert_fusion), channel_id=1, source_target_pairs={{0,4},{1,5},{2,6},{3,7},{4,0},{5,1},{6,2},{7,3},{8,12},{9,13},{10,... | collective-permute-start | bytes 811016 | tf_op jit(solution)/shard_map/ppermute | solution.py:21
  75.4 20.4 %collective-permute-start.17 = (bf16[264,512]{1,0:T(8,128)(2,1)S(1)}, bf16[264,512]{1,0:T(8,128)(2,1)S(1)}, u32[]{:S(2)}, u32[]{:S(2)}) collective-permute-start(bf16[264,512]{1,0:T(8,128)(2,1)S(1)} %get-tuple-element.53), channel_id=1, source_target_pairs={{0,2},{1,3},{2,0},{3,1},{4,6},{5,7},{6,4},{7,5},{8,10},{9,11},{10,... | collective-permute-start | bytes 811016 | tf_op jit(solution)/shard_map/ppermute | solution.py:26
  84.3 13.5 %collective-permute-start.16 = (bf16[264,512]{1,0:T(8,128)(2,1)S(1)}, bf16[264,512]{1,0:T(8,128)(2,1)S(1)}, u32[]{:S(2)}, u32[]{:S(2)}) collective-permute-start(bf16[264,512]{1,0:T(8,128)(2,1)S(1)} %add_convert_fusion.1), channel_id=1, source_target_pairs={{0,4},{1,5},{2,6},{3,7},{4,0},{5,1},{6,2},{7,3},{8,12},{9,13},{10,... | collective-permute-start | bytes 811016 | tf_op jit(solution)/shard_map/ppermute | solution.py:21
  86.3 14.6 %collective-permute-start.15 = (bf16[264,512]{1,0:T(8,128)(2,1)S(1)}, bf16[264,512]{1,0:T(8,128)(2,1)S(1)}, u32[]{:S(2)}, u32[]{:S(2)}) collective-permute-start(bf16[264,512]{1,0:T(8,128)(2,1)S(1)} %get-tuple-element.51), channel_id=1, source_target_pairs={{0,2},{1,3},{2,0},{3,1},{4,6},{5,7},{6,4},{7,5},{8,10},{9,11},{10,... | collective-permute-start | bytes 811016 | tf_op jit(solution)/shard_map/ppermute | solution.py:26

commit v17 on v16

--- a/solution.py
+++ b/solution.py
@@ -168,17 +168,19 @@
     spread_out(total, outs, x.shape[0] // count, rows)
 
 
-def routed_sum(experts, rows, own_ref, routes_ref, gates_ref, home_refs):
+def own_sum(mine, theirs):
+    return (mine[...] + theirs[...].astype(F32)).astype(BF16)
+
+
+def routed_sum(experts, rows, own_ref, routes_ref, gates_ref, blocks):
     block, slot = slots_of(routes_ref[...], own_ref[0], experts)
-    mine, theirs, *crossed_refs = home_refs
-    blocks = [(mine[...] + theirs[...].astype(F32)).astype(BF16)] + [ref[...] for ref in crossed_refs]
-    height = blocks[0].shape[0]
+    height = blocks[0][1].shape[0]
     columns = []
     for p in range(height // rows):
         total = None
-        for j in range(experts):
+        for j, value in blocks:
             chooser = chooser_of(block, slot, j, p, rows, height)
-            part = lax.dot_general(chooser, blocks[j], OVER_ROWS, preferred_element_type=F32)
+            part = lax.dot_general(chooser, value, OVER_ROWS, preferred_element_type=F32)
             total = part if total is None else total + part
         columns.append(total)
     count = block.shape[1]
@@ -189,13 +191,19 @@
     return jnp.concatenate(columns, axis=1) * gates
 
 
-def forward_home_body(experts, rows, own_ref, routes_ref, gates_ref, x_ref, *refs):
-    mixed = routed_sum(experts, rows, own_ref, routes_ref, gates_ref, refs[:-1])
-    refs[-1][...] = (x_ref[...].astype(F32) + mixed).astype(BF16)
+def forward_crossed_body(experts, rows, own_ref, routes_ref, gates_ref, x_ref, *refs):
+    blocks = [(j, ref[...]) for j, ref in enumerate(refs[:-1], 1)]
+    refs[-1][...] = x_ref[...].astype(F32) + routed_sum(experts, rows, own_ref, routes_ref, gates_ref, blocks)
+
+
+def forward_home_body(experts, rows, own_ref, routes_ref, gates_ref, sum_ref, mine, theirs, out):
+    blocks = [(0, own_sum(mine, theirs))]
+    out[...] = (sum_ref[...] + routed_sum(experts, rows, own_ref, routes_ref, gates_ref, blocks)).astype(BF16)
 
 
 def backward_home_body(experts, rows, own_ref, routes_ref, gates_ref, gain_ref, saved_ref, up_ref, *refs):
-    d_norm = routed_sum(experts, rows, own_ref, routes_ref, gates_ref, refs[:-1])
+    blocks = [(0, own_sum(*refs[:2]))] + [(j, ref[...]) for j, ref in enumerate(refs[2:-1], 1)]
+    d_norm = routed_sum(experts, rows, own_ref, routes_ref, gates_ref, blocks)
     base = saved_ref[...].astype(F32)
     inv_scale = inverse_rms(base)
     scaled = d_norm * gain_ref[...]
@@ -312,13 +320,20 @@
         out_specs=whole,
         name="home_bwd",
     )(own, r_bwd, g_bwd, norm_gain, saved_in[0], upstream, *back_b)
+    crossed_sum = local_call(
+        functools.partial(forward_crossed_body, experts, rows),
+        jax.ShapeDtypeStruct((tok_count, width), F32),
+        in_specs=[scalar] + [whole] * (2 + experts),
+        out_specs=whole,
+        name="home_fwd_crossed",
+    )(own, r_fwd, g_fwd, incoming, *home_f)
     act_out = local_call(
         functools.partial(forward_home_body, experts, rows),
         tokens,
-        in_specs=[scalar] + [whole] * (4 + experts),
+        in_specs=[scalar] + [whole] * 5,
         out_specs=whole,
         name="home_fwd",
-    )(own, r_fwd, g_fwd, incoming, *back_f)
+    )(own, r_fwd, g_fwd, crossed_sum, *back_f[:2])
     return (act_out[None], grad_out[None])
 
 

time: 103 us -> 102 us (level)
  transfers between devices with their start and end apart: 18 -> 18, of which waited for: 13 -> 13; matrix products, arithmetic and copies ran while one was open for 0% -> 0% of each run, Pallas kernels for 11% -> 12%
where the time goes in v17:
time: 102 us
  waiting for transfers between devices  52.9 us (52%)
  starting transfers between devices  30.2 us (30%)
  Pallas kernels  17.3 us (17%)
    ppermute x11, waiting for transfers between devices, swapped(): return lax.ppermute(value, axis, [(i, i ^ bit) for i in range(count)])  39.7 us
    ppermute x11, starting transfers between devices, swapped(): return lax.ppermute(value, axis, [(i, i ^ bit) for i in range(count)])  16.4 us
    ppermute x7, starting transfers between devices, shifted(): lax.ppermute(value, axis, [(i, (i + steps) % count) for i in range(count)])  13.7 us
    ppermute x7, waiting for transfers between devices, shifted(): lax.ppermute(value, axis, [(i, (i + steps) % count) for i in range(count)])  13.2 us
    pallas_call x3, Pallas kernels, run_experts(): local_call(functools.partial(body, count, rows), out_shape, scratch=wides...  7.64 us
    pallas_call x1, Pallas kernels, per_device(): local_call(first_body, [jax.ShapeDtypeStruct((3 * w_down.shape[1], width)...  3.76 us
  transfers between devices with their start and end apart: 18, of which 13 were waited for; matrix products, arithmetic and copies ran while one was open for 0% of the time, Pallas kernels for 12%

profile of v17, /device:TPU:0, one launch (start us, length us, event | category | flops | bytes accessed | tf_op | source)
XLA Modules:
  0.0 102.3 jit_solution(6573989120624099368)
XLA Ops:
  0.7 3.8 %join_weights_pack_saved.1 = (bf16[576,2048]{1,0:T(8,128)(2,1)}, bf16[264,512]{1,0:T(8,128)(2,1)}, bf16[264,512]{1,0:T(8,128)(2,1)}) custom-call(s32[1]{0:T(128)} %bitcast.own_ref, s32[1,128]{1,0:T(1,128)} %bitcast.34, f32[1,2048]{1,0:T(1,128)} %gain_ref.3, bf16[128,2048]{1,0:T(8,128)(2,1)} %bitcast.29, bf16[192,2048]{1,0:T(8,128)(2,1)} %bitcast.17, ...), custom_call_target="tpu_custom_call" | custom-call | flops 1000 | bytes 1000 | tf_op jit(solution)/shard_map/join_weights_pack_saved/pallas_call | solution.py:258
  4.5 3.0 %collective-permute-start.8 = (bf16[576,2048]{1,0:T(8,128)(2,1)}, bf16[576,2048]{1,0:T(8,128)(2,1)S(1)}, u32[]{:S(2)}, u32[]{:S(2)}) collective-permute-start(bf16[576,2048]{1,0:T(8,128)(2,1)} %get-tuple-element.39), channel_id=1, source_target_pairs={{0,1},{1,0},{2,3},{3,2},{4,5},{5,4},{6,7},{7,6},{8,9},{9,8},{10,11... | collective-permute-start | bytes 7077896 | tf_op jit(solution)/shard_map/ppermute | solution.py:26
  8.2 2.6 %collective-permute-start.2 = (bf16[264,512]{1,0:T(8,128)(2,1)}, bf16[264,512]{1,0:T(8,128)(2,1)S(1)}, u32[]{:S(2)}, u32[]{:S(2)}) collective-permute-start(bf16[264,512]{1,0:T(8,128)(2,1)} %get-tuple-element.31), channel_id=1, source_target_pairs={{0,4},{1,5},{2,6},{3,7},{4,0},{5,1},{6,2},{7,3},{8,12},{9,13},{10,... | collective-permute-start | bytes 811016 | tf_op jit(solution)/shard_map/ppermute | solution.py:21
  10.8 1.6 %collective-permute-start.3 = (bf16[264,512]{1,0:T(8,128)(2,1)}, bf16[264,512]{1,0:T(8,128)(2,1)S(1)}, u32[]{:S(2)}, u32[]{:S(2)}) collective-permute-start(bf16[264,512]{1,0:T(8,128)(2,1)} %get-tuple-element.28.kept_ref), channel_id=1, source_target_pairs={{0,2},{1,3},{2,0},{3,1},{4,6},{5,7},{6,4},{7,5},{8,10},{9,11},{10,... | collective-permute-start | bytes 811016 | tf_op jit(solution)/shard_map/ppermute | solution.py:26
  12.3 5.0 %collective-permute-done.1.x_ref.up_ref = bf16[128,2048]{1,0:T(8,128)(2,1)S(1)} collective-permute-done((bf16[128,2048]{1,0:T(8,128)(2,1)S(1)}, bf16[128,2048]{1,0:T(8,128)(2,1)S(1)}, u32[]{:S(2)}, u32[]{:S(2)}) %collective-permute-start.1) | collective-permute-done | bytes 524320 | tf_op jit(solution)/shard_map/ppermute | solution.py:21
  18.2 5.0 %collective-permute-start.5 = (bf16[264,512]{1,0:T(8,128)(2,1)S(1)}, bf16[264,512]{1,0:T(8,128)(2,1)S(1)}, u32[]{:S(2)}, u32[]{:S(2)}) collective-permute-start(bf16[264,512]{1,0:T(8,128)(2,1)S(1)} %get-tuple-element.36), channel_id=1, source_target_pairs={{0,4},{1,5},{2,6},{3,7},{4,0},{5,1},{6,2},{7,3},{8,12},{9,13},{10,... | collective-permute-start | bytes 811016 | tf_op jit(solution)/shard_map/ppermute | solution.py:21
  23.4 1.4 %collective-permute-start.6 = (bf16[264,512]{1,0:T(8,128)(2,1)S(1)}, bf16[264,512]{1,0:T(8,128)(2,1)S(1)}, u32[]{:S(2)}, u32[]{:S(2)}) collective-permute-start(bf16[264,512]{1,0:T(8,128)(2,1)S(1)} %get-tuple-element.37.refs_3_), channel_id=1, source_target_pairs={{0,2},{1,3},{2,0},{3,1},{4,6},{5,7},{6,4},{7,5},{8,10},{9,11},{10,... | collective-permute-start | bytes 811016 | tf_op jit(solution)/shard_map/ppermute | solution.py:26
  24.8 1.2 %collective-permute-done.3.refs_2_ = bf16[264,512]{1,0:T(8,128)(2,1)S(1)} collective-permute-done((bf16[264,512]{1,0:T(8,128)(2,1)}, bf16[264,512]{1,0:T(8,128)(2,1)S(1)}, u32[]{:S(2)}, u32[]{:S(2)}) %collective-permute-start.3) | collective-permute-done | bytes 270368 | tf_op jit(solution)/shard_map/ppermute | solution.py:26
  26.1 0.9 copy-done.4
  28.0 2.0 %collective-permute-start.9 = (bf16[264,512]{1,0:T(8,128)(2,1)S(1)}, bf16[264,512]{1,0:T(8,128)(2,1)S(1)}, u32[]{:S(2)}, u32[]{:S(2)}) collective-permute-start(bf16[264,512]{1,0:T(8,128)(2,1)S(1)} %get-tuple-element.43), channel_id=1, source_target_pairs={{0,4},{1,5},{2,6},{3,7},{4,0},{5,1},{6,2},{7,3},{8,12},{9,13},{10,... | collective-permute-start | bytes 811016 | tf_op jit(solution)/shard_map/ppermute | solution.py:21
  29.9 6.2 %collective-permute-done.5.refs_4_ = bf16[264,512]{1,0:T(8,128)(2,1)S(1)} collective-permute-done((bf16[264,512]{1,0:T(8,128)(2,1)S(1)}, bf16[264,512]{1,0:T(8,128)(2,1)S(1)}, u32[]{:S(2)}, u32[]{:S(2)}) %collective-permute-start.5) | collective-permute-done | bytes 270368 | tf_op jit(solution)/shard_map/ppermute | solution.py:21
  36.2 1.2 %collective-permute-start.10 = (bf16[264,512]{1,0:T(8,128)(2,1)S(1)}, bf16[264,512]{1,0:T(8,128)(2,1)S(1)}, u32[]{:S(2)}, u32[]{:S(2)}) collective-permute-start(bf16[264,512]{1,0:T(8,128)(2,1)S(1)} %get-tuple-element.44.refs_0_), channel_id=1, source_target_pairs={{0,2},{1,3},{2,0},{3,1},{4,6},{5,7},{6,4},{7,5},{8,10},{9,11},{10,... | collective-permute-start | bytes 811016 | tf_op jit(solution)/shard_map/ppermute | solution.py:26
  37.4 5.8 %collective-permute-done.6.refs_5_ = bf16[264,512]{1,0:T(8,128)(2,1)S(1)} collective-permute-done((bf16[264,512]{1,0:T(8,128)(2,1)S(1)}, bf16[264,512]{1,0:T(8,128)(2,1)S(1)}, u32[]{:S(2)}, u32[]{:S(2)}) %collective-permute-start.6) | collective-permute-done | bytes 270368 | tf_op jit(solution)/shard_map/ppermute | solution.py:26
  43.2 5.8 %collective-permute-done.4.refs_0_ = bf16[264,512]{1,0:T(8,128)(2,1)S(1)} collective-permute-done((bf16[264,512]{1,0:T(8,128)(2,1)S(1)}, bf16[264,512]{1,0:T(8,128)(2,1)S(1)}, u32[]{:S(2)}, u32[]{:S(2)}) %collective-permute-start.4) | collective-permute-done | bytes 270368 | tf_op jit(solution)/shard_map/ppermute | solution.py:26
  49.0 5.8 %collective-permute-done.10.refs_2_ = bf16[264,512]{1,0:T(8,128)(2,1)S(1)} collective-permute-done((bf16[264,512]{1,0:T(8,128)(2,1)S(1)}, bf16[264,512]{1,0:T(8,128)(2,1)S(1)}, u32[]{:S(2)}, u32[]{:S(2)}) %collective-permute-start.10) | collective-permute-done | bytes 270368 | tf_op jit(solution)/shard_map/ppermute | solution.py:26
  54.8 1.0 collective-permute-start.11
  55.8 4.8 %collective-permute-done.7.refs_1_ = bf16[264,512]{1,0:T(8,128)(2,1)S(1)} collective-permute-done((bf16[264,512]{1,0:T(8,128)(2,1)S(1)}, bf16[264,512]{1,0:T(8,128)(2,1)S(1)}, u32[]{:S(2)}, u32[]{:S(2)}) %collective-permute-start.7) | collective-permute-done | bytes 270368 | tf_op jit(solution)/shard_map/ppermute | solution.py:26
  60.6 2.5 %experts_bwd_far.1 = bf16[264,512]{1,0:T(8,128)(2,1)S(1)} custom-call(bf16[264,512]{1,0:T(8,128)(2,1)S(1)} %collective-permute-done.4.refs_0_, bf16[264,512]{1,0:T(8,128)(2,1)S(1)} %collective-permute-done.7.refs_1_, bf16[192,2048]{1,0:T(8,128)(2,1)S(1)} %bitcast.18, bf16[192,2048]{1,0:T(8,128)(2,1)S(1)} %bitcast.22, bf16[192,2048]{1,0:T(8,128)(2,1)S(1)} %bitcast.26, ...), custom_call_target="tpu_custom_call" | custom-call | flops 1000 | bytes 1000 | tf_op jit(solution)/shard_map/experts_bwd_far/pallas_call | solution.py:301
  63.1 1.0 %collective-permute-start.14 = (bf16[264,512]{1,0:T(8,128)(2,1)S(1)}, bf16[264,512]{1,0:T(8,128)(2,1)S(1)}, u32[]{:S(2)}, u32[]{:S(2)}) collective-permute-start(bf16[264,512]{1,0:T(8,128)(2,1)S(1)} %experts_bwd_far.1), channel_id=1, source_target_pairs={{0,2},{1,3},{2,0},{3,1},{4,6},{5,7},{6,4},{7,5},{8,10},{9,11},{10,... | collective-permute-start | bytes 811016 | tf_op jit(solution)/shard_map/ppermute | solution.py:26
  64.2 2.9 %experts_bwd_near.1 = (f32[264,512]{1,0:T(8,128)S(1)}, f32[264,512]{1,0:T(8,128)S(1)}, bf16[264,512]{1,0:T(8,128)(2,1)S(1)}) custom-call(bf16[264,512]{1,0:T(8,128)(2,1)S(1)} %get-tuple-element.40.refs_0_, bf16[264,512]{1,0:T(8,128)(2,1)S(1)} %collective-permute-done.2.refs_1_, bf16[264,512]{1,0:T(8,128)(2,1)S(1)} %collective-permute-done.3.refs_2_, ...), custom_call_target="tpu_custom_call" | custom-call | flops 1000 | bytes 1000 | tf_op jit(solution)/shard_map/experts_bwd_near/pallas_call | solution.py:301
  67.1 2.3 %experts_fwd.1 = (f32[264,512]{1,0:T(8,128)S(1)}, f32[264,512]{1,0:T(8,128)S(1)}, bf16[264,512]{1,0:T(8,128)(2,1)S(1)}, bf16[264,512]{1,0:T(8,128)(2,1)S(1)}) custom-call(bf16[264,512]{1,0:T(8,128)(2,1)S(1)} %get-tuple-element.44.refs_0_, bf16[264,512]{1,0:T(8,128)(2,1)S(1)} %collective-permute-done.9.refs_1_, ...), custom_call_target="tpu_custom_call" | custom-call | flops 1000 | bytes 1000 | tf_op jit(solution)/shard_map/experts_fwd/pallas_call | solution.py:301
  69.3 1.1 %collective-permute-start.12 = (bf16[264,512]{1,0:T(8,128)(2,1)S(1)}, bf16[264,512]{1,0:T(8,128)(2,1)S(1)}, u32[]{:S(2)}, u32[]{:S(2)}) collective-permute-start(bf16[264,512]{1,0:T(8,128)(2,1)S(1)} %get-tuple-element.47), channel_id=1, source_target_pairs={{0,2},{1,3},{2,0},{3,1},{4,6},{5,7},{6,4},{7,5},{8,10},{9,11},{10,... | collective-permute-start | bytes 811016 | tf_op jit(solution)/shard_map/ppermute | solution.py:26
  70.4 1.4 %collective-permute-done.14 = bf16[264,512]{1,0:T(8,128)(2,1)S(1)} collective-permute-done((bf16[264,512]{1,0:T(8,128)(2,1)S(1)}, bf16[264,512]{1,0:T(8,128)(2,1)S(1)}, u32[]{:S(2)}, u32[]{:S(2)}) %collective-permute-start.14) | collective-permute-done | bytes 270368 | tf_op jit(solution)/shard_map/ppermute | solution.py:26
  71.9 3.4 %collective-permute-start.15 = (bf16[264,512]{1,0:T(8,128)(2,1)S(1)}, bf16[264,512]{1,0:T(8,128)(2,1)S(1)}, u32[]{:S(2)}, u32[]{:S(2)}) collective-permute-start(bf16[264,512]{1,0:T(8,128)(2,1)S(1)} %add_convert_fusion), channel_id=1, source_target_pairs={{0,4},{1,5},{2,6},{3,7},{4,0},{5,1},{6,2},{7,3},{8,12},{9,13},{10,... | collective-permute-start | bytes 811016 | tf_op jit(solution)/shard_map/ppermute | solution.py:21
  75.4 2.5 %collective-permute-start.17 = (bf16[264,512]{1,0:T(8,128)(2,1)S(1)}, bf16[264,512]{1,0:T(8,128)(2,1)S(1)}, u32[]{:S(2)}, u32[]{:S(2)}) collective-permute-start(bf16[264,512]{1,0:T(8,128)(2,1)S(1)} %get-tuple-element.53), channel_id=1, source_target_pairs={{0,2},{1,3},{2,0},{3,1},{4,6},{5,7},{6,4},{7,5},{8,10},{9,11},{10,... | collective-permute-start | bytes 811016 | tf_op jit(solution)/shard_map/ppermute | solution.py:26
  77.8 6.4 %collective-permute-done.12 = bf16[264,512]{1,0:T(8,128)(2,1)S(1)} collective-permute-done((bf16[264,512]{1,0:T(8,128)(2,1)S(1)}, bf16[264,512]{1,0:T(8,128)(2,1)S(1)}, u32[]{:S(2)}, u32[]{:S(2)}) %collective-permute-start.12) | collective-permute-done | bytes 270368 | tf_op jit(solution)/shard_map/ppermute | solution.py:26
  84.4 1.8 %collective-permute-done.15.refs_2_ = bf16[264,512]{1,0:T(8,128)(2,1)S(1)} collective-permute-done((bf16[264,512]{1,0:T(8,128)(2,1)S(1)}, bf16[264,512]{1,0:T(8,128)(2,1)S(1)}, u32[]{:S(2)}, u32[]{:S(2)}) %collective-permute-start.15) | collective-permute-done | bytes 270368 | tf_op jit(solution)/shard_map/ppermute | solution.py:21
  86.2 3.6 %collective-permute-start.16 = (bf16[264,512]{1,0:T(8,128)(2,1)S(1)}, bf16[264,512]{1,0:T(8,128)(2,1)S(1)}, u32[]{:S(2)}, u32[]{:S(2)}) collective-permute-start(bf16[264,512]{1,0:T(8,128)(2,1)S(1)} %get-tuple-element.51), channel_id=1, source_target_pairs={{0,2},{1,3},{2,0},{3,1},{4,6},{5,7},{6,4},{7,5},{8,10},{9,11},{10,... | collective-permute-start | bytes 811016 | tf_op jit(solution)/shard_map/ppermute | solution.py:26
  89.8 6.1 %collective-permute-done.17.refs_1_ = bf16[264,512]{1,0:T(8,128)(2,1)S(1)} collective-permute-done((bf16[264,512]{1,0:T(8,128)(2,1)S(1)}, bf16[264,512]{1,0:T(8,128)(2,1)S(1)}, u32[]{:S(2)}, u32[]{:S(2)}) %collective-permute-start.17) | collective-permute-done | bytes 270368 | tf_op jit(solution)/shard_map/ppermute | solution.py:26
  95.8 2.0 %home_bwd.1 = bf16[128,2048]{1,0:T(8,128)(2,1)} custom-call(s32[1]{0:T(128)} %bitcast.own_ref, s32[1,128]{1,0:T(1,128)S(1)} %bitcast.36, f32[1,128]{1,0:T(1,128)S(1)} %bitcast.39, f32[1,2048]{1,0:T(1,128)S(1)} %copy-done.5, bf16[128,2048]{1,0:T(8,128)(2,1)S(1)} %bitcast.30, bf16[128,2048]{1,0:T(8,128)(2,1)S(1)} %collective-permute-done.1.x_ref.up_ref, ...), custom_call_target="tpu_custom_call" | custom-call | flops 1000 | bytes 1000 | tf_op jit(solution)/shard_map/home_bwd/pallas_call | solution.py:316
  98.5 2.4 %collective-permute-done.16.theirs = bf16[264,512]{1,0:T(8,128)(2,1)S(1)} collective-permute-done((bf16[264,512]{1,0:T(8,128)(2,1)S(1)}, bf16[264,512]{1,0:T(8,128)(2,1)S(1)}, u32[]{:S(2)}, u32[]{:S(2)}) %collective-permute-start.16) | collective-permute-done | bytes 270368 | tf_op jit(solution)/shard_map/ppermute | solution.py:26
  100.9 1.4 %home_fwd.1 = bf16[128,2048]{1,0:T(8,128)(2,1)} custom-call(s32[1]{0:T(128)} %bitcast.own_ref, s32[1,128]{1,0:T(1,128)S(1)} %bitcast.33, f32[1,128]{1,0:T(1,128)S(1)} %bitcast.38, f32[128,2048]{1,0:T(8,128)S(1)} %home_fwd_crossed.1.sum_ref, f32[264,512]{1,0:T(8,128)S(1)} %get-tuple-element.48.mine, bf16[264,512]{1,0:T(8,128)(2,1)S(1)} %collective-permute-done.16.theirs), custom_call_target="tpu_custom_call" | custom-call | flops 1000 | bytes 1000 | tf_op jit(solution)/shard_map/home_fwd/pallas_call | solution.py:330
  (37 shorter events, 3.6 us)
Async XLA Ops:
  0.6 59.9 %copy-start.1 = (bf16[1,2048,192]{1,2,0:T(8,128)(2,1)S(1)}, bf16[1,2048,192]{1,2,0:T(8,128)(2,1)}, u32[]{:S(2)}) copy-start(bf16[1,2048,192]{1,2,0:T(8,128)(2,1)} %param.16) | copy-start | bytes 2359300
  0.6 59.9 %copy-start.2 = (bf16[1,192,2048]{2,1,0:T(8,128)(2,1)S(1)}, bf16[1,192,2048]{2,1,0:T(8,128)(2,1)}, u32[]{:S(2)}) copy-start(bf16[1,192,2048]{2,1,0:T(8,128)(2,1)} %param.17) | copy-start | bytes 2359300
  0.7 59.9 %copy-start = (bf16[1,2048,192]{1,2,0:T(8,128)(2,1)S(1)}, bf16[1,2048,192]{1,2,0:T(8,128)(2,1)}, u32[]{:S(2)}) copy-start(bf16[1,2048,192]{1,2,0:T(8,128)(2,1)} %param.15) | copy-start | bytes 2359300
  0.7 16.7 %copy-start.7 = (s32[1,128,1]{1,2,0:T(1,128)S(1)}, s32[1,128,1]{1,2,0:T(1,128)}, u32[]{:S(2)}) copy-start(s32[1,128,1]{1,2,0:T(1,128)} %param.20) | copy-start | bytes 1540
  0.7 25.4 %copy-start.5 = (f32[1,2048]{1,0:T(1,128)S(1)}, f32[1,2048]{1,0:T(1,128)}, u32[]{:S(2)}) copy-start(f32[1,2048]{1,0:T(1,128)} %gain_ref.3) | copy-start | bytes 24580
  0.7 6.8 %copy-start.10 = (bf16[1,128,2048]{2,1,0:T(8,128)(2,1)S(1)}, bf16[1,128,2048]{2,1,0:T(8,128)(2,1)}, u32[]{:S(2)}) copy-start(bf16[1,128,2048]{2,1,0:T(8,128)(2,1)} %param.13) | copy-start | bytes 1572868
  0.7 25.4 %copy-start.6 = (s32[1,128,1]{1,2,0:T(1,128)S(1)}, s32[1,128,1]{1,2,0:T(1,128)}, u32[]{:S(2)}) copy-start(s32[1,128,1]{1,2,0:T(1,128)} %param.18) | copy-start | bytes 1540
  4.5 56.1 %collective-permute-start.8 = (bf16[576,2048]{1,0:T(8,128)(2,1)}, bf16[576,2048]{1,0:T(8,128)(2,1)S(1)}, u32[]{:S(2)}, u32[]{:S(2)}) collective-permute-start(bf16[576,2048]{1,0:T(8,128)(2,1)} %get-tuple-element.39), channel_id=1, source_target_pairs={{0,1},{1,0},{2,3},{3,2},{4,5},{5,4},{6,7},{7,6},{8,9},{9,8},{10,11... | collective-permute-start | bytes 7077896 | tf_op jit(solution)/shard_map/ppermute | solution.py:26
  7.5 9.9 %collective-permute-start.1 = (bf16[128,2048]{1,0:T(8,128)(2,1)S(1)}, bf16[128,2048]{1,0:T(8,128)(2,1)S(1)}, u32[]{:S(2)}, u32[]{:S(2)}) collective-permute-start(bf16[128,2048]{1,0:T(8,128)(2,1)S(1)} %bitcast.42), channel_id=1, source_target_pairs={{0,24},{8,0},{16,8},{24,16},{1,25},{9,1},{17,9},{25,17},{2,26},{10... | collective-permute-start | bytes 1572872 | tf_op jit(solution)/shard_map/ppermute | solution.py:21
  8.2 15.2 %collective-permute-start.2 = (bf16[264,512]{1,0:T(8,128)(2,1)}, bf16[264,512]{1,0:T(8,128)(2,1)S(1)}, u32[]{:S(2)}, u32[]{:S(2)}) collective-permute-start(bf16[264,512]{1,0:T(8,128)(2,1)} %get-tuple-element.31), channel_id=1, source_target_pairs={{0,4},{1,5},{2,6},{3,7},{4,0},{5,1},{6,2},{7,3},{8,12},{9,13},{10,... | collective-permute-start | bytes 811016 | tf_op jit(solution)/shard_map/ppermute | solution.py:21
  10.8 15.3 %collective-permute-start = (bf16[128,2048]{1,0:T(8,128)(2,1)}, bf16[128,2048]{1,0:T(8,128)(2,1)S(1)}, u32[]{:S(2)}, u32[]{:S(2)}) collective-permute-start(bf16[128,2048]{1,0:T(8,128)(2,1)} %bitcast.43), channel_id=1, source_target_pairs={{0,8},{8,16},{16,24},{24,0},{1,9},{9,17},{17,25},{25,1},{2,10},{10... | collective-permute-start | bytes 1572872 | tf_op jit(solution)/shard_map/ppermute | solution.py:21
  10.8 15.3 %collective-permute-start.3 = (bf16[264,512]{1,0:T(8,128)(2,1)}, bf16[264,512]{1,0:T(8,128)(2,1)S(1)}, u32[]{:S(2)}, u32[]{:S(2)}) collective-permute-start(bf16[264,512]{1,0:T(8,128)(2,1)} %get-tuple-element.28.kept_ref), channel_id=1, source_target_pairs={{0,2},{1,3},{2,0},{3,1},{4,6},{5,7},{6,4},{7,5},{8,10},{9,11},{10,... | collective-permute-start | bytes 811016 | tf_op jit(solution)/shard_map/ppermute | solution.py:26
  18.2 17.9 %collective-permute-start.5 = (bf16[264,512]{1,0:T(8,128)(2,1)S(1)}, bf16[264,512]{1,0:T(8,128)(2,1)S(1)}, u32[]{:S(2)}, u32[]{:S(2)}) collective-permute-start(bf16[264,512]{1,0:T(8,128)(2,1)S(1)} %get-tuple-element.36), channel_id=1, source_target_pairs={{0,4},{1,5},{2,6},{3,7},{4,0},{5,1},{6,2},{7,3},{8,12},{9,13},{10,... | collective-permute-start | bytes 811016 | tf_op jit(solution)/shard_map/ppermute | solution.py:21
  23.4 19.8 %collective-permute-start.6 = (bf16[264,512]{1,0:T(8,128)(2,1)S(1)}, bf16[264,512]{1,0:T(8,128)(2,1)S(1)}, u32[]{:S(2)}, u32[]{:S(2)}) collective-permute-start(bf16[264,512]{1,0:T(8,128)(2,1)S(1)} %get-tuple-element.37.refs_3_), channel_id=1, source_target_pairs={{0,2},{1,3},{2,0},{3,1},{4,6},{5,7},{6,4},{7,5},{8,10},{9,11},{10,... | collective-permute-start | bytes 811016 | tf_op jit(solution)/shard_map/ppermute | solution.py:26
  26.1 22.9 %collective-permute-start.4 = (bf16[264,512]{1,0:T(8,128)(2,1)S(1)}, bf16[264,512]{1,0:T(8,128)(2,1)S(1)}, u32[]{:S(2)}, u32[]{:S(2)}) collective-permute-start(bf16[264,512]{1,0:T(8,128)(2,1)S(1)} %collective-permute-done.2.refs_1_), channel_id=1, source_target_pairs={{0,2},{1,3},{2,0},{3,1},{4,6},{5,7},{6,4},{7,5},{8,10},{9,11},{10,... | collective-permute-start | bytes 811016 | tf_op jit(solution)/shard_map/ppermute | solution.py:26
  26.1 1.0 copy-start.4
  28.0 21.0 %collective-permute-start.9 = (bf16[264,512]{1,0:T(8,128)(2,1)S(1)}, bf16[264,512]{1,0:T(8,128)(2,1)S(1)}, u32[]{:S(2)}, u32[]{:S(2)}) collective-permute-start(bf16[264,512]{1,0:T(8,128)(2,1)S(1)} %get-tuple-element.43), channel_id=1, source_target_pairs={{0,4},{1,5},{2,6},{3,7},{4,0},{5,1},{6,2},{7,3},{8,12},{9,13},{10,... | collective-permute-start | bytes 811016 | tf_op jit(solution)/shard_map/ppermute | solution.py:21
  36.2 18.6 %collective-permute-start.10 = (bf16[264,512]{1,0:T(8,128)(2,1)S(1)}, bf16[264,512]{1,0:T(8,128)(2,1)S(1)}, u32[]{:S(2)}, u32[]{:S(2)}) collective-permute-start(bf16[264,512]{1,0:T(8,128)(2,1)S(1)} %get-tuple-element.44.refs_0_), channel_id=1, source_target_pairs={{0,2},{1,3},{2,0},{3,1},{4,6},{5,7},{6,4},{7,5},{8,10},{9,11},{10,... | collective-permute-start | bytes 811016 | tf_op jit(solution)/shard_map/ppermute | solution.py:26
  43.2 17.4 %collective-permute-start.7 = (bf16[264,512]{1,0:T(8,128)(2,1)S(1)}, bf16[264,512]{1,0:T(8,128)(2,1)S(1)}, u32[]{:S(2)}, u32[]{:S(2)}) collective-permute-start(bf16[264,512]{1,0:T(8,128)(2,1)S(1)} %collective-permute-done.5.refs_4_), channel_id=1, source_target_pairs={{0,2},{1,3},{2,0},{3,1},{4,6},{5,7},{6,4},{7,5},{8,10},{9,11},{10,... | collective-permute-start | bytes 811016 | tf_op jit(solution)/shard_map/ppermute | solution.py:26
  54.8 12.3 %collective-permute-start.11 = (bf16[264,512]{1,0:T(8,128)(2,1)S(1)}, bf16[264,512]{1,0:T(8,128)(2,1)S(1)}, u32[]{:S(2)}, u32[]{:S(2)}) collective-permute-start(bf16[264,512]{1,0:T(8,128)(2,1)S(1)} %collective-permute-done.9.refs_1_), channel_id=1, source_target_pairs={{0,2},{1,3},{2,0},{3,1},{4,6},{5,7},{6,4},{7,5},{8,10},{9,11},{10,... | collective-permute-start | bytes 811016 | tf_op jit(solution)/shard_map/ppermute | solution.py:26
  63.1 8.7 %collective-permute-start.14 = (bf16[264,512]{1,0:T(8,128)(2,1)S(1)}, bf16[264,512]{1,0:T(8,128)(2,1)S(1)}, u32[]{:S(2)}, u32[]{:S(2)}) collective-permute-start(bf16[264,512]{1,0:T(8,128)(2,1)S(1)} %experts_bwd_far.1), channel_id=1, source_target_pairs={{0,2},{1,3},{2,0},{3,1},{4,6},{5,7},{6,4},{7,5},{8,10},{9,11},{10,... | collective-permute-start | bytes 811016 | tf_op jit(solution)/shard_map/ppermute | solution.py:26
  67.0 28.8 %copy-start.9 = (f32[1,128,1]{1,2,0:T(1,128)S(1)}, f32[1,128,1]{1,2,0:T(1,128)}, u32[]{:S(2)}) copy-start(f32[1,128,1]{1,2,0:T(1,128)} %param.21) | copy-start | bytes 1540
  69.3 26.5 %copy-start.3 = (bf16[1,128,2048]{2,1,0:T(8,128)(2,1)S(1)}, bf16[1,128,2048]{2,1,0:T(8,128)(2,1)}, u32[]{:S(2)}) copy-start(bf16[1,128,2048]{2,1,0:T(8,128)(2,1)} %param.12) | copy-start | bytes 1572868
  69.3 14.9 %collective-permute-start.12 = (bf16[264,512]{1,0:T(8,128)(2,1)S(1)}, bf16[264,512]{1,0:T(8,128)(2,1)S(1)}, u32[]{:S(2)}, u32[]{:S(2)}) collective-permute-start(bf16[264,512]{1,0:T(8,128)(2,1)S(1)} %get-tuple-element.47), channel_id=1, source_target_pairs={{0,2},{1,3},{2,0},{3,1},{4,6},{5,7},{6,4},{7,5},{8,10},{9,11},{10,... | collective-permute-start | bytes 811016 | tf_op jit(solution)/shard_map/ppermute | solution.py:26
  71.9 26.0 %copy-start.8 = (f32[1,128,1]{1,2,0:T(1,128)S(1)}, f32[1,128,1]{1,2,0:T(1,128)}, u32[]{:S(2)}) copy-start(f32[1,128,1]{1,2,0:T(1,128)} %param.19) | copy-start | bytes 1540
  71.9 14.2 %collective-permute-start.15 = (bf16[264,512]{1,0:T(8,128)(2,1)S(1)}, bf16[264,512]{1,0:T(8,128)(2,1)S(1)}, u32[]{:S(2)}, u32[]{:S(2)}) collective-permute-start(bf16[264,512]{1,0:T(8,128)(2,1)S(1)} %add_convert_fusion), channel_id=1, source_target_pairs={{0,4},{1,5},{2,6},{3,7},{4,0},{5,1},{6,2},{7,3},{8,12},{9,13},{10,... | collective-permute-start | bytes 811016 | tf_op jit(solution)/shard_map/ppermute | solution.py:21
  75.4 20.5 %collective-permute-start.17 = (bf16[264,512]{1,0:T(8,128)(2,1)S(1)}, bf16[264,512]{1,0:T(8,128)(2,1)S(1)}, u32[]{:S(2)}, u32[]{:S(2)}) collective-permute-start(bf16[264,512]{1,0:T(8,128)(2,1)S(1)} %get-tuple-element.53), channel_id=1, source_target_pairs={{0,2},{1,3},{2,0},{3,1},{4,6},{5,7},{6,4},{7,5},{8,10},{9,11},{10,... | collective-permute-start | bytes 811016 | tf_op jit(solution)/shard_map/ppermute | solution.py:26
  84.3 13.5 %collective-permute-start.13 = (bf16[264,512]{1,0:T(8,128)(2,1)S(1)}, bf16[264,512]{1,0:T(8,128)(2,1)S(1)}, u32[]{:S(2)}, u32[]{:S(2)}) collective-permute-start(bf16[264,512]{1,0:T(8,128)(2,1)S(1)} %add_convert_fusion.1), channel_id=1, source_target_pairs={{0,4},{1,5},{2,6},{3,7},{4,0},{5,1},{6,2},{7,3},{8,12},{9,13},{10,... | collective-permute-start | bytes 811016 | tf_op jit(solution)/shard_map/ppermute | solution.py:21
  86.2 14.7 %collective-permute-start.16 = (bf16[264,512]{1,0:T(8,128)(2,1)S(1)}, bf16[264,512]{1,0:T(8,128)(2,1)S(1)}, u32[]{:S(2)}, u32[]{:S(2)}) collective-permute-start(bf16[264,512]{1,0:T(8,128)(2,1)S(1)} %get-tuple-element.51), channel_id=1, source_target_pairs={{0,2},{1,3},{2,0},{3,1},{4,6},{5,7},{6,4},{7,5},{8,10},{9,11},{10,... | collective-permute-start | bytes 811016 | tf_op jit(solution)/shard_map/ppermute | solution.py:26
